TPU v7x, 32 devices: a whole 2x2x4 slice. The times are simulated.
32 devices in a mesh: section: 2 (over x), seq: 4 (over y, core), wt: 4 (over z).
Axes of the slice: x: 2, y: 2, z: 4, core: 2. Of those that a mesh axis runs over, the one named last changes fastest.
Arguments:
- inputs: bfloat16 [8, 1280, 1024], P('wt', 'seq'), may hold values from -6 to 6
- lengths: int32 [8, 8], P('wt'), may hold values from 1 to 1273, as said below
- cotangent: bfloat16 [8, 1280, 1024], P('wt', 'seq'), may hold values from -6 to 6
- gain_attn: bfloat16 [2, 1024], P('section', ('seq', 'wt')), may hold values from 0.5 to 1.5
- w_query: bfloat16 [2, 1024, 1024], P('section', ('seq', 'wt')), may hold values from -0.1875 to 0.1875
- w_key: bfloat16 [2, 1024, 1024], P('section', ('seq', 'wt')), may hold values from -0.1875 to 0.1875
- w_value: bfloat16 [2, 1024, 1024], P('section', ('seq', 'wt')), may hold values from -0.1875 to 0.1875
- w_out: bfloat16 [2, 1024, 1024], P('section', ('seq', 'wt')), may hold values from -0.75 to 0.75
- gain_mlp: bfloat16 [2, 1024], P('section', ('seq', 'wt')), may hold values from 0.5 to 1.5
- w_gate: bfloat16 [2, 1024, 2816], P('section', ('seq', 'wt')), may hold values from -0.1875 to 0.1875
- w_up: bfloat16 [2, 1024, 2816], P('section', ('seq', 'wt')), may hold values from -0.1875 to 0.1875
- w_down: bfloat16 [2, 2816, 1024], P('section', ('seq', 'wt')), may hold values from -0.15625 to 0.15625
Outputs:
- activations: bfloat16 [2, 8, 1280, 1024], P('section', 'wt', 'seq')
- input_grads: bfloat16 [2, 8, 1280, 1024], P('section', 'wt', 'seq')
- grad_gain_attn: float32 [2, 1024], P('section', ('seq', 'wt'))
- grad_query: float32 [2, 1024, 1024], P('section', ('seq', 'wt'))
- grad_key: float32 [2, 1024, 1024], P('section', ('seq', 'wt'))
- grad_value: float32 [2, 1024, 1024], P('section', ('seq', 'wt'))
- grad_out: float32 [2, 1024, 1024], P('section', ('seq', 'wt'))
- grad_gain_mlp: float32 [2, 1024], P('section', ('seq', 'wt'))
- grad_gate: float32 [2, 1024, 2816], P('section', ('seq', 'wt'))
- grad_up: float32 [2, 1024, 2816], P('section', ('seq', 'wt'))
- grad_down: float32 [2, 2816, 1024], P('section', ('seq', 'wt'))
Inputs may be any that keep to these rules, and one draw needn't show every extreme that they name: `lengths`: each row lists the token counts of 8 documents that fill one sequence of 1280 tokens exactly, each 1 or more. In each aligned group of 2 rows, one row drawn from the seed is a document of 1273 tokens followed by 8 - 1 documents of one token.
All inputs are finite; a program needn't handle non-finite values.
Results may differ from a plain program's by a relative error of at most 0.025.
Values may be sent and summed in bfloat16 or wider, within the bound.
No kernel may reach another device: no remote copies, remote signals or barrier semaphores. Data moves between devices by JAX's collectives and lax.ppermute only.
A program may use at most 320 MiB of HBM per device.

v0:
```python
import jax
import jax.numpy as jnp
from jax import lax
from jax.sharding import PartitionSpec as P

HEAD_DIM = 64
RADIUS = 127


EPSILON = 1e-06


def with_halo(cells, sides, width):
    for axis, dim in sides:
        count = lax.axis_size(axis)
        ends = count - 1
        head = lax.slice_in_dim(cells, 0, width, axis=dim)
        tail = lax.slice_in_dim(cells, cells.shape[dim] - width, cells.shape[dim], axis=dim)
        cells = jnp.concatenate(
            [
                lax.ppermute(tail, axis, [(i, (i + 1) % count) for i in range(ends)]),
                cells,
                lax.ppermute(head, axis, [((i + 1) % count, i) for i in range(ends)]),
            ],
            axis=dim,
        )
    return cells


def shifted(shard, axis, by):
    length = lax.axis_size(axis)
    pairs = [(i, i + by) for i in range(length) if 0 <= i + by < length]
    return lax.ppermute(shard, axis, pairs)


def rms_scale(values, gain_vec):
    return (
        values * lax.rsqrt(jnp.mean(values * values, axis=-1, keepdims=True) + EPSILON) * gain_vec
    )


def gated_unit(gate_pre, up_pre):
    return jax.nn.gelu(gate_pre, approximate=True) * up_pre


def window_allowed(lengths_row, shard_no, rows_local, seq_len):
    key_span = rows_local + 2 * RADIUS
    doc_ends = jnp.cumsum(lengths_row)
    key_pos = shard_no * rows_local - RADIUS + jnp.arange(key_span, dtype=jnp.int32)
    key_seg = jnp.sum((key_pos[:, None] >= doc_ends[None, :]).astype(jnp.int32), axis=-1)
    inside = (key_pos >= 0) & (key_pos < seq_len)
    key_seg = jnp.where(inside, key_seg, -1)
    query_seg = key_seg[RADIUS : RADIUS + rows_local]
    offset = jnp.arange(rows_local)[:, None] + RADIUS - jnp.arange(key_span)[None, :]
    return (jnp.abs(offset) <= RADIUS) & (query_seg[:, None] == key_seg[None, :])


def layer_forward(layer_in, allowed, params):
    gain_one, query_w, key_w, value_w, out_w, gain_two, gate_w, up_w, down_w = params
    rows_local, model_width = layer_in.shape
    head_count = model_width // HEAD_DIM
    score_scale = HEAD_DIM ** (-0.5)
    source = layer_in.astype(jnp.float32)
    normed = rms_scale(source, gain_one.astype(jnp.float32)).astype(jnp.bfloat16)
    queries = jnp.dot(normed, query_w, preferred_element_type=jnp.float32).astype(jnp.bfloat16)
    keys_local = jnp.dot(normed, key_w, preferred_element_type=jnp.float32).astype(jnp.bfloat16)
    values_local = jnp.dot(normed, value_w, preferred_element_type=jnp.float32).astype(jnp.bfloat16)
    extended = with_halo(jnp.stack([keys_local, values_local]), (("seq", 1),), RADIUS)
    query_heads = queries.reshape(rows_local, head_count, HEAD_DIM)
    key_heads = extended[0].reshape(-1, head_count, HEAD_DIM)
    value_heads = extended[1].reshape(-1, head_count, HEAD_DIM)
    scores = (
        jnp.einsum("qhd,khd->hqk", query_heads, key_heads, preferred_element_type=jnp.float32)
        * score_scale
    )
    masked = jnp.where(allowed[None], scores, -1e30)
    exp_scores = jnp.exp(masked - jnp.max(masked, axis=-1, keepdims=True))
    attn_probs = exp_scores / jnp.sum(exp_scores, axis=-1, keepdims=True)
    probs_low = attn_probs.astype(jnp.bfloat16)
    mixed_heads = jnp.einsum(
        "hqk,khd->qhd", probs_low, value_heads, preferred_element_type=jnp.float32
    )
    mixed_low = mixed_heads.reshape(rows_local, model_width).astype(jnp.bfloat16)
    residual = source + jnp.dot(mixed_low, out_w, preferred_element_type=jnp.float32)
    normed_two = rms_scale(residual, gain_two.astype(jnp.float32)).astype(jnp.bfloat16)
    gate_pre = jnp.dot(normed_two, gate_w, preferred_element_type=jnp.float32)
    up_pre = jnp.dot(normed_two, up_w, preferred_element_type=jnp.float32)
    gated_low = gated_unit(gate_pre, up_pre).astype(jnp.bfloat16)
    result = residual + jnp.dot(gated_low, down_w, preferred_element_type=jnp.float32)
    kept_values = (
        source,
        normed,
        query_heads,
        key_heads,
        value_heads,
        attn_probs,
        probs_low,
        mixed_low,
        residual,
        normed_two,
        gate_pre,
        up_pre,
        gated_low,
    )
    return (result, kept_values)


def settle(extended, head_part, tail_part, row_count):
    center = extended[RADIUS : RADIUS + row_count]
    return (
        center
        + jnp.pad(head_part, ((0, row_count - RADIUS), (0, 0)))
        + jnp.pad(tail_part, ((row_count - RADIUS, 0), (0, 0)))
    )


def weight_products(saved, gain_grads):
    (
        normed,
        grad_queries,
        grad_keys,
        grad_values,
        mixed_low,
        grad_branch,
        normed_two,
        grad_gate_pre,
        grad_up_pre,
        gated_low,
        grad_out,
    ) = saved
    grad_query_w = jnp.dot(normed.T, grad_queries, preferred_element_type=jnp.float32)
    grad_key_w = jnp.dot(normed.T, grad_keys, preferred_element_type=jnp.float32)
    grad_value_w = jnp.dot(normed.T, grad_values, preferred_element_type=jnp.float32)
    grad_out_w = jnp.dot(mixed_low.T, grad_branch, preferred_element_type=jnp.float32)
    grad_gate_w = jnp.dot(normed_two.T, grad_gate_pre, preferred_element_type=jnp.float32)
    grad_up_w = jnp.dot(normed_two.T, grad_up_pre, preferred_element_type=jnp.float32)
    grad_down_w = jnp.dot(gated_low.T, grad_out, preferred_element_type=jnp.float32)
    return (
        gain_grads[0],
        grad_query_w,
        grad_key_w,
        grad_value_w,
        grad_out_w,
        gain_grads[1],
        grad_gate_w,
        grad_up_w,
        grad_down_w,
    )


def layer_backward(layer_in, allowed, params, grad_out):
    gain_one, query_w, key_w, value_w, out_w, gain_two, gate_w, up_w, down_w = params
    rows_local, model_width = layer_in.shape
    head_count = model_width // HEAD_DIM
    score_scale = HEAD_DIM ** (-0.5)
    unused_result, kept_values = layer_forward(layer_in, allowed, params)
    (
        source,
        normed,
        query_heads,
        key_heads,
        value_heads,
        attn_probs,
        probs_low,
        mixed_low,
        residual,
        normed_two,
        gate_pre,
        up_pre,
        gated_low,
    ) = kept_values
    grad_gated = jnp.dot(grad_out, down_w.T, preferred_element_type=jnp.float32)
    unused_unit, unit_back = jax.vjp(gated_unit, gate_pre, up_pre)
    grad_gate_pre, grad_up_pre = unit_back(grad_gated)
    grad_gate_pre = grad_gate_pre.astype(jnp.bfloat16)
    grad_up_pre = grad_up_pre.astype(jnp.bfloat16)
    grad_normed_two = jnp.dot(
        grad_gate_pre, gate_w.T, preferred_element_type=jnp.float32
    ) + jnp.dot(grad_up_pre, up_w.T, preferred_element_type=jnp.float32)
    unused_two, norm_back_two = jax.vjp(rms_scale, residual, gain_two.astype(jnp.float32))
    grad_res_norm, grad_gain_two = norm_back_two(grad_normed_two)
    grad_residual = grad_out.astype(jnp.float32) + grad_res_norm
    grad_branch = grad_residual.astype(jnp.bfloat16)
    grad_mixed = jnp.dot(grad_branch, out_w.T, preferred_element_type=jnp.float32).astype(
        jnp.bfloat16
    )
    grad_mixed = grad_mixed.reshape(rows_local, head_count, HEAD_DIM)
    grad_probs = jnp.einsum(
        "qhd,khd->hqk", grad_mixed, value_heads, preferred_element_type=jnp.float32
    )
    grad_value_ext = jnp.einsum(
        "hqk,qhd->khd", probs_low, grad_mixed, preferred_element_type=jnp.float32
    ).reshape(-1, model_width)
    grad_scores = (
        attn_probs * (grad_probs - jnp.sum(attn_probs * grad_probs, axis=-1, keepdims=True))
    ).astype(jnp.bfloat16)
    grad_queries = (
        jnp.einsum("hqk,khd->qhd", grad_scores, key_heads, preferred_element_type=jnp.float32)
        * score_scale
    )
    grad_queries = grad_queries.reshape(rows_local, model_width).astype(jnp.bfloat16)
    grad_key_ext = (
        jnp.einsum("hqk,qhd->khd", grad_scores, query_heads, preferred_element_type=jnp.float32)
        * score_scale
    ).reshape(-1, model_width)
    from_above = shifted(jnp.stack([grad_key_ext[:RADIUS], grad_value_ext[:RADIUS]]), "seq", -1)
    from_below = shifted(
        jnp.stack([grad_key_ext[RADIUS + rows_local :], grad_value_ext[RADIUS + rows_local :]]),
        "seq",
        1,
    )
    grad_keys = settle(grad_key_ext, from_below[0], from_above[0], rows_local).astype(jnp.bfloat16)
    grad_values = settle(grad_value_ext, from_below[1], from_above[1], rows_local).astype(
        jnp.bfloat16
    )
    grad_normed = jnp.dot(grad_queries, query_w.T, preferred_element_type=jnp.float32)
    grad_normed = grad_normed + jnp.dot(grad_keys, key_w.T, preferred_element_type=jnp.float32)
    grad_normed = grad_normed + jnp.dot(grad_values, value_w.T, preferred_element_type=jnp.float32)
    unused_one, norm_back_one = jax.vjp(rms_scale, source, gain_one.astype(jnp.float32))
    grad_src_norm, grad_gain_one = norm_back_one(grad_normed)
    grad_in = grad_residual + grad_src_norm
    saved = (
        normed,
        grad_queries,
        grad_keys,
        grad_values,
        mixed_low,
        grad_branch,
        normed_two,
        grad_gate_pre,
        grad_up_pre,
        gated_low,
        grad_out,
    )
    return (grad_in, (grad_gain_one, grad_gain_two), saved)


def per_device(
    inputs,
    lengths,
    cotangent,
    gain_attn,
    w_query,
    w_key,
    w_value,
    w_out,
    gain_mlp,
    w_gate,
    w_up,
    w_down,
):
    section_no = lax.axis_index("section")
    shard_no = lax.axis_index("seq")
    micro_count, rows_local, model_width = inputs.shape
    seq_len = rows_local * lax.axis_size("seq")
    first_section = section_no == 0
    allowed_all = [
        window_allowed(lengths[number], shard_no, rows_local, seq_len)
        for number in range(micro_count)
    ]
    own_shards = (
        gain_attn[0],
        w_query[0],
        w_key[0],
        w_value[0],
        w_out[0],
        gain_mlp[0],
        w_gate[0],
        w_up[0],
        w_down[0],
    )

    def fetch_layer():
        return (
            lax.all_gather(gain_attn[0], ("seq", "wt"), axis=0, tiled=True),
            lax.all_gather(w_query[0], ("seq", "wt"), axis=0, tiled=True),
            lax.all_gather(w_key[0], ("seq", "wt"), axis=0, tiled=True),
            lax.all_gather(w_value[0], ("seq", "wt"), axis=0, tiled=True),
            lax.all_gather(w_out[0], ("seq", "wt"), axis=0, tiled=True),
            lax.all_gather(gain_mlp[0], ("seq", "wt"), axis=0, tiled=True),
            lax.all_gather(w_gate[0], ("seq", "wt"), axis=0, tiled=True),
            lax.all_gather(w_up[0], ("seq", "wt"), axis=0, tiled=True),
            lax.all_gather(w_down[0], ("seq", "wt"), axis=0, tiled=True),
        )

    def absorb(totals, shard_totals, layer_grads):
        totals = tuple((running + member for running, member in zip(totals, layer_grads)))
        return (totals, shard_totals)

    params_fwd = fetch_layer()
    arrived = jnp.zeros((rows_local, model_width), jnp.bfloat16)
    layer_inputs = []
    layer_outputs = []
    for moment in range(micro_count + 1):
        own_rows = inputs[min(moment, micro_count - 1)]
        layer_in = jnp.where(first_section, own_rows, arrived)
        allowed = jnp.where(
            first_section,
            allowed_all[min(moment, micro_count - 1)],
            allowed_all[max(moment - 1, 0)],
        )
        result, unused_kept = layer_forward(layer_in, allowed, params_fwd)
        result_low = result.astype(jnp.bfloat16)
        layer_inputs.append(layer_in)
        layer_outputs.append(result_low)
        if moment < micro_count:
            arrived = shifted(result_low, "section", 1)
    activations = jnp.stack(
        [
            jnp.where(first_section, layer_outputs[number], layer_outputs[number + 1])
            for number in range(micro_count)
        ]
    )[None]
    params_back = fetch_layer()
    totals = tuple((jnp.zeros(member.shape, jnp.float32) for member in params_back))
    shard_totals = tuple((jnp.zeros(member.shape, jnp.float32) for member in own_shards))
    arrived_grad = jnp.zeros((rows_local, model_width), jnp.bfloat16)
    grad_inputs = []
    for moment in range(micro_count + 1):
        late_index = max(moment - 1, 0)
        early_index = min(moment, micro_count - 1)
        grad_out = jnp.where(first_section, arrived_grad, cotangent[early_index])
        layer_in = jnp.where(
            first_section, layer_inputs[late_index], layer_inputs[min(moment + 1, micro_count)]
        )
        allowed = jnp.where(first_section, allowed_all[late_index], allowed_all[early_index])
        active_flag = jnp.where(first_section, moment >= 1, moment < micro_count)
        grad_in, gain_grads, saved = layer_backward(layer_in, allowed, params_back, grad_out)
        grad_low = grad_in.astype(jnp.bfloat16)
        grad_inputs.append(grad_low)
        if moment < micro_count:
            arrived_grad = shifted(grad_low, "section", -1)
        layer_grads = weight_products(saved, gain_grads)
        layer_grads = tuple((jnp.where(active_flag, member, 0.0) for member in layer_grads))
        totals, shard_totals = absorb(totals, shard_totals, layer_grads)
    summed_all = (
        lax.psum_scatter(totals[0], ("seq", "wt"), scatter_dimension=0, tiled=True),
        lax.psum_scatter(totals[1], ("seq", "wt"), scatter_dimension=0, tiled=True),
        lax.psum_scatter(totals[2], ("seq", "wt"), scatter_dimension=0, tiled=True),
        lax.psum_scatter(totals[3], ("seq", "wt"), scatter_dimension=0, tiled=True),
        lax.psum_scatter(totals[4], ("seq", "wt"), scatter_dimension=0, tiled=True),
        lax.psum_scatter(totals[5], ("seq", "wt"), scatter_dimension=0, tiled=True),
        lax.psum_scatter(totals[6], ("seq", "wt"), scatter_dimension=0, tiled=True),
        lax.psum_scatter(totals[7], ("seq", "wt"), scatter_dimension=0, tiled=True),
        lax.psum_scatter(totals[8], ("seq", "wt"), scatter_dimension=0, tiled=True),
    )
    input_grads = jnp.stack(
        [
            jnp.where(first_section, grad_inputs[number + 1], grad_inputs[number])
            for number in range(micro_count)
        ]
    )[None]
    return (
        activations,
        input_grads,
        summed_all[0][None],
        summed_all[1][None],
        summed_all[2][None],
        summed_all[3][None],
        summed_all[4][None],
        summed_all[5][None],
        summed_all[6][None],
        summed_all[7][None],
        summed_all[8][None],
    )


def solution(mesh):
    placed = (
        P("wt", "seq", None),
        P("wt", None),
        P("wt", "seq", None),
        P("section", ("seq", "wt")),
        P("section", ("seq", "wt"), None),
        P("section", ("seq", "wt"), None),
        P("section", ("seq", "wt"), None),
        P("section", ("seq", "wt"), None),
        P("section", ("seq", "wt")),
        P("section", ("seq", "wt"), None),
        P("section", ("seq", "wt"), None),
        P("section", ("seq", "wt"), None),
    )
    return jax.shard_map(
        per_device,
        mesh=mesh,
        in_specs=placed,
        out_specs=(
            P("section", "wt", "seq", None),
            P("section", "wt", "seq", None),
            P("section", ("seq", "wt")),
            P("section", ("seq", "wt"), None),
            P("section", ("seq", "wt"), None),
            P("section", ("seq", "wt"), None),
            P("section", ("seq", "wt"), None),
            P("section", ("seq", "wt")),
            P("section", ("seq", "wt"), None),
            P("section", ("seq", "wt"), None),
            P("section", ("seq", "wt"), None),
        ),
        check_vma=False,
    )
```

profile of v0, /device:TPU:0, one launch (start us, length us, event | category | flops | bytes accessed | tf_op | source)
XLA Modules:
  0.0 1598.2 jit_solution(2853015082448198328)
XLA Ops:
  15.6 35.4 %all-reduce.17 = (bf16[1024]{0:T(1024)(128)(2,1)S(1)}, bf16[1024]{0:T(1024)(128)(2,1)S(1)}) all-reduce(bf16[1024]{0:T(1024)(128)(2,1)S(1)} %dynamic-update-slice, bf16[1024]{0:T(1024)(128)(2,1)S(1)} %dynamic-update-slice.1), channel_id=2, replica_groups=mesh['section'=2,'seq'=4,'wt'=4] {'seq','wt'}, use_global_device_ids=true, to_apply=%add.12 | all-reduce | flops 2048 | bytes 8192
  56.9 39.9 %all-gather.17.cloned.1.call-done = bf16[1,1024,1024]{2,1,0:T(8,128)(2,1)} async-done(((bf16[1,64,1024]{2,1,0:T(8,128)(2,1)}), bf16[1,1024,1024]{2,1,0:T(8,128)(2,1)}) %all-gather.17.cloned.1.call-update) | async-done | bytes 2097168 | tf_op jit(solution)/shard_map/all_gather | solution.py:277
  107.0 32.6 %all-gather.21.cloned.1.call-done = bf16[1,1024,1024]{2,1,0:T(8,128)(2,1)} async-done(((bf16[1,64,1024]{2,1,0:T(8,128)(2,1)}), bf16[1,1024,1024]{2,1,0:T(8,128)(2,1)}) %all-gather.21.cloned.1.call-update) | async-done | bytes 2097168 | tf_op jit(solution)/shard_map/all_gather | solution.py:276
  165.8 16.0 all-gather.23.cloned.1.call-done
  184.6 57.1 %all-gather.25.cloned.1.call-done = bf16[1,1024,2816]{2,1,0:T(8,128)(2,1)} async-done(((bf16[1,64,2816]{2,1,0:T(8,128)(2,1)}), bf16[1,1024,2816]{2,1,0:T(8,128)(2,1)}) %all-gather.25.cloned.1.call-update) | async-done | bytes 5767184 | tf_op jit(solution)/shard_map/all_gather | solution.py:281
  249.1 52.5 %all-gather.29.cloned.1.call-done = bf16[1,2816,1024]{2,1,0:T(8,128)(2,1)} async-done(((bf16[1,176,1024]{2,1,0:T(8,128)(2,1)}), bf16[1,2816,1024]{2,1,0:T(8,128)(2,1)}) %all-gather.29.cloned.1.call-update) | async-done | bytes 5767184 | tf_op jit(solution)/shard_map/all_gather | solution.py:283
  301.6 60.0 %all-gather.27.cloned.1.call-done = bf16[1,1024,2816]{2,1,0:T(8,128)(2,1)} async-done(((bf16[1,64,2816]{2,1,0:T(8,128)(2,1)}), bf16[1,1024,2816]{2,1,0:T(8,128)(2,1)}) %all-gather.27.cloned.1.call-update) | async-done | bytes 5767184 | tf_op jit(solution)/shard_map/all_gather | solution.py:282
  361.6 10.1 fusion.326
  429.4 8.7 fusion.300
  448.4 10.9 fusion.323
  474.2 11.7 fusion.596
  534.6 11.4 fusion.597
  566.5 11.7 fusion.598
  609.2 9.0 fusion.245
  618.3 13.4 multiply_reduce_fusion.2
  701.8 11.7 collective-permute-done.12
  735.3 9.3 fusion.248
  744.7 13.6 multiply_reduce_fusion.1
  762.8 9.5 multiply_convert_fusion.1
  837.3 10.1 collective-permute-done.17
  868.6 9.7 multiply_reduce_fusion
  878.3 10.8 multiply_convert_fusion
  907.6 8.9 fusion.251
  996.0 9.6 select_add_fusion.2
  1016.5 9.7 select_add_fusion.1
  1040.4 12.9 select_add_fusion
  1100.7 10.1 fusion.461
  1119.5 32.2 %all-reduce.16 = (f32[1024]{0:T(1024)S(1)}, f32[1024]{0:T(1024)S(1)}) all-reduce(f32[1024]{0:T(1024)S(1)} %get-tuple-element.137, f32[1024]{0:T(1024)S(1)} %get-tuple-element.136), channel_id=11, replica_groups=mesh['section'=2,'seq'=4,'wt'=4] {'seq','wt'}, use_global_device_ids=true, to_apply=%region_40.41.clone | all-reduce | flops 2048 | bytes 16384
  1156.0 43.7 %reduce-scatter.12.cloned.1.call-done = f32[64,1024]{1,0:T(8,128)} async-done(((f32[1024,1024]{1,0:T(8,128)}), f32[64,1024]{1,0:T(8,128)}) %reduce-scatter.12.cloned.1.call-update) | async-done | bytes 262160 | tf_op jit(solution)/shard_map/reduce_scatter | solution.py:340
  1199.7 129.6 %reduce-scatter.16.cloned.1.call-done = f32[64,2816]{1,0:T(8,128)} async-done(((f32[1024,2816]{1,0:T(8,128)}), f32[64,2816]{1,0:T(8,128)}) %reduce-scatter.16.cloned.1.call-update) | async-done | bytes 720912 | tf_op jit(solution)/shard_map/reduce_scatter | solution.py:343
  1329.3 131.3 %reduce-scatter.18.cloned.1.call-done = f32[64,2816]{1,0:T(8,128)} async-done(((f32[1024,2816]{1,0:T(8,128)}), f32[64,2816]{1,0:T(8,128)}) %reduce-scatter.18.cloned.1.call-update) | async-done | bytes 720912 | tf_op jit(solution)/shard_map/reduce_scatter | solution.py:344
  1460.6 130.6 %reduce-scatter.20.cloned.1.call-done = f32[176,1024]{1,0:T(8,128)} async-done(((f32[2816,1024]{1,0:T(8,128)}), f32[176,1024]{1,0:T(8,128)}) %reduce-scatter.20.cloned.1.call-update) | async-done | bytes 720912 | tf_op jit(solution)/shard_map/reduce_scatter | solution.py:345
  (714 shorter events, 606.1 us)
Async XLA Ops:
  7.2 47.2 %all-gather.19.cloned.1.call-start = ((), (), s32[]{:S(2)}) async-start(), calls=%async_computation.15 | async-start | bytes 2228224 | tf_op jit(solution)/shard_map/all_gather | solution.py:278
  7.9 88.8 %all-gather.17.cloned.1.call-start = ((), (), s32[]{:S(2)}) async-start(), calls=%async_computation.14 | async-start | bytes 2228224 | tf_op jit(solution)/shard_map/all_gather | solution.py:277
  8.7 130.9 %all-gather.21.cloned.1.call-start = ((), (), s32[]{:S(2)}) async-start(), calls=%async_computation.16 | async-start | bytes 2228224 | tf_op jit(solution)/shard_map/all_gather | solution.py:276
  9.4 172.4 %all-gather.23.cloned.1.call-start = ((), (), s32[]{:S(2)}) async-start(), calls=%async_computation.17 | async-start | bytes 2228224 | tf_op jit(solution)/shard_map/all_gather | solution.py:279
  10.0 231.8 %all-gather.25.cloned.1.call-start = ((), (), s32[]{:S(2)}) async-start(), calls=%async_computation.18 | async-start | bytes 6127616 | tf_op jit(solution)/shard_map/all_gather | solution.py:281
  10.6 291.0 %all-gather.29.cloned.1.call-start = ((), (), s32[]{:S(2)}) async-start(), calls=%async_computation.20 | async-start | bytes 6127616 | tf_op jit(solution)/shard_map/all_gather | solution.py:283
  11.1 350.5 %all-gather.27.cloned.1.call-start = ((), (), s32[]{:S(2)}) async-start(), calls=%async_computation.19 | async-start | bytes 6127616 | tf_op jit(solution)/shard_map/all_gather | solution.py:282
  11.9 1144.1 %reduce-scatter.8.cloned.1.call-start = ((), (), s32[]{:S(2)}) async-start(), calls=%async_computation.7 | async-start | bytes 4456448 | tf_op jit(solution)/shard_map/reduce_scatter | solution.py:338
  100.4 44.0 %collective-permute-start.1 = (bf16[2,127,1024]{2,1,0:T(8,128)(2,1)}, bf16[2,127,1024]{2,1,0:T(8,128)(2,1)}, u32[]{:S(2)}, u32[]{:S(2)}) collective-permute-start(bf16[2,127,1024]{2,1,0:T(8,128)(2,1)} %get-tuple-element.80), channel_id=1, source_target_pairs={{4,0},{8,4},{12,8},{5,1},{9,5},{13,9},{6,2},{10,6},{14,10},{7,3},{... | collective-permute-start | bytes 1560584 | tf_op jit(solution)/shard_map/ppermute | solution.py:23
  101.7 42.7 %collective-permute-start = (bf16[2,127,1024]{2,1,0:T(8,128)(2,1)}, bf16[2,127,1024]{2,1,0:T(8,128)(2,1)}, u32[]{:S(2)}, u32[]{:S(2)}) collective-permute-start(bf16[2,127,1024]{2,1,0:T(8,128)(2,1)} %get-tuple-element.79), channel_id=1, source_target_pairs={{0,4},{4,8},{8,12},{1,5},{5,9},{9,13},{2,6},{6,10},{10,14},{3,7},{... | collective-permute-start | bytes 1560584 | tf_op jit(solution)/shard_map/ppermute | solution.py:21
  394.1 21.8 %collective-permute-start.4 = (bf16[2,127,1024]{2,1,0:T(8,128)(2,1)}, bf16[2,127,1024]{2,1,0:T(8,128)(2,1)}, u32[]{:S(2)}, u32[]{:S(2)}) collective-permute-start(bf16[2,127,1024]{2,1,0:T(8,128)(2,1)} %get-tuple-element.78), channel_id=1, source_target_pairs={{4,0},{8,4},{12,8},{5,1},{9,5},{13,9},{6,2},{10,6},{14,10},{7,3},{... | collective-permute-start | bytes 1560584 | tf_op jit(solution)/shard_map/ppermute | solution.py:23
  395.5 20.4 %collective-permute-start.3 = (bf16[2,127,1024]{2,1,0:T(8,128)(2,1)}, bf16[2,127,1024]{2,1,0:T(8,128)(2,1)}, u32[]{:S(2)}, u32[]{:S(2)}) collective-permute-start(bf16[2,127,1024]{2,1,0:T(8,128)(2,1)} %get-tuple-element.77), channel_id=1, source_target_pairs={{0,4},{4,8},{8,12},{1,5},{5,9},{9,13},{2,6},{6,10},{10,14},{3,7},{... | collective-permute-start | bytes 1560584 | tf_op jit(solution)/shard_map/ppermute | solution.py:21
  406.6 59.2 %collective-permute-start.9 = (bf16[2,127,1024]{2,1,0:T(8,128)(2,1)}, bf16[2,127,1024]{2,1,0:T(8,128)(2,1)}, u32[]{:S(2)}, u32[]{:S(2)}) collective-permute-start(bf16[2,127,1024]{2,1,0:T(8,128)(2,1)} %get-tuple-element.74), channel_id=1, source_target_pairs={{4,0},{8,4},{12,8},{5,1},{9,5},{13,9},{6,2},{10,6},{14,10},{7,3},{... | collective-permute-start | bytes 1560584 | tf_op jit(solution)/shard_map/ppermute | solution.py:23
  407.9 57.9 %collective-permute-start.8 = (bf16[2,127,1024]{2,1,0:T(8,128)(2,1)}, bf16[2,127,1024]{2,1,0:T(8,128)(2,1)}, u32[]{:S(2)}, u32[]{:S(2)}) collective-permute-start(bf16[2,127,1024]{2,1,0:T(8,128)(2,1)} %get-tuple-element.73), channel_id=1, source_target_pairs={{0,4},{4,8},{8,12},{1,5},{5,9},{9,13},{2,6},{6,10},{10,14},{3,7},{... | collective-permute-start | bytes 1560584 | tf_op jit(solution)/shard_map/ppermute | solution.py:21
  459.3 36.3 %collective-permute-start.5 = (bf16[320,1024]{1,0:T(8,128)(2,1)}, bf16[320,1024]{1,0:T(8,128)(2,1)}, u32[]{:S(2)}, u32[]{:S(2)}) collective-permute-start(bf16[320,1024]{1,0:T(8,128)(2,1)} %fusion.323), channel_id=1, source_target_pairs={{0,16},{1,17},{2,18},{3,19},{4,20},{5,21},{6,22},{7,23},{8,24},{9,... | collective-permute-start | bytes 1966088 | tf_op jit(solution)/shard_map/ppermute | solution.py:33
  501.3 24.4 %collective-permute-start.19 = (bf16[2,127,1024]{2,1,0:T(8,128)(2,1)}, bf16[2,127,1024]{2,1,0:T(8,128)(2,1)}, u32[]{:S(2)}, u32[]{:S(2)}) collective-permute-start(bf16[2,127,1024]{2,1,0:T(8,128)(2,1)} %get-tuple-element.70), channel_id=1, source_target_pairs={{4,0},{8,4},{12,8},{5,1},{9,5},{13,9},{6,2},{10,6},{14,10},{7,3},{... | collective-permute-start | bytes 1560584 | tf_op jit(solution)/shard_map/ppermute | solution.py:23
  502.7 23.0 %collective-permute-start.18 = (bf16[2,127,1024]{2,1,0:T(8,128)(2,1)}, bf16[2,127,1024]{2,1,0:T(8,128)(2,1)}, u32[]{:S(2)}, u32[]{:S(2)}) collective-permute-start(bf16[2,127,1024]{2,1,0:T(8,128)(2,1)} %get-tuple-element.69), channel_id=1, source_target_pairs={{0,4},{4,8},{8,12},{1,5},{5,9},{9,13},{2,6},{6,10},{10,14},{3,7},{... | collective-permute-start | bytes 1560584 | tf_op jit(solution)/shard_map/ppermute | solution.py:21
  516.6 41.1 %collective-permute-start.14 = (bf16[2,127,1024]{2,1,0:T(8,128)(2,1)}, bf16[2,127,1024]{2,1,0:T(8,128)(2,1)}, u32[]{:S(2)}, u32[]{:S(2)}) collective-permute-start(bf16[2,127,1024]{2,1,0:T(8,128)(2,1)} %get-tuple-element.72), channel_id=1, source_target_pairs={{4,0},{8,4},{12,8},{5,1},{9,5},{13,9},{6,2},{10,6},{14,10},{7,3},{... | collective-permute-start | bytes 1560584 | tf_op jit(solution)/shard_map/ppermute | solution.py:23
  517.9 39.8 %collective-permute-start.13 = (bf16[2,127,1024]{2,1,0:T(8,128)(2,1)}, bf16[2,127,1024]{2,1,0:T(8,128)(2,1)}, u32[]{:S(2)}, u32[]{:S(2)}) collective-permute-start(bf16[2,127,1024]{2,1,0:T(8,128)(2,1)} %get-tuple-element.71), channel_id=1, source_target_pairs={{0,4},{4,8},{8,12},{1,5},{5,9},{9,13},{2,6},{6,10},{10,14},{3,7},{... | collective-permute-start | bytes 1560584 | tf_op jit(solution)/shard_map/ppermute | solution.py:21
  654.9 25.8 %collective-permute-start.11 = (f32[2,127,1024]{2,0,1:T(2,128)}, f32[2,127,1024]{2,0,1:T(2,128)}, u32[]{:S(2)}, u32[]{:S(2)}) collective-permute-start(f32[2,127,1024]{2,0,1:T(2,128)} %pad_maximum_fusion.7), channel_id=1, source_target_pairs={{4,0},{8,4},{12,8},{5,1},{9,5},{13,9},{6,2},{10,6},{14,10},{7,3},{... | collective-permute-start | bytes 3121160 | tf_op jit(solution)/shard_map/ppermute | solution.py:33
  665.2 19.4 %collective-permute-start.10 = (f32[2,127,1024]{2,0,1:T(2,128)}, f32[2,127,1024]{2,0,1:T(2,128)}, u32[]{:S(2)}, u32[]{:S(2)}) collective-permute-start(f32[2,127,1024]{2,0,1:T(2,128)} %pad_maximum_fusion.6), channel_id=1, source_target_pairs={{0,4},{4,8},{8,12},{1,5},{5,9},{9,13},{2,6},{6,10},{10,14},{3,7},{... | collective-permute-start | bytes 3121160 | tf_op jit(solution)/shard_map/ppermute | solution.py:33
  694.0 19.5 %collective-permute-start.12 = (bf16[320,1024]{1,0:T(8,128)(2,1)S(1)}, bf16[320,1024]{1,0:T(8,128)(2,1)S(1)}, u32[]{:S(2)}, u32[]{:S(2)}) collective-permute-start(bf16[320,1024]{1,0:T(8,128)(2,1)S(1)} %fusion.409), channel_id=1, source_target_pairs={{16,0},{17,1},{18,2},{19,3},{20,4},{21,5},{22,6},{23,7},{24,8},{25... | collective-permute-start | bytes 1966088 | tf_op jit(solution)/shard_map/ppermute | solution.py:33
  781.8 34.1 %collective-permute-start.16 = (f32[2,127,1024]{2,0,1:T(2,128)}, f32[2,127,1024]{2,0,1:T(2,128)}, u32[]{:S(2)}, u32[]{:S(2)}) collective-permute-start(f32[2,127,1024]{2,0,1:T(2,128)} %pad_maximum_fusion.9), channel_id=1, source_target_pairs={{4,0},{8,4},{12,8},{5,1},{9,5},{13,9},{6,2},{10,6},{14,10},{7,3},{... | collective-permute-start | bytes 3121160 | tf_op jit(solution)/shard_map/ppermute | solution.py:33
  828.8 18.7 %collective-permute-start.17 = (bf16[320,1024]{1,0:T(8,128)(2,1)S(1)}, bf16[320,1024]{1,0:T(8,128)(2,1)S(1)}, u32[]{:S(2)}, u32[]{:S(2)}) collective-permute-start(bf16[320,1024]{1,0:T(8,128)(2,1)S(1)} %get-tuple-element.30), channel_id=1, source_target_pairs={{16,0},{17,1},{18,2},{19,3},{20,4},{21,5},{22,6},{23,7},{24,8},{25... | collective-permute-start | bytes 1966088 | tf_op jit(solution)/shard_map/ppermute | solution.py:33
  897.7 258.3 %reduce-scatter.14.cloned.1.call-start = ((), (), s32[]{:S(2)}) async-start(), calls=%async_computation.10 | async-start | bytes 4456448 | tf_op jit(solution)/shard_map/reduce_scatter | solution.py:341
  906.5 249.5 %reduce-scatter.10.cloned.1.call-start = ((), (), s32[]{:S(2)}) async-start(), calls=%async_computation.8 | async-start | bytes 4456448 | tf_op jit(solution)/shard_map/reduce_scatter | solution.py:339
  931.9 22.5 %collective-permute-start.21 = (f32[2,127,1024]{2,0,1:T(2,128)}, f32[2,127,1024]{2,0,1:T(2,128)}, u32[]{:S(2)}, u32[]{:S(2)}) collective-permute-start(f32[2,127,1024]{2,0,1:T(2,128)} %pad_maximum_fusion.11), channel_id=1, source_target_pairs={{4,0},{8,4},{12,8},{5,1},{9,5},{13,9},{6,2},{10,6},{14,10},{7,3},{... | collective-permute-start | bytes 3121160 | tf_op jit(solution)/shard_map/ppermute | solution.py:33
  938.6 19.3 %collective-permute-start.20 = (f32[2,127,1024]{2,0,1:T(2,128)}, f32[2,127,1024]{2,0,1:T(2,128)}, u32[]{:S(2)}, u32[]{:S(2)}) collective-permute-start(f32[2,127,1024]{2,0,1:T(2,128)} %pad_maximum_fusion.10), channel_id=1, source_target_pairs={{0,4},{4,8},{8,12},{1,5},{5,9},{9,13},{2,6},{6,10},{10,14},{3,7},{... | collective-permute-start | bytes 3121160 | tf_op jit(solution)/shard_map/ppermute | solution.py:33
  966.8 232.9 %reduce-scatter.12.cloned.1.call-start = ((), (), s32[]{:S(2)}) async-start(), calls=%async_computation.9 | async-start | bytes 4456448 | tf_op jit(solution)/shard_map/reduce_scatter | solution.py:340
  984.9 344.4 %reduce-scatter.16.cloned.1.call-start = ((), (), s32[]{:S(2)}) async-start(), calls=%async_computation.11 | async-start | bytes 12255232 | tf_op jit(solution)/shard_map/reduce_scatter | solution.py:343
  1005.6 455.0 %reduce-scatter.18.cloned.1.call-start = ((), (), s32[]{:S(2)}) async-start(), calls=%async_computation.12 | async-start | bytes 12255232 | tf_op jit(solution)/shard_map/reduce_scatter | solution.py:344
  1026.3 565.0 %reduce-scatter.20.cloned.1.call-start = ((), (), s32[]{:S(2)}) async-start(), calls=%async_computation.13 | async-start | bytes 12255232 | tf_op jit(solution)/shard_map/reduce_scatter | solution.py:345
  (200 other events, 2589.7 us)
Sparse Core Ops, SparseCore 0:
  10.2 44.0 all-gather.18
  56.6 40.1 all-gather.16
  99.0 40.5 all-gather.20
  141.7 40.0 all-gather.22
  183.9 57.7 all-gather.24
  243.9 57.6 all-gather.28
  303.9 57.6 all-gather.26
  897.8 72.3 reduce-scatter.7
  975.2 71.4 reduce-scatter.13
  1050.9 72.1 reduce-scatter.9
  1128.0 71.6 reduce-scatter.11
  1204.2 125.0 reduce-scatter.15
  1334.5 126.0 reduce-scatter.17
  1465.2 126.0 reduce-scatter.19
where the time goes:
time: 1610 us; the launch traced here: 1600 us
  waiting for transfers between devices  728 us (45%)
  matrix products  479 us (30%)
  local copies, waits for them, and re-layouts  160 us (10%)
  other arithmetic  81.5 us (5%)
  blocking collectives  67.6 us (4%)
  starting transfers between devices  64.1 us (4%)
  between operations  18.4 us (1%)
    reduce_scatter x1, waiting for transfers between devices, per_device(): lax.psum_scatter(totals[7], ('seq', 'wt'), scatter_dimension=0, tiled=True)  131 us
    reduce_scatter x1, waiting for transfers between devices, per_device(): lax.psum_scatter(totals[8], ('seq', 'wt'), scatter_dimension=0, tiled=True)  131 us
    reduce_scatter x1, waiting for transfers between devices, per_device(): lax.psum_scatter(totals[6], ('seq', 'wt'), scatter_dimension=0, tiled=True)  130 us
    unnamed x2, blocking collectives  67.6 us
    all_gather x1, waiting for transfers between devices, fetch_layer(): lax.all_gather(w_up[0], ('seq', 'wt'), axis=0, tiled=True)  60 us
    all_gather x1, waiting for transfers between devices, fetch_layer(): lax.all_gather(w_gate[0], ('seq', 'wt'), axis=0, tiled=True)  57.1 us
    sub x6, matrix products, layer_forward(): exp_scores = jnp.exp(masked - jnp.max(masked, axis=-1, keepdims=True))  54.1 us
    all_gather x1, waiting for transfers between devices, fetch_layer(): lax.all_gather(w_down[0], ('seq', 'wt'), axis=0, tiled=True)  52.5 us
  transfers between devices with their start and end apart: 36, of which 14 were waited for; matrix products, arithmetic and copies ran while one was open for 28% of the time, Pallas kernels for 0%

commit v1 on v0

--- a/solution.py
+++ b/solution.py
@@ -1,6 +1,10 @@
+import functools
+
 import jax
 import jax.numpy as jnp
 from jax import lax
+from jax.experimental import pallas as pl
+from jax.experimental.pallas import tpu as pltpu
 from jax.sharding import PartitionSpec as P
 
 HEAD_DIM = 64
@@ -114,46 +118,135 @@
     )
 
 
-def weight_products(saved, gain_grads):
-    (
-        normed,
-        grad_queries,
-        grad_keys,
-        grad_values,
-        mixed_low,
-        grad_branch,
-        normed_two,
-        grad_gate_pre,
-        grad_up_pre,
-        gated_low,
-        grad_out,
-    ) = saved
-    grad_query_w = jnp.dot(normed.T, grad_queries, preferred_element_type=jnp.float32)
-    grad_key_w = jnp.dot(normed.T, grad_keys, preferred_element_type=jnp.float32)
-    grad_value_w = jnp.dot(normed.T, grad_values, preferred_element_type=jnp.float32)
-    grad_out_w = jnp.dot(mixed_low.T, grad_branch, preferred_element_type=jnp.float32)
-    grad_gate_w = jnp.dot(normed_two.T, grad_gate_pre, preferred_element_type=jnp.float32)
-    grad_up_w = jnp.dot(normed_two.T, grad_up_pre, preferred_element_type=jnp.float32)
-    grad_down_w = jnp.dot(gated_low.T, grad_out, preferred_element_type=jnp.float32)
+def hops():
+    rings, span = lax.axis_size("wt"), lax.axis_size("seq")
+    high = span // 2
+    along = [(i, (i + 1) % rings) for i in range(rings)]
+    across = [(h * 2 + c, ((h + 1) % high) * 2 + c) for h in range(high) for c in range(2)]
+    pairs = [(i, i ^ 1) for i in range(span)]
     return (
-        gain_grads[0],
-        grad_query_w,
-        grad_key_w,
-        grad_value_w,
-        grad_out_w,
-        gain_grads[1],
-        grad_gate_w,
-        grad_up_w,
-        grad_down_w,
-    )
-
-
-def layer_backward(layer_in, allowed, params, grad_out):
+        lambda cells: lax.ppermute(cells, "wt", along),
+        lambda cells: lax.ppermute(cells, "seq", across),
+        lambda cells: lax.ppermute(cells, "seq", pairs),
+    )
+
+
+def places():
+    rings, high = lax.axis_size("wt"), lax.axis_size("seq") // 2
+    shard_no = lax.axis_index("seq")
+    return rings, high, lax.axis_index("wt"), shard_no // 2, shard_no % 2
+
+
+def gather_pieces(shard):
+    along, across, swap = hops()
+    rings, high = lax.axis_size("wt"), lax.axis_size("seq") // 2
+    pieces = {}
+    current = shard
+    for k in range(rings):
+        current = along(current) if k else current
+        cells = current
+        for j in range(high):
+            cells = across(cells) if j else cells
+            pieces[(k, j, 0)] = cells
+    for k, j, _ in list(pieces):
+        pieces[(k, j, 1)] = swap(pieces[(k, j, 0)])
+    return pieces
+
+
+def owner_of(k, j, p):
+    rings, high, z, h, c = places()
+    return (lax.rem(h - j + high, high) * 2 + (c + p) % 2) * rings + lax.rem(z - k + rings, rings)
+
+
+def assemble_kernel(count, rows_list, owners_ref, *refs):
+    parts, wholes, sems = refs[:count], refs[count:-1], refs[-1]
+    copies = []
+    for i in range(count):
+        start = 0
+        for w, rows in enumerate(rows_list):
+            place = pl.multiple_of(owners_ref[i] * rows, rows)
+            copies.append(
+                pltpu.make_async_copy(
+                    parts[i].at[pl.ds(start, rows)],
+                    wholes[w].at[pl.ds(place, rows)],
+                    sems.at[i * len(rows_list) + w],
+                )
+            )
+            start += rows
+    for copy in copies:
+        copy.start()
+    for copy in copies:
+        copy.wait()
+
+
+def assemble(pieces, rows_list):
+    keys = sorted(pieces)
+    count = len(keys)
+    owners = [owner_of(*key) for key in keys]
+    width, kind = pieces[keys[0]].shape[-1], pieces[keys[0]].dtype
+    if any(rows % 16 for rows in rows_list):
+        wholes, start = [], 0
+        for rows in rows_list:
+            whole = jnp.zeros((count * rows, width), kind)
+            for key, place in zip(keys, owners):
+                part = lax.slice_in_dim(pieces[key], start, start + rows, axis=0)
+                whole = lax.dynamic_update_slice_in_dim(whole, part, place * rows, 0)
+            wholes.append(whole)
+            start += rows
+        return wholes
+    return pl.pallas_call(
+        functools.partial(assemble_kernel, count, rows_list),
+        out_shape=[jax.ShapeDtypeStruct((count * rows, width), kind) for rows in rows_list],
+        grid_spec=pltpu.PrefetchScalarGridSpec(
+            num_scalar_prefetch=1,
+            grid=(),
+            in_specs=[pl.BlockSpec(memory_space=pl.ANY)] * count,
+            out_specs=[pl.BlockSpec(memory_space=pltpu.VMEM)] * len(rows_list),
+            scratch_shapes=[pltpu.SemaphoreType.DMA((count * len(rows_list),))],
+        ),
+        compiler_params=pltpu.CompilerParams(vmem_limit_bytes=40 * 2**20),
+    )(jnp.stack(owners).astype(jnp.int32), *[pieces[key] for key in keys])
+
+
+def plus(left, right, kind):
+    return (left.astype(jnp.float32) + right.astype(jnp.float32)).astype(kind)
+
+
+def scatter_sum(partial, kind=jnp.bfloat16):
+    along, across, swap = hops()
+    rings, high, z, h, c = places()
+    rows = partial.shape[0] // (rings * high * 2)
+    cells = partial.reshape(high, 2, rings, rows, -1)
+    mine = lax.dynamic_index_in_dim(cells, c, 1, False)
+    received = swap(lax.dynamic_index_in_dim(cells, 1 - c, 1, False))
+
+    def block(j, k):
+        place = (lax.rem(h - j + high, high), lax.rem(z - k + rings, rings), 0, 0)
+        size = (1, 1, rows, cells.shape[-1])
+        return plus(
+            lax.dynamic_slice(mine, place, size)[0, 0],
+            lax.dynamic_slice(received, place, size)[0, 0],
+            kind,
+        )
+
+    total = None
+    for k in range(1, rings + 1):
+        level = block(1, k)
+        for j in range(2, high + 1):
+            level = plus(across(level), block(j, k), kind)
+        if total is not None:
+            last = k == rings
+            total = plus(along(total), level, jnp.float32 if last else kind)
+        else:
+            total = level
+    return total.astype(jnp.float32)
+
+
+def layer_backward(kept_values, params, grad_out):
     gain_one, query_w, key_w, value_w, out_w, gain_two, gate_w, up_w, down_w = params
-    rows_local, model_width = layer_in.shape
+    rows_local, model_width = grad_out.shape
     head_count = model_width // HEAD_DIM
     score_scale = HEAD_DIM ** (-0.5)
-    unused_result, kept_values = layer_forward(layer_in, allowed, params)
     (
         source,
         normed,
@@ -258,38 +351,23 @@
         window_allowed(lengths[number], shard_no, rows_local, seq_len)
         for number in range(micro_count)
     ]
-    own_shards = (
-        gain_attn[0],
-        w_query[0],
-        w_key[0],
-        w_value[0],
-        w_out[0],
-        gain_mlp[0],
-        w_gate[0],
-        w_up[0],
-        w_down[0],
-    )
-
-    def fetch_layer():
-        return (
-            lax.all_gather(gain_attn[0], ("seq", "wt"), axis=0, tiled=True),
-            lax.all_gather(w_query[0], ("seq", "wt"), axis=0, tiled=True),
-            lax.all_gather(w_key[0], ("seq", "wt"), axis=0, tiled=True),
-            lax.all_gather(w_value[0], ("seq", "wt"), axis=0, tiled=True),
-            lax.all_gather(w_out[0], ("seq", "wt"), axis=0, tiled=True),
-            lax.all_gather(gain_mlp[0], ("seq", "wt"), axis=0, tiled=True),
-            lax.all_gather(w_gate[0], ("seq", "wt"), axis=0, tiled=True),
-            lax.all_gather(w_up[0], ("seq", "wt"), axis=0, tiled=True),
-            lax.all_gather(w_down[0], ("seq", "wt"), axis=0, tiled=True),
-        )
-
-    def absorb(totals, shard_totals, layer_grads):
-        totals = tuple((running + member for running, member in zip(totals, layer_grads)))
-        return (totals, shard_totals)
-
-    params_fwd = fetch_layer()
+    rows = w_query.shape[1]
+    gains = jnp.pad(
+        jnp.concatenate([gain_attn, gain_mlp], 1), ((0, 15), (0, model_width - 2 * rows))
+    )
+    narrow = gather_pieces(jnp.concatenate([w_query[0], w_key[0], w_value[0], w_out[0], gains], 0))
+    wide = gather_pieces(jnp.concatenate([w_gate[0], w_up[0]], 0))
+    deep = gather_pieces(w_down[0])
+    query_w, key_w, value_w, out_w, gain_rows = assemble(narrow, [rows, rows, rows, rows, 16])
+    gate_w, up_w = assemble(wide, [rows, rows])
+    (down_w,) = assemble(deep, [w_down.shape[1]])
+    gain_rows = gain_rows.reshape(-1, 16, model_width)[:, 0]
+    gain_one = gain_rows[:, :rows].reshape(-1)
+    gain_two = gain_rows[:, rows : 2 * rows].reshape(-1)
+    params = (gain_one, query_w, key_w, value_w, out_w, gain_two, gate_w, up_w, down_w)
+
     arrived = jnp.zeros((rows_local, model_width), jnp.bfloat16)
-    layer_inputs = []
+    kept_all = []
     layer_outputs = []
     for moment in range(micro_count + 1):
         own_rows = inputs[min(moment, micro_count - 1)]
@@ -299,9 +377,9 @@
             allowed_all[min(moment, micro_count - 1)],
             allowed_all[max(moment - 1, 0)],
         )
-        result, unused_kept = layer_forward(layer_in, allowed, params_fwd)
+        result, kept = layer_forward(layer_in, allowed, params)
         result_low = result.astype(jnp.bfloat16)
-        layer_inputs.append(layer_in)
+        kept_all.append(kept)
         layer_outputs.append(result_low)
         if moment < micro_count:
             arrived = shifted(result_low, "section", 1)
@@ -311,38 +389,69 @@
             for number in range(micro_count)
         ]
     )[None]
-    params_back = fetch_layer()
-    totals = tuple((jnp.zeros(member.shape, jnp.float32) for member in params_back))
-    shard_totals = tuple((jnp.zeros(member.shape, jnp.float32) for member in own_shards))
     arrived_grad = jnp.zeros((rows_local, model_width), jnp.bfloat16)
     grad_inputs = []
+    saved_all = []
+    gains_all = []
     for moment in range(micro_count + 1):
         late_index = max(moment - 1, 0)
         early_index = min(moment, micro_count - 1)
         grad_out = jnp.where(first_section, arrived_grad, cotangent[early_index])
-        layer_in = jnp.where(
-            first_section, layer_inputs[late_index], layer_inputs[min(moment + 1, micro_count)]
+        kept = tuple(
+            jnp.where(first_section, late, early)
+            for late, early in zip(kept_all[late_index], kept_all[min(moment + 1, micro_count)])
         )
-        allowed = jnp.where(first_section, allowed_all[late_index], allowed_all[early_index])
-        active_flag = jnp.where(first_section, moment >= 1, moment < micro_count)
-        grad_in, gain_grads, saved = layer_backward(layer_in, allowed, params_back, grad_out)
+        grad_in, gain_grads, saved = layer_backward(kept, params, grad_out)
         grad_low = grad_in.astype(jnp.bfloat16)
         grad_inputs.append(grad_low)
         if moment < micro_count:
             arrived_grad = shifted(grad_low, "section", -1)
-        layer_grads = weight_products(saved, gain_grads)
-        layer_grads = tuple((jnp.where(active_flag, member, 0.0) for member in layer_grads))
-        totals, shard_totals = absorb(totals, shard_totals, layer_grads)
-    summed_all = (
-        lax.psum_scatter(totals[0], ("seq", "wt"), scatter_dimension=0, tiled=True),
-        lax.psum_scatter(totals[1], ("seq", "wt"), scatter_dimension=0, tiled=True),
-        lax.psum_scatter(totals[2], ("seq", "wt"), scatter_dimension=0, tiled=True),
-        lax.psum_scatter(totals[3], ("seq", "wt"), scatter_dimension=0, tiled=True),
-        lax.psum_scatter(totals[4], ("seq", "wt"), scatter_dimension=0, tiled=True),
-        lax.psum_scatter(totals[5], ("seq", "wt"), scatter_dimension=0, tiled=True),
-        lax.psum_scatter(totals[6], ("seq", "wt"), scatter_dimension=0, tiled=True),
-        lax.psum_scatter(totals[7], ("seq", "wt"), scatter_dimension=0, tiled=True),
-        lax.psum_scatter(totals[8], ("seq", "wt"), scatter_dimension=0, tiled=True),
+        saved_all.append(saved)
+        gains_all.append(gain_grads)
+
+    def both(index):
+        return jnp.concatenate(
+            [
+                jnp.where(first_section, saved_all[number + 1][index], saved_all[number][index])
+                for number in range(micro_count)
+            ],
+            0,
+        )
+
+    (
+        normed,
+        grad_queries,
+        grad_keys,
+        grad_values,
+        mixed_low,
+        grad_branch,
+        normed_two,
+        grad_gate_pre,
+        grad_up_pre,
+        gated_low,
+        grad_out,
+    ) = [both(index) for index in range(11)]
+
+    def product(left, right):
+        return jnp.dot(left.T, right, preferred_element_type=jnp.float32).astype(jnp.bfloat16)
+
+    grad_down_w = scatter_sum(product(gated_low, grad_out))
+    grad_gate_w = scatter_sum(product(normed_two, grad_gate_pre))
+    grad_up_w = scatter_sum(product(normed_two, grad_up_pre))
+    grad_out_w = scatter_sum(product(mixed_low, grad_branch))
+    grad_qkv_w = scatter_sum(
+        product(normed, jnp.concatenate([grad_queries, grad_keys, grad_values], 1))
+    )
+    grad_query_w, grad_key_w, grad_value_w = jnp.split(grad_qkv_w, 3, axis=1)
+    gain_parts = [
+        sum(
+            jnp.where(first_section, gains_all[number + 1][index], gains_all[number][index])
+            for number in range(micro_count)
+        )
+        for index in range(2)
+    ]
+    gain_sum = scatter_sum(
+        jnp.concatenate([part.reshape(-1, rows) for part in gain_parts], 1), jnp.float32
     )
     input_grads = jnp.stack(
         [
@@ -353,15 +462,15 @@
     return (
         activations,
         input_grads,
-        summed_all[0][None],
-        summed_all[1][None],
-        summed_all[2][None],
-        summed_all[3][None],
-        summed_all[4][None],
-        summed_all[5][None],
-        summed_all[6][None],
-        summed_all[7][None],
-        summed_all[8][None],
+        gain_sum[:, :rows],
+        grad_query_w[None],
+        grad_key_w[None],
+        grad_value_w[None],
+        grad_out_w[None],
+        gain_sum[:, rows:],
+        grad_gate_w[None],
+        grad_up_w[None],
+        grad_down_w[None],
     )
 
 

time: 1610 us -> 1050 us (0.65)
  waiting for transfers between devices: 728 us -> 256 us
  matrix products: 479 us -> 348 us
  blocking collectives: 67.6 us -> 0 us
  other arithmetic: 81.5 us -> 130 us
  starting transfers between devices: 64.1 us -> 107 us
  Pallas kernels: 0 us -> 26.5 us
    reduce_scatter x7 -> x0, waiting for transfers between devices: 435 us -> none  [the longest x1 131 us: per_device(): lax.psum_scatter(totals[7], ('seq', 'wt'), scatter_dimension=0, tiled=True)]
    all_gather x7 -> x0, waiting for transfers between devices: 260 us -> none  [the longest x1 60 us: fetch_layer(): lax.all_gather(w_up[0], ('seq', 'wt'), axis=0, tiled=True)]
    ppermute x0 -> x93, waiting for transfers between devices: none -> 231 us  [the longest x36 150 us: hops(): lax.ppermute(cells, 'seq', across)]
    dot_general x21 -> x5, matrix products: 106 us -> 30.7 us  [product(): jnp.dot(left.T, right, preferred_element_type=jnp.float32)]
    unnamed x2 -> x0, blocking collectives: 67.6 us -> none
    ppermute x0 -> x93, starting transfers between devices: none -> 54.5 us  [the longest x36 36.1 us: hops(): lax.ppermute(cells, 'seq', across)]
    dot_general x3, matrix products: 27.3 us -> 54.2 us  [layer_backward(): jnp.einsum('hqk,qhd->khd', probs_low, grad_mixed, preferred_element_type=...]
    pallas_call x0 -> x3, Pallas kernels: none -> 26.5 us  [assemble(): pl.pallas_call(functools.partial(assemble_kernel, count, rows_list), out_...]
  transfers between devices with their start and end apart: 36 -> 109, of which waited for: 14 -> 38; matrix products, arithmetic and copies ran while one was open for 28% -> 24% of each run, Pallas kernels for 0% -> 2%
where the time goes in v1:
time: 1050 us; the launch traced here: 1040 us
  matrix products  348 us (33%)
  waiting for transfers between devices  256 us (24%)
  local copies, waits for them, and re-layouts  164 us (16%)
  other arithmetic  130 us (12%)
  starting transfers between devices  107 us (10%)
  Pallas kernels  26.5 us (3%)
    ppermute x36, waiting for transfers between devices, hops(): lax.ppermute(cells, 'seq', across)  150 us
    ppermute x27, waiting for transfers between devices, hops(): lax.ppermute(cells, 'wt', along)  78.9 us
    dot_general x3, matrix products, layer_backward(): jnp.einsum('hqk,qhd->khd', probs_low, grad_mixed, preferred_element_type=...  54.2 us
    unnamed x443, local copies, waits for them, and re-layouts  49.4 us
    dot_general x3, matrix products, layer_backward(): jnp.einsum('qhd,khd->hqk', grad_mixed, value_heads, preferred_element_typ...  46.1 us
    ppermute x10, starting transfers between devices, shifted(): return lax.ppermute(shard, axis, pairs)  40.8 us
    convert_element_type x3, other arithmetic, layer_backward(): grad_scores = (attn_probs * (grad_probs - jnp.sum(attn_probs * grad_probs...  40.3 us
    ppermute x36, starting transfers between devices, hops(): lax.ppermute(cells, 'seq', across)  36.1 us
  transfers between devices with their start and end apart: 109, of which 38 were waited for; matrix products, arithmetic and copies ran while one was open for 24% of the time, Pallas kernels for 2%

profile of v1, /device:TPU:0, one launch (start us, length us, event | category | flops | bytes accessed | tf_op | source)
XLA Modules:
  0.0 1036.0 jit_solution(17732606889054226185)
XLA Ops:
  8.1 14.6 %collective-permute-done.3.refs_4_ = bf16[272,1024]{1,0:T(8,128)(2,1)S(1)} collective-permute-done((bf16[272,1024]{1,0:T(8,128)(2,1)S(1)}, bf16[272,1024]{1,0:T(8,128)(2,1)S(1)}, u32[]{:S(2)}, u32[]{:S(2)}) %collective-permute-start.3) | collective-permute-done | bytes 557088 | tf_op jit(solution)/shard_map/ppermute | solution.py:128
  26.1 14.0 %collective-permute-done.7.refs_8_ = bf16[272,1024]{1,0:T(8,128)(2,1)S(1)} collective-permute-done((bf16[272,1024]{1,0:T(8,128)(2,1)S(1)}, bf16[272,1024]{1,0:T(8,128)(2,1)S(1)}, u32[]{:S(2)}, u32[]{:S(2)}) %collective-permute-start.7) | collective-permute-done | bytes 557088 | tf_op jit(solution)/shard_map/ppermute | solution.py:128
  53.4 12.4 %collective-permute-done.39.refs_8_ = bf16[176,1024]{1,0:T(8,128)(2,1)} collective-permute-done((bf16[176,1024]{1,0:T(8,128)(2,1)}, bf16[176,1024]{1,0:T(8,128)(2,1)}, u32[]{:S(2)}, u32[]{:S(2)}) %collective-permute-start.39) | collective-permute-done | bytes 360480 | tf_op jit(solution)/shard_map/ppermute | solution.py:128
  71.3 10.2 collective-permute-done.9.refs_10_
  81.5 9.3 collective-permute-done.13.refs_14_
  113.3 13.9 %shard_map.203 = (bf16[1024,1024]{1,0:T(8,128)(2,1)S(1)}, bf16[1024,1024]{1,0:T(8,128)(2,1)S(1)}, bf16[1024,1024]{1,0:T(8,128)(2,1)}, bf16[1024,1024]{1,0:T(8,128)(2,1)}, bf16[256,1024]{1,0:T(8,128)(2,1)S(1)}) custom-call(s32[16]{0:T(128)S(1)} %stack.200.owners_ref, bf16[272,1024]{1,0:T(8,128)(2,1)S(1)} %fusion.225.refs_0_, ...), custom_call_target="tpu_custom_call" | custom-call | tf_op jit(solution)/shard_map/pallas_call | solution.py:197
  183.7 12.0 %fusion.326 = (f32[16,320]{1,0:T(8,128)}, f32[16,320,574]{2,1,0:T(8,128)}) fusion(pred[320,574]{1,0:T(8,128)(4,1)} %get-tuple-element.182, bf16[320,16,64]{0,2,1:T(8,128)(2,1)} %bitcast.686, bf16[574,16,64]{0,2,1:T(8,128)(2,1)} %bitcast.667), kind=kOutput, calls=%fused_computation.637 | convolution fusion | flops 387932736 | bytes 13790592 | tf_op jit(solution)/shard_map/sub | solution.py:81
  205.0 15.1 %collective-permute-done.30.refs_14_ = bf16[128,2816]{1,0:T(8,128)(2,1)} collective-permute-done((bf16[128,2816]{1,0:T(8,128)(2,1)}, bf16[128,2816]{1,0:T(8,128)(2,1)}, u32[]{:S(2)}, u32[]{:S(2)}) %collective-permute-start.30) | collective-permute-done | bytes 720928 | tf_op jit(solution)/shard_map/ppermute | solution.py:129
  232.0 9.3 shard_map.204
  257.8 12.7 %collective-permute-done.47 = bf16[320,1024]{1,0:T(8,128)(2,1)} collective-permute-done((bf16[320,1024]{1,0:T(8,128)(2,1)S(1)}, bf16[320,1024]{1,0:T(8,128)(2,1)}, u32[]{:S(2)}, u32[]{:S(2)}) %collective-permute-start.47) | collective-permute-done | bytes 655392 | tf_op jit(solution)/shard_map/ppermute | solution.py:37
  292.1 8.8 fusion.327
  322.8 10.7 %fusion.41 = (bf16[320,2816]{1,0:T(8,128)(2,1)S(1)}, bf16[320,2816]{1,0:T(8,128)(2,1)}, bf16[320,2816]{1,0:T(8,128)(2,1)}) fusion(f32[320,2816]{1,0:T(8,128)} %get-tuple-element.192, f32[320,2816]{1,0:T(8,128)} %fusion.331, pred[]{:T(512)S(6)} %eq.146, f32[320,2816]{1,0:T(8,128)} %copy-done.184, f32[320,2816]{1,0:T(8,128)} %fusion.330, ...), kind=kOutput, calls=%fused_computation.72 | convolution fusion | flops 1878261760 | bytes 26248192 | tf_op jit(solution)/shard_map/dot_general | solution.py:265
  348.3 18.2 %fusion.98 = f32[574,16,64]{0,2,1:T(8,128)} fusion(bf16[320,16,64]{0,2,1:T(8,128)(2,1)} %bitcast.782, pred[]{:T(512)S(6)} %eq.146, f32[16,320]{1,0:T(8,128)} %get-tuple-element.187, pred[320,574]{1,0:T(8,128)(4,1)} %get-tuple-element.182, bf16[320,16,64]{0,2,1:T(8,128)(2,1)S(1)} %bitcast.688, bf16[574,16,64]{0,2,1:T(8,128)(2,1)} %bitcast.669, ...), kind=kOutput, calls=%fused_computation.168 | convolution fusion | flops 775870016 | bytes 16817536 | tf_op jit(solution)/shard_map/hqk,qhd->khd/dot_general | solution.py:284
  369.0 15.2 %multiply_reduce_fusion.2 = (f32[16,320]{1,0:T(8,128)S(1)}, f32[16,320,574]{2,1,0:T(8,128)}) fusion(pred[]{:T(512)S(6)} %eq.146, f32[16,320,574]{2,1,0:T(8,128)} %get-tuple-element.188, f32[16,320]{1,0:T(8,128)} %get-tuple-element.187, f32[16,320,574]{2,1,0:T(8,128)} %get-tuple-element.194, f32[16,320]{1,0:T(8,128)} %get-tuple-element.193, ...), kind=kOutput, calls=%fused_computation.8 | convolution fusion | flops 391453696 | bytes 38334464 | tf_op jit(solution)/shard_map/qhd,khd->hqk/dot_general | solution.py:281
  384.3 13.4 %multiply_convert_fusion.2 = bf16[16,320,574]{2,1,0:T(8,128)(2,1)S(1)} fusion(f32[16,320,574]{2,1,0:T(8,128)} %get-tuple-element.199, f32[16,320]{1,0:T(8,128)S(1)} %get-tuple-element.198, pred[]{:T(512)S(6)} %eq.146, f32[16,320,574]{2,1,0:T(8,128)} %get-tuple-element.188, f32[16,320]{1,0:T(8,128)S(1)} %copy-done.148, f32[16,320,574]{2,1,0:T(8,128)} %get-tuple-element.194, ...), kind=kLoop, calls=%fused_computation.7 | loop fusion | flops 17633280 | bytes 41205760 | tf_op jit(solution)/shard_map/convert_element_type | solution.py:289
  427.0 9.5 collective-permute-start.53
  483.9 9.0 fusion.328
  519.5 9.4 broadcast_select_fusion.7
  547.0 18.1 %fusion.101 = f32[574,16,64]{0,2,1:T(8,128)} fusion(bf16[320,16,64]{0,2,1:T(8,128)(2,1)} %bitcast.784, pred[]{:T(512)S(6)} %eq.146, f32[16,320]{1,0:T(8,128)S(1)} %copy-done.149, pred[320,574]{1,0:T(8,128)(4,1)} %get-tuple-element.182, bf16[320,16,64]{0,2,1:T(8,128)(2,1)S(1)} %bitcast.690, bf16[574,16,64]{0,2,1:T(8,128)(2,1)} %bitcast.670, ...), kind=kOutput, calls=%fused_computation.169 | convolution fusion | flops 775870016 | bytes 16817536 | tf_op jit(solution)/shard_map/hqk,qhd->khd/dot_general | solution.py:284
  565.1 16.1 %multiply_reduce_fusion.1 = (f32[16,320]{1,0:T(8,128)S(1)}, f32[16,320,574]{2,1,0:T(8,128)}) fusion(pred[]{:T(512)S(6)} %eq.146, f32[16,320,574]{2,1,0:T(8,128)} %get-tuple-element.188, f32[16,320]{1,0:T(8,128)S(1)} %copy-done.149, f32[16,320,574]{2,1,0:T(8,128)} %get-tuple-element.201, f32[16,320]{1,0:T(8,128)S(1)} %copy-done.152, ...), kind=kOutput, calls=%fused_computation.6 | convolution fusion | flops 391453696 | bytes 38334464 | tf_op jit(solution)/shard_map/qhd,khd->hqk/dot_general | solution.py:281
  583.7 13.4 %multiply_convert_fusion.1 = bf16[16,320,574]{2,1,0:T(8,128)(2,1)S(1)} fusion(f32[16,320,574]{2,1,0:T(8,128)} %get-tuple-element.205, f32[16,320]{1,0:T(8,128)S(1)} %get-tuple-element.204, pred[]{:T(512)S(6)} %eq.146, f32[16,320,574]{2,1,0:T(8,128)} %get-tuple-element.188, f32[16,320]{1,0:T(8,128)S(1)} %copy-done.149, f32[16,320,574]{2,1,0:T(8,128)} %get-tuple-element.201, ...), kind=kLoop, calls=%fused_computation.5 | loop fusion | flops 17633280 | bytes 41205760 | tf_op jit(solution)/shard_map/convert_element_type | solution.py:289
  610.6 11.4 %collective-permute-start.56 = (f32[2,127,1024]{2,0,1:T(2,128)}, f32[2,127,1024]{2,0,1:T(2,128)}, u32[]{:S(2)}, u32[]{:S(2)}) collective-permute-start(f32[2,127,1024]{2,0,1:T(2,128)} %copy.189), channel_id=1, source_target_pairs={{0,4},{4,8},{8,12},{1,5},{5,9},{9,13},{2,6},{6,10},{10,14},{3,7},{... | collective-permute-start | bytes 3121160 | tf_op jit(solution)/shard_map/ppermute | solution.py:37
  664.0 11.7 %collective-permute-done.58 = bf16[320,1024]{1,0:T(8,128)(2,1)} collective-permute-done((bf16[320,1024]{1,0:T(8,128)(2,1)}, bf16[320,1024]{1,0:T(8,128)(2,1)}, u32[]{:S(2)}, u32[]{:S(2)}) %collective-permute-start.58) | collective-permute-done | bytes 655392 | tf_op jit(solution)/shard_map/ppermute | solution.py:37
  678.0 15.9 %broadcast_select_fusion.6 = (bf16[320,2816]{1,0:T(8,128)(2,1)}, bf16[320,2816]{1,0:T(8,128)(2,1)}, bf16[320,2816]{1,0:T(8,128)(2,1)}, bf16[320,2816]{1,0:T(8,12...) fusion(bf16[320,2816]{1,0:T(8,128)(2,1)} %copy-done.187, pred[]{:T(512)S(6)} %eq.146, ...), kind=kOutput, calls=%fused_computation.163 | convolution fusion | flops 1882439680 | bytes 38862848 | tf_op jit(solution)/shard_map/dot_general | solution.py:265
  711.8 17.9 %fusion.104 = f32[574,16,64]{0,2,1:T(8,128)} fusion(bf16[320,16,64]{0,2,1:T(8,128)(2,1)S(1)} %bitcast.786, pred[]{:T(512)S(6)} %eq.146, f32[16,320]{1,0:T(8,128)S(1)} %copy-done.151, pred[320,574]{1,0:T(8,128)(4,1)} %get-tuple-element.181, bf16[320,16,64]{0,2,1:T(8,128)(2,1)} %bitcast.695, bf16[574,16,64]{0,2,1:T(8,128)(2,1)S(1)} %bitcast.676, ...), kind=kOutput, calls=%fused_computation.170 | convolution fusion | flops 775870016 | bytes 16817536 | tf_op jit(solution)/shard_map/hqk,qhd->khd/dot_general | solution.py:284
  729.7 14.7 %multiply_reduce_fusion = (f32[16,320]{1,0:T(8,128)S(1)}, f32[16,320,574]{2,1,0:T(8,128)}) fusion(pred[]{:T(512)S(6)} %eq.146, f32[16,320,574]{2,1,0:T(8,128)} %get-tuple-element.194, f32[16,320]{1,0:T(8,128)S(1)} %copy-done.151, f32[16,320,574]{2,1,0:T(8,128)} %get-tuple-element.201, f32[16,320]{1,0:T(8,128)S(1)} %copy-done.153, ...), kind=kOutput, calls=%fused_computation.4 | convolution fusion | flops 391453696 | bytes 38334464 | tf_op jit(solution)/shard_map/qhd,khd->hqk/dot_general | solution.py:281
  744.4 13.5 %multiply_convert_fusion = bf16[16,320,574]{2,1,0:T(8,128)(2,1)S(1)} fusion(f32[16,320,574]{2,1,0:T(8,128)} %get-tuple-element.209, f32[16,320]{1,0:T(8,128)S(1)} %get-tuple-element.208, pred[]{:T(512)S(6)} %eq.146, f32[16,320,574]{2,1,0:T(8,128)} %get-tuple-element.194, f32[16,320]{1,0:T(8,128)S(1)} %copy-done.151, f32[16,320,574]{2,1,0:T(8,128)} %get-tuple-element.201, ...), kind=kLoop, calls=%fused_computation.3 | loop fusion | flops 17633280 | bytes 41205760 | tf_op jit(solution)/shard_map/convert_element_type | solution.py:289
  785.7 9.7 convolution_convert_fusion
  958.4 18.4 %collective-permute-done.70 = bf16[64,3072]{1,0:T(8,128)(2,1)S(1)} collective-permute-done((bf16[64,3072]{1,0:T(8,128)(2,1)S(1)}, bf16[64,3072]{1,0:T(8,128)(2,1)S(1)}, u32[]{:S(2)}, u32[]{:S(2)}) %collective-permute-start.70) | collective-permute-done | bytes 393248 | tf_op jit(solution)/shard_map/ppermute | solution.py:129
  984.1 12.4 %collective-permute-done.72 = bf16[64,3072]{1,0:T(8,128)(2,1)S(1)} collective-permute-done((bf16[64,3072]{1,0:T(8,128)(2,1)S(1)}, bf16[64,3072]{1,0:T(8,128)(2,1)S(1)}, u32[]{:S(2)}, u32[]{:S(2)}) %collective-permute-start.72) | collective-permute-done | bytes 393248 | tf_op jit(solution)/shard_map/ppermute | solution.py:129
  1001.4 15.9 %collective-permute-done.74 = bf16[64,3072]{1,0:T(8,128)(2,1)S(1)} collective-permute-done((bf16[64,3072]{1,0:T(8,128)(2,1)S(1)}, bf16[64,3072]{1,0:T(8,128)(2,1)S(1)}, u32[]{:S(2)}, u32[]{:S(2)}) %collective-permute-start.74) | collective-permute-done | bytes 393248 | tf_op jit(solution)/shard_map/ppermute | solution.py:129
  1021.4 8.8 collective-permute-done.107
  (875 shorter events, 616.3 us)
Async XLA Ops:
  22.7 25.2 %collective-permute-start.35 = (bf16[176,1024]{1,0:T(8,128)(2,1)}, bf16[176,1024]{1,0:T(8,128)(2,1)}, u32[]{:S(2)}, u32[]{:S(2)}) collective-permute-start(bf16[176,1024]{1,0:T(8,128)(2,1)} %bitcast.662), channel_id=1, source_target_pairs={{0,1},{1,2},{2,3},{3,0},{4,5},{5,6},{6,7},{7,4},{8,9},{9,10},{10,1... | collective-permute-start | bytes 1081352 | tf_op jit(solution)/shard_map/ppermute | solution.py:128
  25.6 26.5 %collective-permute-start.1 = (bf16[272,1024]{1,0:T(8,128)(2,1)S(1)}, bf16[272,1024]{1,0:T(8,128)(2,1)S(1)}, u32[]{:S(2)}, u32[]{:S(2)}) collective-permute-start(bf16[272,1024]{1,0:T(8,128)(2,1)S(1)} %fusion.225.refs_0_), channel_id=1, source_target_pairs={{0,8},{4,12},{8,0},{12,4},{1,9},{5,13},{9,1},{13,5},{2,10},{6,14},... | collective-permute-start | bytes 1671176 | tf_op jit(solution)/shard_map/ppermute | solution.py:129
  26.1 26.0 %collective-permute-start = (bf16[272,1024]{1,0:T(8,128)(2,1)S(1)}, bf16[272,1024]{1,0:T(8,128)(2,1)S(1)}, u32[]{:S(2)}, u32[]{:S(2)}) collective-permute-start(bf16[272,1024]{1,0:T(8,128)(2,1)S(1)} %fusion.225.refs_0_), channel_id=1, source_target_pairs={{0,4},{4,0},{8,12},{12,8},{1,5},{5,1},{9,13},{13,9},{2,6},{6,2},{1... | collective-permute-start | bytes 1671176 | tf_op jit(solution)/shard_map/ppermute | solution.py:130
  40.1 27.0 %collective-permute-start.11 = (bf16[272,1024]{1,0:T(8,128)(2,1)S(1)}, bf16[272,1024]{1,0:T(8,128)(2,1)}, u32[]{:S(2)}, u32[]{:S(2)}) collective-permute-start(bf16[272,1024]{1,0:T(8,128)(2,1)S(1)} %collective-permute-done.7.refs_8_), channel_id=1, source_target_pairs={{0,1},{1,2},{2,3},{3,0},{4,5},{5,6},{6,7},{7,4},{8,9},{9,10},{10,1... | collective-permute-start | bytes 1671176 | tf_op jit(solution)/shard_map/ppermute | solution.py:128
  92.8 39.3 %collective-permute-start.20 = (bf16[128,2816]{1,0:T(8,128)(2,1)S(1)}, bf16[128,2816]{1,0:T(8,128)(2,1)}, u32[]{:S(2)}, u32[]{:S(2)}) collective-permute-start(bf16[128,2816]{1,0:T(8,128)(2,1)S(1)} %pad_maximum_fusion.12.refs_0_), channel_id=1, source_target_pairs={{0,1},{1,2},{2,3},{3,0},{4,5},{5,6},{6,7},{7,4},{8,9},{9,10},{10,1... | collective-permute-start | bytes 2162696 | tf_op jit(solution)/shard_map/ppermute | solution.py:128
  93.7 35.1 %collective-permute-start.37 = (bf16[176,1024]{1,0:T(8,128)(2,1)}, bf16[176,1024]{1,0:T(8,128)(2,1)}, u32[]{:S(2)}, u32[]{:S(2)}) collective-permute-start(bf16[176,1024]{1,0:T(8,128)(2,1)} %collective-permute-done.35.refs_4_), channel_id=1, source_target_pairs={{0,8},{4,12},{8,0},{12,4},{1,9},{5,13},{9,1},{13,5},{2,10},{6,14},... | collective-permute-start | bytes 1081352 | tf_op jit(solution)/shard_map/ppermute | solution.py:129
  95.5 34.3 %collective-permute-start.36 = (bf16[176,1024]{1,0:T(8,128)(2,1)}, bf16[176,1024]{1,0:T(8,128)(2,1)}, u32[]{:S(2)}, u32[]{:S(2)}) collective-permute-start(bf16[176,1024]{1,0:T(8,128)(2,1)} %collective-permute-done.35.refs_4_), channel_id=1, source_target_pairs={{0,4},{4,0},{8,12},{12,8},{1,5},{5,1},{9,13},{13,9},{2,6},{6,2},{1... | collective-permute-start | bytes 1081352 | tf_op jit(solution)/shard_map/ppermute | solution.py:130
  96.6 33.3 %collective-permute-start.34 = (bf16[176,1024]{1,0:T(8,128)(2,1)}, bf16[176,1024]{1,0:T(8,128)(2,1)}, u32[]{:S(2)}, u32[]{:S(2)}) collective-permute-start(bf16[176,1024]{1,0:T(8,128)(2,1)} %collective-permute-done.33.refs_2_), channel_id=1, source_target_pairs={{0,4},{4,0},{8,12},{12,8},{1,5},{5,1},{9,13},{13,9},{2,6},{6,2},{1... | collective-permute-start | bytes 1081352 | tf_op jit(solution)/shard_map/ppermute | solution.py:130
  97.7 32.7 %collective-permute-start.43 = (bf16[176,1024]{1,0:T(8,128)(2,1)}, bf16[176,1024]{1,0:T(8,128)(2,1)}, u32[]{:S(2)}, u32[]{:S(2)}) collective-permute-start(bf16[176,1024]{1,0:T(8,128)(2,1)} %collective-permute-done.39.refs_8_), channel_id=1, source_target_pairs={{0,1},{1,2},{2,3},{3,0},{4,5},{5,6},{6,7},{7,4},{8,9},{9,10},{10,1... | collective-permute-start | bytes 1081352 | tf_op jit(solution)/shard_map/ppermute | solution.py:128
  140.4 29.2 %collective-permute-start.18 = (bf16[128,2816]{1,0:T(8,128)(2,1)S(1)}, bf16[128,2816]{1,0:T(8,128)(2,1)}, u32[]{:S(2)}, u32[]{:S(2)}) collective-permute-start(bf16[128,2816]{1,0:T(8,128)(2,1)S(1)} %pad_maximum_fusion.12.refs_0_), channel_id=1, source_target_pairs={{0,8},{4,12},{8,0},{12,4},{1,9},{5,13},{9,1},{13,5},{2,10},{6,14},... | collective-permute-start | bytes 2162696 | tf_op jit(solution)/shard_map/ppermute | solution.py:129
  169.6 26.1 %collective-permute-start.22 = (bf16[128,2816]{1,0:T(8,128)(2,1)}, bf16[128,2816]{1,0:T(8,128)(2,1)}, u32[]{:S(2)}, u32[]{:S(2)}) collective-permute-start(bf16[128,2816]{1,0:T(8,128)(2,1)} %collective-permute-done.20.refs_4_), channel_id=1, source_target_pairs={{0,8},{4,12},{8,0},{12,4},{1,9},{5,13},{9,1},{13,5},{2,10},{6,14},... | collective-permute-start | bytes 2162696 | tf_op jit(solution)/shard_map/ppermute | solution.py:129
  175.0 30.0 %collective-permute-start.26 = (bf16[128,2816]{1,0:T(8,128)(2,1)S(1)}, bf16[128,2816]{1,0:T(8,128)(2,1)}, u32[]{:S(2)}, u32[]{:S(2)}) collective-permute-start(bf16[128,2816]{1,0:T(8,128)(2,1)S(1)} %collective-permute-done.24.refs_8_), channel_id=1, source_target_pairs={{0,8},{4,12},{8,0},{12,4},{1,9},{5,13},{9,1},{13,5},{2,10},{6,14},... | collective-permute-start | bytes 2162696 | tf_op jit(solution)/shard_map/ppermute | solution.py:129
  175.1 44.9 %collective-permute-start.30 = (bf16[128,2816]{1,0:T(8,128)(2,1)}, bf16[128,2816]{1,0:T(8,128)(2,1)}, u32[]{:S(2)}, u32[]{:S(2)}) collective-permute-start(bf16[128,2816]{1,0:T(8,128)(2,1)} %collective-permute-done.28.refs_12_), channel_id=1, source_target_pairs={{0,8},{4,12},{8,0},{12,4},{1,9},{5,13},{9,1},{13,5},{2,10},{6,14},... | collective-permute-start | bytes 2162696 | tf_op jit(solution)/shard_map/ppermute | solution.py:129
  195.7 36.2 %collective-permute-start.25 = (bf16[128,2816]{1,0:T(8,128)(2,1)S(1)}, bf16[128,2816]{1,0:T(8,128)(2,1)}, u32[]{:S(2)}, u32[]{:S(2)}) collective-permute-start(bf16[128,2816]{1,0:T(8,128)(2,1)S(1)} %collective-permute-done.24.refs_8_), channel_id=1, source_target_pairs={{0,4},{4,0},{8,12},{12,8},{1,5},{5,1},{9,13},{13,9},{2,6},{6,2},{1... | collective-permute-start | bytes 2162696 | tf_op jit(solution)/shard_map/ppermute | solution.py:130
  195.7 36.2 %collective-permute-start.23 = (bf16[128,2816]{1,0:T(8,128)(2,1)}, bf16[128,2816]{1,0:T(8,128)(2,1)}, u32[]{:S(2)}, u32[]{:S(2)}) collective-permute-start(bf16[128,2816]{1,0:T(8,128)(2,1)} %collective-permute-done.22.refs_6_), channel_id=1, source_target_pairs={{0,4},{4,0},{8,12},{12,8},{1,5},{5,1},{9,13},{13,9},{2,6},{6,2},{1... | collective-permute-start | bytes 2162696 | tf_op jit(solution)/shard_map/ppermute | solution.py:130
  196.2 35.7 %collective-permute-start.29 = (bf16[128,2816]{1,0:T(8,128)(2,1)}, bf16[128,2816]{1,0:T(8,128)(2,1)}, u32[]{:S(2)}, u32[]{:S(2)}) collective-permute-start(bf16[128,2816]{1,0:T(8,128)(2,1)} %collective-permute-done.28.refs_12_), channel_id=1, source_target_pairs={{0,4},{4,0},{8,12},{12,8},{1,5},{5,1},{9,13},{13,9},{2,6},{6,2},{1... | collective-permute-start | bytes 2162696 | tf_op jit(solution)/shard_map/ppermute | solution.py:130
  205.0 27.0 %collective-permute-start.27 = (bf16[128,2816]{1,0:T(8,128)(2,1)}, bf16[128,2816]{1,0:T(8,128)(2,1)}, u32[]{:S(2)}, u32[]{:S(2)}) collective-permute-start(bf16[128,2816]{1,0:T(8,128)(2,1)} %collective-permute-done.26.refs_10_), channel_id=1, source_target_pairs={{0,4},{4,0},{8,12},{12,8},{1,5},{5,1},{9,13},{13,9},{2,6},{6,2},{1... | collective-permute-start | bytes 2162696 | tf_op jit(solution)/shard_map/ppermute | solution.py:130
  404.6 40.6 %collective-permute-start.54 = (f32[2,127,1024]{2,0,1:T(2,128)}, f32[2,127,1024]{2,0,1:T(2,128)}, u32[]{:S(2)}, u32[]{:S(2)}) collective-permute-start(f32[2,127,1024]{2,0,1:T(2,128)} %copy.183), channel_id=1, source_target_pairs={{4,0},{8,4},{12,8},{5,1},{9,5},{13,9},{6,2},{10,6},{14,10},{7,3},{... | collective-permute-start | bytes 3121160 | tf_op jit(solution)/shard_map/ppermute | solution.py:37
  417.1 40.6 %collective-permute-start.50 = (bf16[320,1024]{1,0:T(8,128)(2,1)}, bf16[320,1024]{1,0:T(8,128)(2,1)}, u32[]{:S(2)}, u32[]{:S(2)}) collective-permute-start(bf16[320,1024]{1,0:T(8,128)(2,1)} %fusion.111), channel_id=1, source_target_pairs={{0,16},{1,17},{2,18},{3,19},{4,20},{5,21},{6,22},{7,23},{8,24},{9,... | collective-permute-start | bytes 1966088 | tf_op jit(solution)/shard_map/ppermute | solution.py:37
  475.4 41.8 %collective-permute-start.55 = (bf16[320,1024]{1,0:T(8,128)(2,1)}, bf16[320,1024]{1,0:T(8,128)(2,1)}, u32[]{:S(2)}, u32[]{:S(2)}) collective-permute-start(bf16[320,1024]{1,0:T(8,128)(2,1)} %fusion.115), channel_id=1, source_target_pairs={{16,0},{17,1},{18,2},{19,3},{20,4},{21,5},{22,6},{23,7},{24,8},{25... | collective-permute-start | bytes 1966088 | tf_op jit(solution)/shard_map/ppermute | solution.py:37
  604.9 33.8 %collective-permute-start.57 = (f32[2,127,1024]{2,0,1:T(2,128)}, f32[2,127,1024]{2,0,1:T(2,128)}, u32[]{:S(2)}, u32[]{:S(2)}) collective-permute-start(f32[2,127,1024]{2,0,1:T(2,128)} %copy.192), channel_id=1, source_target_pairs={{4,0},{8,4},{12,8},{5,1},{9,5},{13,9},{6,2},{10,6},{14,10},{7,3},{... | collective-permute-start | bytes 3121160 | tf_op jit(solution)/shard_map/ppermute | solution.py:37
  610.6 31.0 %collective-permute-start.56 = (f32[2,127,1024]{2,0,1:T(2,128)}, f32[2,127,1024]{2,0,1:T(2,128)}, u32[]{:S(2)}, u32[]{:S(2)}) collective-permute-start(f32[2,127,1024]{2,0,1:T(2,128)} %copy.189), channel_id=1, source_target_pairs={{0,4},{4,8},{8,12},{1,5},{5,9},{9,13},{2,6},{6,10},{10,14},{3,7},{... | collective-permute-start | bytes 3121160 | tf_op jit(solution)/shard_map/ppermute | solution.py:37
  779.5 118.7 %collective-permute-start.85 = (bf16[2,4,64,2816]{3,2,1,0:T(8,128)(2,1)}, bf16[2,4,64,2816]{3,2,1,0:T(8,128)(2,1)}, u32[]{:S(2)}, u32[]{:S(2)}) collective-permute-start(bf16[2,4,64,2816]{3,2,1,0:T(8,128)(2,1)} %dynamic-slice_bitcast_fusion.3), channel_id=1, source_target_pairs={{0,4},{4,0},{8,12},{12,8},{1,5},{5,1},{9,13},{13,9},{2,6},{6,2},{1... | collective-permute-start | bytes 8650760 | tf_op jit(solution)/shard_map/ppermute | solution.py:130
  779.5 119.9 %collective-permute-start.93 = (bf16[2,4,64,2816]{3,2,1,0:T(8,128)(2,1)}, bf16[2,4,64,2816]{3,2,1,0:T(8,128)(2,1)}, u32[]{:S(2)}, u32[]{:S(2)}) collective-permute-start(bf16[2,4,64,2816]{3,2,1,0:T(8,128)(2,1)} %dynamic-slice_bitcast_fusion.2), channel_id=1, source_target_pairs={{0,4},{4,0},{8,12},{12,8},{1,5},{5,1},{9,13},{13,9},{2,6},{6,2},{1... | collective-permute-start | bytes 8650760 | tf_op jit(solution)/shard_map/ppermute | solution.py:130
  784.4 39.7 %collective-permute-start.60 = (f32[2,127,1024]{2,0,1:T(2,128)}, f32[2,127,1024]{2,0,1:T(2,128)}, u32[]{:S(2)}, u32[]{:S(2)}) collective-permute-start(f32[2,127,1024]{2,0,1:T(2,128)} %copy.201), channel_id=1, source_target_pairs={{4,0},{8,4},{12,8},{5,1},{9,5},{13,9},{6,2},{10,6},{14,10},{7,3},{... | collective-permute-start | bytes 3121160 | tf_op jit(solution)/shard_map/ppermute | solution.py:37
  810.6 41.9 %collective-permute-start.77 = (bf16[2,4,64,1024]{3,2,1,0:T(8,128)(2,1)}, bf16[2,4,64,1024]{3,2,1,0:T(8,128)(2,1)}, u32[]{:S(2)}, u32[]{:S(2)}) collective-permute-start(bf16[2,4,64,1024]{3,2,1,0:T(8,128)(2,1)} %dynamic-slice_bitcast_fusion.4), channel_id=1, source_target_pairs={{0,4},{4,0},{8,12},{12,8},{1,5},{5,1},{9,13},{13,9},{2,6},{6,2},{1... | collective-permute-start | bytes 3145736 | tf_op jit(solution)/shard_map/ppermute | solution.py:130
  824.1 78.4 %collective-permute-start.101 = (bf16[2,4,176,1024]{3,2,1,0:T(8,128)(2,1)}, bf16[2,4,176,1024]{3,2,1,0:T(8,128)(2,1)}, u32[]{:S(2)}, u32[]{:S(2)}) collective-permute-start(bf16[2,4,176,1024]{3,2,1,0:T(8,128)(2,1)} %dynamic-slice_bitcast_fusion.1), channel_id=1, source_target_pairs={{0,4},{4,0},{8,12},{12,8},{1,5},{5,1},{9,13},{13,9},{2,6},{6,2},{1... | collective-permute-start | bytes 8650760 | tf_op jit(solution)/shard_map/ppermute | solution.py:130
  892.6 58.4 %collective-permute-start.69 = (bf16[2,4,64,3072]{3,2,1,0:T(8,128)(2,1)S(1)}, bf16[2,4,64,3072]{3,2,1,0:T(8,128)(2,1)S(1)}, u32[]{:S(2)}, u32[]{:S(2)}) collective-permute-start(bf16[2,4,64,3072]{3,2,1,0:T(8,128)(2,1)S(1)} %dynamic-slice_bitcast_fusion), channel_id=1, source_target_pairs={{0,4},{4,0},{8,12},{12,8},{1,5},{5,1},{9,13},{13,9},{2,6},{6,2},{1... | collective-permute-start | bytes 9437192 | tf_op jit(solution)/shard_map/ppermute | solution.py:130
  949.3 29.6 %collective-permute-start.98 = (bf16[64,2816]{1,0:T(8,128)(2,1)S(1)}, bf16[64,2816]{1,0:T(8,128)(2,1)S(1)}, u32[]{:S(2)}, u32[]{:S(2)}) collective-permute-start(bf16[64,2816]{1,0:T(8,128)(2,1)S(1)} %get-tuple-element.102), channel_id=1, source_target_pairs={{0,8},{4,12},{8,0},{12,4},{1,9},{5,13},{9,1},{13,5},{2,10},{6,14},... | collective-permute-start | bytes 1081352 | tf_op jit(solution)/shard_map/ppermute | solution.py:129
  949.3 29.8 %collective-permute-start.97 = (bf16[64,2816]{1,0:T(8,128)(2,1)S(1)}, bf16[64,2816]{1,0:T(8,128)(2,1)S(1)}, u32[]{:S(2)}, u32[]{:S(2)}) collective-permute-start(bf16[64,2816]{1,0:T(8,128)(2,1)S(1)} %get-tuple-element.103), channel_id=1, source_target_pairs={{0,1},{1,2},{2,3},{3,0},{4,5},{5,6},{6,7},{7,4},{8,9},{9,10},{10,1... | collective-permute-start | bytes 1081352 | tf_op jit(solution)/shard_map/ppermute | solution.py:128
  951.0 29.5 %collective-permute-start.106 = (bf16[176,1024]{1,0:T(8,128)(2,1)S(1)}, bf16[176,1024]{1,0:T(8,128)(2,1)S(1)}, u32[]{:S(2)}, u32[]{:S(2)}) collective-permute-start(bf16[176,1024]{1,0:T(8,128)(2,1)S(1)} %get-tuple-element.96), channel_id=1, source_target_pairs={{0,8},{4,12},{8,0},{12,4},{1,9},{5,13},{9,1},{13,5},{2,10},{6,14},... | collective-permute-start | bytes 1081352 | tf_op jit(solution)/shard_map/ppermute | solution.py:129
  980.6 38.8 %collective-permute-start.100 = (bf16[64,2816]{1,0:T(8,128)(2,1)S(1)}, bf16[64,2816]{1,0:T(8,128)(2,1)S(1)}, u32[]{:S(2)}, u32[]{:S(2)}) collective-permute-start(bf16[64,2816]{1,0:T(8,128)(2,1)S(1)} %get-tuple-element.100), channel_id=1, source_target_pairs={{0,8},{4,12},{8,0},{12,4},{1,9},{5,13},{9,1},{13,5},{2,10},{6,14},... | collective-permute-start | bytes 1081352 | tf_op jit(solution)/shard_map/ppermute | solution.py:129
  (290 other events, 3779.8 us)

commit v2 on v0

v2 whole, which is shorter than its diff:
```python
import functools

import jax
import jax.numpy as jnp
from jax import lax
from jax.experimental import pallas as pl
from jax.experimental.pallas import tpu as pltpu
from jax.sharding import PartitionSpec as P

HEAD_DIM = 64
RADIUS = 127


EPSILON = 1e-06


def shifted(shard, axis, by):
    length = lax.axis_size(axis)
    pairs = [(i, i + by) for i in range(length) if 0 <= i + by < length]
    return lax.ppermute(shard, axis, pairs)


HALO = 128
BLOCK = 128
WIDE = 256
NEVER = -1e30


def call(kernel, grid, scalars, ins, in_specs, outs, out_specs, scratch=(), aliases=None, cost=None):
    return pl.pallas_call(
        kernel,
        out_shape=outs,
        grid_spec=pltpu.PrefetchScalarGridSpec(
            num_scalar_prefetch=1,
            grid=grid,
            in_specs=in_specs,
            out_specs=out_specs,
            scratch_shapes=list(scratch),
        ),
        input_output_aliases=aliases or {},
        compiler_params=pltpu.CompilerParams(
            vmem_limit_bytes=56 * 2**20, dimension_semantics=("arbitrary",) * len(grid)
        ),
        cost_estimate=cost,
    )(scalars, *ins)


def cost_of(flops, moved, transcendentals=0):
    return pl.CostEstimate(
        flops=int(flops), bytes_accessed=int(moved), transcendentals=int(transcendentals)
    )


def nt_dot(left, right):
    return lax.dot_general(
        left, right, (((1,), (1,)), ((), ())), preferred_element_type=jnp.float32
    )


def tn_dot(left, right):
    return lax.dot_general(
        left, right, (((0,), (0,)), ((), ())), preferred_element_type=jnp.float32
    )


def dot(left, right):
    return jnp.dot(left, right, preferred_element_type=jnp.float32)


def inverse_rms(values):
    return lax.rsqrt(jnp.mean(values * values, axis=-1, keepdims=True) + EPSILON)


def project_kernel(idx, own, arrived, gain, wq, wk, wv, *rest):
    x_out, n_out, q_out, kv_out, tail_out, head_out = rest[-6:]

    @pl.when(pl.program_id(0) == 0)
    def _():
        picked = jnp.where(
            idx[0] == 1, own[...].astype(jnp.float32), arrived[...].astype(jnp.float32)
        )
        x_out[...] = picked.astype(jnp.bfloat16)
        n_out[...] = (picked * inverse_rms(picked) * gain[...].astype(jnp.float32)).astype(
            jnp.bfloat16
        )

    normed = n_out[...]
    kv_out[0] = dot(normed, wk[...]).astype(jnp.bfloat16)
    kv_out[1] = dot(normed, wv[...]).astype(jnp.bfloat16)
    q_out[...] = dot(normed, wq[...]).astype(jnp.bfloat16)
    tail_out[...] = kv_out[:, pl.ds(kv_out.shape[1] - HALO, HALO)]
    head_out[...] = kv_out[:, pl.ds(0, HALO)]


def slot_call(kernel, grid, scalars, ins, in_specs, kept, fresh, store, slots, moment, scratch=(), cost=None):
    aliases, extra = {}, []
    outs, out_specs = [], []
    for name, shape, block, index, kind in kept:
        outs.append(jax.ShapeDtypeStruct((slots,) + shape, kind))
        if block is None:
            out_specs.append(pl.BlockSpec(memory_space=pl.ANY))
        else:
            out_specs.append(
                pl.BlockSpec((None,) + block, lambda j, s, index=index: (moment,) + index(j))
            )
        if name in store:
            aliases[1 + len(ins) + len(extra)] = len(outs) - 1
            extra.append(store[name])
    for shape, kind, spec in fresh:
        outs.append(jax.ShapeDtypeStruct(shape, kind))
        out_specs.append(spec)
    results = call(
        kernel,
        grid,
        scalars,
        list(ins) + extra,
        list(in_specs) + [pl.BlockSpec(memory_space=pl.ANY)] * len(extra),
        outs,
        out_specs,
        scratch,
        aliases,
        cost,
    )
    for (name, *_), value in zip(kept, results):
        store[name] = value
    return results[len(kept) :]


def whole_spec(shape):
    return pl.BlockSpec(shape, lambda j, s: (0,) * len(shape))


def project(store, slots, moment, scalars, own, arrived, params):
    rows, width = arrived.shape
    gain_one, query_w, key_w, value_w = params[:4]
    tile = WIDE
    columns = pl.BlockSpec((width, tile), lambda j, s: (0, j))
    at_start = lambda j: (0, 0)
    halo_spec = pl.BlockSpec((2, HALO, tile), lambda j, s: (0, 0, j))
    return slot_call(
        project_kernel,
        (width // tile,),
        scalars,
        [own, arrived, gain_one, query_w, key_w, value_w],
        [whole_spec((rows, width)), whole_spec((rows, width)), whole_spec((1, width))]
        + [columns] * 3,
        [
            ("source", (rows, width), (rows, width), at_start, jnp.bfloat16),
            ("normed", (rows, width), (rows, width), at_start, jnp.bfloat16),
            ("queries", (rows, width), (rows, tile), lambda j: (0, j), jnp.bfloat16),
        ],
        [
            (
                (2, rows, width),
                jnp.bfloat16,
                pl.BlockSpec((2, rows, tile), lambda j, s: (0, 0, j)),
            ),
            ((2, HALO, width), jnp.bfloat16, halo_spec),
            ((2, HALO, width), jnp.bfloat16, halo_spec),
        ],
        store,
        slots,
        moment,
        cost=cost_of(6 * rows * width * width, 6 * width * width + 14 * rows * width),
    )


def row_blocks(rows):
    return [(start, min(BLOCK, rows - start)) for start in range(0, rows, BLOCK)]


def head_masks(kind):
    lane = lax.broadcasted_iota(jnp.int32, (1, 2 * HEAD_DIM), 1)
    low = (lane < HEAD_DIM).astype(kind)
    return (low, (1 - low).astype(kind))


def wide_tile(size):
    return max(tile for tile in range(128, 1409, 128) if size % tile == 0)


def chunks(size, tile):
    return [(start, min(tile, size - start)) for start in range(0, size, tile)]


def stacked_heads(pair):
    return jnp.concatenate([pair * mask for mask in head_masks(pair.dtype)], 0)


def unstacked_heads(stacked):
    rows = stacked.shape[0] // 2
    low = lax.broadcasted_iota(jnp.int32, (1, 2 * HEAD_DIM), 1) < HEAD_DIM
    return jnp.where(low, stacked[:rows], stacked[rows:])


def attend_feed_kernel(
    moment, idx, q, kv, low, high, bias, wo, source, gain, wg, wu, wd, *rest
):
    (k_out, v_out, mixed_out, lse_out, res_out, two_out, gate_out, up_out, gated_out, result) = rest[-18:-8]
    total, gate_w, up_w, down_w, gate_all, up_all, gated_all, sems = rest[-8:]
    step = pl.program_id(0)
    rows, width = source.shape
    tiles = chunks(wg.shape[1], wide_tile(wg.shape[1]))
    ends = pl.num_programs(0) - 1

    def fetches():
        found = []
        for start, size in tiles:
            lanes = pl.ds(start, size)
            found.append(
                [
                    (wg.at[:, lanes], gate_w.at[:, lanes]),
                    (wu.at[:, lanes], up_w.at[:, lanes]),
                    (wd.at[lanes], down_w.at[lanes]),
                ]
            )
        return found

    def fetch(number, part):
        return pltpu.make_async_copy(
            *fetches()[number][part], sems.at[number * 3 + part]
        )

    @pl.when(step == 0)
    def _():
        for number in range(len(tiles)):
            for part in range(3):
                fetch(number, part).start()

    @pl.when(step < ends)
    def _():
        for place, out in ((0, k_out), (1, v_out)):
            out[pl.ds(0, HALO)] = low[place]
            out[pl.ds(HALO, rows)] = kv[place]
            out[pl.ds(HALO + rows, HALO)] = high[place]
        scale = jnp.bfloat16(HEAD_DIM**-0.5)
        for start, count in row_blocks(rows):
            span = count + 2 * HALO
            block_bias = bias[pl.ds(start, count), :span]
            both_bias = jnp.concatenate([block_bias, block_bias], 0)
            sums = []
            for pair in range(WIDE // (2 * HEAD_DIM)):
                lanes = slice(pair * 2 * HEAD_DIM, (pair + 1) * 2 * HEAD_DIM)
                q_both = stacked_heads(q[pl.ds(start, count), lanes] * scale)
                scores = nt_dot(q_both, k_out[pl.ds(start, span), lanes]) + both_bias
                most = jnp.max(scores, axis=-1, keepdims=True)
                powers = jnp.exp(scores - most)
                total_power = jnp.sum(powers, axis=-1, keepdims=True)
                probs = (powers * (1.0 / total_power)).astype(jnp.bfloat16)
                mixed = dot(probs, v_out[pl.ds(start, span), lanes])
                mixed_out[pl.ds(start, count), lanes] = unstacked_heads(mixed).astype(
                    jnp.bfloat16
                )
                log_sum = most + jnp.log(total_power)
                sums += [log_sum[:count], log_sum[count:]]
            lane = lax.broadcasted_iota(jnp.int32, (count, 2 * HEAD_DIM), 1)
            wide = jnp.zeros((count, 2 * HEAD_DIM), jnp.float32)
            for number, value in enumerate(sums):
                wide = jnp.where(lane == number, value, wide)
            lse_out[pl.ds(start, count)] = wide
        part = dot(mixed_out[...], wo[...])

        @pl.when(step == 0)
        def _():
            total[...] = source[...].astype(jnp.float32) + part

        @pl.when(step > 0)
        def _():
            total[...] += part

    @pl.when(step == ends)
    def _():
        residual = total[...]
        res_out[...] = residual
        normed = (residual * inverse_rms(residual) * gain[...].astype(jnp.float32)).astype(
            jnp.bfloat16
        )
        two_out[...] = normed
        base, stores = 3 * len(tiles), []
        for number, (start, size) in enumerate(tiles):
            lanes = slice(start, start + size)
            fetch(number, 0).wait()
            gate = dot(normed, gate_w[:, lanes])
            fetch(number, 1).wait()
            up = dot(normed, up_w[:, lanes])
            half, _, _ = gelu_parts(gate)
            gated = (gate * half * up).astype(jnp.bfloat16)
            gate_all[:, lanes] = gate.astype(jnp.bfloat16)
            up_all[:, lanes] = up.astype(jnp.bfloat16)
            gated_all[:, lanes] = gated
            for part, (here, there) in enumerate(
                ((gate_all, gate_out), (up_all, up_out), (gated_all, gated_out))
            ):
                copy = pltpu.make_async_copy(
                    here.at[:, pl.ds(start, size)],
                    there.at[moment, :, pl.ds(start, size)],
                    sems.at[base + 3 * number + part],
                )
                copy.start()
                stores.append(copy)
            fetch(number, 2).wait()
            total[...] += dot(gated, down_w[lanes])
        result[...] = total[...].astype(jnp.bfloat16)
        for copy in stores:
            copy.wait()


def attend_feed(store, slots, moment, scalars, kv, low, high, bias, params):
    rows, width = kv.shape[1:]
    out_w, gain_two, gate_w, up_w, down_w = params[4:]
    hidden = gate_w.shape[1]
    ext = rows + 2 * HALO
    quads = width // WIDE
    last = lambda j: jnp.minimum(j, quads - 1)
    at_start = lambda j: (0, 0)
    at_tile = lambda j: (0, last(j))
    halo_spec = pl.BlockSpec((2, HALO, WIDE), lambda j, s: (0, 0, last(j)))
    work = width * rows * ((BLOCK + 2 * HALO) * 8 + width * 2 + hidden * 6)
    tiles = len(chunks(hidden, wide_tile(hidden)))
    anywhere = pl.BlockSpec(memory_space=pl.ANY)
    (result,) = slot_call(
        functools.partial(attend_feed_kernel, moment),
        (quads + 1,),
        scalars,
        [store["queries"], kv, low, high, bias, out_w, store["source"], gain_two]
        + [gate_w, up_w, down_w],
        [
            pl.BlockSpec((None, rows, WIDE), lambda j, s: (moment, 0, last(j))),
            pl.BlockSpec((2, rows, WIDE), lambda j, s: (0, 0, last(j))),
            halo_spec,
            halo_spec,
            pl.BlockSpec((None,) + bias.shape[1:], lambda j, s: (s[2], 0, 0)),
            pl.BlockSpec((WIDE, width), lambda j, s: (last(j), 0)),
            pl.BlockSpec((None, rows, width), lambda j, s: (moment, 0, 0)),
            whole_spec((1, width)),
        ]
        + [anywhere] * 3,
        [
            ("keys", (ext, width), (ext, WIDE), at_tile, jnp.bfloat16),
            ("values", (ext, width), (ext, WIDE), at_tile, jnp.bfloat16),
            ("mixed", (rows, width), (rows, WIDE), at_tile, jnp.bfloat16),
            ("lse", (rows, quads * BLOCK), (rows, BLOCK), at_tile, jnp.float32),
            ("residual", (rows, width), (rows, width), at_start, jnp.float32),
            ("normed_two", (rows, width), (rows, width), at_start, jnp.bfloat16),
            ("gate", (rows, hidden), None, None, jnp.bfloat16),
            ("up", (rows, hidden), None, None, jnp.bfloat16),
            ("gated", (rows, hidden), None, None, jnp.bfloat16),
        ],
        [((rows, width), jnp.bfloat16, whole_spec((rows, width)))],
        store,
        slots,
        moment,
        [
            pltpu.VMEM((rows, width), jnp.float32),
            pltpu.VMEM((width, hidden), jnp.bfloat16),
            pltpu.VMEM((width, hidden), jnp.bfloat16),
            pltpu.VMEM((hidden, width), jnp.bfloat16),
            pltpu.VMEM((rows, hidden), jnp.bfloat16),
            pltpu.VMEM((rows, hidden), jnp.bfloat16),
            pltpu.VMEM((rows, hidden), jnp.bfloat16),
            pltpu.SemaphoreType.DMA((6 * tiles,)),
        ],
        cost_of(work, 6 * width * hidden + 2 * width * width + 20 * rows * width),
    )
    return result


def gelu_parts(gate):
    root = 0.7978845608028654
    bend = jnp.tanh(root * (gate + 0.044715 * gate * gate * gate))
    return 0.5 * (1.0 + bend), bend, root


def feed_back_kernel(idx, arrived, own, gate, up, residual, gain, wd, wg, wu, wo, *rest):
    g_out, dg_out, du_out, branch_out, gain_out, res_out, mixed_out, total = rest[-8:]
    step = pl.program_id(0)

    @pl.when(step == 0)
    def _():
        g_out[...] = jnp.where(
            idx[0] == 1, arrived[...].astype(jnp.float32), own[...].astype(jnp.float32)
        ).astype(jnp.bfloat16)

    gate_pre = gate[...].astype(jnp.float32)
    up_pre = up[...].astype(jnp.float32)
    grad_gated = nt_dot(g_out[...], wd[...])
    half, bend, root = gelu_parts(gate_pre)
    slope = half + 0.5 * gate_pre * (1.0 - bend * bend) * root * (
        1.0 + 3.0 * 0.044715 * gate_pre * gate_pre
    )
    grad_gate = (grad_gated * up_pre * slope).astype(jnp.bfloat16)
    grad_up = (grad_gated * gate_pre * half).astype(jnp.bfloat16)
    dg_out[...] = grad_gate
    du_out[...] = grad_up
    part = nt_dot(grad_gate, wg[...]) + nt_dot(grad_up, wu[...])

    @pl.when(step == 0)
    def _():
        total[...] = part

    @pl.when(step > 0)
    def _():
        total[...] += part

    @pl.when(step == pl.num_programs(0) - 1)
    def _():
        grads, grad_gain = norm_back(total[...], residual[...], gain[...].astype(jnp.float32))
        gain_out[...] = jnp.broadcast_to(grad_gain, gain_out.shape)
        grad_residual = g_out[...].astype(jnp.float32) + grads
        res_out[...] = grad_residual
        branch = grad_residual.astype(jnp.bfloat16)
        branch_out[...] = branch
        mixed_out[...] = nt_dot(branch, wo[...]).astype(jnp.bfloat16)


def norm_back(grads, values, gain):
    scale = inverse_rms(values)
    pulled = grads * gain
    mean = jnp.mean(pulled * values, axis=-1, keepdims=True)
    return (
        scale * pulled - values * (scale * scale * scale * mean),
        jnp.sum(grads * values * scale, axis=0, keepdims=True),
    )


def feed_back(store, slots, moment, scalars, arrived, own, params):
    out_w, gain_two, gate_w, up_w, down_w = params[4:]
    rows, width = arrived.shape
    hidden = gate_w.shape[1]
    tile = wide_tile(hidden)
    at_tile = lambda j: (0, j)
    at_start = lambda j: (0, 0)
    taken_tile = pl.BlockSpec((None, rows, tile), lambda j, s: (s[1], 0, j))
    return slot_call(
        feed_back_kernel,
        (hidden // tile,),
        scalars,
        [arrived, own, store["gate"], store["up"], store["residual"], gain_two]
        + [down_w, gate_w, up_w, out_w],
        [whole_spec((rows, width)), whole_spec((rows, width)), taken_tile, taken_tile]
        + [pl.BlockSpec((None, rows, width), lambda j, s: (s[1], 0, 0)), whole_spec((1, width))]
        + [pl.BlockSpec((tile, width), lambda j, s: (j, 0))]
        + [pl.BlockSpec((width, tile), lambda j, s: (0, j))] * 2
        + [whole_spec((width, width))],
        [
            ("grad_result", (rows, width), (rows, width), at_start, jnp.bfloat16),
            ("grad_gate", (rows, hidden), (rows, tile), at_tile, jnp.bfloat16),
            ("grad_up", (rows, hidden), (rows, tile), at_tile, jnp.bfloat16),
            ("grad_branch", (rows, width), (rows, width), at_start, jnp.bfloat16),
            ("gain_two", (8, width), (8, width), at_start, jnp.float32),
        ],
        [
            ((rows, width), jnp.float32, whole_spec((rows, width))),
            ((rows, width), jnp.bfloat16, whole_spec((rows, width))),
        ],
        store,
        slots,
        moment,
        [pltpu.VMEM((rows, width), jnp.float32)],
        cost_of(6 * rows * width * hidden + 2 * rows * width * width, 6 * width * hidden),
    )


def attend_back_kernel(idx, q, keys, values, mixed, lse, grad_mixed, bias, *rest):
    q_out, center, top, bottom, k_total, v_total = rest[-6:]
    rows = q.shape[0]
    scale = jnp.bfloat16(HEAD_DIM**-0.5)
    k_total[...] = jnp.zeros_like(k_total)
    v_total[...] = jnp.zeros_like(v_total)
    for start, count in row_blocks(rows):
        span = count + 2 * HALO
        block_bias = bias[pl.ds(start, count), :span]
        both_bias = jnp.concatenate([block_bias, block_bias], 0)
        for pair in range(WIDE // (2 * HEAD_DIM)):
            lanes = slice(pair * 2 * HEAD_DIM, (pair + 1) * 2 * HEAD_DIM)
            q_both = stacked_heads(q[pl.ds(start, count), lanes] * scale)
            g_both = stacked_heads(grad_mixed[pl.ds(start, count), lanes])
            m_pair = mixed[pl.ds(start, count), lanes].astype(jnp.float32)
            k_pair = keys[pl.ds(start, span), lanes]
            log_sum = jnp.concatenate(
                [lse[pl.ds(start, count), 2 * pair + n : 2 * pair + n + 1] for n in range(2)], 0
            )
            probs = jnp.exp(nt_dot(q_both, k_pair) + (both_bias - log_sum))
            grad_probs = nt_dot(g_both, values[pl.ds(start, span), lanes])
            mean = jnp.sum(
                g_both.astype(jnp.float32) * jnp.concatenate([m_pair, m_pair], 0),
                axis=-1,
                keepdims=True,
            )
            grad_scores = (probs * (grad_probs - mean)).astype(jnp.bfloat16)
            q_out[pl.ds(start, count), lanes] = (
                unstacked_heads(dot(grad_scores, k_pair)) * (HEAD_DIM**-0.5)
            ).astype(jnp.bfloat16)
            k_total[pl.ds(start, span), lanes] += tn_dot(grad_scores, q_both)
            v_total[pl.ds(start, span), lanes] += tn_dot(probs.astype(jnp.bfloat16), g_both)
    for place, total in ((0, k_total), (1, v_total)):
        top[place] = total[pl.ds(0, HALO)].astype(jnp.bfloat16)
        center[place] = total[pl.ds(HALO, rows)]
        bottom[place] = total[pl.ds(HALO + rows, HALO)].astype(jnp.bfloat16)


def attend_back(store, slots, moment, scalars, grad_mixed, bias):
    rows, width = grad_mixed.shape
    ext = rows + 2 * HALO
    taken = pl.BlockSpec((None, rows, WIDE), lambda j, s: (s[1], 0, j))
    taken_ext = pl.BlockSpec((None, ext, WIDE), lambda j, s: (s[1], 0, j))
    halo_spec = pl.BlockSpec((2, HALO, WIDE), lambda j, s: (0, 0, j))
    work = width * rows * (BLOCK + 2 * HALO) * 2
    return slot_call(
        attend_back_kernel,
        (width // WIDE,),
        scalars,
        [store["queries"], store["keys"], store["values"], store["mixed"], store["lse"]]
        + [grad_mixed, bias],
        [
            taken,
            taken_ext,
            taken_ext,
            taken,
            pl.BlockSpec((None, rows, BLOCK), lambda j, s: (s[1], 0, j)),
            pl.BlockSpec((rows, WIDE), lambda j, s: (0, j)),
            pl.BlockSpec((None,) + bias.shape[1:], lambda j, s: (s[2], 0, 0)),
        ],
        [("grad_queries", (rows, width), (rows, WIDE), lambda j: (0, j), jnp.bfloat16)],
        [
            (
                (2, rows, width),
                jnp.float32,
                pl.BlockSpec((2, rows, WIDE), lambda j, s: (0, 0, j)),
            ),
            ((2, HALO, width), jnp.bfloat16, halo_spec),
            ((2, HALO, width), jnp.bfloat16, halo_spec),
        ],
        store,
        slots,
        moment,
        [pltpu.VMEM((ext, WIDE), jnp.float32)] * 2,
        cost_of(work * 20, 24 * rows * width),
    )


def project_back_kernel(
    idx, grad_q, center, below, above, source, gain, grad_res, wq, wk, wv, *rest
):
    k_out, v_out, gain_out, in_out, total = rest[-5:]
    step = pl.program_id(0)
    rows = source.shape[0]
    for place, out in ((0, k_out), (1, v_out)):
        head = center[place, pl.ds(0, HALO)] + below[place].astype(jnp.float32)
        tail = center[place, pl.ds(rows - HALO, HALO)] + above[place].astype(jnp.float32)
        out[pl.ds(0, HALO)] = head.astype(jnp.bfloat16)
        out[pl.ds(HALO, rows - 2 * HALO)] = center[place, pl.ds(HALO, rows - 2 * HALO)].astype(
            jnp.bfloat16
        )
        out[pl.ds(rows - HALO, HALO)] = tail.astype(jnp.bfloat16)
    part = nt_dot(grad_q[...], wq[...]) + nt_dot(k_out[...], wk[...]) + nt_dot(v_out[...], wv[...])

    @pl.when(step == 0)
    def _():
        total[...] = part

    @pl.when(step > 0)
    def _():
        total[...] += part

    @pl.when(step == pl.num_programs(0) - 1)
    def _():
        grads, grad_gain = norm_back(
            total[...], source[...].astype(jnp.float32), gain[...].astype(jnp.float32)
        )
        gain_out[...] = jnp.broadcast_to(grad_gain, gain_out.shape)
        in_out[...] = (grad_res[...] + grads).astype(jnp.bfloat16)


def project_back(store, slots, moment, scalars, center, below, above, grad_res, params):
    rows, width = grad_res.shape
    gain_one, query_w, key_w, value_w = params[:4]
    at_tile = lambda j: (0, j)
    at_start = lambda j: (0, 0)
    halo_spec = pl.BlockSpec((2, HALO, WIDE), lambda j, s: (0, 0, j))
    columns = pl.BlockSpec((width, WIDE), lambda j, s: (0, j))
    return slot_call(
        project_back_kernel,
        (width // WIDE,),
        scalars,
        [store["grad_queries"], center, below, above, store["source"], gain_one, grad_res]
        + [query_w, key_w, value_w],
        [
            pl.BlockSpec((None, rows, WIDE), lambda j, s: (moment, 0, j)),
            pl.BlockSpec((2, rows, WIDE), lambda j, s: (0, 0, j)),
            halo_spec,
            halo_spec,
            pl.BlockSpec((None, rows, width), lambda j, s: (s[1], 0, 0)),
            whole_spec((1, width)),
            whole_spec((rows, width)),
        ]
        + [columns] * 3,
        [
            ("grad_keys", (rows, width), (rows, WIDE), at_tile, jnp.bfloat16),
            ("grad_values", (rows, width), (rows, WIDE), at_tile, jnp.bfloat16),
            ("gain_one", (8, width), (8, width), at_start, jnp.float32),
        ],
        [((rows, width), jnp.bfloat16, whole_spec((rows, width)))],
        store,
        slots,
        moment,
        [pltpu.VMEM((rows, width), jnp.float32)],
        cost_of(6 * rows * width * width, 6 * width * width + 20 * rows * width),
    )


def window_bias(lengths_row, shard_no, rows, seq_len):
    ends = jnp.cumsum(lengths_row)
    first = shard_no * rows
    row = jnp.arange(rows, dtype=jnp.int32)
    place = (row // BLOCK * BLOCK)[:, None] - HALO + jnp.arange(BLOCK + 2 * HALO, dtype=jnp.int32)

    def document(position):
        return jnp.sum((position[..., None] >= ends).astype(jnp.int32), axis=-1)

    key = first + place
    allowed = (
        (jnp.abs(row[:, None] - place) <= RADIUS)
        & (key >= 0)
        & (key < seq_len)
        & (document(first + row)[:, None] == document(key))
    )
    return jnp.where(allowed, 0.0, NEVER).astype(jnp.float32)


def after(cells, *others):
    return lax.optimization_barrier((cells,) + others)[0] if others else cells


class Link:
    def __init__(self, axis, pairs, depth):
        self.axis, self.pairs, self.depth, self.sent = axis, pairs, depth, []

    def __call__(self, cells):
        if self.depth and len(self.sent) >= self.depth:
            cells = after(cells, self.sent[-self.depth])
        self.sent.append(lax.ppermute(cells, self.axis, self.pairs))
        return self.sent[-1]


def links(depth=2):
    span = lax.axis_size("seq")
    high = span // 2
    across = [(h * 2 + c, ((h + 1) % high) * 2 + c) for h in range(high) for c in range(2)]
    pairs = [(i, i ^ 1) for i in range(span)]
    rings = lax.axis_size("wt")
    along = [(i, (i + 1) % rings) for i in range(rings)]
    return Link("seq", across, depth), Link("seq", pairs, 0), Link("wt", along, 0)


def places():
    high = lax.axis_size("seq") // 2
    shard_no = lax.axis_index("seq")
    return high, shard_no // 2, shard_no % 2


class Gather:
    def __init__(self, shard, lines):
        self.across, self.swap = lines[:2]
        self.level = lax.all_gather(shard, "wt", axis=0)

    def cross(self, *others):
        self.row = [after(self.level, *others)]
        for _ in range(1, lax.axis_size("seq") // 2):
            self.row.append(self.across(self.row[-1]))
        return self

    def pieces(self, *others):
        found = {}
        for j, part in enumerate(self.row):
            part = after(part, *others) if j else part
            found[(None, j, 0)] = part
            found[(None, j, 1)] = self.swap(part)
        return found


def ring_gather(shard, lines):
    across, swap, along = lines
    found, current = {}, shard
    for k in range(lax.axis_size("wt")):
        current = along(current) if k else current
        cells = current
        for j in range(lax.axis_size("seq") // 2):
            cells = across(cells) if j else cells
            found[(k, j, 0)] = cells
            found[(k, j, 1)] = swap(cells)
    return found


def assemble_kernel(count, plan, seat_ref, *refs):
    parts, wholes, sems = refs[:count], refs[count:-1], refs[-1]
    copies = []
    for number, (source, start, rows, seat, ring, whole, to) in enumerate(plan):
        there = wholes[whole].at[seat_ref[seat]]
        if ring is None:
            here, there = parts[source].at[:, pl.ds(start, rows)], there.at[:, pl.ds(to, rows)]
        else:
            here = parts[source].at[pl.ds(start, rows)]
            there = there.at[seat_ref[ring], pl.ds(to, rows)]
        copies.append(pltpu.make_async_copy(here, there, sems.at[number]))
    for copy in copies:
        copy.start()
    for copy in copies:
        copy.wait()


def assemble(pieces, pack):
    high, h, c = places()
    rings, z = lax.axis_size("wt"), lax.axis_index("wt")
    seats = [
        lax.rem(h - j + high, high) * 2 + (c + p) % 2 for j in range(high) for p in range(2)
    ] + [lax.rem(z - k + rings, rings) for k in range(rings)]
    sources, plan = [], []
    for (k, j, p), part in pieces.items():
        start = 0
        for whole, rows in enumerate(pack):
            ring = None if k is None else 2 * high + k
            plan.append((len(sources), start, rows, j * 2 + p, ring, whole, 0))
            start += rows
        sources.append(part)
    width, kind = sources[0].shape[-1], sources[0].dtype
    shapes = [(2 * high, rings, rows, width) for rows in pack]
    if any(rows % 16 for rows in pack):
        wholes = [jnp.zeros(shape, kind) for shape in shapes]
        for source, start, rows, seat, ring, whole, to in plan:
            part = sources[source]
            part = part[None] if ring is None else part[None, None]
            part = part[:, :, start : start + rows]
            place = (seats[seat], 0 if ring is None else seats[ring], to, 0)
            wholes[whole] = lax.dynamic_update_slice(wholes[whole], part, place)
    else:
        wholes = pl.pallas_call(
            functools.partial(assemble_kernel, len(sources), plan),
            out_shape=[jax.ShapeDtypeStruct(shape, kind) for shape in shapes],
            grid_spec=pltpu.PrefetchScalarGridSpec(
                num_scalar_prefetch=1,
                grid=(),
                in_specs=[pl.BlockSpec(memory_space=pl.ANY)] * len(sources),
                out_specs=[pl.BlockSpec(memory_space=pltpu.VMEM)] * len(shapes),
                scratch_shapes=[pltpu.SemaphoreType.DMA((len(plan),))],
            ),
            compiler_params=pltpu.CompilerParams(vmem_limit_bytes=40 * 2**20),
            cost_estimate=cost_of(0, 2 * sum(source.size * 2 for source in sources)),
        )(jnp.stack(seats).astype(jnp.int32), *sources)
    return [whole.reshape(-1, width) for whole in wholes]


def plus(left, right, kind):
    return (left.astype(jnp.float32) + right.astype(jnp.float32)).astype(kind)


class Scatter:
    def __init__(self, partial, lines, kind=jnp.bfloat16, along_first=False):
        self.across, self.swap = lines[:2]
        self.kind, self.along_first = kind, along_first
        high, h, c = places()
        self.high, self.h = high, h
        cells = partial.reshape(high, 2, -1, partial.shape[-1])
        self.mine = lax.dynamic_index_in_dim(cells, c, 1, False)
        self.received = self.swap(lax.dynamic_index_in_dim(cells, 1 - c, 1, False))
        if along_first:
            rows = self.mine.shape[1]
            rings = lax.axis_size("wt")
            whole = plus(self.mine, self.received, kind)
            whole = whole.reshape(high, rings, rows // rings, -1).swapaxes(0, 1)
            self.summed = whole.reshape(high * rows, -1)
            summed = lax.psum_scatter(self.summed, "wt", scatter_dimension=0, tiled=True)
            self.mine = summed.reshape(high, rows // rings, -1)
            self.level = None
        else:
            self.level = self.block(1)

    def block(self, j):
        place = lax.rem(self.h - j + self.high, self.high)
        mine = lax.dynamic_index_in_dim(self.mine, place, 0, False)
        if self.along_first:
            return mine
        return plus(mine, lax.dynamic_index_in_dim(self.received, place, 0, False), self.kind)

    def cross(self, *others):
        self.level = self.block(1) if self.level is None else self.level
        self.arrived = self.across(after(self.level, *others))
        return self

    def add(self, *others):
        level = self.arrived
        for j in range(2, self.high + 1):
            level = plus(after(level, *others), self.block(j), self.kind)
            if j < self.high:
                level = self.across(level)
        self.level = level
        return self

    def finish(self):
        level = self.level
        if not self.along_first:
            level = lax.psum_scatter(level, "wt", scatter_dimension=0, tiled=True)
        return level.astype(jnp.float32)


def ring_scatter(partial, lines):
    across, swap, along = lines
    high, h, c = places()
    rings, z = lax.axis_size("wt"), lax.axis_index("wt")
    cells = partial.reshape(high, 2, rings, -1, partial.shape[-1])
    mine = lax.dynamic_index_in_dim(cells, c, 1, False)
    received = swap(lax.dynamic_index_in_dim(cells, 1 - c, 1, False))
    size = (1, 1) + cells.shape[3:]

    def block(j, k):
        place = (lax.rem(h - j + high, high), lax.rem(z - k + rings, rings), 0, 0)
        return plus(
            lax.dynamic_slice(mine, place, size)[0, 0],
            lax.dynamic_slice(received, place, size)[0, 0],
            jnp.bfloat16,
        )

    total = None
    for k in range(1, rings + 1):
        level = block(1, k)
        for j in range(2, high + 1):
            level = plus(across(level), block(j, k), jnp.bfloat16)
        if total is None:
            total = level
        else:
            total = plus(along(total), level, jnp.float32 if k == rings else jnp.bfloat16)
    return total.astype(jnp.float32)


def per_device(
    inputs,
    lengths,
    cotangent,
    gain_attn,
    w_query,
    w_key,
    w_value,
    w_out,
    gain_mlp,
    w_gate,
    w_up,
    w_down,
):
    section_no = lax.axis_index("section")
    shard_no = lax.axis_index("seq")
    micro_count, rows_local, model_width = inputs.shape
    seq_len = rows_local * lax.axis_size("seq")
    is_first = (section_no == 0).astype(jnp.int32)
    slots = micro_count + 1
    bias = jnp.stack(
        [
            window_bias(lengths[number], shard_no, rows_local, seq_len)
            for number in range(micro_count)
        ]
    )

    def choose(of_first, of_second):
        return is_first * of_first + (1 - is_first) * of_second

    rows = w_query.shape[1]
    gains = jnp.pad(
        jnp.concatenate([gain_attn, gain_mlp], 1), ((0, 15), (0, model_width - 2 * rows))
    )
    lines = links()
    narrow = jnp.concatenate([w_query[0], w_key[0], w_value[0], w_out[0], gains], 0)
    gate_gather = Gather(w_gate[0], lines)
    up_gather = Gather(w_up[0], lines)
    down_gather = Gather(w_down[0], lines)
    query_w, key_w, value_w, out_w, gain_rows = assemble(
        ring_gather(narrow, lines), [rows, rows, rows, rows, 16]
    )
    gate_gather.cross()
    gain_rows = gain_rows.reshape(-1, 16, model_width)[:, 0]
    gain_one = gain_rows[:, :rows].reshape(1, -1)
    gain_two = gain_rows[:, rows : 2 * rows].reshape(1, -1)
    params = (gain_one, query_w, key_w, value_w, out_w, gain_two)

    store, results, grad_sources = {}, [], []
    arrived = jnp.zeros((rows_local, model_width), jnp.bfloat16)
    for moment in range(slots):
        early, late = min(moment, micro_count - 1), max(moment - 1, 0)
        scalars = jnp.stack([is_first, is_first * 0 + moment, choose(early, late)])
        kv, tail, head = project(store, slots, moment, scalars, inputs[early], arrived, params)
        low = shifted(tail, "seq", 1)
        high = shifted(head, "seq", -1)
        if moment == 0:
            up_gather.cross(kv)
            down_gather.cross(kv)
            (gate_w,) = assemble(gate_gather.pieces(kv), [rows])
            (up_w,) = assemble(up_gather.pieces(kv), [rows])
            (down_w,) = assemble(down_gather.pieces(kv), [w_down.shape[1]])
            params = params + (gate_w, up_w, down_w)
        result = attend_feed(store, slots, moment, scalars, kv, low, high, bias, params)
        results.append(result)
        if moment < micro_count:
            arrived = shifted(result, "section", 1)
    activations = jnp.stack(
        [
            jnp.where(is_first == 1, results[number], results[number + 1])
            for number in range(micro_count)
        ]
    )[None]

    def both(name, start):
        chosen = lax.dynamic_slice_in_dim(store[name], start, micro_count, 0)
        return chosen.reshape(-1, chosen.shape[-1])

    def product(left, *right):
        left = both(left, 1 - is_first)
        right = jnp.concatenate([both(name, is_first) for name in right], 1)
        return jnp.dot(left.T, right, preferred_element_type=jnp.float32).astype(jnp.bfloat16)

    arrived_grad = jnp.zeros((rows_local, model_width), jnp.bfloat16)
    for moment in range(slots):
        early, late = min(moment, micro_count - 1), max(moment - 1, 0)
        scalars = jnp.stack(
            [is_first, choose(late, min(moment + 1, micro_count)), choose(late, early)]
        )
        grad_res, grad_mixed = feed_back(
            store, slots, moment, scalars, arrived_grad, cotangent[early], params
        )
        if moment == micro_count:
            lines = links()
            out_part = product("mixed", "grad_branch")
            out_sum = Scatter(out_part, lines, along_first=True)
            gate_sum = Scatter(after(product("normed_two", "grad_gate"), out_part), lines)
            down_sum = Scatter(after(product("gated", "grad_result"), out_sum.summed), lines)
            gate_sum.cross(out_sum.summed)
            up_part = product("normed_two", "grad_up")
            grad_mixed = after(grad_mixed, up_part, down_sum.level)
            up_sum = Scatter(up_part, lines)
            down_sum.cross()
        center, top, bottom = attend_back(store, slots, moment, scalars, grad_mixed, bias)
        above = shifted(top, "seq", -1)
        below = shifted(bottom, "seq", 1)
        if moment == micro_count:
            gate_sum.add(center)
            center = after(center, gate_sum.level, up_sum.level)
        (grad_source,) = project_back(
            store, slots, moment, scalars, center, below, above, grad_res, params
        )
        grad_sources.append(grad_source)
        if moment < micro_count:
            arrived_grad = shifted(grad_source, "section", -1)
    input_grads = jnp.stack(
        [
            jnp.where(is_first == 1, grad_sources[number + 1], grad_sources[number])
            for number in range(micro_count)
        ]
    )[None]
    up_sum.cross()
    down_sum.add(grad_source)
    gain_rows = jnp.concatenate(
        [
            jnp.sum(lax.dynamic_slice_in_dim(store[name], is_first, micro_count, 0), 0)
            for name in ("gain_one", "gain_two")
        ]
    ).astype(jnp.bfloat16)
    picked = jnp.arange(2 * 8)[:, None] == jnp.arange(BLOCK)[None] * 8
    right = jnp.concatenate(
        [both(name, is_first) for name in ("grad_queries", "grad_keys", "grad_values")], 1
    )
    right = jnp.concatenate(
        [
            jnp.pad(right, ((0, 0), (0, BLOCK))),
            jnp.pad(picked.astype(jnp.bfloat16), ((0, 0), (right.shape[1], 0))),
        ]
    )
    left = jnp.concatenate([both("normed", 1 - is_first), gain_rows])
    qkv_part = jnp.dot(left.T, right, preferred_element_type=jnp.float32).astype(jnp.bfloat16)
    up_sum.add(qkv_part)
    qkv_all = ring_scatter(after(qkv_part, down_sum.level), lines)
    grad_out_w = out_sum.cross().add().finish()
    grad_gate_w, grad_down_w, grad_up_w = gate_sum.finish(), down_sum.finish(), up_sum.finish()
    grad_query_w, grad_key_w, grad_value_w, gain_sum = (
        qkv_all[:, number * model_width : (number + 1) * model_width] for number in range(4)
    )
    return (
        activations,
        input_grads,
        gain_sum[:, 0][None],
        grad_query_w[None],
        grad_key_w[None],
        grad_value_w[None],
        grad_out_w[None],
        gain_sum[:, 1][None],
        grad_gate_w[None],
        grad_up_w[None],
        grad_down_w[None],
    )


def solution(mesh):
    placed = (
        P("wt", "seq", None),
        P("wt", None),
        P("wt", "seq", None),
        P("section", ("seq", "wt")),
        P("section", ("seq", "wt"), None),
        P("section", ("seq", "wt"), None),
        P("section", ("seq", "wt"), None),
        P("section", ("seq", "wt"), None),
        P("section", ("seq", "wt")),
        P("section", ("seq", "wt"), None),
        P("section", ("seq", "wt"), None),
        P("section", ("seq", "wt"), None),
    )
    return jax.shard_map(
        per_device,
        mesh=mesh,
        in_specs=placed,
        out_specs=(
            P("section", "wt", "seq", None),
            P("section", "wt", "seq", None),
            P("section", ("seq", "wt")),
            P("section", ("seq", "wt"), None),
            P("section", ("seq", "wt"), None),
            P("section", ("seq", "wt"), None),
            P("section", ("seq", "wt"), None),
            P("section", ("seq", "wt")),
            P("section", ("seq", "wt"), None),
            P("section", ("seq", "wt"), None),
            P("section", ("seq", "wt"), None),
        ),
        check_vma=False,
    )
```

time: 1610 us -> 795 us (0.49)
  waiting for transfers between devices: 728 us -> 272 us
  matrix products: 479 us -> 27.6 us
  Pallas kernels: 0 us -> 241 us
  local copies, waits for them, and re-layouts: 160 us -> 53.7 us
  blocking collectives: 67.6 us -> 0 us
  starting transfers between devices: 64.1 us -> 120 us
  other arithmetic: 81.5 us -> 56.8 us
    reduce_scatter x7 -> x4, waiting for transfers between devices: 435 us -> 0.01 us  [the longest x3 0.01 us: finish(): level = lax.psum_scatter(level, 'wt', scatter_dimension=0, tiled=True)]
    dot_general x96 -> x5, matrix products: 424 us -> 27.6 us  [the longest x4 20 us: product(): jnp.dot(left.T, right, preferred_element_type=jnp.float32)]
    all_gather x7 -> x3, waiting for transfers between devices: 260 us -> 7.69 us  [__init__(): self.level = lax.all_gather(shard, 'wt', axis=0)]
    pallas_call x0 -> x19, Pallas kernels: none -> 241 us  [the longest x15 222 us: call(): pl.pallas_call(kernel, out_shape=outs, grid_spec=pltpu.PrefetchScalarGrid...]
    ppermute x12 -> x40, waiting for transfers between devices: 0.03 us -> 206 us  [__call__(): self.sent.append(lax.ppermute(cells, self.axis, self.pairs))]
    slice x44 -> x3, local copies, waits for them, and re-layouts: 86.4 us -> 0.81 us  [the longest x1 0.7 us: per_device(): gain_sum[:, 1][None]]
    unnamed x2 -> x0, blocking collectives: 67.6 us -> none
    sub x6 -> x0, matrix products: 54.1 us -> none  [layer_forward(): exp_scores = jnp.exp(masked - jnp.max(masked, axis=-1, keepdims=True))]
  transfers between devices with their start and end apart: 36 -> 63, of which waited for: 14 -> 28; matrix products, arithmetic and copies ran while one was open for 28% -> 12% of each run, Pallas kernels for 0% -> 6%
where the time goes in v2:
time: 795 us; the launch traced here: 787 us
  waiting for transfers between devices  272 us (34%)
  Pallas kernels  241 us (30%)
  starting transfers between devices  120 us (15%)
  other arithmetic  56.8 us (7%)
  local copies, waits for them, and re-layouts  53.7 us (7%)
  matrix products  27.6 us (3%)
  between operations  15.1 us (2%)
    pallas_call x15, Pallas kernels, call(): pl.pallas_call(kernel, out_shape=outs, grid_spec=pltpu.PrefetchScalarGrid...  222 us
    ppermute x40, waiting for transfers between devices, __call__(): self.sent.append(lax.ppermute(cells, self.axis, self.pairs))  206 us
    ppermute x40, starting transfers between devices, __call__(): self.sent.append(lax.ppermute(cells, self.axis, self.pairs))  69.7 us
    ppermute x16, waiting for transfers between devices, shifted(): return lax.ppermute(shard, axis, pairs)  56.4 us
    ppermute x16, starting transfers between devices, shifted(): return lax.ppermute(shard, axis, pairs)  50.5 us
    convert_element_type x11, other arithmetic, plus(): return (left.astype(jnp.float32) + right.astype(jnp.float32)).astype(kind)  31 us
    unnamed x95, local copies, waits for them, and re-layouts  27 us
    dot_general x4, matrix products, product(): jnp.dot(left.T, right, preferred_element_type=jnp.float32)  20 us
  transfers between devices with their start and end apart: 63, of which 28 were waited for; matrix products, arithmetic and copies ran while one was open for 12% of the time, Pallas kernels for 6%

profile of v2, /device:TPU:0, one launch (start us, length us, event | category | flops | bytes accessed | tf_op | source)
XLA Modules:
  0.0 786.7 jit_solution(15255595689235657771)
XLA Ops:
  16.2 21.9 %collective-permute-done.3.refs_4_ = bf16[272,1024]{1,0:T(8,128)(2,1)S(1)} collective-permute-done((bf16[272,1024]{1,0:T(8,128)(2,1)S(1)}, bf16[272,1024]{1,0:T(8,128)(2,1)S(1)}, u32[]{:S(2)}, u32[]{:S(2)}) %collective-permute-start.3) | collective-permute-done | bytes 557088 | tf_op jit(solution)/shard_map/ppermute | solution.py:642
  38.0 7.8 collective-permute-start.7
  48.0 18.0 %collective-permute-done.7.refs_8_ = bf16[272,1024]{1,0:T(8,128)(2,1)S(1)} collective-permute-done((bf16[272,1024]{1,0:T(8,128)(2,1)S(1)}, bf16[272,1024]{1,0:T(8,128)(2,1)S(1)}, u32[]{:S(2)}, u32[]{:S(2)}) %collective-permute-start.7) | collective-permute-done | bytes 557088 | tf_op jit(solution)/shard_map/ppermute | solution.py:642
  68.1 20.8 %collective-permute-done.11.refs_12_ = bf16[272,1024]{1,0:T(8,128)(2,1)} collective-permute-done((bf16[272,1024]{1,0:T(8,128)(2,1)S(1)}, bf16[272,1024]{1,0:T(8,128)(2,1)}, u32[]{:S(2)}, u32[]{:S(2)}) %collective-permute-start.11) | collective-permute-done | bytes 557088 | tf_op jit(solution)/shard_map/ppermute | solution.py:642
  93.2 12.3 %collective-permute-done.13.refs_14_ = bf16[272,1024]{1,0:T(8,128)(2,1)} collective-permute-done((bf16[272,1024]{1,0:T(8,128)(2,1)}, bf16[272,1024]{1,0:T(8,128)(2,1)}, u32[]{:S(2)}, u32[]{:S(2)}) %collective-permute-start.13) | collective-permute-done | bytes 557088 | tf_op jit(solution)/shard_map/ppermute | solution.py:642
  108.7 10.3 %shard_map.203 = (bf16[4,4,64,1024]{3,2,1,0:T(8,128)(2,1)S(1)}, bf16[4,4,64,1024]{3,2,1,0:T(8,128)(2,1)S(1)}, bf16[4,4,64,1024]{3,2,1,0:T(8,128)(2,1)}, bf16[4,4...) custom-call(s32[8]{0:T(128)S(1)} %stack.62.seat_ref, bf16[272,1024]{1,0:T(8,128)(2,1)S(1)} %fusion.54.refs_0_, ...), custom_call_target="tpu_custom_call" | custom-call | bytes 17825792 | tf_op jit(solution)/shard_map/pallas_call | solution.py:737
  131.2 7.7 all-gather.6.cloned.1.call-done.refs_0_
  141.4 32.3 %collective-permute-done.21.refs_2_ = bf16[4,64,2816]{2,1,0:T(8,128)(2,1)} collective-permute-done((bf16[4,64,2816]{2,1,0:T(8,128)(2,1)}, bf16[4,64,2816]{2,1,0:T(8,128)(2,1)}, u32[]{:S(2)}, u32[]{:S(2)}) %collective-permute-start.21) | collective-permute-done | bytes 1441824 | tf_op jit(solution)/shard_map/ppermute | solution.py:642
  173.7 29.0 %collective-permute-done.24.refs_2_ = bf16[4,176,1024]{2,1,0:T(8,128)(2,1)} collective-permute-done((bf16[4,176,1024]{2,1,0:T(8,128)(2,1)}, bf16[4,176,1024]{2,1,0:T(8,128)(2,1)}, u32[]{:S(2)}, u32[]{:S(2)}) %collective-permute-start.24) | collective-permute-done | bytes 1441824 | tf_op jit(solution)/shard_map/ppermute | solution.py:642
  231.4 25.1 %shard_map.208 = (bf16[3,576,1024]{2,1,0:T(8,128)(2,1)}, bf16[3,576,1024]{2,1,0:T(8,128)(2,1)}, bf16[3,320,1024]{2,1,0:T(8,128)(2,1)}, f32[3,320,512]{2,1,0:T(8,...) custom-call(s32[3]{0:T(128)} %stack.53.idx, ...), custom_call_target="tpu_custom_call" | custom-call | flops 7214202880 | bytes 25952256 | tf_op jit(solution)/shard_map/pallas_call | solution.py:30
  260.5 14.4 %collective-permute-done.26.arrived = bf16[320,1024]{1,0:T(8,128)(2,1)S(1)} collective-permute-done((bf16[320,1024]{1,0:T(8,128)(2,1)}, bf16[320,1024]{1,0:T(8,128)(2,1)S(1)}, u32[]{:S(2)}, u32[]{:S(2)}) %collective-permute-start.26) | collective-permute-done | bytes 655392 | tf_op jit(solution)/shard_map/ppermute | solution.py:20
  291.6 25.2 %shard_map.210 = (bf16[3,576,1024]{2,1,0:T(8,128)(2,1)}, bf16[3,576,1024]{2,1,0:T(8,128)(2,1)}, bf16[3,320,1024]{2,1,0:T(8,128)(2,1)}, f32[3,320,512]{2,1,0:T(8,...) custom-call(s32[3]{0:T(128)} %pad_add_fusion.2.idx, ...), custom_call_target="tpu_custom_call", output_to_operand_aliasing={{0}: (12, {}), {1}: (13, {}), {2}: (14, {}), {3}: (15, {}),... | custom-call | flops 7214202880 | bytes 25952256 | tf_op jit(solution)/shard_map/pallas_call | solution.py:30
  321.7 8.5 %collective-permute-done.29.arrived = bf16[320,1024]{1,0:T(8,128)(2,1)S(1)} collective-permute-done((bf16[320,1024]{1,0:T(8,128)(2,1)}, bf16[320,1024]{1,0:T(8,128)(2,1)S(1)}, u32[]{:S(2)}, u32[]{:S(2)}) %collective-permute-start.29) | collective-permute-done | bytes 655392 | tf_op jit(solution)/shard_map/ppermute | solution.py:20
  338.7 8.3 %collective-permute-start.30 = (bf16[2,128,1024]{2,1,0:T(8,128)(2,1)}, bf16[2,128,1024]{2,1,0:T(8,128)(2,1)S(1)}, u32[]{:S(2)}, u32[]{:S(2)}) collective-permute-start(bf16[2,128,1024]{2,1,0:T(8,128)(2,1)} %get-tuple-element.174), channel_id=1, source_target_pairs={{0,4},{4,8},{8,12},{1,5},{5,9},{9,13},{2,6},{6,10},{10,14},{3,7},{... | collective-permute-start | bytes 1572872 | tf_op jit(solution)/shard_map/ppermute | solution.py:20
  351.9 25.1 %shard_map.212 = (bf16[3,576,1024]{2,1,0:T(8,128)(2,1)}, bf16[3,576,1024]{2,1,0:T(8,128)(2,1)}, bf16[3,320,1024]{2,1,0:T(8,128)(2,1)}, f32[3,320,512]{2,1,0:T(8,...) custom-call(s32[3]{0:T(128)} %pad_add_fusion.1.idx, ...), custom_call_target="tpu_custom_call", output_to_operand_aliasing={{0}: (12, {}), {1}: (13, {}), {2}: (14, {}), {3}: (15, {}),... | custom-call | flops 7214202880 | bytes 25952256 | tf_op jit(solution)/shard_map/pallas_call | solution.py:30
  377.0 18.6 %shard_map.213 = (bf16[3,320,1024]{2,1,0:T(8,128)(2,1)}, bf16[3,320,2816]{2,1,0:T(8,128)(2,1)}, bf16[3,320,2816]{2,1,0:T(8,128)(2,1)}, bf16[3,320,1024]{2,1,0:T(...) custom-call(s32[3]{0:T(128)} %pad_add_fusion.4.idx, ...), custom_call_target="tpu_custom_call" | custom-call | flops 6207569920 | bytes 17301504 | tf_op jit(solution)/shard_map/pallas_call | solution.py:30
  395.6 12.8 %shard_map.214 = (bf16[3,320,1024]{2,1,0:T(8,128)(2,1)}, f32[2,320,1024]{2,1,0:T(8,128)}, bf16[2,128,1024]{2,1,0:T(8,128)(2,1)}, bf16[2,128,1024]{2,1,0:T(8,128)(2,1)}) custom-call(s32[3]{0:T(128)} %pad_add_fusion.4.idx, bf16[3,320,1024]{2,1,0:T(8,128)(2,1)} %get-tuple-element.172.q, bf16[3,576,1024]{2,1,0:T(8,128)(2,1)} %get-tuple-element.187.keys, ...), custom_call_target="tpu_custom_call" | custom-call | flops 5033164800 | bytes 7864320 | tf_op jit(solution)/shard_map/pallas_call | solution.py:30
  408.4 8.6 %collective-permute-start.32 = (bf16[2,128,1024]{2,1,0:T(8,128)(2,1)}, bf16[2,128,1024]{2,1,0:T(8,128)(2,1)S(1)}, u32[]{:S(2)}, u32[]{:S(2)}) collective-permute-start(bf16[2,128,1024]{2,1,0:T(8,128)(2,1)} %get-tuple-element.197), channel_id=1, source_target_pairs={{0,4},{4,8},{8,12},{1,5},{5,9},{9,13},{2,6},{6,10},{10,14},{3,7},{... | collective-permute-start | bytes 1572872 | tf_op jit(solution)/shard_map/ppermute | solution.py:20
  421.9 9.6 %shard_map.215 = (bf16[3,320,1024]{2,1,0:T(8,128)(2,1)}, bf16[3,320,1024]{2,1,0:T(8,128)(2,1)}, f32[3,8,1024]{2,1,0:T(8,128)}, bf16[320,1024]{1,0:T(8,128)(2,1)}) custom-call(s32[3]{0:T(128)} %pad_add_fusion.4.idx, bf16[3,320,1024]{2,1,0:T(8,128)(2,1)} %get-tuple-element.195.grad_q.rest_0_, f32[2,320,1024]{2,1,0:T(8,128)} %get-tuple-element.196.center, ...), custom_call_target="tpu_custom_call" | custom-call | flops 2013265920 | bytes 12845056 | tf_op jit(solution)/shard_map/pallas_call | solution.py:30
  433.5 12.0 %collective-permute-done.34.arrived = bf16[320,1024]{1,0:T(8,128)(2,1)S(1)} collective-permute-done((bf16[320,1024]{1,0:T(8,128)(2,1)}, bf16[320,1024]{1,0:T(8,128)(2,1)S(1)}, u32[]{:S(2)}, u32[]{:S(2)}) %collective-permute-start.34) | collective-permute-done | bytes 655392 | tf_op jit(solution)/shard_map/ppermute | solution.py:20
  446.3 18.7 %shard_map.216 = (bf16[3,320,1024]{2,1,0:T(8,128)(2,1)}, bf16[3,320,2816]{2,1,0:T(8,128)(2,1)}, bf16[3,320,2816]{2,1,0:T(8,128)(2,1)}, bf16[3,320,1024]{2,1,0:T(...) custom-call(s32[3]{0:T(128)} %pad_add_fusion.3.idx, ...), custom_call_target="tpu_custom_call", output_to_operand_aliasing={{0}: (11, {}), {1}: (12, {}), {2}: (13, {}), {3}: (14, {}),... | custom-call | flops 6207569920 | bytes 17301504 | tf_op jit(solution)/shard_map/pallas_call | solution.py:30
  464.9 12.9 %shard_map.217 = (bf16[3,320,1024]{2,1,0:T(8,128)(2,1)}, f32[2,320,1024]{2,1,0:T(8,128)}, bf16[2,128,1024]{2,1,0:T(8,128)(2,1)}, bf16[2,128,1024]{2,1,0:T(8,128)(2,1)}) custom-call(s32[3]{0:T(128)} %pad_add_fusion.3.idx, bf16[3,320,1024]{2,1,0:T(8,128)(2,1)} %get-tuple-element.172.q, ...), custom_call_target="tpu_custom_call", output_to_operand_aliasing={{0}: (8, {})} | custom-call | flops 5033164800 | bytes 7864320 | tf_op jit(solution)/shard_map/pallas_call | solution.py:30
  490.2 9.7 %shard_map.218 = (bf16[3,320,1024]{2,1,0:T(8,128)(2,1)}, bf16[3,320,1024]{2,1,0:T(8,128)(2,1)}, f32[3,8,1024]{2,1,0:T(8,128)}, bf16[320,1024]{1,0:T(8,128)(2,1)}) custom-call(s32[3]{0:T(128)} %pad_add_fusion.3.idx, bf16[3,320,1024]{2,1,0:T(8,128)(2,1)} %get-tuple-element.207.grad_q.rest_0_, ...), custom_call_target="tpu_custom_call", output_to_operand_aliasing={{0}: (11, {}), {1}: (12, {}), {2}: (13, {})} | custom-call | flops 2013265920 | bytes 12845056 | tf_op jit(solution)/shard_map/pallas_call | solution.py:30
  501.8 12.0 %collective-permute-done.37.arrived = bf16[320,1024]{1,0:T(8,128)(2,1)S(1)} collective-permute-done((bf16[320,1024]{1,0:T(8,128)(2,1)}, bf16[320,1024]{1,0:T(8,128)(2,1)S(1)}, u32[]{:S(2)}, u32[]{:S(2)}) %collective-permute-start.37) | collective-permute-done | bytes 655392 | tf_op jit(solution)/shard_map/ppermute | solution.py:20
  514.7 18.9 %shard_map.219 = (bf16[3,320,1024]{2,1,0:T(8,128)(2,1)}, bf16[3,320,2816]{2,1,0:T(8,128)(2,1)}, bf16[3,320,2816]{2,1,0:T(8,128)(2,1)}, bf16[3,320,1024]{2,1,0:T(...) custom-call(s32[3]{0:T(128)} %pad_add_fusion.idx, ...), custom_call_target="tpu_custom_call", output_to_operand_aliasing={{0}: (11, {}), {1}: (12, {}), {2}: (13, {}), {3}: (14, {}),... | custom-call | flops 6207569920 | bytes 17301504 | tf_op jit(solution)/shard_map/pallas_call | solution.py:30
  583.0 12.8 %shard_map.220 = (bf16[3,320,1024]{2,1,0:T(8,128)(2,1)}, f32[2,320,1024]{2,1,0:T(8,128)}, bf16[2,128,1024]{2,1,0:T(8,128)(2,1)}, bf16[2,128,1024]{2,1,0:T(8,128)(2,1)}) custom-call(s32[3]{0:T(128)} %pad_add_fusion.idx, bf16[3,320,1024]{2,1,0:T(8,128)(2,1)} %get-tuple-element.172.q, ...), custom_call_target="tpu_custom_call", output_to_operand_aliasing={{0}: (8, {})} | custom-call | flops 5033164800 | bytes 7864320 | tf_op jit(solution)/shard_map/pallas_call | solution.py:30
  600.4 8.3 %collective-permute-done.41 = bf16[256,2816]{1,0:T(8,128)(2,1)} collective-permute-done((bf16[256,2816]{1,0:T(8,128)(2,1)}, bf16[256,2816]{1,0:T(8,128)(2,1)}, u32[]{:S(2)}, u32[]{:S(2)}) %collective-permute-start.41) | collective-permute-done | bytes 1441824 | tf_op jit(solution)/shard_map/ppermute | solution.py:642
  613.4 10.0 %shard_map.221 = (bf16[3,320,1024]{2,1,0:T(8,128)(2,1)}, bf16[3,320,1024]{2,1,0:T(8,128)(2,1)}, f32[3,8,1024]{2,1,0:T(8,128)}, bf16[320,1024]{1,0:T(8,128)(2,1)}) custom-call(s32[3]{0:T(128)} %pad_add_fusion.idx, bf16[3,320,1024]{2,1,0:T(8,128)(2,1)} %get-tuple-element.229.grad_q, ...), custom_call_target="tpu_custom_call", output_to_operand_aliasing={{0}: (11, {}), {1}: (12, {}), {2}: (13, {})} | custom-call | flops 2013265920 | bytes 12845056 | tf_op jit(solution)/shard_map/pallas_call | solution.py:30
  647.4 27.0 %collective-permute-start.46 = (bf16[2,4,64,3200]{3,2,1,0:T(8,128)(2,1)}, bf16[2,4,64,3200]{3,2,1,0:T(8,128)(2,1)S(1)}, u32[]{:S(2)}, u32[]{:S(2)}) collective-permute-start(bf16[2,4,64,3200]{3,2,1,0:T(8,128)(2,1)} %dynamic-slice_bitcast_fusion), channel_id=1, source_target_pairs={{0,4},{4,0},{8,12},{12,8},{1,5},{5,1},{9,13},{13,9},{2,6},{6,2},{1... | collective-permute-start | bytes 9830408 | tf_op jit(solution)/shard_map/ppermute | solution.py:642
  687.5 21.6 %collective-permute-done.49 = bf16[256,2816]{1,0:T(8,128)(2,1)} collective-permute-done((bf16[256,2816]{1,0:T(8,128)(2,1)}, bf16[256,2816]{1,0:T(8,128)(2,1)}, u32[]{:S(2)}, u32[]{:S(2)}) %collective-permute-start.49) | collective-permute-done | bytes 1441824 | tf_op jit(solution)/shard_map/ppermute | solution.py:642
  709.2 7.8 collective-permute-done.47
  747.1 12.1 %collective-permute-done.51 = bf16[64,3200]{1,0:T(8,128)(2,1)} collective-permute-done((bf16[64,3200]{1,0:T(8,128)(2,1)}, bf16[64,3200]{1,0:T(8,128)(2,1)}, u32[]{:S(2)}, u32[]{:S(2)}) %collective-permute-start.51) | collective-permute-done | bytes 409632 | tf_op jit(solution)/shard_map/ppermute | solution.py:642
  (285 shorter events, 271.5 us)
Async XLA Ops:
  7.2 84.1 %all-gather.4.cloned.1.call-start = ((), (), s32[]{:S(2)}) async-start(), calls=%async_computation.4 | async-start | bytes 1802240 | tf_op jit(solution)/shard_map/all_gather | solution.py:665
  7.9 123.3 %all-gather.8.cloned.1.call-start = ((), (), s32[]{:S(2)}) async-start(), calls=%async_computation.6 | async-start | bytes 1802240 | tf_op jit(solution)/shard_map/all_gather | solution.py:665
  8.7 130.2 %all-gather.6.cloned.1.call-start = ((), (), s32[]{:S(2)}) async-start(), calls=%async_computation.5 | async-start | bytes 1802240 | tf_op jit(solution)/shard_map/all_gather | solution.py:665
  13.1 24.9 %collective-permute-start.3 = (bf16[272,1024]{1,0:T(8,128)(2,1)S(1)}, bf16[272,1024]{1,0:T(8,128)(2,1)S(1)}, u32[]{:S(2)}, u32[]{:S(2)}) collective-permute-start(bf16[272,1024]{1,0:T(8,128)(2,1)S(1)} %fusion.54.refs_0_), channel_id=1, source_target_pairs={{0,1},{1,2},{2,3},{3,0},{4,5},{5,6},{6,7},{7,4},{8,9},{9,10},{10,1... | collective-permute-start | bytes 1671176 | tf_op jit(solution)/shard_map/ppermute | solution.py:642
  38.0 28.0 %collective-permute-start.7 = (bf16[272,1024]{1,0:T(8,128)(2,1)S(1)}, bf16[272,1024]{1,0:T(8,128)(2,1)S(1)}, u32[]{:S(2)}, u32[]{:S(2)}) collective-permute-start(bf16[272,1024]{1,0:T(8,128)(2,1)S(1)} %collective-permute-done.3.refs_4_), channel_id=1, source_target_pairs={{0,1},{1,2},{2,3},{3,0},{4,5},{5,6},{6,7},{7,4},{8,9},{9,10},{10,1... | collective-permute-start | bytes 1671176 | tf_op jit(solution)/shard_map/ppermute | solution.py:642
  47.3 636.2 %reduce-scatter.5.cloned.1.call-start = ((), (), s32[]{:S(2)}) async-start(), calls=%async_computation.7 | async-start | bytes 1310720 | tf_op jit(solution)/shard_map/reduce_scatter | solution.py:772
  47.4 20.7 %collective-permute-start.5 = (bf16[272,1024]{1,0:T(8,128)(2,1)S(1)}, bf16[272,1024]{1,0:T(8,128)(2,1)S(1)}, u32[]{:S(2)}, u32[]{:S(2)}) collective-permute-start(bf16[272,1024]{1,0:T(8,128)(2,1)S(1)} %collective-permute-done.3.refs_4_), channel_id=1, source_target_pairs={{0,8},{4,12},{8,0},{12,4},{1,9},{5,13},{9,1},{13,5},{2,10},{6,14},... | collective-permute-start | bytes 1671176 | tf_op jit(solution)/shard_map/ppermute | solution.py:642
  66.0 22.9 %collective-permute-start.11 = (bf16[272,1024]{1,0:T(8,128)(2,1)S(1)}, bf16[272,1024]{1,0:T(8,128)(2,1)}, u32[]{:S(2)}, u32[]{:S(2)}) collective-permute-start(bf16[272,1024]{1,0:T(8,128)(2,1)S(1)} %collective-permute-done.7.refs_8_), channel_id=1, source_target_pairs={{0,1},{1,2},{2,3},{3,0},{4,5},{5,6},{6,7},{7,4},{8,9},{9,10},{10,1... | collective-permute-start | bytes 1671176 | tf_op jit(solution)/shard_map/ppermute | solution.py:642
  66.0 22.9 %collective-permute-start.9 = (bf16[272,1024]{1,0:T(8,128)(2,1)S(1)}, bf16[272,1024]{1,0:T(8,128)(2,1)S(1)}, u32[]{:S(2)}, u32[]{:S(2)}) collective-permute-start(bf16[272,1024]{1,0:T(8,128)(2,1)S(1)} %collective-permute-done.7.refs_8_), channel_id=1, source_target_pairs={{0,8},{4,12},{8,0},{12,4},{1,9},{5,13},{9,1},{13,5},{2,10},{6,14},... | collective-permute-start | bytes 1671176 | tf_op jit(solution)/shard_map/ppermute | solution.py:642
  67.5 23.8 %collective-permute-start = (bf16[272,1024]{1,0:T(8,128)(2,1)S(1)}, bf16[272,1024]{1,0:T(8,128)(2,1)S(1)}, u32[]{:S(2)}, u32[]{:S(2)}) collective-permute-start(bf16[272,1024]{1,0:T(8,128)(2,1)S(1)} %fusion.54.refs_0_), channel_id=1, source_target_pairs={{0,4},{4,0},{8,12},{12,8},{1,5},{5,1},{9,13},{13,9},{2,6},{6,2},{1... | collective-permute-start | bytes 1671176 | tf_op jit(solution)/shard_map/ppermute | solution.py:642
  67.5 25.1 %collective-permute-start.4 = (bf16[272,1024]{1,0:T(8,128)(2,1)S(1)}, bf16[272,1024]{1,0:T(8,128)(2,1)}, u32[]{:S(2)}, u32[]{:S(2)}) collective-permute-start(bf16[272,1024]{1,0:T(8,128)(2,1)S(1)} %collective-permute-done.3.refs_4_), channel_id=1, source_target_pairs={{0,4},{4,0},{8,12},{12,8},{1,5},{5,1},{9,13},{13,9},{2,6},{6,2},{1... | collective-permute-start | bytes 1671176 | tf_op jit(solution)/shard_map/ppermute | solution.py:642
  68.0 24.6 %collective-permute-start.2 = (bf16[272,1024]{1,0:T(8,128)(2,1)}, bf16[272,1024]{1,0:T(8,128)(2,1)}, u32[]{:S(2)}, u32[]{:S(2)}) collective-permute-start(bf16[272,1024]{1,0:T(8,128)(2,1)} %collective-permute-done.1.refs_2_), channel_id=1, source_target_pairs={{0,4},{4,0},{8,12},{12,8},{1,5},{5,1},{9,13},{13,9},{2,6},{6,2},{1... | collective-permute-start | bytes 1671176 | tf_op jit(solution)/shard_map/ppermute | solution.py:642
  92.1 48.2 %collective-permute-start.18 = (bf16[4,64,2816]{2,1,0:T(8,128)(2,1)}, bf16[4,64,2816]{2,1,0:T(8,128)(2,1)S(1)}, u32[]{:S(2)}, u32[]{:S(2)}) collective-permute-start(bf16[4,64,2816]{2,1,0:T(8,128)(2,1)} %all-gather.4.cloned.1.call-done.refs_0_), channel_id=1, source_target_pairs={{0,8},{4,12},{8,0},{12,4},{1,9},{5,13},{9,1},{13,5},{2,10},{6,14},... | collective-permute-start | bytes 4325384 | tf_op jit(solution)/shard_map/ppermute | solution.py:642
  138.9 34.8 %collective-permute-start.21 = (bf16[4,64,2816]{2,1,0:T(8,128)(2,1)}, bf16[4,64,2816]{2,1,0:T(8,128)(2,1)}, u32[]{:S(2)}, u32[]{:S(2)}) collective-permute-start(bf16[4,64,2816]{2,1,0:T(8,128)(2,1)} %all-gather.6.cloned.1.call-done.refs_0_), channel_id=1, source_target_pairs={{0,8},{4,12},{8,0},{12,4},{1,9},{5,13},{9,1},{13,5},{2,10},{6,14},... | collective-permute-start | bytes 4325384 | tf_op jit(solution)/shard_map/ppermute | solution.py:642
  140.3 62.3 %collective-permute-start.24 = (bf16[4,176,1024]{2,1,0:T(8,128)(2,1)}, bf16[4,176,1024]{2,1,0:T(8,128)(2,1)}, u32[]{:S(2)}, u32[]{:S(2)}) collective-permute-start(bf16[4,176,1024]{2,1,0:T(8,128)(2,1)} %all-gather.8.cloned.1.call-done.refs_0_), channel_id=1, source_target_pairs={{0,8},{4,12},{8,0},{12,4},{1,9},{5,13},{9,1},{13,5},{2,10},{6,14},... | collective-permute-start | bytes 4325384 | tf_op jit(solution)/shard_map/ppermute | solution.py:642
  140.9 61.8 %collective-permute-start.17 = (bf16[4,64,2816]{2,1,0:T(8,128)(2,1)S(1)}, bf16[4,64,2816]{2,1,0:T(8,128)(2,1)S(1)}, u32[]{:S(2)}, u32[]{:S(2)}) collective-permute-start(bf16[4,64,2816]{2,1,0:T(8,128)(2,1)S(1)} %copy-done.6), channel_id=1, source_target_pairs={{0,4},{4,0},{8,12},{12,8},{1,5},{5,1},{9,13},{13,9},{2,6},{6,2},{1... | collective-permute-start | bytes 4325384 | tf_op jit(solution)/shard_map/ppermute | solution.py:642
  140.9 66.4 %collective-permute-start.20 = (bf16[4,64,2816]{2,1,0:T(8,128)(2,1)}, bf16[4,64,2816]{2,1,0:T(8,128)(2,1)}, u32[]{:S(2)}, u32[]{:S(2)}) collective-permute-start(bf16[4,64,2816]{2,1,0:T(8,128)(2,1)} %all-gather.6.cloned.1.call-done.refs_0_), channel_id=1, source_target_pairs={{0,4},{4,0},{8,12},{12,8},{1,5},{5,1},{9,13},{13,9},{2,6},{6,2},{1... | collective-permute-start | bytes 4325384 | tf_op jit(solution)/shard_map/ppermute | solution.py:642
  141.4 68.6 %collective-permute-start.19 = (bf16[4,64,2816]{2,1,0:T(8,128)(2,1)S(1)}, bf16[4,64,2816]{2,1,0:T(8,128)(2,1)}, u32[]{:S(2)}, u32[]{:S(2)}) collective-permute-start(bf16[4,64,2816]{2,1,0:T(8,128)(2,1)S(1)} %collective-permute-done.18.refs_2_), channel_id=1, source_target_pairs={{0,4},{4,0},{8,12},{12,8},{1,5},{5,1},{9,13},{13,9},{2,6},{6,2},{1... | collective-permute-start | bytes 4325384 | tf_op jit(solution)/shard_map/ppermute | solution.py:642
  173.7 52.2 %collective-permute-start.23 = (bf16[4,176,1024]{2,1,0:T(8,128)(2,1)}, bf16[4,176,1024]{2,1,0:T(8,128)(2,1)}, u32[]{:S(2)}, u32[]{:S(2)}) collective-permute-start(bf16[4,176,1024]{2,1,0:T(8,128)(2,1)} %all-gather.8.cloned.1.call-done.refs_0_), channel_id=1, source_target_pairs={{0,4},{4,0},{8,12},{12,8},{1,5},{5,1},{9,13},{13,9},{2,6},{6,2},{1... | collective-permute-start | bytes 4325384 | tf_op jit(solution)/shard_map/ppermute | solution.py:642
  203.8 22.1 %collective-permute-start.25 = (bf16[4,176,1024]{2,1,0:T(8,128)(2,1)}, bf16[4,176,1024]{2,1,0:T(8,128)(2,1)}, u32[]{:S(2)}, u32[]{:S(2)}) collective-permute-start(bf16[4,176,1024]{2,1,0:T(8,128)(2,1)} %collective-permute-done.24.refs_2_), channel_id=1, source_target_pairs={{0,4},{4,0},{8,12},{12,8},{1,5},{5,1},{9,13},{13,9},{2,6},{6,2},{1... | collective-permute-start | bytes 4325384 | tf_op jit(solution)/shard_map/ppermute | solution.py:642
  207.3 24.1 %collective-permute-start.15 = (bf16[2,128,1024]{2,1,0:T(8,128)(2,1)}, bf16[2,128,1024]{2,1,0:T(8,128)(2,1)}, u32[]{:S(2)}, u32[]{:S(2)}) collective-permute-start(bf16[2,128,1024]{2,1,0:T(8,128)(2,1)} %get-tuple-element.142), channel_id=1, source_target_pairs={{0,4},{4,8},{8,12},{1,5},{5,9},{9,13},{2,6},{6,10},{10,14},{3,7},{... | collective-permute-start | bytes 1572872 | tf_op jit(solution)/shard_map/ppermute | solution.py:20
  210.0 21.4 %collective-permute-start.16 = (bf16[2,128,1024]{2,1,0:T(8,128)(2,1)}, bf16[2,128,1024]{2,1,0:T(8,128)(2,1)}, u32[]{:S(2)}, u32[]{:S(2)}) collective-permute-start(bf16[2,128,1024]{2,1,0:T(8,128)(2,1)} %get-tuple-element.143), channel_id=1, source_target_pairs={{4,0},{8,4},{12,8},{5,1},{9,5},{13,9},{6,2},{10,6},{14,10},{7,3},{... | collective-permute-start | bytes 1572872 | tf_op jit(solution)/shard_map/ppermute | solution.py:20
  570.6 167.4 %reduce-scatter.7.cloned.1.call-start = ((), (), s32[]{:S(2)}) async-start(), calls=%async_computation.8 | async-start | bytes 1802240 | tf_op jit(solution)/shard_map/reduce_scatter | solution.py:802
  574.0 34.7 %collective-permute-start.41 = (bf16[256,2816]{1,0:T(8,128)(2,1)}, bf16[256,2816]{1,0:T(8,128)(2,1)}, u32[]{:S(2)}, u32[]{:S(2)}) collective-permute-start(bf16[256,2816]{1,0:T(8,128)(2,1)} %fusion.15), channel_id=1, source_target_pairs={{0,8},{4,12},{8,0},{12,4},{1,9},{5,13},{9,1},{13,5},{2,10},{6,14},... | collective-permute-start | bytes 4325384 | tf_op jit(solution)/shard_map/ppermute | solution.py:642
  581.0 58.1 %collective-permute-start.45 = (bf16[704,1024]{1,0:T(8,128)(2,1)S(1)}, bf16[704,1024]{1,0:T(8,128)(2,1)}, u32[]{:S(2)}, u32[]{:S(2)}) collective-permute-start(bf16[704,1024]{1,0:T(8,128)(2,1)S(1)} %fusion.16), channel_id=1, source_target_pairs={{0,8},{4,12},{8,0},{12,4},{1,9},{5,13},{9,1},{13,5},{2,10},{6,14},... | collective-permute-start | bytes 4325384 | tf_op jit(solution)/shard_map/ppermute | solution.py:642
  612.5 127.3 %reduce-scatter.11.cloned.1.call-start = ((), (), s32[]{:S(2)}) async-start(), calls=%async_computation.10 | async-start | bytes 1802240 | tf_op jit(solution)/shard_map/reduce_scatter | solution.py:802
  647.4 32.7 %collective-permute-start.46 = (bf16[2,4,64,3200]{3,2,1,0:T(8,128)(2,1)}, bf16[2,4,64,3200]{3,2,1,0:T(8,128)(2,1)S(1)}, u32[]{:S(2)}, u32[]{:S(2)}) collective-permute-start(bf16[2,4,64,3200]{3,2,1,0:T(8,128)(2,1)} %dynamic-slice_bitcast_fusion), channel_id=1, source_target_pairs={{0,4},{4,0},{8,12},{12,8},{1,5},{5,1},{9,13},{13,9},{2,6},{6,2},{1... | collective-permute-start | bytes 9830408 | tf_op jit(solution)/shard_map/ppermute | solution.py:642
  674.4 34.8 %collective-permute-start.49 = (bf16[256,2816]{1,0:T(8,128)(2,1)}, bf16[256,2816]{1,0:T(8,128)(2,1)}, u32[]{:S(2)}, u32[]{:S(2)}) collective-permute-start(bf16[256,2816]{1,0:T(8,128)(2,1)} %fusion.13), channel_id=1, source_target_pairs={{0,8},{4,12},{8,0},{12,4},{1,9},{5,13},{9,1},{13,5},{2,10},{6,14},... | collective-permute-start | bytes 4325384 | tf_op jit(solution)/shard_map/ppermute | solution.py:642
  675.6 92.0 %reduce-scatter.9.cloned.1.call-start = ((), (), s32[]{:S(2)}) async-start(), calls=%async_computation.9 | async-start | bytes 1802240 | tf_op jit(solution)/shard_map/reduce_scatter | solution.py:802
  682.0 35.0 %collective-permute-start.47 = (bf16[64,3200]{1,0:T(8,128)(2,1)}, bf16[64,3200]{1,0:T(8,128)(2,1)}, u32[]{:S(2)}, u32[]{:S(2)}) collective-permute-start(bf16[64,3200]{1,0:T(8,128)(2,1)} %fusion.35), channel_id=1, source_target_pairs={{0,8},{4,12},{8,0},{12,4},{1,9},{5,13},{9,1},{13,5},{2,10},{6,14},... | collective-permute-start | bytes 1228808 | tf_op jit(solution)/shard_map/ppermute | solution.py:642
  736.8 22.3 %collective-permute-start.51 = (bf16[64,3200]{1,0:T(8,128)(2,1)}, bf16[64,3200]{1,0:T(8,128)(2,1)}, u32[]{:S(2)}, u32[]{:S(2)}) collective-permute-start(bf16[64,3200]{1,0:T(8,128)(2,1)} %get-tuple-element.266), channel_id=1, source_target_pairs={{0,1},{1,2},{2,3},{3,0},{4,5},{5,6},{6,7},{7,4},{8,9},{9,10},{10,1... | collective-permute-start | bytes 1228808 | tf_op jit(solution)/shard_map/ppermute | solution.py:642
  746.8 22.7 %collective-permute-start.55 = (bf16[64,1024]{1,0:T(8,128)(2,1)}, bf16[64,1024]{1,0:T(8,128)(2,1)}, u32[]{:S(2)}, u32[]{:S(2)}) collective-permute-start(bf16[64,1024]{1,0:T(8,128)(2,1)} %dynamic-slice_bitcast_fusion.5), channel_id=1, source_target_pairs={{0,8},{4,12},{8,0},{12,4},{1,9},{5,13},{9,1},{13,5},{2,10},{6,14},... | collective-permute-start | bytes 393224 | tf_op jit(solution)/shard_map/ppermute | solution.py:642
  (76 other events, 714.2 us)
Sparse Core Ops, SparseCore 0:
  9.6 51.1 all-gather.3
  62.3 41.3 all-gather.7
  105.3 33.4 all-gather.5
  570.7 25.9 reduce-scatter.4
  612.7 31.9 reduce-scatter.6
  675.7 32.2 reduce-scatter.10
  726.1 40.6 reduce-scatter.8

commit v3 on v2

--- a/solution.py
+++ b/solution.py
@@ -71,6 +71,16 @@
     return lax.rsqrt(jnp.mean(values * values, axis=-1, keepdims=True) + EPSILON)
 
 
+def flat(ref):
+    cells = ref[...]
+    return cells.reshape(-1, cells.shape[-1])
+
+
+def packed_spec(packed, number, tile):
+    rows = (packed.shape[1] - 16) // 4
+    return pl.BlockSpec((packed.shape[0], rows, tile), lambda j, s: (0, number, j))
+
+
 def project_kernel(idx, own, arrived, gain, wq, wk, wv, *rest):
     x_out, n_out, q_out, kv_out, tail_out, head_out = rest[-6:]
 
@@ -85,9 +95,9 @@
         )
 
     normed = n_out[...]
-    kv_out[0] = dot(normed, wk[...]).astype(jnp.bfloat16)
-    kv_out[1] = dot(normed, wv[...]).astype(jnp.bfloat16)
-    q_out[...] = dot(normed, wq[...]).astype(jnp.bfloat16)
+    kv_out[0] = dot(normed, flat(wk)).astype(jnp.bfloat16)
+    kv_out[1] = dot(normed, flat(wv)).astype(jnp.bfloat16)
+    q_out[...] = dot(normed, flat(wq)).astype(jnp.bfloat16)
     tail_out[...] = kv_out[:, pl.ds(kv_out.shape[1] - HALO, HALO)]
     head_out[...] = kv_out[:, pl.ds(0, HALO)]
 
@@ -132,18 +142,17 @@
 
 def project(store, slots, moment, scalars, own, arrived, params):
     rows, width = arrived.shape
-    gain_one, query_w, key_w, value_w = params[:4]
+    gain_one, packed = params[:2]
     tile = WIDE
-    columns = pl.BlockSpec((width, tile), lambda j, s: (0, j))
     at_start = lambda j: (0, 0)
     halo_spec = pl.BlockSpec((2, HALO, tile), lambda j, s: (0, 0, j))
     return slot_call(
         project_kernel,
         (width // tile,),
         scalars,
-        [own, arrived, gain_one, query_w, key_w, value_w],
+        [own, arrived, gain_one, packed, packed, packed],
         [whole_spec((rows, width)), whole_spec((rows, width)), whole_spec((1, width))]
-        + [columns] * 3,
+        + [packed_spec(packed, number, tile) for number in range(3)],
         [
             ("source", (rows, width), (rows, width), at_start, jnp.bfloat16),
             ("normed", (rows, width), (rows, width), at_start, jnp.bfloat16),
@@ -193,72 +202,44 @@
     return jnp.where(low, stacked[:rows], stacked[rows:])
 
 
-def attend_feed_kernel(
-    moment, idx, q, kv, low, high, bias, wo, source, gain, wg, wu, wd, *rest
-):
-    (k_out, v_out, mixed_out, lse_out, res_out, two_out, gate_out, up_out, gated_out, result) = rest[-18:-8]
-    total, gate_w, up_w, down_w, gate_all, up_all, gated_all, sems = rest[-8:]
+def attend_step(q, kv, low, high, bias, wo, k_out, v_out, mixed_out, lse_out):
+    rows = q.shape[0]
+    for place, out in ((0, k_out), (1, v_out)):
+        out[pl.ds(0, HALO)] = low[place]
+        out[pl.ds(HALO, rows)] = kv[place]
+        out[pl.ds(HALO + rows, HALO)] = high[place]
+    scale = jnp.bfloat16(HEAD_DIM**-0.5)
+    for start, count in row_blocks(rows):
+        span = count + 2 * HALO
+        block_bias = bias[pl.ds(start, count), :span]
+        both_bias = jnp.concatenate([block_bias, block_bias], 0)
+        sums = []
+        for pair in range(WIDE // (2 * HEAD_DIM)):
+            lanes = slice(pair * 2 * HEAD_DIM, (pair + 1) * 2 * HEAD_DIM)
+            q_both = stacked_heads(q[pl.ds(start, count), lanes] * scale)
+            scores = nt_dot(q_both, k_out[pl.ds(start, span), lanes]) + both_bias
+            most = jnp.max(scores, axis=-1, keepdims=True)
+            powers = jnp.exp(scores - most)
+            total_power = jnp.sum(powers, axis=-1, keepdims=True)
+            probs = (powers * (1.0 / total_power)).astype(jnp.bfloat16)
+            mixed = dot(probs, v_out[pl.ds(start, span), lanes])
+            mixed_out[pl.ds(start, count), lanes] = unstacked_heads(mixed).astype(jnp.bfloat16)
+            log_sum = most + jnp.log(total_power)
+            sums += [log_sum[:count], log_sum[count:]]
+        lane = lax.broadcasted_iota(jnp.int32, (count, 2 * HEAD_DIM), 1)
+        wide = jnp.zeros((count, 2 * HEAD_DIM), jnp.float32)
+        for number, value in enumerate(sums):
+            wide = jnp.where(lane == number, value, wide)
+        lse_out[pl.ds(start, count)] = wide
+    return dot(mixed_out[...], flat(wo))
+
+
+def attend_steps(parts, source, gain, res_out, two_out, total, steps):
     step = pl.program_id(0)
-    rows, width = source.shape
-    tiles = chunks(wg.shape[1], wide_tile(wg.shape[1]))
-    ends = pl.num_programs(0) - 1
-
-    def fetches():
-        found = []
-        for start, size in tiles:
-            lanes = pl.ds(start, size)
-            found.append(
-                [
-                    (wg.at[:, lanes], gate_w.at[:, lanes]),
-                    (wu.at[:, lanes], up_w.at[:, lanes]),
-                    (wd.at[lanes], down_w.at[lanes]),
-                ]
-            )
-        return found
-
-    def fetch(number, part):
-        return pltpu.make_async_copy(
-            *fetches()[number][part], sems.at[number * 3 + part]
-        )
-
-    @pl.when(step == 0)
+
+    @pl.when(step < steps)
     def _():
-        for number in range(len(tiles)):
-            for part in range(3):
-                fetch(number, part).start()
-
-    @pl.when(step < ends)
-    def _():
-        for place, out in ((0, k_out), (1, v_out)):
-            out[pl.ds(0, HALO)] = low[place]
-            out[pl.ds(HALO, rows)] = kv[place]
-            out[pl.ds(HALO + rows, HALO)] = high[place]
-        scale = jnp.bfloat16(HEAD_DIM**-0.5)
-        for start, count in row_blocks(rows):
-            span = count + 2 * HALO
-            block_bias = bias[pl.ds(start, count), :span]
-            both_bias = jnp.concatenate([block_bias, block_bias], 0)
-            sums = []
-            for pair in range(WIDE // (2 * HEAD_DIM)):
-                lanes = slice(pair * 2 * HEAD_DIM, (pair + 1) * 2 * HEAD_DIM)
-                q_both = stacked_heads(q[pl.ds(start, count), lanes] * scale)
-                scores = nt_dot(q_both, k_out[pl.ds(start, span), lanes]) + both_bias
-                most = jnp.max(scores, axis=-1, keepdims=True)
-                powers = jnp.exp(scores - most)
-                total_power = jnp.sum(powers, axis=-1, keepdims=True)
-                probs = (powers * (1.0 / total_power)).astype(jnp.bfloat16)
-                mixed = dot(probs, v_out[pl.ds(start, span), lanes])
-                mixed_out[pl.ds(start, count), lanes] = unstacked_heads(mixed).astype(
-                    jnp.bfloat16
-                )
-                log_sum = most + jnp.log(total_power)
-                sums += [log_sum[:count], log_sum[count:]]
-            lane = lax.broadcasted_iota(jnp.int32, (count, 2 * HEAD_DIM), 1)
-            wide = jnp.zeros((count, 2 * HEAD_DIM), jnp.float32)
-            for number, value in enumerate(sums):
-                wide = jnp.where(lane == number, value, wide)
-            lse_out[pl.ds(start, count)] = wide
-        part = dot(mixed_out[...], wo[...])
+        part = attend_step(*parts)
 
         @pl.when(step == 0)
         def _():
@@ -268,73 +249,126 @@
         def _():
             total[...] += part
 
-    @pl.when(step == ends)
-    def _():
-        residual = total[...]
-        res_out[...] = residual
-        normed = (residual * inverse_rms(residual) * gain[...].astype(jnp.float32)).astype(
-            jnp.bfloat16
+        @pl.when(step == steps - 1)
+        def _():
+            residual = total[...]
+            res_out[...] = residual
+            two_out[...] = (
+                residual * inverse_rms(residual) * gain[...].astype(jnp.float32)
+            ).astype(jnp.bfloat16)
+
+
+def attend_kernel(steps, idx, q, kv, low, high, bias, wo, source, gain, *rest):
+    k_out, v_out, mixed_out, lse_out, res_out, two_out, total = rest[-7:]
+    parts = (q, kv, low, high, bias, wo, k_out, v_out, mixed_out, lse_out)
+    attend_steps(parts, source, gain, res_out, two_out, total, steps)
+
+
+class Feed:
+    def __init__(self, moment, weights, outs, held, sems):
+        self.moment, self.weights, self.outs, self.held, self.sems = (
+            moment,
+            weights,
+            outs,
+            held,
+            sems,
         )
-        two_out[...] = normed
-        base, stores = 3 * len(tiles), []
-        for number, (start, size) in enumerate(tiles):
+        size = weights[0].shape[1]
+        self.tiles = chunks(size, wide_tile(size))
+
+    def fetch(self, number, part):
+        start, size = self.tiles[number]
+        place = (slice(None), pl.ds(start, size)) if part < 2 else (pl.ds(start, size),)
+        return pltpu.make_async_copy(
+            self.weights[part].at[place], self.held[part].at[place], self.sems.at[3 * number + part]
+        )
+
+    def start(self):
+        for number in range(len(self.tiles)):
+            for part in range(3):
+                self.fetch(number, part).start()
+
+    def run(self, normed, total, result):
+        gate_w, up_w, down_w = self.held[:3]
+        stores = []
+        for number, (start, size) in enumerate(self.tiles):
             lanes = slice(start, start + size)
-            fetch(number, 0).wait()
+            self.fetch(number, 0).wait()
             gate = dot(normed, gate_w[:, lanes])
-            fetch(number, 1).wait()
+            self.fetch(number, 1).wait()
             up = dot(normed, up_w[:, lanes])
             half, _, _ = gelu_parts(gate)
             gated = (gate * half * up).astype(jnp.bfloat16)
-            gate_all[:, lanes] = gate.astype(jnp.bfloat16)
-            up_all[:, lanes] = up.astype(jnp.bfloat16)
-            gated_all[:, lanes] = gated
-            for part, (here, there) in enumerate(
-                ((gate_all, gate_out), (up_all, up_out), (gated_all, gated_out))
-            ):
+            values = (gate.astype(jnp.bfloat16), up.astype(jnp.bfloat16), gated)
+            for part, value in enumerate(values):
+                held = self.held[3 + part]
+                held[:, lanes] = value
                 copy = pltpu.make_async_copy(
-                    here.at[:, pl.ds(start, size)],
-                    there.at[moment, :, pl.ds(start, size)],
-                    sems.at[base + 3 * number + part],
+                    held.at[:, pl.ds(start, size)],
+                    self.outs[part].at[self.moment, :, pl.ds(start, size)],
+                    self.sems.at[3 * len(self.tiles) + 3 * number + part],
                 )
                 copy.start()
                 stores.append(copy)
-            fetch(number, 2).wait()
+            self.fetch(number, 2).wait()
             total[...] += dot(gated, down_w[lanes])
         result[...] = total[...].astype(jnp.bfloat16)
         for copy in stores:
             copy.wait()
 
 
-def attend_feed(store, slots, moment, scalars, kv, low, high, bias, params):
+def feed_kernel(moment, idx, two, residual, wg, wu, wd, *rest):
+    outs, result, total, held, sems = rest[-12:-9], rest[-9], rest[-8], rest[-7:-1], rest[-1]
+    feed = Feed(moment, (wg, wu, wd), outs, held, sems)
+    feed.start()
+    total[...] = residual[...]
+    feed.run(two[...], total, result)
+
+
+def attend_feed_kernel(
+    moment, steps, idx, q, kv, low, high, bias, wo, source, gain, wg, wu, wd, *rest
+):
+    k_out, v_out, mixed_out, lse_out, res_out, two_out = rest[-18:-12]
+    outs, result, total, held, sems = rest[-12:-9], rest[-9], rest[-8], rest[-7:-1], rest[-1]
+    feed = Feed(moment, (wg, wu, wd), outs, held, sems)
+    pl.when(pl.program_id(0) == 0)(feed.start)
+    parts = (q, kv, low, high, bias, wo, k_out, v_out, mixed_out, lse_out)
+    attend_steps(parts, source, gain, res_out, two_out, total, steps)
+
+    @pl.when(pl.program_id(0) == steps)
+    def _():
+        feed.run(two_out[...], total, result)
+
+
+def attend(store, slots, moment, scalars, kv, low, high, bias, params):
     rows, width = kv.shape[1:]
-    out_w, gain_two, gate_w, up_w, down_w = params[4:]
-    hidden = gate_w.shape[1]
+    packed, gain_two = params[1:3]
+    weights = params[3:]
+    shard = (packed.shape[1] - 16) // 4
     ext = rows + 2 * HALO
     quads = width // WIDE
     last = lambda j: jnp.minimum(j, quads - 1)
     at_start = lambda j: (0, 0)
     at_tile = lambda j: (0, last(j))
     halo_spec = pl.BlockSpec((2, HALO, WIDE), lambda j, s: (0, 0, last(j)))
-    work = width * rows * ((BLOCK + 2 * HALO) * 8 + width * 2 + hidden * 6)
-    tiles = len(chunks(hidden, wide_tile(hidden)))
-    anywhere = pl.BlockSpec(memory_space=pl.ANY)
-    (result,) = slot_call(
-        functools.partial(attend_feed_kernel, moment),
-        (quads + 1,),
+    fed = feed_parts(rows, width, weights) if weights else ([], [], [], 0)
+    kernel = functools.partial(attend_feed_kernel, moment) if weights else attend_kernel
+    return slot_call(
+        functools.partial(kernel, quads),
+        (quads + (1 if weights else 0),),
         scalars,
-        [store["queries"], kv, low, high, bias, out_w, store["source"], gain_two]
-        + [gate_w, up_w, down_w],
+        [store["queries"], kv, low, high, bias, packed, store["source"], gain_two, *weights],
         [
             pl.BlockSpec((None, rows, WIDE), lambda j, s: (moment, 0, last(j))),
             pl.BlockSpec((2, rows, WIDE), lambda j, s: (0, 0, last(j))),
             halo_spec,
             halo_spec,
             pl.BlockSpec((None,) + bias.shape[1:], lambda j, s: (s[2], 0, 0)),
-            pl.BlockSpec((WIDE, width), lambda j, s: (last(j), 0)),
+            pl.BlockSpec((WIDE // shard, shard, width), lambda j, s: (last(j), 3, 0)),
             pl.BlockSpec((None, rows, width), lambda j, s: (moment, 0, 0)),
             whole_spec((1, width)),
         ]
-        + [anywhere] * 3,
+        + [pl.BlockSpec(memory_space=pl.ANY)] * len(weights),
         [
             ("keys", (ext, width), (ext, WIDE), at_tile, jnp.bfloat16),
             ("values", (ext, width), (ext, WIDE), at_tile, jnp.bfloat16),
@@ -342,27 +376,52 @@
             ("lse", (rows, quads * BLOCK), (rows, BLOCK), at_tile, jnp.float32),
             ("residual", (rows, width), (rows, width), at_start, jnp.float32),
             ("normed_two", (rows, width), (rows, width), at_start, jnp.bfloat16),
-            ("gate", (rows, hidden), None, None, jnp.bfloat16),
-            ("up", (rows, hidden), None, None, jnp.bfloat16),
-            ("gated", (rows, hidden), None, None, jnp.bfloat16),
-        ],
-        [((rows, width), jnp.bfloat16, whole_spec((rows, width)))],
+        ]
+        + fed[0],
+        fed[1],
         store,
         slots,
         moment,
-        [
-            pltpu.VMEM((rows, width), jnp.float32),
-            pltpu.VMEM((width, hidden), jnp.bfloat16),
-            pltpu.VMEM((width, hidden), jnp.bfloat16),
-            pltpu.VMEM((hidden, width), jnp.bfloat16),
-            pltpu.VMEM((rows, hidden), jnp.bfloat16),
-            pltpu.VMEM((rows, hidden), jnp.bfloat16),
-            pltpu.VMEM((rows, hidden), jnp.bfloat16),
-            pltpu.SemaphoreType.DMA((6 * tiles,)),
-        ],
-        cost_of(work, 6 * width * hidden + 2 * width * width + 20 * rows * width),
-    )
-    return result
+        [pltpu.VMEM((rows, width), jnp.float32)] + fed[2],
+        cost_of(
+            width * rows * ((BLOCK + 2 * HALO) * 8 + width * 2) + fed[3],
+            2 * width * width + 20 * rows * width + fed[3] // rows,
+        ),
+    )
+
+
+def feed_parts(rows, width, weights):
+    hidden = weights[0].shape[1]
+    tiles = len(chunks(hidden, wide_tile(hidden)))
+    return (
+        [(name, (rows, hidden), None, None, jnp.bfloat16) for name in ("gate", "up", "gated")],
+        [((rows, width), jnp.bfloat16, whole_spec((rows, width)))],
+        [pltpu.VMEM(weight.shape, jnp.bfloat16) for weight in weights]
+        + [pltpu.VMEM((rows, hidden), jnp.bfloat16)] * 3
+        + [pltpu.SemaphoreType.DMA((6 * tiles,))],
+        6 * rows * width * hidden,
+    )
+
+
+def feed(store, slots, moment, scalars, params):
+    weights = params[3:]
+    rows, width = store["residual"].shape[1:]
+    fed = feed_parts(rows, width, weights)
+    return slot_call(
+        functools.partial(feed_kernel, moment),
+        (1,),
+        scalars,
+        [store["normed_two"], store["residual"], *weights],
+        [pl.BlockSpec((None, rows, width), lambda j, s: (moment, 0, 0))] * 2
+        + [pl.BlockSpec(memory_space=pl.ANY)] * 3,
+        fed[0],
+        fed[1],
+        store,
+        slots,
+        moment,
+        [pltpu.VMEM((rows, width), jnp.float32)] + fed[2],
+        cost_of(fed[3], fed[3] // rows + 10 * rows * width),
+    )
 
 
 def gelu_parts(gate):
@@ -410,7 +469,7 @@
         res_out[...] = grad_residual
         branch = grad_residual.astype(jnp.bfloat16)
         branch_out[...] = branch
-        mixed_out[...] = nt_dot(branch, wo[...]).astype(jnp.bfloat16)
+        mixed_out[...] = nt_dot(branch, flat(wo)).astype(jnp.bfloat16)
 
 
 def norm_back(grads, values, gain):
@@ -424,7 +483,7 @@
 
 
 def feed_back(store, slots, moment, scalars, arrived, own, params):
-    out_w, gain_two, gate_w, up_w, down_w = params[4:]
+    packed, gain_two, gate_w, up_w, down_w = params[1:]
     rows, width = arrived.shape
     hidden = gate_w.shape[1]
     tile = wide_tile(hidden)
@@ -436,12 +495,16 @@
         (hidden // tile,),
         scalars,
         [arrived, own, store["gate"], store["up"], store["residual"], gain_two]
-        + [down_w, gate_w, up_w, out_w],
+        + [down_w, gate_w, up_w, packed],
         [whole_spec((rows, width)), whole_spec((rows, width)), taken_tile, taken_tile]
         + [pl.BlockSpec((None, rows, width), lambda j, s: (s[1], 0, 0)), whole_spec((1, width))]
         + [pl.BlockSpec((tile, width), lambda j, s: (j, 0))]
         + [pl.BlockSpec((width, tile), lambda j, s: (0, j))] * 2
-        + [whole_spec((width, width))],
+        + [
+            pl.BlockSpec(
+                (packed.shape[0], (packed.shape[1] - 16) // 4, width), lambda j, s: (0, 3, 0)
+            )
+        ],
         [
             ("grad_result", (rows, width), (rows, width), at_start, jnp.bfloat16),
             ("grad_gate", (rows, hidden), (rows, tile), at_tile, jnp.bfloat16),
@@ -553,7 +616,8 @@
             jnp.bfloat16
         )
         out[pl.ds(rows - HALO, HALO)] = tail.astype(jnp.bfloat16)
-    part = nt_dot(grad_q[...], wq[...]) + nt_dot(k_out[...], wk[...]) + nt_dot(v_out[...], wv[...])
+    part = nt_dot(grad_q[...], flat(wq))
+    part += nt_dot(k_out[...], flat(wk)) + nt_dot(v_out[...], flat(wv))
 
     @pl.when(step == 0)
     def _():
@@ -574,17 +638,16 @@
 
 def project_back(store, slots, moment, scalars, center, below, above, grad_res, params):
     rows, width = grad_res.shape
-    gain_one, query_w, key_w, value_w = params[:4]
+    gain_one, packed = params[:2]
     at_tile = lambda j: (0, j)
     at_start = lambda j: (0, 0)
     halo_spec = pl.BlockSpec((2, HALO, WIDE), lambda j, s: (0, 0, j))
-    columns = pl.BlockSpec((width, WIDE), lambda j, s: (0, j))
     return slot_call(
         project_back_kernel,
         (width // WIDE,),
         scalars,
         [store["grad_queries"], center, below, above, store["source"], gain_one, grad_res]
-        + [query_w, key_w, value_w],
+        + [packed] * 3,
         [
             pl.BlockSpec((None, rows, WIDE), lambda j, s: (moment, 0, j)),
             pl.BlockSpec((2, rows, WIDE), lambda j, s: (0, 0, j)),
@@ -594,7 +657,7 @@
             whole_spec((1, width)),
             whole_spec((rows, width)),
         ]
-        + [columns] * 3,
+        + [packed_spec(packed, number, WIDE) for number in range(3)],
         [
             ("grad_keys", (rows, width), (rows, WIDE), at_tile, jnp.bfloat16),
             ("grad_values", (rows, width), (rows, WIDE), at_tile, jnp.bfloat16),
@@ -636,9 +699,10 @@
     def __init__(self, axis, pairs, depth):
         self.axis, self.pairs, self.depth, self.sent = axis, pairs, depth, []
 
-    def __call__(self, cells):
-        if self.depth and len(self.sent) >= self.depth:
-            cells = after(cells, self.sent[-self.depth])
+    def __call__(self, cells, depth=None):
+        depth = self.depth if depth is None else depth
+        if depth and len(self.sent) >= depth:
+            cells = after(cells, self.sent[-depth])
         self.sent.append(lax.ppermute(cells, self.axis, self.pairs))
         return self.sent[-1]
 
@@ -679,14 +743,17 @@
         return found
 
 
-def ring_gather(shard, lines):
+def ring_gather(shard, lines, between):
     across, swap, along = lines
     found, current = {}, shard
     for k in range(lax.axis_size("wt")):
         current = along(current) if k else current
+        if k == lax.axis_size("wt") - 1:
+            between()
         cells = current
         for j in range(lax.axis_size("seq") // 2):
-            cells = across(cells) if j else cells
+            if j:
+                cells = across(cells, 1) if k == lax.axis_size("wt") - 1 else across(cells)
             found[(k, j, 0)] = cells
             found[(k, j, 1)] = swap(cells)
     return found
@@ -871,14 +938,13 @@
     gate_gather = Gather(w_gate[0], lines)
     up_gather = Gather(w_up[0], lines)
     down_gather = Gather(w_down[0], lines)
-    query_w, key_w, value_w, out_w, gain_rows = assemble(
-        ring_gather(narrow, lines), [rows, rows, rows, rows, 16]
-    )
-    gate_gather.cross()
-    gain_rows = gain_rows.reshape(-1, 16, model_width)[:, 0]
+    pieces = ring_gather(narrow, lines, gate_gather.cross)
+    (packed,) = assemble(pieces, [narrow.shape[0]])
+    packed = packed.reshape(-1, narrow.shape[0], model_width)
+    gain_rows = packed[:, 4 * rows]
     gain_one = gain_rows[:, :rows].reshape(1, -1)
     gain_two = gain_rows[:, rows : 2 * rows].reshape(1, -1)
-    params = (gain_one, query_w, key_w, value_w, out_w, gain_two)
+    params = (gain_one, packed, gain_two)
 
     store, results, grad_sources = {}, [], []
     arrived = jnp.zeros((rows_local, model_width), jnp.bfloat16)
@@ -889,13 +955,18 @@
         low = shifted(tail, "seq", 1)
         high = shifted(head, "seq", -1)
         if moment == 0:
-            up_gather.cross(kv)
-            down_gather.cross(kv)
+            up_gather.cross()
+            down_gather.cross(low, high)
+            kv = after(kv, up_gather.row[-1])
+            attend(store, slots, moment, scalars, kv, low, high, bias, params)
+            two = store["normed_two"]
             (gate_w,) = assemble(gate_gather.pieces(kv), [rows])
             (up_w,) = assemble(up_gather.pieces(kv), [rows])
-            (down_w,) = assemble(down_gather.pieces(kv), [w_down.shape[1]])
+            (down_w,) = assemble(down_gather.pieces(two, gate_w, up_w), [w_down.shape[1]])
             params = params + (gate_w, up_w, down_w)
-        result = attend_feed(store, slots, moment, scalars, kv, low, high, bias, params)
+            (result,) = feed(store, slots, moment, scalars, params)
+        else:
+            (result,) = attend(store, slots, moment, scalars, kv, low, high, bias, params)
         results.append(result)
         if moment < micro_count:
             arrived = shifted(result, "section", 1)
@@ -929,18 +1000,18 @@
             out_part = product("mixed", "grad_branch")
             out_sum = Scatter(out_part, lines, along_first=True)
             gate_sum = Scatter(after(product("normed_two", "grad_gate"), out_part), lines)
-            down_sum = Scatter(after(product("gated", "grad_result"), out_sum.summed), lines)
+            up_sum = Scatter(after(product("normed_two", "grad_up"), out_sum.summed), lines)
             gate_sum.cross(out_sum.summed)
-            up_part = product("normed_two", "grad_up")
-            grad_mixed = after(grad_mixed, up_part, down_sum.level)
-            up_sum = Scatter(up_part, lines)
-            down_sum.cross()
+            down_part = product("gated", "grad_result")
+            grad_mixed = after(grad_mixed, down_part, up_sum.level)
+            down_sum = Scatter(down_part, lines)
         center, top, bottom = attend_back(store, slots, moment, scalars, grad_mixed, bias)
         above = shifted(top, "seq", -1)
         below = shifted(bottom, "seq", 1)
         if moment == micro_count:
+            up_sum.cross(above, below)
             gate_sum.add(center)
-            center = after(center, gate_sum.level, up_sum.level)
+            center = after(center, gate_sum.level, down_sum.level)
         (grad_source,) = project_back(
             store, slots, moment, scalars, center, below, above, grad_res, params
         )
@@ -953,8 +1024,8 @@
             for number in range(micro_count)
         ]
     )[None]
-    up_sum.cross()
-    down_sum.add(grad_source)
+    down_sum.cross(above, below)
+    up_sum.add(grad_source)
     gain_rows = jnp.concatenate(
         [
             jnp.sum(lax.dynamic_slice_in_dim(store[name], is_first, micro_count, 0), 0)
@@ -971,12 +1042,13 @@
             jnp.pad(picked.astype(jnp.bfloat16), ((0, 0), (right.shape[1], 0))),
         ]
     )
-    left = jnp.concatenate([both("normed", 1 - is_first), gain_rows])
+    left = after(jnp.concatenate([both("normed", 1 - is_first), gain_rows]), up_sum.level)
     qkv_part = jnp.dot(left.T, right, preferred_element_type=jnp.float32).astype(jnp.bfloat16)
-    up_sum.add(qkv_part)
-    qkv_all = ring_scatter(after(qkv_part, down_sum.level), lines)
+    grad_up_w = up_sum.finish()
+    down_sum.add(qkv_part, grad_up_w)
+    qkv_all = ring_scatter(qkv_part, lines)
     grad_out_w = out_sum.cross().add().finish()
-    grad_gate_w, grad_down_w, grad_up_w = gate_sum.finish(), down_sum.finish(), up_sum.finish()
+    grad_gate_w, grad_down_w = gate_sum.finish(), down_sum.finish()
     grad_query_w, grad_key_w, grad_value_w, gain_sum = (
         qkv_all[:, number * model_width : (number + 1) * model_width] for number in range(4)
     )

time: 795 us -> 745 us (0.937)
  starting transfers between devices: 120 us -> 100 us
  waiting for transfers between devices: 272 us -> 253 us
  local copies, waits for them, and re-layouts: 53.7 us -> 45.7 us
    ppermute x40, starting transfers between devices: 69.7 us -> 49.3 us  [__call__(): self.sent.append(lax.ppermute(cells, self.axis, self.pairs))]
    ppermute x40, waiting for transfers between devices: 206 us -> 190 us  [__call__(): self.sent.append(lax.ppermute(cells, self.axis, self.pairs))]
    unnamed x95 -> x87, local copies, waits for them, and re-layouts: 27 us -> 22.2 us
    pallas_call x15 -> x16, Pallas kernels: 222 us -> 221 us  [call(): pl.pallas_call(kernel, out_shape=outs, grid_spec=pltpu.PrefetchScalarGrid...]
  transfers between devices with their start and end apart: 63 -> 63, of which waited for: 28 -> 31; matrix products, arithmetic and copies ran while one was open for 12% -> 14% of each run, Pallas kernels for 6% -> 8%
where the time goes in v3:
time: 745 us; the launch traced here: 740 us
  waiting for transfers between devices  253 us (34%)
  Pallas kernels  237 us (32%)
  starting transfers between devices  100 us (13%)
  other arithmetic  59 us (8%)
  local copies, waits for them, and re-layouts  45.7 us (6%)
  matrix products  30 us (4%)
  between operations  15.1 us (2%)
    pallas_call x16, Pallas kernels, call(): pl.pallas_call(kernel, out_shape=outs, grid_spec=pltpu.PrefetchScalarGrid...  221 us
    ppermute x40, waiting for transfers between devices, __call__(): self.sent.append(lax.ppermute(cells, self.axis, self.pairs))  190 us
    ppermute x16, waiting for transfers between devices, shifted(): return lax.ppermute(shard, axis, pairs)  56.7 us
    ppermute x16, starting transfers between devices, shifted(): return lax.ppermute(shard, axis, pairs)  50.5 us
    ppermute x40, starting transfers between devices, __call__(): self.sent.append(lax.ppermute(cells, self.axis, self.pairs))  49.3 us
    convert_element_type x11, other arithmetic, plus(): return (left.astype(jnp.float32) + right.astype(jnp.float32)).astype(kind)  32.4 us
    unnamed x87, local copies, waits for them, and re-layouts  22.2 us
    dot_general x4, matrix products, product(): jnp.dot(left.T, right, preferred_element_type=jnp.float32)  22.1 us
  transfers between devices with their start and end apart: 63, of which 31 were waited for; matrix products, arithmetic and copies ran while one was open for 14% of the time, Pallas kernels for 8%

profile of v3, /device:TPU:0, one launch (start us, length us, event | category | flops | bytes accessed | tf_op | source)
XLA Modules:
  0.0 739.7 jit_solution(5013979106577554521)
XLA Ops:
  15.5 21.0 %collective-permute-done.3.refs_4_ = bf16[272,1024]{1,0:T(8,128)(2,1)S(1)} collective-permute-done((bf16[272,1024]{1,0:T(8,128)(2,1)S(1)}, bf16[272,1024]{1,0:T(8,128)(2,1)S(1)}, u32[]{:S(2)}, u32[]{:S(2)}) %collective-permute-start.3) | collective-permute-done | bytes 557088 | tf_op jit(solution)/shard_map/ppermute | solution.py:706
  38.3 10.3 %collective-permute-done.5.refs_6_ = bf16[272,1024]{1,0:T(8,128)(2,1)S(1)} collective-permute-done((bf16[272,1024]{1,0:T(8,128)(2,1)S(1)}, bf16[272,1024]{1,0:T(8,128)(2,1)S(1)}, u32[]{:S(2)}, u32[]{:S(2)}) %collective-permute-start.5) | collective-permute-done | bytes 557088 | tf_op jit(solution)/shard_map/ppermute | solution.py:706
  55.7 21.3 %collective-permute-done.7.refs_8_ = bf16[272,1024]{1,0:T(8,128)(2,1)S(1)} collective-permute-done((bf16[272,1024]{1,0:T(8,128)(2,1)S(1)}, bf16[272,1024]{1,0:T(8,128)(2,1)S(1)}, u32[]{:S(2)}, u32[]{:S(2)}) %collective-permute-start.7) | collective-permute-done | bytes 557088 | tf_op jit(solution)/shard_map/ppermute | solution.py:706
  80.8 18.5 %collective-permute-done.1.refs_2_ = bf16[272,1024]{1,0:T(8,128)(2,1)S(1)} collective-permute-done((bf16[272,1024]{1,0:T(8,128)(2,1)S(1)}, bf16[272,1024]{1,0:T(8,128)(2,1)S(1)}, u32[]{:S(2)}, u32[]{:S(2)}) %collective-permute-start.1) | collective-permute-done | bytes 557088 | tf_op jit(solution)/shard_map/ppermute | solution.py:706
  110.6 9.8 %collective-permute-done.9.refs_10_ = bf16[272,1024]{1,0:T(8,128)(2,1)} collective-permute-done((bf16[272,1024]{1,0:T(8,128)(2,1)S(1)}, bf16[272,1024]{1,0:T(8,128)(2,1)}, u32[]{:S(2)}, u32[]{:S(2)}) %collective-permute-start.9) | collective-permute-done | bytes 557088 | tf_op jit(solution)/shard_map/ppermute | solution.py:706
  140.7 7.7 %shard_map.204 = (bf16[3,320,1024]{2,1,0:T(8,128)(2,1)}, bf16[3,320,1024]{2,1,0:T(8,128)(2,1)}, bf16[3,320,1024]{2,1,0:T(8,128)(2,1)}, bf16[2,320,1024]{2,1,0:T(...) custom-call(s32[3]{0:T(128)} %stack.53.idx, bf16[320,1024]{1,0:T(8,128)(2,1)} %get-tuple-element.265.own, ...), custom_call_target="tpu_custom_call" | custom-call | flops 2013265920 | bytes 10878976 | tf_op jit(solution)/shard_map/pallas_call | solution.py:30
  173.1 16.0 %shard_map.205 = (bf16[3,576,1024]{2,1,0:T(8,128)(2,1)}, bf16[3,576,1024]{2,1,0:T(8,128)(2,1)}, bf16[3,320,1024]{2,1,0:T(8,128)(2,1)}, f32[3,320,512]{2,1,0:T(8,...) custom-call(s32[3]{0:T(128)} %stack.53.idx, bf16[3,320,1024]{2,1,0:T(8,128)(2,1)} %get-tuple-element.134.q.rest_2_, ...), custom_call_target="tpu_custom_call" | custom-call | flops 1677721600 | bytes 8650752 | tf_op jit(solution)/shard_map/pallas_call | solution.py:30
  208.9 12.7 %shard_map.209 = (bf16[3,320,2816]{2,1,0:T(8,128)(2,1)}, bf16[3,320,2816]{2,1,0:T(8,128)(2,1)}, bf16[3,320,2816]{2,1,0:T(8,128)(2,1)}, bf16[320,1024]{1,0:T(8,128)(2,1)}) custom-call(s32[3]{0:T(128)} %stack.53.idx, bf16[3,320,1024]{2,1,0:T(8,128)(2,1)} %get-tuple-element.141.two.rest_5_, f32[3,320,1024]{2,1,0:T(8,128)} %get-tuple-element.142.residual.rest_4_, ...), custom_call_target="tpu_custom_call" | custom-call | flops 5536481280 | bytes 20578304 | tf_op jit(solution)/shard_map/pallas_call | solution.py:30
  225.9 14.0 %collective-permute-done.26.arrived = bf16[320,1024]{1,0:T(8,128)(2,1)S(1)} collective-permute-done((bf16[320,1024]{1,0:T(8,128)(2,1)}, bf16[320,1024]{1,0:T(8,128)(2,1)S(1)}, u32[]{:S(2)}, u32[]{:S(2)}) %collective-permute-start.26) | collective-permute-done | bytes 655392 | tf_op jit(solution)/shard_map/ppermute | solution.py:20
  256.1 24.9 %shard_map.211 = (bf16[3,576,1024]{2,1,0:T(8,128)(2,1)}, bf16[3,576,1024]{2,1,0:T(8,128)(2,1)}, bf16[3,320,1024]{2,1,0:T(8,128)(2,1)}, f32[3,320,512]{2,1,0:T(8,...) custom-call(s32[3]{0:T(128)} %pad_add_fusion.2.idx, ...), custom_call_target="tpu_custom_call", output_to_operand_aliasing={{0}: (12, {}), {1}: (13, {}), {2}: (14, {}), {3}: (15, {}),... | custom-call | flops 7214202880 | bytes 25952256 | tf_op jit(solution)/shard_map/pallas_call | solution.py:30
  286.0 8.5 %collective-permute-done.29.arrived = bf16[320,1024]{1,0:T(8,128)(2,1)S(1)} collective-permute-done((bf16[320,1024]{1,0:T(8,128)(2,1)}, bf16[320,1024]{1,0:T(8,128)(2,1)S(1)}, u32[]{:S(2)}, u32[]{:S(2)}) %collective-permute-start.29) | collective-permute-done | bytes 655392 | tf_op jit(solution)/shard_map/ppermute | solution.py:20
  295.3 7.7 %shard_map.212 = (bf16[3,320,1024]{2,1,0:T(8,128)(2,1)}, bf16[3,320,1024]{2,1,0:T(8,128)(2,1)}, bf16[3,320,1024]{2,1,0:T(8,128)(2,1)}, bf16[2,320,1024]{2,1,0:T(...) custom-call(s32[3]{0:T(128)} %pad_add_fusion.1.idx, ...), custom_call_target="tpu_custom_call", output_to_operand_aliasing={{0}: (7, {}), {1}: (8, {}), {2}: (9, {})} | custom-call | flops 2013265920 | bytes 10878976 | tf_op jit(solution)/shard_map/pallas_call | solution.py:30
  303.0 8.4 %collective-permute-start.30 = (bf16[2,128,1024]{2,1,0:T(8,128)(2,1)}, bf16[2,128,1024]{2,1,0:T(8,128)(2,1)S(1)}, u32[]{:S(2)}, u32[]{:S(2)}) collective-permute-start(bf16[2,128,1024]{2,1,0:T(8,128)(2,1)} %get-tuple-element.166), channel_id=1, source_target_pairs={{0,4},{4,8},{8,12},{1,5},{5,9},{9,13},{2,6},{6,10},{10,14},{3,7},{... | collective-permute-start | bytes 1572872 | tf_op jit(solution)/shard_map/ppermute | solution.py:20
  316.2 25.0 %shard_map.213 = (bf16[3,576,1024]{2,1,0:T(8,128)(2,1)}, bf16[3,576,1024]{2,1,0:T(8,128)(2,1)}, bf16[3,320,1024]{2,1,0:T(8,128)(2,1)}, f32[3,320,512]{2,1,0:T(8,...) custom-call(s32[3]{0:T(128)} %pad_add_fusion.1.idx, ...), custom_call_target="tpu_custom_call", output_to_operand_aliasing={{0}: (12, {}), {1}: (13, {}), {2}: (14, {}), {3}: (15, {}),... | custom-call | flops 7214202880 | bytes 25952256 | tf_op jit(solution)/shard_map/pallas_call | solution.py:30
  341.2 17.5 %shard_map.214 = (bf16[3,320,1024]{2,1,0:T(8,128)(2,1)}, bf16[3,320,2816]{2,1,0:T(8,128)(2,1)}, bf16[3,320,2816]{2,1,0:T(8,128)(2,1)}, bf16[3,320,1024]{2,1,0:T(...) custom-call(s32[3]{0:T(128)} %pad_add_fusion.4.idx, ...), custom_call_target="tpu_custom_call" | custom-call | flops 6207569920 | bytes 17301504 | tf_op jit(solution)/shard_map/pallas_call | solution.py:30
  358.7 12.8 %shard_map.215 = (bf16[3,320,1024]{2,1,0:T(8,128)(2,1)}, f32[2,320,1024]{2,1,0:T(8,128)}, bf16[2,128,1024]{2,1,0:T(8,128)(2,1)}, bf16[2,128,1024]{2,1,0:T(8,128)(2,1)}) custom-call(s32[3]{0:T(128)} %pad_add_fusion.4.idx, bf16[3,320,1024]{2,1,0:T(8,128)(2,1)} %get-tuple-element.164.q, bf16[3,576,1024]{2,1,0:T(8,128)(2,1)} %get-tuple-element.179.keys, ...), custom_call_target="tpu_custom_call" | custom-call | flops 5033164800 | bytes 7864320 | tf_op jit(solution)/shard_map/pallas_call | solution.py:30
  371.5 8.6 %collective-permute-start.32 = (bf16[2,128,1024]{2,1,0:T(8,128)(2,1)}, bf16[2,128,1024]{2,1,0:T(8,128)(2,1)S(1)}, u32[]{:S(2)}, u32[]{:S(2)}) collective-permute-start(bf16[2,128,1024]{2,1,0:T(8,128)(2,1)} %get-tuple-element.189), channel_id=1, source_target_pairs={{0,4},{4,8},{8,12},{1,5},{5,9},{9,13},{2,6},{6,10},{10,14},{3,7},{... | collective-permute-start | bytes 1572872 | tf_op jit(solution)/shard_map/ppermute | solution.py:20
  384.9 9.3 %shard_map.216 = (bf16[3,320,1024]{2,1,0:T(8,128)(2,1)}, bf16[3,320,1024]{2,1,0:T(8,128)(2,1)}, f32[3,8,1024]{2,1,0:T(8,128)}, bf16[320,1024]{1,0:T(8,128)(2,1)}) custom-call(s32[3]{0:T(128)} %pad_add_fusion.4.idx, bf16[3,320,1024]{2,1,0:T(8,128)(2,1)} %get-tuple-element.187.grad_q.rest_0_, f32[2,320,1024]{2,1,0:T(8,128)} %get-tuple-element.188.center, ...), custom_call_target="tpu_custom_call" | custom-call | flops 2013265920 | bytes 12845056 | tf_op jit(solution)/shard_map/pallas_call | solution.py:30
  396.2 12.0 %collective-permute-done.34.arrived = bf16[320,1024]{1,0:T(8,128)(2,1)S(1)} collective-permute-done((bf16[320,1024]{1,0:T(8,128)(2,1)}, bf16[320,1024]{1,0:T(8,128)(2,1)S(1)}, u32[]{:S(2)}, u32[]{:S(2)}) %collective-permute-start.34) | collective-permute-done | bytes 655392 | tf_op jit(solution)/shard_map/ppermute | solution.py:20
  409.0 17.5 %shard_map.217 = (bf16[3,320,1024]{2,1,0:T(8,128)(2,1)}, bf16[3,320,2816]{2,1,0:T(8,128)(2,1)}, bf16[3,320,2816]{2,1,0:T(8,128)(2,1)}, bf16[3,320,1024]{2,1,0:T(...) custom-call(s32[3]{0:T(128)} %pad_add_fusion.3.idx, ...), custom_call_target="tpu_custom_call", output_to_operand_aliasing={{0}: (11, {}), {1}: (12, {}), {2}: (13, {}), {3}: (14, {}),... | custom-call | flops 6207569920 | bytes 17301504 | tf_op jit(solution)/shard_map/pallas_call | solution.py:30
  426.5 12.9 %shard_map.218 = (bf16[3,320,1024]{2,1,0:T(8,128)(2,1)}, f32[2,320,1024]{2,1,0:T(8,128)}, bf16[2,128,1024]{2,1,0:T(8,128)(2,1)}, bf16[2,128,1024]{2,1,0:T(8,128)(2,1)}) custom-call(s32[3]{0:T(128)} %pad_add_fusion.3.idx, bf16[3,320,1024]{2,1,0:T(8,128)(2,1)} %get-tuple-element.164.q, ...), custom_call_target="tpu_custom_call", output_to_operand_aliasing={{0}: (8, {})} | custom-call | flops 5033164800 | bytes 7864320 | tf_op jit(solution)/shard_map/pallas_call | solution.py:30
  451.8 9.3 %shard_map.219 = (bf16[3,320,1024]{2,1,0:T(8,128)(2,1)}, bf16[3,320,1024]{2,1,0:T(8,128)(2,1)}, f32[3,8,1024]{2,1,0:T(8,128)}, bf16[320,1024]{1,0:T(8,128)(2,1)}) custom-call(s32[3]{0:T(128)} %pad_add_fusion.3.idx, bf16[3,320,1024]{2,1,0:T(8,128)(2,1)} %get-tuple-element.199.grad_q.rest_0_, ...), custom_call_target="tpu_custom_call", output_to_operand_aliasing={{0}: (11, {}), {1}: (12, {}), {2}: (13, {})} | custom-call | flops 2013265920 | bytes 12845056 | tf_op jit(solution)/shard_map/pallas_call | solution.py:30
  463.0 12.0 %collective-permute-done.37.arrived = bf16[320,1024]{1,0:T(8,128)(2,1)S(1)} collective-permute-done((bf16[320,1024]{1,0:T(8,128)(2,1)}, bf16[320,1024]{1,0:T(8,128)(2,1)S(1)}, u32[]{:S(2)}, u32[]{:S(2)}) %collective-permute-start.37) | collective-permute-done | bytes 655392 | tf_op jit(solution)/shard_map/ppermute | solution.py:20
  475.9 17.8 %shard_map.220 = (bf16[3,320,1024]{2,1,0:T(8,128)(2,1)}, bf16[3,320,2816]{2,1,0:T(8,128)(2,1)}, bf16[3,320,2816]{2,1,0:T(8,128)(2,1)}, bf16[3,320,1024]{2,1,0:T(...) custom-call(s32[3]{0:T(128)} %pad_add_fusion.idx, ...), custom_call_target="tpu_custom_call", output_to_operand_aliasing={{0}: (11, {}), {1}: (12, {}), {2}: (13, {}), {3}: (14, {}),... | custom-call | flops 6207569920 | bytes 17301504 | tf_op jit(solution)/shard_map/pallas_call | solution.py:30
  541.3 13.0 %shard_map.221 = (bf16[3,320,1024]{2,1,0:T(8,128)(2,1)}, f32[2,320,1024]{2,1,0:T(8,128)}, bf16[2,128,1024]{2,1,0:T(8,128)(2,1)}, bf16[2,128,1024]{2,1,0:T(8,128)(2,1)}) custom-call(s32[3]{0:T(128)} %pad_add_fusion.idx, bf16[3,320,1024]{2,1,0:T(8,128)(2,1)} %get-tuple-element.164.q, ...), custom_call_target="tpu_custom_call", output_to_operand_aliasing={{0}: (8, {})} | custom-call | flops 5033164800 | bytes 7864320 | tf_op jit(solution)/shard_map/pallas_call | solution.py:30
  562.4 8.8 %collective-permute-done.41 = bf16[256,2816]{1,0:T(8,128)(2,1)} collective-permute-done((bf16[256,2816]{1,0:T(8,128)(2,1)}, bf16[256,2816]{1,0:T(8,128)(2,1)}, u32[]{:S(2)}, u32[]{:S(2)}) %collective-permute-start.41) | collective-permute-done | bytes 1441824 | tf_op jit(solution)/shard_map/ppermute | solution.py:706
  581.1 9.7 %shard_map.222 = (bf16[3,320,1024]{2,1,0:T(8,128)(2,1)}, bf16[3,320,1024]{2,1,0:T(8,128)(2,1)}, f32[3,8,1024]{2,1,0:T(8,128)}, bf16[320,1024]{1,0:T(8,128)(2,1)}) custom-call(s32[3]{0:T(128)} %pad_add_fusion.idx, bf16[3,320,1024]{2,1,0:T(8,128)(2,1)} %get-tuple-element.221.grad_q, ...), custom_call_target="tpu_custom_call", output_to_operand_aliasing={{0}: (11, {}), {1}: (12, {}), {2}: (13, {})} | custom-call | flops 2013265920 | bytes 12845056 | tf_op jit(solution)/shard_map/pallas_call | solution.py:30
  596.9 12.5 %collective-permute-done.45 = bf16[256,2816]{1,0:T(8,128)(2,1)} collective-permute-done((bf16[256,2816]{1,0:T(8,128)(2,1)}, bf16[256,2816]{1,0:T(8,128)(2,1)}, u32[]{:S(2)}, u32[]{:S(2)}) %collective-permute-start.45) | collective-permute-done | bytes 1441824 | tf_op jit(solution)/shard_map/ppermute | solution.py:706
  613.0 7.9 %convolution_convert_fusion = bf16[1024,3200]{1,0:T(8,128)(2,1)S(1)} fusion(bf16[656,1024]{1,0:T(8,128)(2,1)S(1)} %copy-done.22, bf16[16,3200]{1,0:T(8,128)(2,1)S(1)} %pad_convert_fusion, bf16[640,3200]{1,0:T(8,128)(2,1)} %fusion.7), kind=kOutput, calls=%fused_computation.7 | convolution fusion | flops 4310835200 | bytes 12095488 | tf_op jit(solution)/shard_map/dot_general | solution.py:1046
  636.2 24.0 %collective-permute-done.49 = bf16[704,1024]{1,0:T(8,128)(2,1)} collective-permute-done((bf16[704,1024]{1,0:T(8,128)(2,1)}, bf16[704,1024]{1,0:T(8,128)(2,1)}, u32[]{:S(2)}, u32[]{:S(2)}) %collective-permute-start.49) | collective-permute-done | bytes 1441824 | tf_op jit(solution)/shard_map/ppermute | solution.py:706
  673.6 7.8 %collective-permute-done.50 = bf16[64,3200]{1,0:T(8,128)(2,1)} collective-permute-done((bf16[64,3200]{1,0:T(8,128)(2,1)}, bf16[64,3200]{1,0:T(8,128)(2,1)}, u32[]{:S(2)}, u32[]{:S(2)}) %collective-permute-start.50) | collective-permute-done | bytes 409632 | tf_op jit(solution)/shard_map/ppermute | solution.py:706
  681.4 13.0 %collective-permute-done.48 = bf16[64,3200]{1,0:T(8,128)(2,1)} collective-permute-done((bf16[64,3200]{1,0:T(8,128)(2,1)}, bf16[64,3200]{1,0:T(8,128)(2,1)}, u32[]{:S(2)}, u32[]{:S(2)}) %collective-permute-start.48) | collective-permute-done | bytes 409632 | tf_op jit(solution)/shard_map/ppermute | solution.py:706
  (278 shorter events, 292.3 us)
Async XLA Ops:
  7.2 46.5 %all-gather.4.cloned.1.call-start = ((), (), s32[]{:S(2)}) async-start(), calls=%async_computation.4 | async-start | bytes 1802240 | tf_op jit(solution)/shard_map/all_gather | solution.py:729
  7.9 118.5 %all-gather.6.cloned.1.call-start = ((), (), s32[]{:S(2)}) async-start(), calls=%async_computation.5 | async-start | bytes 1802240 | tf_op jit(solution)/shard_map/all_gather | solution.py:729
  12.4 24.1 %collective-permute-start.3 = (bf16[272,1024]{1,0:T(8,128)(2,1)S(1)}, bf16[272,1024]{1,0:T(8,128)(2,1)S(1)}, u32[]{:S(2)}, u32[]{:S(2)}) collective-permute-start(bf16[272,1024]{1,0:T(8,128)(2,1)S(1)} %fusion.49.refs_0_), channel_id=1, source_target_pairs={{0,1},{1,2},{2,3},{3,0},{4,5},{5,6},{6,7},{7,4},{8,9},{9,10},{10,1... | collective-permute-start | bytes 1671176 | tf_op jit(solution)/shard_map/ppermute | solution.py:706
  15.4 150.1 %all-gather.8.cloned.1.call-start = ((), (), s32[]{:S(2)}) async-start(), calls=%async_computation.6 | async-start | bytes 1802240 | tf_op jit(solution)/shard_map/all_gather | solution.py:729
  53.6 53.3 %collective-permute-start.13 = (bf16[4,64,2816]{2,1,0:T(8,128)(2,1)}, bf16[4,64,2816]{2,1,0:T(8,128)(2,1)}, u32[]{:S(2)}, u32[]{:S(2)}) collective-permute-start(bf16[4,64,2816]{2,1,0:T(8,128)(2,1)} %all-gather.4.cloned.1.call-done.refs_0_), channel_id=1, source_target_pairs={{0,8},{4,12},{8,0},{12,4},{1,9},{5,13},{9,1},{13,5},{2,10},{6,14},... | collective-permute-start | bytes 4325384 | tf_op jit(solution)/shard_map/ppermute | solution.py:706
  55.2 21.9 %collective-permute-start.7 = (bf16[272,1024]{1,0:T(8,128)(2,1)S(1)}, bf16[272,1024]{1,0:T(8,128)(2,1)S(1)}, u32[]{:S(2)}, u32[]{:S(2)}) collective-permute-start(bf16[272,1024]{1,0:T(8,128)(2,1)S(1)} %collective-permute-done.3.refs_4_), channel_id=1, source_target_pairs={{0,1},{1,2},{2,3},{3,0},{4,5},{5,6},{6,7},{7,4},{8,9},{9,10},{10,1... | collective-permute-start | bytes 1671176 | tf_op jit(solution)/shard_map/ppermute | solution.py:706
  55.2 44.2 %collective-permute-start.1 = (bf16[272,1024]{1,0:T(8,128)(2,1)S(1)}, bf16[272,1024]{1,0:T(8,128)(2,1)S(1)}, u32[]{:S(2)}, u32[]{:S(2)}) collective-permute-start(bf16[272,1024]{1,0:T(8,128)(2,1)S(1)} %fusion.49.refs_0_), channel_id=1, source_target_pairs={{0,8},{4,12},{8,0},{12,4},{1,9},{5,13},{9,1},{13,5},{2,10},{6,14},... | collective-permute-start | bytes 1671176 | tf_op jit(solution)/shard_map/ppermute | solution.py:706
  77.0 29.4 %collective-permute-start.11 = (bf16[272,1024]{1,0:T(8,128)(2,1)S(1)}, bf16[272,1024]{1,0:T(8,128)(2,1)S(1)}, u32[]{:S(2)}, u32[]{:S(2)}) collective-permute-start(bf16[272,1024]{1,0:T(8,128)(2,1)S(1)} %collective-permute-done.7.refs_8_), channel_id=1, source_target_pairs={{0,1},{1,2},{2,3},{3,0},{4,5},{5,6},{6,7},{7,4},{8,9},{9,10},{10,1... | collective-permute-start | bytes 1671176 | tf_op jit(solution)/shard_map/ppermute | solution.py:706
  80.2 28.3 %collective-permute-start = (bf16[272,1024]{1,0:T(8,128)(2,1)S(1)}, bf16[272,1024]{1,0:T(8,128)(2,1)}, u32[]{:S(2)}, u32[]{:S(2)}) collective-permute-start(bf16[272,1024]{1,0:T(8,128)(2,1)S(1)} %fusion.49.refs_0_), channel_id=1, source_target_pairs={{0,4},{4,0},{8,12},{12,8},{1,5},{5,1},{9,13},{13,9},{2,6},{6,2},{1... | collective-permute-start | bytes 1671176 | tf_op jit(solution)/shard_map/ppermute | solution.py:706
  80.2 548.6 %reduce-scatter.5.cloned.1.call-start = ((), (), s32[]{:S(2)}) async-start(), calls=%async_computation.7 | async-start | bytes 1310720 | tf_op jit(solution)/shard_map/reduce_scatter | solution.py:839
  80.3 28.3 %collective-permute-start.4 = (bf16[272,1024]{1,0:T(8,128)(2,1)S(1)}, bf16[272,1024]{1,0:T(8,128)(2,1)S(1)}, u32[]{:S(2)}, u32[]{:S(2)}) collective-permute-start(bf16[272,1024]{1,0:T(8,128)(2,1)S(1)} %collective-permute-done.3.refs_4_), channel_id=1, source_target_pairs={{0,4},{4,0},{8,12},{12,8},{1,5},{5,1},{9,13},{13,9},{2,6},{6,2},{1... | collective-permute-start | bytes 1671176 | tf_op jit(solution)/shard_map/ppermute | solution.py:706
  107.0 19.5 %collective-permute-start.14 = (bf16[272,1024]{1,0:T(8,128)(2,1)S(1)}, bf16[272,1024]{1,0:T(8,128)(2,1)}, u32[]{:S(2)}, u32[]{:S(2)}) collective-permute-start(bf16[272,1024]{1,0:T(8,128)(2,1)S(1)} %collective-permute-done.11.refs_12_), channel_id=1, source_target_pairs={{0,8},{4,12},{8,0},{12,4},{1,9},{5,13},{9,1},{13,5},{2,10},{6,14},... | collective-permute-start | bytes 1671176 | tf_op jit(solution)/shard_map/ppermute | solution.py:706
  108.5 17.9 %collective-permute-start.8 = (bf16[272,1024]{1,0:T(8,128)(2,1)S(1)}, bf16[272,1024]{1,0:T(8,128)(2,1)}, u32[]{:S(2)}, u32[]{:S(2)}) collective-permute-start(bf16[272,1024]{1,0:T(8,128)(2,1)S(1)} %collective-permute-done.7.refs_8_), channel_id=1, source_target_pairs={{0,4},{4,0},{8,12},{12,8},{1,5},{5,1},{9,13},{13,9},{2,6},{6,2},{1... | collective-permute-start | bytes 1671176 | tf_op jit(solution)/shard_map/ppermute | solution.py:706
  109.3 21.8 %collective-permute-start.6 = (bf16[272,1024]{1,0:T(8,128)(2,1)S(1)}, bf16[272,1024]{1,0:T(8,128)(2,1)}, u32[]{:S(2)}, u32[]{:S(2)}) collective-permute-start(bf16[272,1024]{1,0:T(8,128)(2,1)S(1)} %collective-permute-done.5.refs_6_), channel_id=1, source_target_pairs={{0,4},{4,0},{8,12},{12,8},{1,5},{5,1},{9,13},{13,9},{2,6},{6,2},{1... | collective-permute-start | bytes 1671176 | tf_op jit(solution)/shard_map/ppermute | solution.py:706
  110.6 20.5 %collective-permute-start.12 = (bf16[272,1024]{1,0:T(8,128)(2,1)S(1)}, bf16[272,1024]{1,0:T(8,128)(2,1)}, u32[]{:S(2)}, u32[]{:S(2)}) collective-permute-start(bf16[272,1024]{1,0:T(8,128)(2,1)S(1)} %collective-permute-done.11.refs_12_), channel_id=1, source_target_pairs={{0,4},{4,0},{8,12},{12,8},{1,5},{5,1},{9,13},{13,9},{2,6},{6,2},{1... | collective-permute-start | bytes 1671176 | tf_op jit(solution)/shard_map/ppermute | solution.py:706
  126.4 34.3 %collective-permute-start.16 = (bf16[4,64,2816]{2,1,0:T(8,128)(2,1)}, bf16[4,64,2816]{2,1,0:T(8,128)(2,1)}, u32[]{:S(2)}, u32[]{:S(2)}) collective-permute-start(bf16[4,64,2816]{2,1,0:T(8,128)(2,1)} %all-gather.6.cloned.1.call-done.refs_0_), channel_id=1, source_target_pairs={{0,8},{4,12},{8,0},{12,4},{1,9},{5,13},{9,1},{13,5},{2,10},{6,14},... | collective-permute-start | bytes 4325384 | tf_op jit(solution)/shard_map/ppermute | solution.py:706
  152.8 42.1 %collective-permute-start.21 = (bf16[4,64,2816]{2,1,0:T(8,128)(2,1)S(1)}, bf16[4,64,2816]{2,1,0:T(8,128)(2,1)}, u32[]{:S(2)}, u32[]{:S(2)}) collective-permute-start(bf16[4,64,2816]{2,1,0:T(8,128)(2,1)S(1)} %copy-done.4), channel_id=1, source_target_pairs={{0,4},{4,0},{8,12},{12,8},{1,5},{5,1},{9,13},{13,9},{2,6},{6,2},{1... | collective-permute-start | bytes 4325384 | tf_op jit(solution)/shard_map/ppermute | solution.py:706
  154.0 35.2 %collective-permute-start.19 = (bf16[4,64,2816]{2,1,0:T(8,128)(2,1)S(1)}, bf16[4,64,2816]{2,1,0:T(8,128)(2,1)}, u32[]{:S(2)}, u32[]{:S(2)}) collective-permute-start(bf16[4,64,2816]{2,1,0:T(8,128)(2,1)S(1)} %copy-done.3), channel_id=1, source_target_pairs={{0,4},{4,0},{8,12},{12,8},{1,5},{5,1},{9,13},{13,9},{2,6},{6,2},{1... | collective-permute-start | bytes 4325384 | tf_op jit(solution)/shard_map/ppermute | solution.py:706
  160.8 28.7 %collective-permute-start.20 = (bf16[4,64,2816]{2,1,0:T(8,128)(2,1)}, bf16[4,64,2816]{2,1,0:T(8,128)(2,1)}, u32[]{:S(2)}, u32[]{:S(2)}) collective-permute-start(bf16[4,64,2816]{2,1,0:T(8,128)(2,1)} %collective-permute-done.13.refs_2_), channel_id=1, source_target_pairs={{0,4},{4,0},{8,12},{12,8},{1,5},{5,1},{9,13},{13,9},{2,6},{6,2},{1... | collective-permute-start | bytes 4325384 | tf_op jit(solution)/shard_map/ppermute | solution.py:706
  160.8 34.2 %collective-permute-start.22 = (bf16[4,64,2816]{2,1,0:T(8,128)(2,1)}, bf16[4,64,2816]{2,1,0:T(8,128)(2,1)}, u32[]{:S(2)}, u32[]{:S(2)}) collective-permute-start(bf16[4,64,2816]{2,1,0:T(8,128)(2,1)} %collective-permute-done.16.refs_2_), channel_id=1, source_target_pairs={{0,4},{4,0},{8,12},{12,8},{1,5},{5,1},{9,13},{13,9},{2,6},{6,2},{1... | collective-permute-start | bytes 4325384 | tf_op jit(solution)/shard_map/ppermute | solution.py:706
  165.5 34.9 %collective-permute-start.24 = (bf16[4,176,1024]{2,1,0:T(8,128)(2,1)}, bf16[4,176,1024]{2,1,0:T(8,128)(2,1)}, u32[]{:S(2)}, u32[]{:S(2)}) collective-permute-start(bf16[4,176,1024]{2,1,0:T(8,128)(2,1)} %all-gather.8.cloned.1.call-done.refs_0_), channel_id=1, source_target_pairs={{0,8},{4,12},{8,0},{12,4},{1,9},{5,13},{9,1},{13,5},{2,10},{6,14},... | collective-permute-start | bytes 4325384 | tf_op jit(solution)/shard_map/ppermute | solution.py:706
  221.6 18.2 %collective-permute-start.26 = (bf16[320,1024]{1,0:T(8,128)(2,1)}, bf16[320,1024]{1,0:T(8,128)(2,1)S(1)}, u32[]{:S(2)}, u32[]{:S(2)}) collective-permute-start(bf16[320,1024]{1,0:T(8,128)(2,1)} %get-tuple-element.148), channel_id=1, source_target_pairs={{0,16},{1,17},{2,18},{3,19},{4,20},{5,21},{6,22},{7,23},{8,24},{9,... | collective-permute-start | bytes 1966088 | tf_op jit(solution)/shard_map/ppermute | solution.py:20
  509.6 24.5 %collective-permute-start.40 = (bf16[2,256,2816]{2,1,0:T(8,128)(2,1)}, bf16[2,256,2816]{2,1,0:T(8,128)(2,1)}, u32[]{:S(2)}, u32[]{:S(2)}) collective-permute-start(bf16[2,256,2816]{2,1,0:T(8,128)(2,1)} %dynamic-slice_bitcast_fusion.2), channel_id=1, source_target_pairs={{0,4},{4,0},{8,12},{12,8},{1,5},{5,1},{9,13},{13,9},{2,6},{6,2},{1... | collective-permute-start | bytes 8650760 | tf_op jit(solution)/shard_map/ppermute | solution.py:706
  533.6 25.1 %collective-permute-start.42 = (bf16[2,704,1024]{2,1,0:T(8,128)(2,1)}, bf16[2,704,1024]{2,1,0:T(8,128)(2,1)}, u32[]{:S(2)}, u32[]{:S(2)}) collective-permute-start(bf16[2,704,1024]{2,1,0:T(8,128)(2,1)} %dynamic-slice_bitcast_fusion.1), channel_id=1, source_target_pairs={{0,4},{4,0},{8,12},{12,8},{1,5},{5,1},{9,13},{13,9},{2,6},{6,2},{1... | collective-permute-start | bytes 8650760 | tf_op jit(solution)/shard_map/ppermute | solution.py:706
  534.1 137.6 %reduce-scatter.7.cloned.1.call-start = ((), (), s32[]{:S(2)}) async-start(), calls=%async_computation.8 | async-start | bytes 1802240 | tf_op jit(solution)/shard_map/reduce_scatter | solution.py:869
  537.4 33.9 %collective-permute-start.41 = (bf16[256,2816]{1,0:T(8,128)(2,1)}, bf16[256,2816]{1,0:T(8,128)(2,1)}, u32[]{:S(2)}, u32[]{:S(2)}) collective-permute-start(bf16[256,2816]{1,0:T(8,128)(2,1)} %fusion.15), channel_id=1, source_target_pairs={{0,8},{4,12},{8,0},{12,4},{1,9},{5,13},{9,1},{13,5},{2,10},{6,14},... | collective-permute-start | bytes 4325384 | tf_op jit(solution)/shard_map/ppermute | solution.py:706
  571.3 38.1 %collective-permute-start.45 = (bf16[256,2816]{1,0:T(8,128)(2,1)}, bf16[256,2816]{1,0:T(8,128)(2,1)}, u32[]{:S(2)}, u32[]{:S(2)}) collective-permute-start(bf16[256,2816]{1,0:T(8,128)(2,1)} %fusion.16), channel_id=1, source_target_pairs={{0,8},{4,12},{8,0},{12,4},{1,9},{5,13},{9,1},{13,5},{2,10},{6,14},... | collective-permute-start | bytes 4325384 | tf_op jit(solution)/shard_map/ppermute | solution.py:706
  581.0 122.0 %reduce-scatter.9.cloned.1.call-start = ((), (), s32[]{:S(2)}) async-start(), calls=%async_computation.9 | async-start | bytes 1802240 | tf_op jit(solution)/shard_map/reduce_scatter | solution.py:869
  625.3 93.3 %reduce-scatter.11.cloned.1.call-start = ((), (), s32[]{:S(2)}) async-start(), calls=%async_computation.10 | async-start | bytes 1802240 | tf_op jit(solution)/shard_map/reduce_scatter | solution.py:869
  625.4 34.8 %collective-permute-start.49 = (bf16[704,1024]{1,0:T(8,128)(2,1)}, bf16[704,1024]{1,0:T(8,128)(2,1)}, u32[]{:S(2)}, u32[]{:S(2)}) collective-permute-start(bf16[704,1024]{1,0:T(8,128)(2,1)} %fusion.13), channel_id=1, source_target_pairs={{0,8},{4,12},{8,0},{12,4},{1,9},{5,13},{9,1},{13,5},{2,10},{6,14},... | collective-permute-start | bytes 4325384 | tf_op jit(solution)/shard_map/ppermute | solution.py:706
  633.7 34.3 %collective-permute-start.47 = (bf16[64,3200]{1,0:T(8,128)(2,1)}, bf16[64,3200]{1,0:T(8,128)(2,1)}, u32[]{:S(2)}, u32[]{:S(2)}) collective-permute-start(bf16[64,3200]{1,0:T(8,128)(2,1)} %fusion.30), channel_id=1, source_target_pairs={{0,8},{4,12},{8,0},{12,4},{1,9},{5,13},{9,1},{13,5},{2,10},{6,14},... | collective-permute-start | bytes 1228808 | tf_op jit(solution)/shard_map/ppermute | solution.py:706
  671.7 22.7 %collective-permute-start.48 = (bf16[64,3200]{1,0:T(8,128)(2,1)}, bf16[64,3200]{1,0:T(8,128)(2,1)}, u32[]{:S(2)}, u32[]{:S(2)}) collective-permute-start(bf16[64,3200]{1,0:T(8,128)(2,1)} %get-tuple-element.262), channel_id=1, source_target_pairs={{0,1},{1,2},{2,3},{3,0},{4,5},{5,6},{6,7},{7,4},{8,9},{9,10},{10,1... | collective-permute-start | bytes 1228808 | tf_op jit(solution)/shard_map/ppermute | solution.py:706
  (72 other events, 609.5 us)
Sparse Core Ops, SparseCore 0:
  9.6 44.0 all-gather.3
  55.2 50.2 all-gather.5
  107.1 33.1 all-gather.7
  534.2 26.1 reduce-scatter.4
  581.1 32.5 reduce-scatter.6
  625.4 32.5 reduce-scatter.8
  664.6 41.1 reduce-scatter.10

commit v4 on v3

--- a/solution.py
+++ b/solution.py
@@ -209,27 +209,41 @@
         out[pl.ds(HALO, rows)] = kv[place]
         out[pl.ds(HALO + rows, HALO)] = high[place]
     scale = jnp.bfloat16(HEAD_DIM**-0.5)
+    tiles = [
+        (start, count, pair)
+        for start, count in row_blocks(rows)
+        for pair in range(WIDE // (2 * HEAD_DIM))
+    ]
+    sums = {}
+    scores, powers, totals = {}, {}, {}
+    for start, count, pair in tiles:
+        span = count + 2 * HALO
+        lanes = slice(pair * 2 * HEAD_DIM, (pair + 1) * 2 * HEAD_DIM)
+        q_both = stacked_heads(q[pl.ds(start, count), lanes] * scale)
+        block_bias = bias[pl.ds(start, count), :span]
+        scores[start, pair] = nt_dot(
+            q_both, k_out[pl.ds(start, span), lanes]
+        ) + jnp.concatenate([block_bias, block_bias], 0)
+    for start, count, pair in tiles:
+        value = scores[start, pair]
+        most = jnp.max(value, axis=-1, keepdims=True)
+        power = jnp.exp(value - most)
+        powers[start, pair] = power.astype(jnp.bfloat16)
+        totals[start, pair] = jnp.sum(power, axis=-1, keepdims=True)
+        log_sum = most + jnp.log(totals[start, pair])
+        sums[start, pair] = (log_sum[:count], log_sum[count:])
+    for start, count, pair in tiles:
+        span = count + 2 * HALO
+        lanes = slice(pair * 2 * HEAD_DIM, (pair + 1) * 2 * HEAD_DIM)
+        mixed = dot(powers[start, pair], v_out[pl.ds(start, span), lanes])
+        mixed = mixed * (1.0 / totals[start, pair])
+        mixed_out[pl.ds(start, count), lanes] = unstacked_heads(mixed).astype(jnp.bfloat16)
     for start, count in row_blocks(rows):
-        span = count + 2 * HALO
-        block_bias = bias[pl.ds(start, count), :span]
-        both_bias = jnp.concatenate([block_bias, block_bias], 0)
-        sums = []
-        for pair in range(WIDE // (2 * HEAD_DIM)):
-            lanes = slice(pair * 2 * HEAD_DIM, (pair + 1) * 2 * HEAD_DIM)
-            q_both = stacked_heads(q[pl.ds(start, count), lanes] * scale)
-            scores = nt_dot(q_both, k_out[pl.ds(start, span), lanes]) + both_bias
-            most = jnp.max(scores, axis=-1, keepdims=True)
-            powers = jnp.exp(scores - most)
-            total_power = jnp.sum(powers, axis=-1, keepdims=True)
-            probs = (powers * (1.0 / total_power)).astype(jnp.bfloat16)
-            mixed = dot(probs, v_out[pl.ds(start, span), lanes])
-            mixed_out[pl.ds(start, count), lanes] = unstacked_heads(mixed).astype(jnp.bfloat16)
-            log_sum = most + jnp.log(total_power)
-            sums += [log_sum[:count], log_sum[count:]]
         lane = lax.broadcasted_iota(jnp.int32, (count, 2 * HEAD_DIM), 1)
         wide = jnp.zeros((count, 2 * HEAD_DIM), jnp.float32)
-        for number, value in enumerate(sums):
-            wide = jnp.where(lane == number, value, wide)
+        for pair in range(WIDE // (2 * HEAD_DIM)):
+            for number, value in enumerate(sums[start, pair]):
+                wide = jnp.where(lane == 2 * pair + number, value, wide)
         lse_out[pl.ds(start, count)] = wide
     return dot(mixed_out[...], flat(wo))
 
@@ -530,32 +544,45 @@
     scale = jnp.bfloat16(HEAD_DIM**-0.5)
     k_total[...] = jnp.zeros_like(k_total)
     v_total[...] = jnp.zeros_like(v_total)
-    for start, count in row_blocks(rows):
+    tiles = [
+        (start, count, slice(pair * 2 * HEAD_DIM, (pair + 1) * 2 * HEAD_DIM), pair)
+        for start, count in row_blocks(rows)
+        for pair in range(WIDE // (2 * HEAD_DIM))
+    ]
+    held = {}
+    for start, count, lanes, pair in tiles:
         span = count + 2 * HALO
+        q_both = stacked_heads(q[pl.ds(start, count), lanes] * scale)
+        g_both = stacked_heads(grad_mixed[pl.ds(start, count), lanes])
+        scores = nt_dot(q_both, keys[pl.ds(start, span), lanes])
+        grad_probs = nt_dot(g_both, values[pl.ds(start, span), lanes])
+        held[start, pair] = (q_both, g_both, scores, grad_probs)
+    for start, count, lanes, pair in tiles:
+        span = count + 2 * HALO
+        q_both, g_both, scores, grad_probs = held[start, pair]
         block_bias = bias[pl.ds(start, count), :span]
         both_bias = jnp.concatenate([block_bias, block_bias], 0)
-        for pair in range(WIDE // (2 * HEAD_DIM)):
-            lanes = slice(pair * 2 * HEAD_DIM, (pair + 1) * 2 * HEAD_DIM)
-            q_both = stacked_heads(q[pl.ds(start, count), lanes] * scale)
-            g_both = stacked_heads(grad_mixed[pl.ds(start, count), lanes])
-            m_pair = mixed[pl.ds(start, count), lanes].astype(jnp.float32)
-            k_pair = keys[pl.ds(start, span), lanes]
-            log_sum = jnp.concatenate(
-                [lse[pl.ds(start, count), 2 * pair + n : 2 * pair + n + 1] for n in range(2)], 0
-            )
-            probs = jnp.exp(nt_dot(q_both, k_pair) + (both_bias - log_sum))
-            grad_probs = nt_dot(g_both, values[pl.ds(start, span), lanes])
-            mean = jnp.sum(
-                g_both.astype(jnp.float32) * jnp.concatenate([m_pair, m_pair], 0),
-                axis=-1,
-                keepdims=True,
-            )
-            grad_scores = (probs * (grad_probs - mean)).astype(jnp.bfloat16)
-            q_out[pl.ds(start, count), lanes] = (
-                unstacked_heads(dot(grad_scores, k_pair)) * (HEAD_DIM**-0.5)
-            ).astype(jnp.bfloat16)
-            k_total[pl.ds(start, span), lanes] += tn_dot(grad_scores, q_both)
-            v_total[pl.ds(start, span), lanes] += tn_dot(probs.astype(jnp.bfloat16), g_both)
+        m_pair = mixed[pl.ds(start, count), lanes].astype(jnp.float32)
+        log_sum = jnp.concatenate(
+            [lse[pl.ds(start, count), 2 * pair + n : 2 * pair + n + 1] for n in range(2)], 0
+        )
+        probs = jnp.exp(scores + (both_bias - log_sum))
+        mean = jnp.sum(
+            g_both.astype(jnp.float32) * jnp.concatenate([m_pair, m_pair], 0),
+            axis=-1,
+            keepdims=True,
+        )
+        grad_scores = (probs * (grad_probs - mean)).astype(jnp.bfloat16)
+        held[start, pair] = (q_both, g_both, probs.astype(jnp.bfloat16), grad_scores)
+    for start, count, lanes, pair in tiles:
+        span = count + 2 * HALO
+        q_both, g_both, probs, grad_scores = held[start, pair]
+        grad_q = dot(grad_scores, keys[pl.ds(start, span), lanes])
+        q_out[pl.ds(start, count), lanes] = (
+            unstacked_heads(grad_q) * (HEAD_DIM**-0.5)
+        ).astype(jnp.bfloat16)
+        k_total[pl.ds(start, span), lanes] += tn_dot(grad_scores, q_both)
+        v_total[pl.ds(start, span), lanes] += tn_dot(probs, g_both)
     for place, total in ((0, k_total), (1, v_total)):
         top[place] = total[pl.ds(0, HALO)].astype(jnp.bfloat16)
         center[place] = total[pl.ds(HALO, rows)]
@@ -851,7 +878,8 @@
 
     def cross(self, *others):
         self.level = self.block(1) if self.level is None else self.level
-        self.arrived = self.across(after(self.level, *others))
+        self.sent = after(self.level, *others)
+        self.arrived = self.across(self.sent)
         return self
 
     def add(self, *others):
@@ -946,12 +974,15 @@
     gain_two = gain_rows[:, rows : 2 * rows].reshape(1, -1)
     params = (gain_one, packed, gain_two)
 
-    store, results, grad_sources = {}, [], []
-    arrived = jnp.zeros((rows_local, model_width), jnp.bfloat16)
-    for moment in range(slots):
+    store, results, grad_sources, sums = {}, [], [], {}
+    arrived = [jnp.zeros((rows_local, model_width), jnp.bfloat16)]
+    arrived_grad = [arrived[0]]
+
+    def forward(moment, params):
         early, late = min(moment, micro_count - 1), max(moment - 1, 0)
         scalars = jnp.stack([is_first, is_first * 0 + moment, choose(early, late)])
-        kv, tail, head = project(store, slots, moment, scalars, inputs[early], arrived, params)
+        layer_in = after(arrived[moment], *grad_sources[-1:])
+        kv, tail, head = project(store, slots, moment, scalars, inputs[early], layer_in, params)
         low = shifted(tail, "seq", 1)
         high = shifted(head, "seq", -1)
         if moment == 0:
@@ -969,42 +1000,39 @@
             (result,) = attend(store, slots, moment, scalars, kv, low, high, bias, params)
         results.append(result)
         if moment < micro_count:
-            arrived = shifted(result, "section", 1)
-    activations = jnp.stack(
-        [
-            jnp.where(is_first == 1, results[number], results[number + 1])
-            for number in range(micro_count)
-        ]
-    )[None]
+            arrived.append(shifted(result, "section", 1))
+        return params
 
     def both(name, start):
         chosen = lax.dynamic_slice_in_dim(store[name], start, micro_count, 0)
         return chosen.reshape(-1, chosen.shape[-1])
 
-    def product(left, *right):
-        left = both(left, 1 - is_first)
-        right = jnp.concatenate([both(name, is_first) for name in right], 1)
-        return jnp.dot(left.T, right, preferred_element_type=jnp.float32).astype(jnp.bfloat16)
-
-    arrived_grad = jnp.zeros((rows_local, model_width), jnp.bfloat16)
-    for moment in range(slots):
+    def product(left, right, then=()):
+        left = after(both(left, 1 - is_first), *then)
+        return jnp.dot(
+            left.T, both(right, is_first), preferred_element_type=jnp.float32
+        ).astype(jnp.bfloat16)
+
+    def backward(moment):
         early, late = min(moment, micro_count - 1), max(moment - 1, 0)
         scalars = jnp.stack(
             [is_first, choose(late, min(moment + 1, micro_count)), choose(late, early)]
         )
         grad_res, grad_mixed = feed_back(
-            store, slots, moment, scalars, arrived_grad, cotangent[early], params
+            store, slots, moment, scalars, arrived_grad[moment], cotangent[early], params
         )
         if moment == micro_count:
             lines = links()
-            out_part = product("mixed", "grad_branch")
+            gate_part = product("normed_two", "grad_gate")
+            gate_sum = Scatter(gate_part, lines)
+            out_part = product("mixed", "grad_branch", then=(gate_part,))
             out_sum = Scatter(out_part, lines, along_first=True)
-            gate_sum = Scatter(after(product("normed_two", "grad_gate"), out_part), lines)
-            up_sum = Scatter(after(product("normed_two", "grad_up"), out_sum.summed), lines)
-            gate_sum.cross(out_sum.summed)
-            down_part = product("gated", "grad_result")
+            up_part = product("normed_two", "grad_up", then=(out_part,))
+            up_sum = Scatter(up_part, lines)
+            gate_sum.cross(up_part)
+            down_part = product("gated", "grad_result", then=(gate_sum.sent, out_sum.summed))
+            down_sum = Scatter(down_part, lines)
             grad_mixed = after(grad_mixed, down_part, up_sum.level)
-            down_sum = Scatter(down_part, lines)
         center, top, bottom = attend_back(store, slots, moment, scalars, grad_mixed, bias)
         above = shifted(top, "seq", -1)
         below = shifted(bottom, "seq", 1)
@@ -1012,20 +1040,37 @@
             up_sum.cross(above, below)
             gate_sum.add(center)
             center = after(center, gate_sum.level, down_sum.level)
+            down_sum.cross(above, below)
+            sums.update(lines=lines, gate=gate_sum, up=up_sum, down=down_sum, out=out_sum)
         (grad_source,) = project_back(
             store, slots, moment, scalars, center, below, above, grad_res, params
         )
         grad_sources.append(grad_source)
         if moment < micro_count:
-            arrived_grad = shifted(grad_source, "section", -1)
+            arrived_grad.append(shifted(grad_source, "section", -1))
+
+    params = forward(0, params)
+    for moment in range(1, slots):
+        forward(moment, params)
+        backward(moment - 1)
+    backward(micro_count)
+
+    activations = jnp.stack(
+        [
+            jnp.where(is_first == 1, results[number], results[number + 1])
+            for number in range(micro_count)
+        ]
+    )[None]
     input_grads = jnp.stack(
         [
             jnp.where(is_first == 1, grad_sources[number + 1], grad_sources[number])
             for number in range(micro_count)
         ]
     )[None]
-    down_sum.cross(above, below)
-    up_sum.add(grad_source)
+    lines, gate_sum, up_sum, down_sum, out_sum = (
+        sums[name] for name in ("lines", "gate", "up", "down", "out")
+    )
+    up_sum.add(grad_sources[-1])
     gain_rows = jnp.concatenate(
         [
             jnp.sum(lax.dynamic_slice_in_dim(store[name], is_first, micro_count, 0), 0)

time: 745 us -> 721 us (0.968)
  waiting for transfers between devices: 253 us -> 230 us
  Pallas kernels: 237 us -> 221 us
  local copies, waits for them, and re-layouts: 45.7 us -> 58.8 us
    ppermute x16, waiting for transfers between devices: 56.7 us -> 38 us  [shifted(): return lax.ppermute(shard, axis, pairs)]
    pallas_call x16, Pallas kernels: 221 us -> 206 us  [call(): pl.pallas_call(kernel, out_shape=outs, grid_spec=pltpu.PrefetchScalarGrid...]
    ppermute x40, starting transfers between devices: 49.3 us -> 59.7 us  [__call__(): self.sent.append(lax.ppermute(cells, self.axis, self.pairs))]
    dynamic_slice x3 -> x8, local copies, waits for them, and re-layouts: 1.81 us -> 11.5 us  [both(): chosen = lax.dynamic_slice_in_dim(store[name], start, micro_count, 0)]
    unnamed x87 -> x103, local copies, waits for them, and re-layouts: 22.2 us -> 26.4 us
  transfers between devices with their start and end apart: 63 -> 63, of which waited for: 31 -> 29; matrix products, arithmetic and copies ran while one was open for 14% -> 15% of each run, Pallas kernels for 8% -> 12%
where the time goes in v4:
time: 721 us; the launch traced here: 716 us
  waiting for transfers between devices  230 us (32%)
  Pallas kernels  221 us (31%)
  starting transfers between devices  106 us (15%)
  local copies, waits for them, and re-layouts  58.8 us (8%)
  other arithmetic  58 us (8%)
  matrix products  27 us (4%)
  between operations  15.2 us (2%)
    pallas_call x16, Pallas kernels, call(): pl.pallas_call(kernel, out_shape=outs, grid_spec=pltpu.PrefetchScalarGrid...  206 us
    ppermute x40, waiting for transfers between devices, __call__(): self.sent.append(lax.ppermute(cells, self.axis, self.pairs))  186 us
    ppermute x40, starting transfers between devices, __call__(): self.sent.append(lax.ppermute(cells, self.axis, self.pairs))  59.7 us
    ppermute x16, starting transfers between devices, shifted(): return lax.ppermute(shard, axis, pairs)  45.6 us
    ppermute x16, waiting for transfers between devices, shifted(): return lax.ppermute(shard, axis, pairs)  38 us
    convert_element_type x11, other arithmetic, plus(): return (left.astype(jnp.float32) + right.astype(jnp.float32)).astype(kind)  33.1 us
    unnamed x103, local copies, waits for them, and re-layouts  26.4 us
    dot_general x4, matrix products, product(): jnp.dot(left.T, both(right, is_first), preferred_element_type=jnp.float32)  21.2 us
  transfers between devices with their start and end apart: 63, of which 29 were waited for; matrix products, arithmetic and copies ran while one was open for 15% of the time, Pallas kernels for 12%

profile of v4, /device:TPU:0, one launch (start us, length us, event | category | flops | bytes accessed | tf_op | source)
XLA Modules:
  0.0 716.0 jit_solution(480523201251518006)
XLA Ops:
  15.5 21.0 %collective-permute-done.3.refs_4_ = bf16[272,1024]{1,0:T(8,128)(2,1)S(1)} collective-permute-done((bf16[272,1024]{1,0:T(8,128)(2,1)S(1)}, bf16[272,1024]{1,0:T(8,128)(2,1)S(1)}, u32[]{:S(2)}, u32[]{:S(2)}) %collective-permute-start.3) | collective-permute-done | bytes 557088 | tf_op jit(solution)/shard_map/ppermute | solution.py:733
  38.3 10.3 %collective-permute-done.5.refs_6_ = bf16[272,1024]{1,0:T(8,128)(2,1)S(1)} collective-permute-done((bf16[272,1024]{1,0:T(8,128)(2,1)S(1)}, bf16[272,1024]{1,0:T(8,128)(2,1)S(1)}, u32[]{:S(2)}, u32[]{:S(2)}) %collective-permute-start.5) | collective-permute-done | bytes 557088 | tf_op jit(solution)/shard_map/ppermute | solution.py:733
  55.7 21.3 %collective-permute-done.7.refs_8_ = bf16[272,1024]{1,0:T(8,128)(2,1)S(1)} collective-permute-done((bf16[272,1024]{1,0:T(8,128)(2,1)S(1)}, bf16[272,1024]{1,0:T(8,128)(2,1)S(1)}, u32[]{:S(2)}, u32[]{:S(2)}) %collective-permute-start.7) | collective-permute-done | bytes 557088 | tf_op jit(solution)/shard_map/ppermute | solution.py:733
  80.8 18.5 %collective-permute-done.1.refs_2_ = bf16[272,1024]{1,0:T(8,128)(2,1)S(1)} collective-permute-done((bf16[272,1024]{1,0:T(8,128)(2,1)S(1)}, bf16[272,1024]{1,0:T(8,128)(2,1)S(1)}, u32[]{:S(2)}, u32[]{:S(2)}) %collective-permute-start.1) | collective-permute-done | bytes 557088 | tf_op jit(solution)/shard_map/ppermute | solution.py:733
  99.3 7.1 collective-permute-done.11.refs_12_
  110.6 9.8 %collective-permute-done.9.refs_10_ = bf16[272,1024]{1,0:T(8,128)(2,1)} collective-permute-done((bf16[272,1024]{1,0:T(8,128)(2,1)S(1)}, bf16[272,1024]{1,0:T(8,128)(2,1)}, u32[]{:S(2)}, u32[]{:S(2)}) %collective-permute-start.9) | collective-permute-done | bytes 557088 | tf_op jit(solution)/shard_map/ppermute | solution.py:733
  140.8 7.7 %shard_map.204 = (bf16[3,320,1024]{2,1,0:T(8,128)(2,1)}, bf16[3,320,1024]{2,1,0:T(8,128)(2,1)}, bf16[3,320,1024]{2,1,0:T(8,128)(2,1)}, bf16[2,320,1024]{2,1,0:T(...) custom-call(s32[3]{0:T(128)} %stack.53.idx, bf16[320,1024]{1,0:T(8,128)(2,1)} %get-tuple-element.269.own, ...), custom_call_target="tpu_custom_call" | custom-call | flops 2013265920 | bytes 10878976 | tf_op jit(solution)/shard_map/pallas_call | solution.py:30
  173.1 10.3 %shard_map.205 = (bf16[3,576,1024]{2,1,0:T(8,128)(2,1)}, bf16[3,576,1024]{2,1,0:T(8,128)(2,1)}, bf16[3,320,1024]{2,1,0:T(8,128)(2,1)}, f32[3,320,512]{2,1,0:T(8,...) custom-call(s32[3]{0:T(128)} %stack.53.idx, bf16[3,320,1024]{2,1,0:T(8,128)(2,1)} %get-tuple-element.136.q.rest_2_, ...), custom_call_target="tpu_custom_call" | custom-call | flops 1677721600 | bytes 8650752 | tf_op jit(solution)/shard_map/pallas_call | solution.py:30
  208.9 12.7 %shard_map.209 = (bf16[3,320,2816]{2,1,0:T(8,128)(2,1)}, bf16[3,320,2816]{2,1,0:T(8,128)(2,1)}, bf16[3,320,2816]{2,1,0:T(8,128)(2,1)}, bf16[320,1024]{1,0:T(8,128)(2,1)}) custom-call(s32[3]{0:T(128)} %stack.53.idx, bf16[3,320,1024]{2,1,0:T(8,128)(2,1)} %get-tuple-element.143.two.rest_5_, f32[3,320,1024]{2,1,0:T(8,128)} %get-tuple-element.144.residual.rest_4_, ...), custom_call_target="tpu_custom_call" | custom-call | flops 5536481280 | bytes 20578304 | tf_op jit(solution)/shard_map/pallas_call | solution.py:30
  225.7 14.0 %collective-permute-done.26.arrived = bf16[320,1024]{1,0:T(8,128)(2,1)S(1)} collective-permute-done((bf16[320,1024]{1,0:T(8,128)(2,1)}, bf16[320,1024]{1,0:T(8,128)(2,1)S(1)}, u32[]{:S(2)}, u32[]{:S(2)}) %collective-permute-start.26) | collective-permute-done | bytes 655392 | tf_op jit(solution)/shard_map/ppermute | solution.py:20
  240.5 7.7 %shard_map.210 = (bf16[3,320,1024]{2,1,0:T(8,128)(2,1)}, bf16[3,320,1024]{2,1,0:T(8,128)(2,1)}, bf16[3,320,1024]{2,1,0:T(8,128)(2,1)}, bf16[2,320,1024]{2,1,0:T(...) custom-call(s32[3]{0:T(128)} %pad_add_fusion.2.idx, ...), custom_call_target="tpu_custom_call", output_to_operand_aliasing={{0}: (7, {}), {1}: (8, {}), {2}: (9, {})} | custom-call | flops 2013265920 | bytes 10878976 | tf_op jit(solution)/shard_map/pallas_call | solution.py:30
  256.3 22.4 %shard_map.211 = (bf16[3,576,1024]{2,1,0:T(8,128)(2,1)}, bf16[3,576,1024]{2,1,0:T(8,128)(2,1)}, bf16[3,320,1024]{2,1,0:T(8,128)(2,1)}, f32[3,320,512]{2,1,0:T(8,...) custom-call(s32[3]{0:T(128)} %pad_add_fusion.2.idx, ...), custom_call_target="tpu_custom_call", output_to_operand_aliasing={{0}: (12, {}), {1}: (13, {}), {2}: (14, {}), {3}: (15, {}),... | custom-call | flops 7214202880 | bytes 25952256 | tf_op jit(solution)/shard_map/pallas_call | solution.py:30
  278.7 17.3 %shard_map.212 = (bf16[3,320,1024]{2,1,0:T(8,128)(2,1)}, bf16[3,320,2816]{2,1,0:T(8,128)(2,1)}, bf16[3,320,2816]{2,1,0:T(8,128)(2,1)}, bf16[3,320,1024]{2,1,0:T(...) custom-call(s32[3]{0:T(128)} %pad_add_fusion.3.idx, ...), custom_call_target="tpu_custom_call" | custom-call | flops 6207569920 | bytes 17301504 | tf_op jit(solution)/shard_map/pallas_call | solution.py:30
  296.0 11.4 %shard_map.213 = (bf16[3,320,1024]{2,1,0:T(8,128)(2,1)}, f32[2,320,1024]{2,1,0:T(8,128)}, bf16[2,128,1024]{2,1,0:T(8,128)(2,1)}, bf16[2,128,1024]{2,1,0:T(8,128)(2,1)}) custom-call(s32[3]{0:T(128)} %pad_add_fusion.3.idx, bf16[3,320,1024]{2,1,0:T(8,128)(2,1)} %get-tuple-element.152.q.rest_2_, bf16[3,576,1024]{2,1,0:T(8,128)(2,1)} %get-tuple-element.165.keys.rest_0_, ...), custom_call_target="tpu_custom_call" | custom-call | flops 5033164800 | bytes 7864320 | tf_op jit(solution)/shard_map/pallas_call | solution.py:30
  307.4 9.1 %collective-permute-start.30 = (bf16[2,128,1024]{2,1,0:T(8,128)(2,1)}, bf16[2,128,1024]{2,1,0:T(8,128)(2,1)S(1)}, u32[]{:S(2)}, u32[]{:S(2)}) collective-permute-start(bf16[2,128,1024]{2,1,0:T(8,128)(2,1)} %get-tuple-element.175), channel_id=1, source_target_pairs={{0,4},{4,8},{8,12},{1,5},{5,9},{9,13},{2,6},{6,10},{10,14},{3,7},{... | collective-permute-start | bytes 1572872 | tf_op jit(solution)/shard_map/ppermute | solution.py:20
  323.7 9.4 %shard_map.214 = (bf16[3,320,1024]{2,1,0:T(8,128)(2,1)}, bf16[3,320,1024]{2,1,0:T(8,128)(2,1)}, f32[3,8,1024]{2,1,0:T(8,128)}, bf16[320,1024]{1,0:T(8,128)(2,1)}) custom-call(s32[3]{0:T(128)} %pad_add_fusion.3.idx, bf16[3,320,1024]{2,1,0:T(8,128)(2,1)} %get-tuple-element.173.grad_q.rest_0_, f32[2,320,1024]{2,1,0:T(8,128)} %get-tuple-element.174.center, ...), custom_call_target="tpu_custom_call" | custom-call | flops 2013265920 | bytes 12845056 | tf_op jit(solution)/shard_map/pallas_call | solution.py:30
  337.9 7.7 %shard_map.215 = (bf16[3,320,1024]{2,1,0:T(8,128)(2,1)}, bf16[3,320,1024]{2,1,0:T(8,128)(2,1)}, bf16[3,320,1024]{2,1,0:T(8,128)(2,1)}, bf16[2,320,1024]{2,1,0:T(...) custom-call(s32[3]{0:T(128)} %pad_add_fusion.1.idx, ...), custom_call_target="tpu_custom_call", output_to_operand_aliasing={{0}: (7, {}), {1}: (8, {}), {2}: (9, {})} | custom-call | flops 2013265920 | bytes 10878976 | tf_op jit(solution)/shard_map/pallas_call | solution.py:30
  352.8 22.4 %shard_map.216 = (bf16[3,576,1024]{2,1,0:T(8,128)(2,1)}, bf16[3,576,1024]{2,1,0:T(8,128)(2,1)}, bf16[3,320,1024]{2,1,0:T(8,128)(2,1)}, f32[3,320,512]{2,1,0:T(8,...) custom-call(s32[3]{0:T(128)} %pad_add_fusion.1.idx, ...), custom_call_target="tpu_custom_call", output_to_operand_aliasing={{0}: (12, {}), {1}: (13, {}), {2}: (14, {}), {3}: (15, {}),... | custom-call | flops 7214202880 | bytes 25952256 | tf_op jit(solution)/shard_map/pallas_call | solution.py:30
  376.0 17.3 %shard_map.217 = (bf16[3,320,1024]{2,1,0:T(8,128)(2,1)}, bf16[3,320,2816]{2,1,0:T(8,128)(2,1)}, bf16[3,320,2816]{2,1,0:T(8,128)(2,1)}, bf16[3,320,1024]{2,1,0:T(...) custom-call(s32[3]{0:T(128)} %pad_add_fusion.4.idx, ...), custom_call_target="tpu_custom_call", output_to_operand_aliasing={{0}: (11, {}), {1}: (12, {}), {2}: (13, {}), {3}: (14, {}),... | custom-call | flops 6207569920 | bytes 17301504 | tf_op jit(solution)/shard_map/pallas_call | solution.py:30
  393.3 11.5 %shard_map.218 = (bf16[3,320,1024]{2,1,0:T(8,128)(2,1)}, f32[2,320,1024]{2,1,0:T(8,128)}, bf16[2,128,1024]{2,1,0:T(8,128)(2,1)}, bf16[2,128,1024]{2,1,0:T(8,128)(2,1)}) custom-call(s32[3]{0:T(128)} %pad_add_fusion.4.idx, bf16[3,320,1024]{2,1,0:T(8,128)(2,1)} %get-tuple-element.181.q, ...), custom_call_target="tpu_custom_call", output_to_operand_aliasing={{0}: (8, {})} | custom-call | flops 5033164800 | bytes 7864320 | tf_op jit(solution)/shard_map/pallas_call | solution.py:30
  404.8 8.9 %collective-permute-start.35 = (bf16[2,128,1024]{2,1,0:T(8,128)(2,1)}, bf16[2,128,1024]{2,1,0:T(8,128)(2,1)S(1)}, u32[]{:S(2)}, u32[]{:S(2)}) collective-permute-start(bf16[2,128,1024]{2,1,0:T(8,128)(2,1)} %get-tuple-element.204), channel_id=1, source_target_pairs={{0,4},{4,8},{8,12},{1,5},{5,9},{9,13},{2,6},{6,10},{10,14},{3,7},{... | collective-permute-start | bytes 1572872 | tf_op jit(solution)/shard_map/ppermute | solution.py:20
  418.5 9.4 %shard_map.219 = (bf16[3,320,1024]{2,1,0:T(8,128)(2,1)}, bf16[3,320,1024]{2,1,0:T(8,128)(2,1)}, f32[3,8,1024]{2,1,0:T(8,128)}, bf16[320,1024]{1,0:T(8,128)(2,1)}) custom-call(s32[3]{0:T(128)} %pad_add_fusion.4.idx, bf16[3,320,1024]{2,1,0:T(8,128)(2,1)} %get-tuple-element.202.grad_q.rest_0_, ...), custom_call_target="tpu_custom_call", output_to_operand_aliasing={{0}: (11, {}), {1}: (12, {}), {2}: (13, {})} | custom-call | flops 2013265920 | bytes 12845056 | tf_op jit(solution)/shard_map/pallas_call | solution.py:30
  431.5 10.4 %collective-permute-done.37.arrived = bf16[320,1024]{1,0:T(8,128)(2,1)S(1)} collective-permute-done((bf16[320,1024]{1,0:T(8,128)(2,1)}, bf16[320,1024]{1,0:T(8,128)(2,1)S(1)}, u32[]{:S(2)}, u32[]{:S(2)}) %collective-permute-start.37) | collective-permute-done | bytes 655392 | tf_op jit(solution)/shard_map/ppermute | solution.py:20
  442.8 17.3 %shard_map.220 = (bf16[3,320,1024]{2,1,0:T(8,128)(2,1)}, bf16[3,320,2816]{2,1,0:T(8,128)(2,1)}, bf16[3,320,2816]{2,1,0:T(8,128)(2,1)}, bf16[3,320,1024]{2,1,0:T(...) custom-call(s32[3]{0:T(128)} %pad_add_fusion.idx, ...), custom_call_target="tpu_custom_call", output_to_operand_aliasing={{0}: (11, {}), {1}: (12, {}), {2}: (13, {}), {3}: (14, {}),... | custom-call | flops 6207569920 | bytes 17301504 | tf_op jit(solution)/shard_map/pallas_call | solution.py:30
  501.7 7.1 convolution_convert_fusion.1
  516.3 11.2 %shard_map.221 = (bf16[3,320,1024]{2,1,0:T(8,128)(2,1)}, f32[2,320,1024]{2,1,0:T(8,128)}, bf16[2,128,1024]{2,1,0:T(8,128)(2,1)}, bf16[2,128,1024]{2,1,0:T(8,128)(2,1)}) custom-call(s32[3]{0:T(128)} %pad_add_fusion.idx, bf16[3,320,1024]{2,1,0:T(8,128)(2,1)} %get-tuple-element.181.q, ...), custom_call_target="tpu_custom_call", output_to_operand_aliasing={{0}: (8, {})} | custom-call | flops 5033164800 | bytes 7864320 | tf_op jit(solution)/shard_map/pallas_call | solution.py:30
  535.2 17.3 %collective-permute-start.45 = (bf16[256,2816]{1,0:T(8,128)(2,1)}, bf16[256,2816]{1,0:T(8,128)(2,1)}, u32[]{:S(2)}, u32[]{:S(2)}) collective-permute-start(bf16[256,2816]{1,0:T(8,128)(2,1)} %fusion.13), channel_id=1, source_target_pairs={{0,8},{4,12},{8,0},{12,4},{1,9},{5,13},{9,1},{13,5},{2,10},{6,14},... | collective-permute-start | bytes 4325384 | tf_op jit(solution)/shard_map/ppermute | solution.py:733
  559.7 9.8 %shard_map.222 = (bf16[3,320,1024]{2,1,0:T(8,128)(2,1)}, bf16[3,320,1024]{2,1,0:T(8,128)(2,1)}, f32[3,8,1024]{2,1,0:T(8,128)}, bf16[320,1024]{1,0:T(8,128)(2,1)}) custom-call(s32[3]{0:T(128)} %pad_add_fusion.idx, bf16[3,320,1024]{2,1,0:T(8,128)(2,1)} %get-tuple-element.228.grad_q, ...), custom_call_target="tpu_custom_call", output_to_operand_aliasing={{0}: (11, {}), {1}: (12, {}), {2}: (13, {})} | custom-call | flops 2013265920 | bytes 12845056 | tf_op jit(solution)/shard_map/pallas_call | solution.py:30
  573.3 11.5 %collective-permute-done.45 = bf16[256,2816]{1,0:T(8,128)(2,1)} collective-permute-done((bf16[256,2816]{1,0:T(8,128)(2,1)}, bf16[256,2816]{1,0:T(8,128)(2,1)}, u32[]{:S(2)}, u32[]{:S(2)}) %collective-permute-start.45) | collective-permute-done | bytes 1441824 | tf_op jit(solution)/shard_map/ppermute | solution.py:733
  612.5 24.0 %collective-permute-done.49 = bf16[704,1024]{1,0:T(8,128)(2,1)} collective-permute-done((bf16[704,1024]{1,0:T(8,128)(2,1)}, bf16[704,1024]{1,0:T(8,128)(2,1)}, u32[]{:S(2)}, u32[]{:S(2)}) %collective-permute-start.49) | collective-permute-done | bytes 1441824 | tf_op jit(solution)/shard_map/ppermute | solution.py:733
  649.8 7.8 %collective-permute-done.50 = bf16[64,3200]{1,0:T(8,128)(2,1)} collective-permute-done((bf16[64,3200]{1,0:T(8,128)(2,1)}, bf16[64,3200]{1,0:T(8,128)(2,1)}, u32[]{:S(2)}, u32[]{:S(2)}) %collective-permute-start.50) | collective-permute-done | bytes 409632 | tf_op jit(solution)/shard_map/ppermute | solution.py:733
  657.6 13.0 %collective-permute-done.48 = bf16[64,3200]{1,0:T(8,128)(2,1)} collective-permute-done((bf16[64,3200]{1,0:T(8,128)(2,1)}, bf16[64,3200]{1,0:T(8,128)(2,1)}, u32[]{:S(2)}, u32[]{:S(2)}) %collective-permute-start.48) | collective-permute-done | bytes 409632 | tf_op jit(solution)/shard_map/ppermute | solution.py:733
  (299 shorter events, 284.0 us)
Async XLA Ops:
  7.2 46.5 %all-gather.4.cloned.1.call-start = ((), (), s32[]{:S(2)}) async-start(), calls=%async_computation.4 | async-start | bytes 1802240 | tf_op jit(solution)/shard_map/all_gather | solution.py:756
  7.9 118.5 %all-gather.6.cloned.1.call-start = ((), (), s32[]{:S(2)}) async-start(), calls=%async_computation.5 | async-start | bytes 1802240 | tf_op jit(solution)/shard_map/all_gather | solution.py:756
  12.4 24.1 %collective-permute-start.3 = (bf16[272,1024]{1,0:T(8,128)(2,1)S(1)}, bf16[272,1024]{1,0:T(8,128)(2,1)S(1)}, u32[]{:S(2)}, u32[]{:S(2)}) collective-permute-start(bf16[272,1024]{1,0:T(8,128)(2,1)S(1)} %fusion.42.refs_0_), channel_id=1, source_target_pairs={{0,1},{1,2},{2,3},{3,0},{4,5},{5,6},{6,7},{7,4},{8,9},{9,10},{10,1... | collective-permute-start | bytes 1671176 | tf_op jit(solution)/shard_map/ppermute | solution.py:733
  15.4 150.1 %all-gather.8.cloned.1.call-start = ((), (), s32[]{:S(2)}) async-start(), calls=%async_computation.6 | async-start | bytes 1802240 | tf_op jit(solution)/shard_map/all_gather | solution.py:756
  53.6 53.3 %collective-permute-start.13 = (bf16[4,64,2816]{2,1,0:T(8,128)(2,1)}, bf16[4,64,2816]{2,1,0:T(8,128)(2,1)}, u32[]{:S(2)}, u32[]{:S(2)}) collective-permute-start(bf16[4,64,2816]{2,1,0:T(8,128)(2,1)} %all-gather.4.cloned.1.call-done.refs_0_), channel_id=1, source_target_pairs={{0,8},{4,12},{8,0},{12,4},{1,9},{5,13},{9,1},{13,5},{2,10},{6,14},... | collective-permute-start | bytes 4325384 | tf_op jit(solution)/shard_map/ppermute | solution.py:733
  55.2 21.9 %collective-permute-start.7 = (bf16[272,1024]{1,0:T(8,128)(2,1)S(1)}, bf16[272,1024]{1,0:T(8,128)(2,1)S(1)}, u32[]{:S(2)}, u32[]{:S(2)}) collective-permute-start(bf16[272,1024]{1,0:T(8,128)(2,1)S(1)} %collective-permute-done.3.refs_4_), channel_id=1, source_target_pairs={{0,1},{1,2},{2,3},{3,0},{4,5},{5,6},{6,7},{7,4},{8,9},{9,10},{10,1... | collective-permute-start | bytes 1671176 | tf_op jit(solution)/shard_map/ppermute | solution.py:733
  55.2 44.2 %collective-permute-start.1 = (bf16[272,1024]{1,0:T(8,128)(2,1)S(1)}, bf16[272,1024]{1,0:T(8,128)(2,1)S(1)}, u32[]{:S(2)}, u32[]{:S(2)}) collective-permute-start(bf16[272,1024]{1,0:T(8,128)(2,1)S(1)} %fusion.42.refs_0_), channel_id=1, source_target_pairs={{0,8},{4,12},{8,0},{12,4},{1,9},{5,13},{9,1},{13,5},{2,10},{6,14},... | collective-permute-start | bytes 1671176 | tf_op jit(solution)/shard_map/ppermute | solution.py:733
  77.0 29.4 %collective-permute-start.11 = (bf16[272,1024]{1,0:T(8,128)(2,1)S(1)}, bf16[272,1024]{1,0:T(8,128)(2,1)S(1)}, u32[]{:S(2)}, u32[]{:S(2)}) collective-permute-start(bf16[272,1024]{1,0:T(8,128)(2,1)S(1)} %collective-permute-done.7.refs_8_), channel_id=1, source_target_pairs={{0,1},{1,2},{2,3},{3,0},{4,5},{5,6},{6,7},{7,4},{8,9},{9,10},{10,1... | collective-permute-start | bytes 1671176 | tf_op jit(solution)/shard_map/ppermute | solution.py:733
  80.2 28.3 %collective-permute-start = (bf16[272,1024]{1,0:T(8,128)(2,1)S(1)}, bf16[272,1024]{1,0:T(8,128)(2,1)}, u32[]{:S(2)}, u32[]{:S(2)}) collective-permute-start(bf16[272,1024]{1,0:T(8,128)(2,1)S(1)} %fusion.42.refs_0_), channel_id=1, source_target_pairs={{0,4},{4,0},{8,12},{12,8},{1,5},{5,1},{9,13},{13,9},{2,6},{6,2},{1... | collective-permute-start | bytes 1671176 | tf_op jit(solution)/shard_map/ppermute | solution.py:733
  80.2 524.8 %reduce-scatter.5.cloned.1.call-start = ((), (), s32[]{:S(2)}) async-start(), calls=%async_computation.7 | async-start | bytes 1310720 | tf_op jit(solution)/shard_map/reduce_scatter | solution.py:866
  80.3 28.3 %collective-permute-start.4 = (bf16[272,1024]{1,0:T(8,128)(2,1)S(1)}, bf16[272,1024]{1,0:T(8,128)(2,1)S(1)}, u32[]{:S(2)}, u32[]{:S(2)}) collective-permute-start(bf16[272,1024]{1,0:T(8,128)(2,1)S(1)} %collective-permute-done.3.refs_4_), channel_id=1, source_target_pairs={{0,4},{4,0},{8,12},{12,8},{1,5},{5,1},{9,13},{13,9},{2,6},{6,2},{1... | collective-permute-start | bytes 1671176 | tf_op jit(solution)/shard_map/ppermute | solution.py:733
  107.0 19.5 %collective-permute-start.14 = (bf16[272,1024]{1,0:T(8,128)(2,1)S(1)}, bf16[272,1024]{1,0:T(8,128)(2,1)}, u32[]{:S(2)}, u32[]{:S(2)}) collective-permute-start(bf16[272,1024]{1,0:T(8,128)(2,1)S(1)} %collective-permute-done.11.refs_12_), channel_id=1, source_target_pairs={{0,8},{4,12},{8,0},{12,4},{1,9},{5,13},{9,1},{13,5},{2,10},{6,14},... | collective-permute-start | bytes 1671176 | tf_op jit(solution)/shard_map/ppermute | solution.py:733
  109.3 21.8 %collective-permute-start.6 = (bf16[272,1024]{1,0:T(8,128)(2,1)S(1)}, bf16[272,1024]{1,0:T(8,128)(2,1)}, u32[]{:S(2)}, u32[]{:S(2)}) collective-permute-start(bf16[272,1024]{1,0:T(8,128)(2,1)S(1)} %collective-permute-done.5.refs_6_), channel_id=1, source_target_pairs={{0,4},{4,0},{8,12},{12,8},{1,5},{5,1},{9,13},{13,9},{2,6},{6,2},{1... | collective-permute-start | bytes 1671176 | tf_op jit(solution)/shard_map/ppermute | solution.py:733
  110.6 20.5 %collective-permute-start.12 = (bf16[272,1024]{1,0:T(8,128)(2,1)S(1)}, bf16[272,1024]{1,0:T(8,128)(2,1)}, u32[]{:S(2)}, u32[]{:S(2)}) collective-permute-start(bf16[272,1024]{1,0:T(8,128)(2,1)S(1)} %collective-permute-done.11.refs_12_), channel_id=1, source_target_pairs={{0,4},{4,0},{8,12},{12,8},{1,5},{5,1},{9,13},{13,9},{2,6},{6,2},{1... | collective-permute-start | bytes 1671176 | tf_op jit(solution)/shard_map/ppermute | solution.py:733
  126.4 34.3 %collective-permute-start.16 = (bf16[4,64,2816]{2,1,0:T(8,128)(2,1)}, bf16[4,64,2816]{2,1,0:T(8,128)(2,1)}, u32[]{:S(2)}, u32[]{:S(2)}) collective-permute-start(bf16[4,64,2816]{2,1,0:T(8,128)(2,1)} %all-gather.6.cloned.1.call-done.refs_0_), channel_id=1, source_target_pairs={{0,8},{4,12},{8,0},{12,4},{1,9},{5,13},{9,1},{13,5},{2,10},{6,14},... | collective-permute-start | bytes 4325384 | tf_op jit(solution)/shard_map/ppermute | solution.py:733
  152.8 30.7 %collective-permute-start.21 = (bf16[4,64,2816]{2,1,0:T(8,128)(2,1)S(1)}, bf16[4,64,2816]{2,1,0:T(8,128)(2,1)}, u32[]{:S(2)}, u32[]{:S(2)}) collective-permute-start(bf16[4,64,2816]{2,1,0:T(8,128)(2,1)S(1)} %copy-done.4), channel_id=1, source_target_pairs={{0,4},{4,0},{8,12},{12,8},{1,5},{5,1},{9,13},{13,9},{2,6},{6,2},{1... | collective-permute-start | bytes 4325384 | tf_op jit(solution)/shard_map/ppermute | solution.py:733
  154.0 35.3 %collective-permute-start.19 = (bf16[4,64,2816]{2,1,0:T(8,128)(2,1)S(1)}, bf16[4,64,2816]{2,1,0:T(8,128)(2,1)}, u32[]{:S(2)}, u32[]{:S(2)}) collective-permute-start(bf16[4,64,2816]{2,1,0:T(8,128)(2,1)S(1)} %copy-done.3), channel_id=1, source_target_pairs={{0,4},{4,0},{8,12},{12,8},{1,5},{5,1},{9,13},{13,9},{2,6},{6,2},{1... | collective-permute-start | bytes 4325384 | tf_op jit(solution)/shard_map/ppermute | solution.py:733
  160.8 23.0 %collective-permute-start.22 = (bf16[4,64,2816]{2,1,0:T(8,128)(2,1)}, bf16[4,64,2816]{2,1,0:T(8,128)(2,1)}, u32[]{:S(2)}, u32[]{:S(2)}) collective-permute-start(bf16[4,64,2816]{2,1,0:T(8,128)(2,1)} %collective-permute-done.16.refs_2_), channel_id=1, source_target_pairs={{0,4},{4,0},{8,12},{12,8},{1,5},{5,1},{9,13},{13,9},{2,6},{6,2},{1... | collective-permute-start | bytes 4325384 | tf_op jit(solution)/shard_map/ppermute | solution.py:733
  160.8 28.5 %collective-permute-start.20 = (bf16[4,64,2816]{2,1,0:T(8,128)(2,1)}, bf16[4,64,2816]{2,1,0:T(8,128)(2,1)}, u32[]{:S(2)}, u32[]{:S(2)}) collective-permute-start(bf16[4,64,2816]{2,1,0:T(8,128)(2,1)} %collective-permute-done.13.refs_2_), channel_id=1, source_target_pairs={{0,4},{4,0},{8,12},{12,8},{1,5},{5,1},{9,13},{13,9},{2,6},{6,2},{1... | collective-permute-start | bytes 4325384 | tf_op jit(solution)/shard_map/ppermute | solution.py:733
  165.5 34.9 %collective-permute-start.24 = (bf16[4,176,1024]{2,1,0:T(8,128)(2,1)}, bf16[4,176,1024]{2,1,0:T(8,128)(2,1)}, u32[]{:S(2)}, u32[]{:S(2)}) collective-permute-start(bf16[4,176,1024]{2,1,0:T(8,128)(2,1)} %all-gather.8.cloned.1.call-done.refs_0_), channel_id=1, source_target_pairs={{0,8},{4,12},{8,0},{12,4},{1,9},{5,13},{9,1},{13,5},{2,10},{6,14},... | collective-permute-start | bytes 4325384 | tf_op jit(solution)/shard_map/ppermute | solution.py:733
  349.8 25.3 %collective-permute-start.34 = (bf16[320,1024]{1,0:T(8,128)(2,1)S(1)}, bf16[320,1024]{1,0:T(8,128)(2,1)S(1)}, u32[]{:S(2)}, u32[]{:S(2)}) collective-permute-start(bf16[320,1024]{1,0:T(8,128)(2,1)S(1)} %copy-done.32), channel_id=1, source_target_pairs={{16,0},{17,1},{18,2},{19,3},{20,4},{21,5},{22,6},{23,7},{24,8},{25... | collective-permute-start | bytes 1966088 | tf_op jit(solution)/shard_map/ppermute | solution.py:20
  471.3 27.2 %collective-permute-start.38 = (bf16[2,256,2816]{2,1,0:T(8,128)(2,1)}, bf16[2,256,2816]{2,1,0:T(8,128)(2,1)}, u32[]{:S(2)}, u32[]{:S(2)}) collective-permute-start(bf16[2,256,2816]{2,1,0:T(8,128)(2,1)} %dynamic-slice_bitcast_fusion.3), channel_id=1, source_target_pairs={{0,4},{4,0},{8,12},{12,8},{1,5},{5,1},{9,13},{13,9},{2,6},{6,2},{1... | collective-permute-start | bytes 8650760 | tf_op jit(solution)/shard_map/ppermute | solution.py:733
  490.9 21.6 %collective-permute-start.40 = (bf16[2,256,2816]{2,1,0:T(8,128)(2,1)}, bf16[2,256,2816]{2,1,0:T(8,128)(2,1)S(1)}, u32[]{:S(2)}, u32[]{:S(2)}) collective-permute-start(bf16[2,256,2816]{2,1,0:T(8,128)(2,1)} %dynamic-slice_bitcast_fusion.2), channel_id=1, source_target_pairs={{0,4},{4,0},{8,12},{12,8},{1,5},{5,1},{9,13},{13,9},{2,6},{6,2},{1... | collective-permute-start | bytes 8650760 | tf_op jit(solution)/shard_map/ppermute | solution.py:733
  512.2 44.0 %collective-permute-start.42 = (bf16[2,704,1024]{2,1,0:T(8,128)(2,1)}, bf16[2,704,1024]{2,1,0:T(8,128)(2,1)}, u32[]{:S(2)}, u32[]{:S(2)}) collective-permute-start(bf16[2,704,1024]{2,1,0:T(8,128)(2,1)} %dynamic-slice_bitcast_fusion.1), channel_id=1, source_target_pairs={{0,4},{4,0},{8,12},{12,8},{1,5},{5,1},{9,13},{13,9},{2,6},{6,2},{1... | collective-permute-start | bytes 8650760 | tf_op jit(solution)/shard_map/ppermute | solution.py:733
  512.2 135.6 %reduce-scatter.7.cloned.1.call-start = ((), (), s32[]{:S(2)}) async-start(), calls=%async_computation.8 | async-start | bytes 1802240 | tf_op jit(solution)/shard_map/reduce_scatter | solution.py:897
  512.3 40.3 %collective-permute-start.41 = (bf16[256,2816]{1,0:T(8,128)(2,1)}, bf16[256,2816]{1,0:T(8,128)(2,1)S(1)}, u32[]{:S(2)}, u32[]{:S(2)}) collective-permute-start(bf16[256,2816]{1,0:T(8,128)(2,1)} %fusion.14), channel_id=1, source_target_pairs={{0,8},{4,12},{8,0},{12,4},{1,9},{5,13},{9,1},{13,5},{2,10},{6,14},... | collective-permute-start | bytes 4325384 | tf_op jit(solution)/shard_map/ppermute | solution.py:733
  535.2 49.6 %collective-permute-start.45 = (bf16[256,2816]{1,0:T(8,128)(2,1)}, bf16[256,2816]{1,0:T(8,128)(2,1)}, u32[]{:S(2)}, u32[]{:S(2)}) collective-permute-start(bf16[256,2816]{1,0:T(8,128)(2,1)} %fusion.13), channel_id=1, source_target_pairs={{0,8},{4,12},{8,0},{12,4},{1,9},{5,13},{9,1},{13,5},{2,10},{6,14},... | collective-permute-start | bytes 4325384 | tf_op jit(solution)/shard_map/ppermute | solution.py:733
  556.1 123.2 %reduce-scatter.9.cloned.1.call-start = ((), (), s32[]{:S(2)}) async-start(), calls=%async_computation.9 | async-start | bytes 1802240 | tf_op jit(solution)/shard_map/reduce_scatter | solution.py:897
  601.5 93.2 %reduce-scatter.11.cloned.1.call-start = ((), (), s32[]{:S(2)}) async-start(), calls=%async_computation.10 | async-start | bytes 1802240 | tf_op jit(solution)/shard_map/reduce_scatter | solution.py:897
  601.6 34.8 %collective-permute-start.49 = (bf16[704,1024]{1,0:T(8,128)(2,1)}, bf16[704,1024]{1,0:T(8,128)(2,1)}, u32[]{:S(2)}, u32[]{:S(2)}) collective-permute-start(bf16[704,1024]{1,0:T(8,128)(2,1)} %fusion.11), channel_id=1, source_target_pairs={{0,8},{4,12},{8,0},{12,4},{1,9},{5,13},{9,1},{13,5},{2,10},{6,14},... | collective-permute-start | bytes 4325384 | tf_op jit(solution)/shard_map/ppermute | solution.py:733
  609.9 34.4 %collective-permute-start.47 = (bf16[64,3200]{1,0:T(8,128)(2,1)}, bf16[64,3200]{1,0:T(8,128)(2,1)}, u32[]{:S(2)}, u32[]{:S(2)}) collective-permute-start(bf16[64,3200]{1,0:T(8,128)(2,1)} %fusion.23), channel_id=1, source_target_pairs={{0,8},{4,12},{8,0},{12,4},{1,9},{5,13},{9,1},{13,5},{2,10},{6,14},... | collective-permute-start | bytes 1228808 | tf_op jit(solution)/shard_map/ppermute | solution.py:733
  647.9 22.7 %collective-permute-start.48 = (bf16[64,3200]{1,0:T(8,128)(2,1)}, bf16[64,3200]{1,0:T(8,128)(2,1)}, u32[]{:S(2)}, u32[]{:S(2)}) collective-permute-start(bf16[64,3200]{1,0:T(8,128)(2,1)} %get-tuple-element.266), channel_id=1, source_target_pairs={{0,1},{1,2},{2,3},{3,0},{4,5},{5,6},{6,7},{7,4},{8,9},{9,10},{10,1... | collective-permute-start | bytes 1228808 | tf_op jit(solution)/shard_map/ppermute | solution.py:733
  (80 other events, 684.8 us)
Sparse Core Ops, SparseCore 0:
  9.6 44.0 all-gather.3
  55.2 50.2 all-gather.5
  107.1 33.1 all-gather.7
  512.4 26.2 reduce-scatter.4
  556.2 32.5 reduce-scatter.6
  601.6 32.5 reduce-scatter.8
  640.9 41.1 reduce-scatter.10

commit v5 on v4

--- a/solution.py
+++ b/solution.py
@@ -105,13 +105,16 @@
 def slot_call(kernel, grid, scalars, ins, in_specs, kept, fresh, store, slots, moment, scratch=(), cost=None):
     aliases, extra = {}, []
     outs, out_specs = [], []
-    for name, shape, block, index, kind in kept:
+    for name, shape, block, index, kind, *own in kept:
+        slot = own[0] if own else moment
         outs.append(jax.ShapeDtypeStruct((slots,) + shape, kind))
         if block is None:
             out_specs.append(pl.BlockSpec(memory_space=pl.ANY))
         else:
             out_specs.append(
-                pl.BlockSpec((None,) + block, lambda j, s, index=index: (moment,) + index(j))
+                pl.BlockSpec(
+                    (None,) + block, lambda j, s, index=index, slot=slot: (slot,) + index(j)
+                )
             )
         if name in store:
             aliases[1 + len(ins) + len(extra)] = len(outs) - 1
@@ -354,7 +357,105 @@
         feed.run(two_out[...], total, result)
 
 
-def attend(store, slots, moment, scalars, kv, low, high, bias, params):
+def attend_feed_back_kernel(
+    moment, steps, extras, idx, q, kv, low, high, bias, wo, source, gain, wg, wu, wd, *rest
+):
+    arrived, own, packed = rest[:3]
+    older = rest[3 : 3 + extras]
+    k_out, v_out, mixed_out, lse_out, res_out, two_out = rest[3 + extras : 9 + extras]
+    outs, g_out = rest[9 + extras : 12 + extras], rest[12 + extras]
+    grad_outs = rest[13 + extras : 15 + extras]
+    branch_out, gain_out, result, grad_out, grad_mixed = rest[15 + extras : 20 + extras]
+    total, held, sems = rest[20 + extras], rest[21 + extras : 27 + extras], rest[27 + extras]
+    gate_back, up_back, res_back, dg_all, du_all, g_arrived, g_own, wo_all, more = rest[28 + extras :]
+    feed = Feed(moment, (wg, wu, wd), outs, held, sems)
+    taken = idx[1]
+    shard = wo_all.shape[1]
+    fixed = [
+        (arrived, g_arrived),
+        (own, g_own),
+        (packed.at[:, pl.ds(3 * shard, shard)], wo_all),
+    ]
+    kept = [
+        (older[6].at[taken], gate_back),
+        (older[7].at[taken], up_back),
+        (older[4].at[taken], res_back),
+    ]
+
+    def copy(number):
+        here, there = (fixed + kept)[number]
+        return pltpu.make_async_copy(here, there, more.at[number])
+
+    @pl.when(pl.program_id(0) == 0)
+    def _():
+        feed.start()
+        for number in range(3):
+            copy(number).start()
+
+        @pl.when(taken != moment)
+        def _():
+            for number in range(3, 6):
+                copy(number).start()
+
+    parts = (q, kv, low, high, bias, wo, k_out, v_out, mixed_out, lse_out)
+    attend_steps(parts, source, gain, res_out, two_out, total, steps)
+
+    @pl.when(pl.program_id(0) == steps)
+    def _():
+        feed.run(two_out[...], total, result)
+
+        @pl.when(taken != moment)
+        def _():
+            for number in range(3, 6):
+                copy(number).wait()
+
+        @pl.when(taken == moment)
+        def _():
+            gate_back[...] = held[3][...]
+            up_back[...] = held[4][...]
+            res_back[...] = res_out[...]
+
+        for number in range(3):
+            copy(number).wait()
+        grads = jnp.where(
+            idx[0] == 1, g_arrived[...].astype(jnp.float32), g_own[...].astype(jnp.float32)
+        ).astype(jnp.bfloat16)
+        g_out[...] = grads
+        gate_w, up_w, down_w = held[:3]
+        stores = []
+        for number, (start, size) in enumerate(feed.tiles):
+            lanes = slice(start, start + size)
+            grad_gate, grad_up = feed_grads(
+                nt_dot(grads, down_w[lanes]), gate_back[:, lanes], up_back[:, lanes]
+            )
+            for part, (value, all_of) in enumerate(((grad_gate, dg_all), (grad_up, du_all))):
+                all_of[:, lanes] = value
+                store = pltpu.make_async_copy(
+                    all_of.at[:, pl.ds(start, size)],
+                    grad_outs[part].at[moment - 1, :, pl.ds(start, size)],
+                    more.at[6 + 2 * number + part],
+                )
+                store.start()
+                stores.append(store)
+            part = nt_dot(grad_gate, gate_w[:, lanes]) + nt_dot(grad_up, up_w[:, lanes])
+            if number:
+                total[...] += part
+            else:
+                total[...] = part
+        pulled, grad_gain = norm_back(
+            total[...], res_back[...], gain[...].astype(jnp.float32)
+        )
+        gain_out[...] = jnp.broadcast_to(grad_gain, gain_out.shape)
+        grad_residual = grads.astype(jnp.float32) + pulled
+        grad_out[...] = grad_residual
+        branch = grad_residual.astype(jnp.bfloat16)
+        branch_out[...] = branch
+        grad_mixed[...] = nt_dot(branch, flat(wo_all)).astype(jnp.bfloat16)
+        for store in stores:
+            store.wait()
+
+
+def attend(store, slots, moment, scalars, kv, low, high, bias, params, back=None):
     rows, width = kv.shape[1:]
     packed, gain_two = params[1:3]
     weights = params[3:]
@@ -367,11 +468,38 @@
     halo_spec = pl.BlockSpec((2, HALO, WIDE), lambda j, s: (0, 0, last(j)))
     fed = feed_parts(rows, width, weights) if weights else ([], [], [], 0)
     kernel = functools.partial(attend_feed_kernel, moment) if weights else attend_kernel
+    kernel = functools.partial(kernel, quads)
+    back_ins, kept, fresh, scratch = [], [], [], []
+    if back is not None:
+        back_ins = [*back, packed]
+        hidden = weights[0].shape[1]
+        kept = [
+            ("grad_result", (rows, width), (rows, width), at_start, jnp.bfloat16, moment - 1),
+            ("grad_gate", (rows, hidden), None, None, jnp.bfloat16),
+            ("grad_up", (rows, hidden), None, None, jnp.bfloat16),
+            ("grad_branch", (rows, width), (rows, width), at_start, jnp.bfloat16, moment - 1),
+            ("gain_two", (8, width), (8, width), at_start, jnp.float32, moment - 1),
+        ]
+        fresh = [
+            ((rows, width), jnp.float32, whole_spec((rows, width))),
+            ((rows, width), jnp.bfloat16, whole_spec((rows, width))),
+        ]
+        scratch = (
+            [pltpu.VMEM((rows, hidden), jnp.bfloat16)] * 2
+            + [pltpu.VMEM((rows, width), jnp.float32)]
+            + [pltpu.VMEM((rows, hidden), jnp.bfloat16)] * 2
+            + [pltpu.VMEM((rows, width), jnp.bfloat16)] * 2
+            + [pltpu.VMEM((packed.shape[0], shard, width), jnp.bfloat16)]
+            + [pltpu.SemaphoreType.DMA((6 + 2 * len(chunks(hidden, wide_tile(hidden))),))]
+        )
+        extras = 9 + sum(entry[0] in store for entry in kept)
+        kernel = functools.partial(attend_feed_back_kernel, moment, quads, extras)
     return slot_call(
-        functools.partial(kernel, quads),
+        kernel,
         (quads + (1 if weights else 0),),
         scalars,
-        [store["queries"], kv, low, high, bias, packed, store["source"], gain_two, *weights],
+        [store["queries"], kv, low, high, bias, packed, store["source"], gain_two]
+        + [*weights, *back_ins],
         [
             pl.BlockSpec((None, rows, WIDE), lambda j, s: (moment, 0, last(j))),
             pl.BlockSpec((2, rows, WIDE), lambda j, s: (0, 0, last(j))),
@@ -382,7 +510,7 @@
             pl.BlockSpec((None, rows, width), lambda j, s: (moment, 0, 0)),
             whole_spec((1, width)),
         ]
-        + [pl.BlockSpec(memory_space=pl.ANY)] * len(weights),
+        + [pl.BlockSpec(memory_space=pl.ANY)] * (len(weights) + len(back_ins)),
         [
             ("keys", (ext, width), (ext, WIDE), at_tile, jnp.bfloat16),
             ("values", (ext, width), (ext, WIDE), at_tile, jnp.bfloat16),
@@ -391,12 +519,13 @@
             ("residual", (rows, width), (rows, width), at_start, jnp.float32),
             ("normed_two", (rows, width), (rows, width), at_start, jnp.bfloat16),
         ]
-        + fed[0],
-        fed[1],
+        + fed[0]
+        + kept,
+        fed[1] + fresh,
         store,
         slots,
         moment,
-        [pltpu.VMEM((rows, width), jnp.float32)] + fed[2],
+        [pltpu.VMEM((rows, width), jnp.float32)] + fed[2] + scratch,
         cost_of(
             width * rows * ((BLOCK + 2 * HALO) * 8 + width * 2) + fed[3],
             2 * width * width + 20 * rows * width + fed[3] // rows,
@@ -444,6 +573,16 @@
     return 0.5 * (1.0 + bend), bend, root
 
 
+def feed_grads(grad_gated, gate, up):
+    gate, up = gate.astype(jnp.float32), up.astype(jnp.float32)
+    half, bend, root = gelu_parts(gate)
+    slope = half + 0.5 * gate * (1.0 - bend * bend) * root * (1.0 + 3.0 * 0.044715 * gate * gate)
+    return (
+        (grad_gated * up * slope).astype(jnp.bfloat16),
+        (grad_gated * gate * half).astype(jnp.bfloat16),
+    )
+
+
 def feed_back_kernel(idx, arrived, own, gate, up, residual, gain, wd, wg, wu, wo, *rest):
     g_out, dg_out, du_out, branch_out, gain_out, res_out, mixed_out, total = rest[-8:]
     step = pl.program_id(0)
@@ -454,15 +593,8 @@
             idx[0] == 1, arrived[...].astype(jnp.float32), own[...].astype(jnp.float32)
         ).astype(jnp.bfloat16)
 
-    gate_pre = gate[...].astype(jnp.float32)
-    up_pre = up[...].astype(jnp.float32)
     grad_gated = nt_dot(g_out[...], wd[...])
-    half, bend, root = gelu_parts(gate_pre)
-    slope = half + 0.5 * gate_pre * (1.0 - bend * bend) * root * (
-        1.0 + 3.0 * 0.044715 * gate_pre * gate_pre
-    )
-    grad_gate = (grad_gated * up_pre * slope).astype(jnp.bfloat16)
-    grad_up = (grad_gated * gate_pre * half).astype(jnp.bfloat16)
+    grad_gate, grad_up = feed_grads(grad_gated, gate[...], up[...])
     dg_out[...] = grad_gate
     du_out[...] = grad_up
     part = nt_dot(grad_gate, wg[...]) + nt_dot(grad_up, wu[...])
@@ -978,9 +1110,13 @@
     arrived = [jnp.zeros((rows_local, model_width), jnp.bfloat16)]
     arrived_grad = [arrived[0]]
 
+    def taken_slot(moment):
+        return choose(max(moment - 1, 0), min(moment + 1, micro_count))
+
     def forward(moment, params):
         early, late = min(moment, micro_count - 1), max(moment - 1, 0)
-        scalars = jnp.stack([is_first, is_first * 0 + moment, choose(early, late)])
+        scalars = jnp.stack([is_first, taken_slot(moment - 1), choose(early, late)])
+        started = None
         layer_in = after(arrived[moment], *grad_sources[-1:])
         kv, tail, head = project(store, slots, moment, scalars, inputs[early], layer_in, params)
         low = shifted(tail, "seq", 1)
@@ -997,11 +1133,14 @@
             params = params + (gate_w, up_w, down_w)
             (result,) = feed(store, slots, moment, scalars, params)
         else:
-            (result,) = attend(store, slots, moment, scalars, kv, low, high, bias, params)
+            back = (arrived_grad[moment - 1], cotangent[min(moment - 1, micro_count - 1)])
+            result, *started = attend(
+                store, slots, moment, scalars, kv, low, high, bias, params, back
+            )
         results.append(result)
         if moment < micro_count:
             arrived.append(shifted(result, "section", 1))
-        return params
+        return params, started
 
     def both(name, start):
         chosen = lax.dynamic_slice_in_dim(store[name], start, micro_count, 0)
@@ -1013,12 +1152,12 @@
             left.T, both(right, is_first), preferred_element_type=jnp.float32
         ).astype(jnp.bfloat16)
 
-    def backward(moment):
+    def backward(moment, started=None):
         early, late = min(moment, micro_count - 1), max(moment - 1, 0)
         scalars = jnp.stack(
-            [is_first, choose(late, min(moment + 1, micro_count)), choose(late, early)]
-        )
-        grad_res, grad_mixed = feed_back(
+            [is_first, taken_slot(moment), choose(late, early)]
+        )
+        grad_res, grad_mixed = started or feed_back(
             store, slots, moment, scalars, arrived_grad[moment], cotangent[early], params
         )
         if moment == micro_count:
@@ -1049,10 +1188,10 @@
         if moment < micro_count:
             arrived_grad.append(shifted(grad_source, "section", -1))
 
-    params = forward(0, params)
+    params, _ = forward(0, params)
     for moment in range(1, slots):
-        forward(moment, params)
-        backward(moment - 1)
+        _, started = forward(moment, params)
+        backward(moment - 1, started)
     backward(micro_count)
 
     activations = jnp.stack(

time: 721 us -> 710 us (0.985)
  Pallas kernels: 221 us -> 209 us
    pallas_call x16 -> x14, Pallas kernels: 206 us -> 194 us  [call(): pl.pallas_call(kernel, out_shape=outs, grid_spec=pltpu.PrefetchScalarGrid...]
    unnamed x103 -> x101, local copies, waits for them, and re-layouts: 26.4 us -> 25.6 us
  transfers between devices with their start and end apart: 63 -> 63, of which waited for: 29 -> 29; matrix products, arithmetic and copies ran while one was open for 15% -> 16% of each run, Pallas kernels for 12% -> 10%
where the time goes in v5:
time: 710 us; the launch traced here: 705 us
  waiting for transfers between devices  230 us (32%)
  Pallas kernels  209 us (29%)
  starting transfers between devices  106 us (15%)
  other arithmetic  58.1 us (8%)
  local copies, waits for them, and re-layouts  58 us (8%)
  matrix products  27 us (4%)
  between operations  15.2 us (2%)
    pallas_call x14, Pallas kernels, call(): pl.pallas_call(kernel, out_shape=outs, grid_spec=pltpu.PrefetchScalarGrid...  194 us
    ppermute x40, waiting for transfers between devices, __call__(): self.sent.append(lax.ppermute(cells, self.axis, self.pairs))  186 us
    ppermute x40, starting transfers between devices, __call__(): self.sent.append(lax.ppermute(cells, self.axis, self.pairs))  59.8 us
    ppermute x16, starting transfers between devices, shifted(): return lax.ppermute(shard, axis, pairs)  46.1 us
    ppermute x16, waiting for transfers between devices, shifted(): return lax.ppermute(shard, axis, pairs)  38.2 us
    convert_element_type x11, other arithmetic, plus(): return (left.astype(jnp.float32) + right.astype(jnp.float32)).astype(kind)  33 us
    unnamed x101, local copies, waits for them, and re-layouts  25.6 us
    dot_general x4, matrix products, product(): jnp.dot(left.T, both(right, is_first), preferred_element_type=jnp.float32)  21.2 us
  transfers between devices with their start and end apart: 63, of which 29 were waited for; matrix products, arithmetic and copies ran while one was open for 16% of the time, Pallas kernels for 10%

profile of v5, /device:TPU:0, one launch (start us, length us, event | category | flops | bytes accessed | tf_op | source)
XLA Modules:
  0.0 704.5 jit_solution(17236788126857507297)
XLA Ops:
  15.5 21.0 %collective-permute-done.3.refs_4_ = bf16[272,1024]{1,0:T(8,128)(2,1)S(1)} collective-permute-done((bf16[272,1024]{1,0:T(8,128)(2,1)S(1)}, bf16[272,1024]{1,0:T(8,128)(2,1)S(1)}, u32[]{:S(2)}, u32[]{:S(2)}) %collective-permute-start.3) | collective-permute-done | bytes 557088 | tf_op jit(solution)/shard_map/ppermute | solution.py:865
  38.3 10.3 %collective-permute-done.5.refs_6_ = bf16[272,1024]{1,0:T(8,128)(2,1)S(1)} collective-permute-done((bf16[272,1024]{1,0:T(8,128)(2,1)S(1)}, bf16[272,1024]{1,0:T(8,128)(2,1)S(1)}, u32[]{:S(2)}, u32[]{:S(2)}) %collective-permute-start.5) | collective-permute-done | bytes 557088 | tf_op jit(solution)/shard_map/ppermute | solution.py:865
  55.7 21.3 %collective-permute-done.7.refs_8_ = bf16[272,1024]{1,0:T(8,128)(2,1)S(1)} collective-permute-done((bf16[272,1024]{1,0:T(8,128)(2,1)S(1)}, bf16[272,1024]{1,0:T(8,128)(2,1)S(1)}, u32[]{:S(2)}, u32[]{:S(2)}) %collective-permute-start.7) | collective-permute-done | bytes 557088 | tf_op jit(solution)/shard_map/ppermute | solution.py:865
  80.8 18.5 %collective-permute-done.1.refs_2_ = bf16[272,1024]{1,0:T(8,128)(2,1)S(1)} collective-permute-done((bf16[272,1024]{1,0:T(8,128)(2,1)S(1)}, bf16[272,1024]{1,0:T(8,128)(2,1)S(1)}, u32[]{:S(2)}, u32[]{:S(2)}) %collective-permute-start.1) | collective-permute-done | bytes 557088 | tf_op jit(solution)/shard_map/ppermute | solution.py:865
  99.3 7.1 %collective-permute-done.11.refs_12_ = bf16[272,1024]{1,0:T(8,128)(2,1)S(1)} collective-permute-done((bf16[272,1024]{1,0:T(8,128)(2,1)S(1)}, bf16[272,1024]{1,0:T(8,128)(2,1)S(1)}, u32[]{:S(2)}, u32[]{:S(2)}) %collective-permute-start.11) | collective-permute-done | bytes 557088 | tf_op jit(solution)/shard_map/ppermute | solution.py:865
  110.6 9.8 %collective-permute-done.9.refs_10_ = bf16[272,1024]{1,0:T(8,128)(2,1)} collective-permute-done((bf16[272,1024]{1,0:T(8,128)(2,1)S(1)}, bf16[272,1024]{1,0:T(8,128)(2,1)}, u32[]{:S(2)}, u32[]{:S(2)}) %collective-permute-start.9) | collective-permute-done | bytes 557088 | tf_op jit(solution)/shard_map/ppermute | solution.py:865
  140.8 7.7 %shard_map.204 = (bf16[3,320,1024]{2,1,0:T(8,128)(2,1)}, bf16[3,320,1024]{2,1,0:T(8,128)(2,1)}, bf16[3,320,1024]{2,1,0:T(8,128)(2,1)}, bf16[2,320,1024]{2,1,0:T(...) custom-call(s32[3]{0:T(128)} %stack.53.idx, bf16[320,1024]{1,0:T(8,128)(2,1)} %get-tuple-element.269.own, ...), custom_call_target="tpu_custom_call" | custom-call | flops 2013265920 | bytes 10878976 | tf_op jit(solution)/shard_map/pallas_call | solution.py:30
  173.1 10.3 %shard_map.205 = (bf16[3,576,1024]{2,1,0:T(8,128)(2,1)}, bf16[3,576,1024]{2,1,0:T(8,128)(2,1)}, bf16[3,320,1024]{2,1,0:T(8,128)(2,1)}, f32[3,320,512]{2,1,0:T(8,...) custom-call(s32[3]{0:T(128)} %stack.53.idx, bf16[3,320,1024]{2,1,0:T(8,128)(2,1)} %get-tuple-element.136.q.rest_2_, ...), custom_call_target="tpu_custom_call" | custom-call | flops 1677721600 | bytes 8650752 | tf_op jit(solution)/shard_map/pallas_call | solution.py:30
  208.9 12.7 %shard_map.209 = (bf16[3,320,2816]{2,1,0:T(8,128)(2,1)}, bf16[3,320,2816]{2,1,0:T(8,128)(2,1)}, bf16[3,320,2816]{2,1,0:T(8,128)(2,1)}, bf16[320,1024]{1,0:T(8,128)(2,1)}) custom-call(s32[3]{0:T(128)} %stack.53.idx, bf16[3,320,1024]{2,1,0:T(8,128)(2,1)} %get-tuple-element.143.two.rest_8_, f32[3,320,1024]{2,1,0:T(8,128)} %get-tuple-element.144.residual.rest_7_, ...), custom_call_target="tpu_custom_call" | custom-call | flops 5536481280 | bytes 20578304 | tf_op jit(solution)/shard_map/pallas_call | solution.py:30
  225.6 14.0 %collective-permute-done.26.arrived = bf16[320,1024]{1,0:T(8,128)(2,1)S(1)} collective-permute-done((bf16[320,1024]{1,0:T(8,128)(2,1)}, bf16[320,1024]{1,0:T(8,128)(2,1)S(1)}, u32[]{:S(2)}, u32[]{:S(2)}) %collective-permute-start.26) | collective-permute-done | bytes 655392 | tf_op jit(solution)/shard_map/ppermute | solution.py:20
  240.4 7.7 %shard_map.210 = (bf16[3,320,1024]{2,1,0:T(8,128)(2,1)}, bf16[3,320,1024]{2,1,0:T(8,128)(2,1)}, bf16[3,320,1024]{2,1,0:T(8,128)(2,1)}, bf16[2,320,1024]{2,1,0:T(...) custom-call(s32[3]{0:T(128)} %pad_add_fusion.2.idx, ...), custom_call_target="tpu_custom_call", output_to_operand_aliasing={{0}: (7, {}), {1}: (8, {}), {2}: (9, {})} | custom-call | flops 2013265920 | bytes 10878976 | tf_op jit(solution)/shard_map/pallas_call | solution.py:30
  256.2 34.5 %shard_map.211 = (bf16[3,576,1024]{2,1,0:T(8,128)(2,1)}, bf16[3,576,1024]{2,1,0:T(8,128)(2,1)}, bf16[3,320,1024]{2,1,0:T(8,128)(2,1)}, f32[3,320,512]{2,1,0:T(8,...) custom-call(s32[3]{0:T(128)} %pad_add_fusion.2.idx, ...), custom_call_target="tpu_custom_call", output_to_operand_aliasing={{0}: (15, {}), {1}: (16, {}), {2}: (17, {}), {3}: (18, {}),... | custom-call | flops 7214202880 | bytes 25952256 | tf_op jit(solution)/shard_map/pallas_call | solution.py:30
  290.7 11.2 %shard_map.212 = (bf16[3,320,1024]{2,1,0:T(8,128)(2,1)}, f32[2,320,1024]{2,1,0:T(8,128)}, bf16[2,128,1024]{2,1,0:T(8,128)(2,1)}, bf16[2,128,1024]{2,1,0:T(8,128)(2,1)}) custom-call(s32[3]{0:T(128)} %pad_add_fusion.5.idx, bf16[3,320,1024]{2,1,0:T(8,128)(2,1)} %get-tuple-element.152.q.rest_2_, bf16[3,576,1024]{2,1,0:T(8,128)(2,1)} %get-tuple-element.165.keys.rest_3_, ...), custom_call_target="tpu_custom_call" | custom-call | flops 5033164800 | bytes 7864320 | tf_op jit(solution)/shard_map/pallas_call | solution.py:30
  301.9 9.1 %collective-permute-start.30 = (bf16[2,128,1024]{2,1,0:T(8,128)(2,1)}, bf16[2,128,1024]{2,1,0:T(8,128)(2,1)S(1)}, u32[]{:S(2)}, u32[]{:S(2)}) collective-permute-start(bf16[2,128,1024]{2,1,0:T(8,128)(2,1)} %get-tuple-element.172), channel_id=1, source_target_pairs={{0,4},{4,8},{8,12},{1,5},{5,9},{9,13},{2,6},{6,10},{10,14},{3,7},{... | collective-permute-start | bytes 1572872 | tf_op jit(solution)/shard_map/ppermute | solution.py:20
  317.2 9.4 %shard_map.213 = (bf16[3,320,1024]{2,1,0:T(8,128)(2,1)}, bf16[3,320,1024]{2,1,0:T(8,128)(2,1)}, f32[3,8,1024]{2,1,0:T(8,128)}, bf16[320,1024]{1,0:T(8,128)(2,1)}) custom-call(s32[3]{0:T(128)} %pad_add_fusion.5.idx, bf16[3,320,1024]{2,1,0:T(8,128)(2,1)} %get-tuple-element.170.grad_q.rest_0_, f32[2,320,1024]{2,1,0:T(8,128)} %get-tuple-element.171.center, ...), custom_call_target="tpu_custom_call" | custom-call | flops 2013265920 | bytes 12845056 | tf_op jit(solution)/shard_map/pallas_call | solution.py:30
  331.3 7.5 %shard_map.214 = (bf16[3,320,1024]{2,1,0:T(8,128)(2,1)}, bf16[3,320,1024]{2,1,0:T(8,128)(2,1)}, bf16[3,320,1024]{2,1,0:T(8,128)(2,1)}, bf16[2,320,1024]{2,1,0:T(...) custom-call(s32[3]{0:T(128)} %pad_add_fusion.1.idx, ...), custom_call_target="tpu_custom_call", output_to_operand_aliasing={{0}: (7, {}), {1}: (8, {}), {2}: (9, {})} | custom-call | flops 2013265920 | bytes 10878976 | tf_op jit(solution)/shard_map/pallas_call | solution.py:30
  348.5 34.3 %shard_map.215 = (bf16[3,576,1024]{2,1,0:T(8,128)(2,1)}, bf16[3,576,1024]{2,1,0:T(8,128)(2,1)}, bf16[3,320,1024]{2,1,0:T(8,128)(2,1)}, f32[3,320,512]{2,1,0:T(8,...) custom-call(s32[3]{0:T(128)} %pad_add_fusion.1.idx, ...), custom_call_target="tpu_custom_call", output_to_operand_aliasing={{0}: (15, {}), {1}: (16, {}), {2}: (17, {}), {3}: (18, {}),... | custom-call | flops 7214202880 | bytes 25952256 | tf_op jit(solution)/shard_map/pallas_call | solution.py:30
  382.8 11.1 %shard_map.216 = (bf16[3,320,1024]{2,1,0:T(8,128)(2,1)}, f32[2,320,1024]{2,1,0:T(8,128)}, bf16[2,128,1024]{2,1,0:T(8,128)(2,1)}, bf16[2,128,1024]{2,1,0:T(8,128)(2,1)}) custom-call(s32[3]{0:T(128)} %pad_add_fusion.6.idx, bf16[3,320,1024]{2,1,0:T(8,128)(2,1)} %get-tuple-element.178.q, ...), custom_call_target="tpu_custom_call", output_to_operand_aliasing={{0}: (8, {})} | custom-call | flops 5033164800 | bytes 7864320 | tf_op jit(solution)/shard_map/pallas_call | solution.py:30
  393.9 8.6 %collective-permute-start.35 = (bf16[2,128,1024]{2,1,0:T(8,128)(2,1)}, bf16[2,128,1024]{2,1,0:T(8,128)(2,1)S(1)}, u32[]{:S(2)}, u32[]{:S(2)}) collective-permute-start(bf16[2,128,1024]{2,1,0:T(8,128)(2,1)} %get-tuple-element.201), channel_id=1, source_target_pairs={{0,4},{4,8},{8,12},{1,5},{5,9},{9,13},{2,6},{6,10},{10,14},{3,7},{... | collective-permute-start | bytes 1572872 | tf_op jit(solution)/shard_map/ppermute | solution.py:20
  407.3 9.4 %shard_map.217 = (bf16[3,320,1024]{2,1,0:T(8,128)(2,1)}, bf16[3,320,1024]{2,1,0:T(8,128)(2,1)}, f32[3,8,1024]{2,1,0:T(8,128)}, bf16[320,1024]{1,0:T(8,128)(2,1)}) custom-call(s32[3]{0:T(128)} %pad_add_fusion.6.idx, bf16[3,320,1024]{2,1,0:T(8,128)(2,1)} %get-tuple-element.199.grad_q.rest_0_, ...), custom_call_target="tpu_custom_call", output_to_operand_aliasing={{0}: (11, {}), {1}: (12, {}), {2}: (13, {})} | custom-call | flops 2013265920 | bytes 12845056 | tf_op jit(solution)/shard_map/pallas_call | solution.py:30
  420.3 10.4 %collective-permute-done.37.arrived = bf16[320,1024]{1,0:T(8,128)(2,1)S(1)} collective-permute-done((bf16[320,1024]{1,0:T(8,128)(2,1)}, bf16[320,1024]{1,0:T(8,128)(2,1)S(1)}, u32[]{:S(2)}, u32[]{:S(2)}) %collective-permute-start.37) | collective-permute-done | bytes 655392 | tf_op jit(solution)/shard_map/ppermute | solution.py:20
  431.5 17.3 %shard_map.218 = (bf16[3,320,1024]{2,1,0:T(8,128)(2,1)}, bf16[3,320,2816]{2,1,0:T(8,128)(2,1)}, bf16[3,320,2816]{2,1,0:T(8,128)(2,1)}, bf16[3,320,1024]{2,1,0:T(...) custom-call(s32[3]{0:T(128)} %pad_add_fusion.idx, ...), custom_call_target="tpu_custom_call", output_to_operand_aliasing={{0}: (11, {}), {1}: (12, {}), {2}: (13, {}), {3}: (14, {}),... | custom-call | flops 6207569920 | bytes 17301504 | tf_op jit(solution)/shard_map/pallas_call | solution.py:30
  448.8 7.0 bitcast_convert_fusion
  490.3 7.1 %convolution_convert_fusion.1 = bf16[2816,1024]{1,0:T(8,128)(2,1)S(1)} fusion(bf16[640,2816]{1,0:T(8,128)(2,1)} %bitcast.278, bf16[640,1024]{1,0:T(8,128)(2,1)} %bitcast.282), kind=kOutput, calls=%fused_computation.6 | convolution fusion | flops 3693871104 | bytes 10682368 | tf_op jit(solution)/shard_map/dot_general | solution.py:1151
  505.0 11.2 %shard_map.219 = (bf16[3,320,1024]{2,1,0:T(8,128)(2,1)}, f32[2,320,1024]{2,1,0:T(8,128)}, bf16[2,128,1024]{2,1,0:T(8,128)(2,1)}, bf16[2,128,1024]{2,1,0:T(8,128)(2,1)}) custom-call(s32[3]{0:T(128)} %pad_add_fusion.idx, bf16[3,320,1024]{2,1,0:T(8,128)(2,1)} %get-tuple-element.178.q, ...), custom_call_target="tpu_custom_call", output_to_operand_aliasing={{0}: (8, {})} | custom-call | flops 5033164800 | bytes 7864320 | tf_op jit(solution)/shard_map/pallas_call | solution.py:30
  523.8 17.4 %collective-permute-start.45 = (bf16[256,2816]{1,0:T(8,128)(2,1)}, bf16[256,2816]{1,0:T(8,128)(2,1)}, u32[]{:S(2)}, u32[]{:S(2)}) collective-permute-start(bf16[256,2816]{1,0:T(8,128)(2,1)} %fusion.13), channel_id=1, source_target_pairs={{0,8},{4,12},{8,0},{12,4},{1,9},{5,13},{9,1},{13,5},{2,10},{6,14},... | collective-permute-start | bytes 4325384 | tf_op jit(solution)/shard_map/ppermute | solution.py:865
  548.3 9.8 %shard_map.220 = (bf16[3,320,1024]{2,1,0:T(8,128)(2,1)}, bf16[3,320,1024]{2,1,0:T(8,128)(2,1)}, f32[3,8,1024]{2,1,0:T(8,128)}, bf16[320,1024]{1,0:T(8,128)(2,1)}) custom-call(s32[3]{0:T(128)} %pad_add_fusion.idx, bf16[3,320,1024]{2,1,0:T(8,128)(2,1)} %get-tuple-element.228.grad_q, ...), custom_call_target="tpu_custom_call", output_to_operand_aliasing={{0}: (11, {}), {1}: (12, {}), {2}: (13, {})} | custom-call | flops 2013265920 | bytes 12845056 | tf_op jit(solution)/shard_map/pallas_call | solution.py:30
  561.9 11.5 %collective-permute-done.45 = bf16[256,2816]{1,0:T(8,128)(2,1)} collective-permute-done((bf16[256,2816]{1,0:T(8,128)(2,1)}, bf16[256,2816]{1,0:T(8,128)(2,1)}, u32[]{:S(2)}, u32[]{:S(2)}) %collective-permute-start.45) | collective-permute-done | bytes 1441824 | tf_op jit(solution)/shard_map/ppermute | solution.py:865
  601.1 24.0 %collective-permute-done.49 = bf16[704,1024]{1,0:T(8,128)(2,1)} collective-permute-done((bf16[704,1024]{1,0:T(8,128)(2,1)}, bf16[704,1024]{1,0:T(8,128)(2,1)}, u32[]{:S(2)}, u32[]{:S(2)}) %collective-permute-start.49) | collective-permute-done | bytes 1441824 | tf_op jit(solution)/shard_map/ppermute | solution.py:865
  638.4 7.8 %collective-permute-done.50 = bf16[64,3200]{1,0:T(8,128)(2,1)} collective-permute-done((bf16[64,3200]{1,0:T(8,128)(2,1)}, bf16[64,3200]{1,0:T(8,128)(2,1)}, u32[]{:S(2)}, u32[]{:S(2)}) %collective-permute-start.50) | collective-permute-done | bytes 409632 | tf_op jit(solution)/shard_map/ppermute | solution.py:865
  646.2 13.0 %collective-permute-done.48 = bf16[64,3200]{1,0:T(8,128)(2,1)} collective-permute-done((bf16[64,3200]{1,0:T(8,128)(2,1)}, bf16[64,3200]{1,0:T(8,128)(2,1)}, u32[]{:S(2)}, u32[]{:S(2)}) %collective-permute-start.48) | collective-permute-done | bytes 409632 | tf_op jit(solution)/shard_map/ppermute | solution.py:865
  672.3 6.9 collective-permute-done.51
  (295 shorter events, 270.5 us)
Async XLA Ops:
  7.2 46.5 %all-gather.4.cloned.1.call-start = ((), (), s32[]{:S(2)}) async-start(), calls=%async_computation.4 | async-start | bytes 1802240 | tf_op jit(solution)/shard_map/all_gather | solution.py:888
  7.9 118.5 %all-gather.6.cloned.1.call-start = ((), (), s32[]{:S(2)}) async-start(), calls=%async_computation.5 | async-start | bytes 1802240 | tf_op jit(solution)/shard_map/all_gather | solution.py:888
  12.4 24.1 %collective-permute-start.3 = (bf16[272,1024]{1,0:T(8,128)(2,1)S(1)}, bf16[272,1024]{1,0:T(8,128)(2,1)S(1)}, u32[]{:S(2)}, u32[]{:S(2)}) collective-permute-start(bf16[272,1024]{1,0:T(8,128)(2,1)S(1)} %fusion.42.refs_0_), channel_id=1, source_target_pairs={{0,1},{1,2},{2,3},{3,0},{4,5},{5,6},{6,7},{7,4},{8,9},{9,10},{10,1... | collective-permute-start | bytes 1671176 | tf_op jit(solution)/shard_map/ppermute | solution.py:865
  15.4 150.1 %all-gather.8.cloned.1.call-start = ((), (), s32[]{:S(2)}) async-start(), calls=%async_computation.6 | async-start | bytes 1802240 | tf_op jit(solution)/shard_map/all_gather | solution.py:888
  53.6 53.3 %collective-permute-start.13 = (bf16[4,64,2816]{2,1,0:T(8,128)(2,1)}, bf16[4,64,2816]{2,1,0:T(8,128)(2,1)}, u32[]{:S(2)}, u32[]{:S(2)}) collective-permute-start(bf16[4,64,2816]{2,1,0:T(8,128)(2,1)} %all-gather.4.cloned.1.call-done.refs_0_), channel_id=1, source_target_pairs={{0,8},{4,12},{8,0},{12,4},{1,9},{5,13},{9,1},{13,5},{2,10},{6,14},... | collective-permute-start | bytes 4325384 | tf_op jit(solution)/shard_map/ppermute | solution.py:865
  55.2 21.9 %collective-permute-start.7 = (bf16[272,1024]{1,0:T(8,128)(2,1)S(1)}, bf16[272,1024]{1,0:T(8,128)(2,1)S(1)}, u32[]{:S(2)}, u32[]{:S(2)}) collective-permute-start(bf16[272,1024]{1,0:T(8,128)(2,1)S(1)} %collective-permute-done.3.refs_4_), channel_id=1, source_target_pairs={{0,1},{1,2},{2,3},{3,0},{4,5},{5,6},{6,7},{7,4},{8,9},{9,10},{10,1... | collective-permute-start | bytes 1671176 | tf_op jit(solution)/shard_map/ppermute | solution.py:865
  55.2 44.2 %collective-permute-start.1 = (bf16[272,1024]{1,0:T(8,128)(2,1)S(1)}, bf16[272,1024]{1,0:T(8,128)(2,1)S(1)}, u32[]{:S(2)}, u32[]{:S(2)}) collective-permute-start(bf16[272,1024]{1,0:T(8,128)(2,1)S(1)} %fusion.42.refs_0_), channel_id=1, source_target_pairs={{0,8},{4,12},{8,0},{12,4},{1,9},{5,13},{9,1},{13,5},{2,10},{6,14},... | collective-permute-start | bytes 1671176 | tf_op jit(solution)/shard_map/ppermute | solution.py:865
  77.0 29.4 %collective-permute-start.11 = (bf16[272,1024]{1,0:T(8,128)(2,1)S(1)}, bf16[272,1024]{1,0:T(8,128)(2,1)S(1)}, u32[]{:S(2)}, u32[]{:S(2)}) collective-permute-start(bf16[272,1024]{1,0:T(8,128)(2,1)S(1)} %collective-permute-done.7.refs_8_), channel_id=1, source_target_pairs={{0,1},{1,2},{2,3},{3,0},{4,5},{5,6},{6,7},{7,4},{8,9},{9,10},{10,1... | collective-permute-start | bytes 1671176 | tf_op jit(solution)/shard_map/ppermute | solution.py:865
  80.2 28.3 %collective-permute-start = (bf16[272,1024]{1,0:T(8,128)(2,1)S(1)}, bf16[272,1024]{1,0:T(8,128)(2,1)}, u32[]{:S(2)}, u32[]{:S(2)}) collective-permute-start(bf16[272,1024]{1,0:T(8,128)(2,1)S(1)} %fusion.42.refs_0_), channel_id=1, source_target_pairs={{0,4},{4,0},{8,12},{12,8},{1,5},{5,1},{9,13},{13,9},{2,6},{6,2},{1... | collective-permute-start | bytes 1671176 | tf_op jit(solution)/shard_map/ppermute | solution.py:865
  80.2 513.4 %reduce-scatter.5.cloned.1.call-start = ((), (), s32[]{:S(2)}) async-start(), calls=%async_computation.7 | async-start | bytes 1310720 | tf_op jit(solution)/shard_map/reduce_scatter | solution.py:998
  80.3 28.3 %collective-permute-start.4 = (bf16[272,1024]{1,0:T(8,128)(2,1)S(1)}, bf16[272,1024]{1,0:T(8,128)(2,1)S(1)}, u32[]{:S(2)}, u32[]{:S(2)}) collective-permute-start(bf16[272,1024]{1,0:T(8,128)(2,1)S(1)} %collective-permute-done.3.refs_4_), channel_id=1, source_target_pairs={{0,4},{4,0},{8,12},{12,8},{1,5},{5,1},{9,13},{13,9},{2,6},{6,2},{1... | collective-permute-start | bytes 1671176 | tf_op jit(solution)/shard_map/ppermute | solution.py:865
  107.0 19.5 %collective-permute-start.14 = (bf16[272,1024]{1,0:T(8,128)(2,1)S(1)}, bf16[272,1024]{1,0:T(8,128)(2,1)}, u32[]{:S(2)}, u32[]{:S(2)}) collective-permute-start(bf16[272,1024]{1,0:T(8,128)(2,1)S(1)} %collective-permute-done.11.refs_12_), channel_id=1, source_target_pairs={{0,8},{4,12},{8,0},{12,4},{1,9},{5,13},{9,1},{13,5},{2,10},{6,14},... | collective-permute-start | bytes 1671176 | tf_op jit(solution)/shard_map/ppermute | solution.py:865
  109.3 21.8 %collective-permute-start.6 = (bf16[272,1024]{1,0:T(8,128)(2,1)S(1)}, bf16[272,1024]{1,0:T(8,128)(2,1)}, u32[]{:S(2)}, u32[]{:S(2)}) collective-permute-start(bf16[272,1024]{1,0:T(8,128)(2,1)S(1)} %collective-permute-done.5.refs_6_), channel_id=1, source_target_pairs={{0,4},{4,0},{8,12},{12,8},{1,5},{5,1},{9,13},{13,9},{2,6},{6,2},{1... | collective-permute-start | bytes 1671176 | tf_op jit(solution)/shard_map/ppermute | solution.py:865
  110.6 20.5 %collective-permute-start.12 = (bf16[272,1024]{1,0:T(8,128)(2,1)S(1)}, bf16[272,1024]{1,0:T(8,128)(2,1)}, u32[]{:S(2)}, u32[]{:S(2)}) collective-permute-start(bf16[272,1024]{1,0:T(8,128)(2,1)S(1)} %collective-permute-done.11.refs_12_), channel_id=1, source_target_pairs={{0,4},{4,0},{8,12},{12,8},{1,5},{5,1},{9,13},{13,9},{2,6},{6,2},{1... | collective-permute-start | bytes 1671176 | tf_op jit(solution)/shard_map/ppermute | solution.py:865
  126.4 34.3 %collective-permute-start.16 = (bf16[4,64,2816]{2,1,0:T(8,128)(2,1)}, bf16[4,64,2816]{2,1,0:T(8,128)(2,1)}, u32[]{:S(2)}, u32[]{:S(2)}) collective-permute-start(bf16[4,64,2816]{2,1,0:T(8,128)(2,1)} %all-gather.6.cloned.1.call-done.refs_0_), channel_id=1, source_target_pairs={{0,8},{4,12},{8,0},{12,4},{1,9},{5,13},{9,1},{13,5},{2,10},{6,14},... | collective-permute-start | bytes 4325384 | tf_op jit(solution)/shard_map/ppermute | solution.py:865
  152.8 30.7 %collective-permute-start.21 = (bf16[4,64,2816]{2,1,0:T(8,128)(2,1)S(1)}, bf16[4,64,2816]{2,1,0:T(8,128)(2,1)}, u32[]{:S(2)}, u32[]{:S(2)}) collective-permute-start(bf16[4,64,2816]{2,1,0:T(8,128)(2,1)S(1)} %copy-done.4), channel_id=1, source_target_pairs={{0,4},{4,0},{8,12},{12,8},{1,5},{5,1},{9,13},{13,9},{2,6},{6,2},{1... | collective-permute-start | bytes 4325384 | tf_op jit(solution)/shard_map/ppermute | solution.py:865
  154.0 35.3 %collective-permute-start.19 = (bf16[4,64,2816]{2,1,0:T(8,128)(2,1)S(1)}, bf16[4,64,2816]{2,1,0:T(8,128)(2,1)}, u32[]{:S(2)}, u32[]{:S(2)}) collective-permute-start(bf16[4,64,2816]{2,1,0:T(8,128)(2,1)S(1)} %copy-done.3), channel_id=1, source_target_pairs={{0,4},{4,0},{8,12},{12,8},{1,5},{5,1},{9,13},{13,9},{2,6},{6,2},{1... | collective-permute-start | bytes 4325384 | tf_op jit(solution)/shard_map/ppermute | solution.py:865
  160.8 23.0 %collective-permute-start.22 = (bf16[4,64,2816]{2,1,0:T(8,128)(2,1)}, bf16[4,64,2816]{2,1,0:T(8,128)(2,1)}, u32[]{:S(2)}, u32[]{:S(2)}) collective-permute-start(bf16[4,64,2816]{2,1,0:T(8,128)(2,1)} %collective-permute-done.16.refs_2_), channel_id=1, source_target_pairs={{0,4},{4,0},{8,12},{12,8},{1,5},{5,1},{9,13},{13,9},{2,6},{6,2},{1... | collective-permute-start | bytes 4325384 | tf_op jit(solution)/shard_map/ppermute | solution.py:865
  160.8 28.5 %collective-permute-start.20 = (bf16[4,64,2816]{2,1,0:T(8,128)(2,1)}, bf16[4,64,2816]{2,1,0:T(8,128)(2,1)}, u32[]{:S(2)}, u32[]{:S(2)}) collective-permute-start(bf16[4,64,2816]{2,1,0:T(8,128)(2,1)} %collective-permute-done.13.refs_2_), channel_id=1, source_target_pairs={{0,4},{4,0},{8,12},{12,8},{1,5},{5,1},{9,13},{13,9},{2,6},{6,2},{1... | collective-permute-start | bytes 4325384 | tf_op jit(solution)/shard_map/ppermute | solution.py:865
  165.5 34.9 %collective-permute-start.24 = (bf16[4,176,1024]{2,1,0:T(8,128)(2,1)}, bf16[4,176,1024]{2,1,0:T(8,128)(2,1)}, u32[]{:S(2)}, u32[]{:S(2)}) collective-permute-start(bf16[4,176,1024]{2,1,0:T(8,128)(2,1)} %all-gather.8.cloned.1.call-done.refs_0_), channel_id=1, source_target_pairs={{0,8},{4,12},{8,0},{12,4},{1,9},{5,13},{9,1},{13,5},{2,10},{6,14},... | collective-permute-start | bytes 4325384 | tf_op jit(solution)/shard_map/ppermute | solution.py:865
  326.6 20.9 %collective-permute-start.34 = (bf16[320,1024]{1,0:T(8,128)(2,1)}, bf16[320,1024]{1,0:T(8,128)(2,1)S(1)}, u32[]{:S(2)}, u32[]{:S(2)}) collective-permute-start(bf16[320,1024]{1,0:T(8,128)(2,1)} %get-tuple-element.175), channel_id=1, source_target_pairs={{16,0},{17,1},{18,2},{19,3},{20,4},{21,5},{22,6},{23,7},{24,8},{25... | collective-permute-start | bytes 1966088 | tf_op jit(solution)/shard_map/ppermute | solution.py:20
  460.0 27.1 %collective-permute-start.38 = (bf16[2,256,2816]{2,1,0:T(8,128)(2,1)}, bf16[2,256,2816]{2,1,0:T(8,128)(2,1)}, u32[]{:S(2)}, u32[]{:S(2)}) collective-permute-start(bf16[2,256,2816]{2,1,0:T(8,128)(2,1)} %dynamic-slice_bitcast_fusion.3), channel_id=1, source_target_pairs={{0,4},{4,0},{8,12},{12,8},{1,5},{5,1},{9,13},{13,9},{2,6},{6,2},{1... | collective-permute-start | bytes 8650760 | tf_op jit(solution)/shard_map/ppermute | solution.py:865
  479.6 21.6 %collective-permute-start.40 = (bf16[2,256,2816]{2,1,0:T(8,128)(2,1)}, bf16[2,256,2816]{2,1,0:T(8,128)(2,1)S(1)}, u32[]{:S(2)}, u32[]{:S(2)}) collective-permute-start(bf16[2,256,2816]{2,1,0:T(8,128)(2,1)} %dynamic-slice_bitcast_fusion.2), channel_id=1, source_target_pairs={{0,4},{4,0},{8,12},{12,8},{1,5},{5,1},{9,13},{13,9},{2,6},{6,2},{1... | collective-permute-start | bytes 8650760 | tf_op jit(solution)/shard_map/ppermute | solution.py:865
  500.8 44.0 %collective-permute-start.42 = (bf16[2,704,1024]{2,1,0:T(8,128)(2,1)}, bf16[2,704,1024]{2,1,0:T(8,128)(2,1)}, u32[]{:S(2)}, u32[]{:S(2)}) collective-permute-start(bf16[2,704,1024]{2,1,0:T(8,128)(2,1)} %dynamic-slice_bitcast_fusion.1), channel_id=1, source_target_pairs={{0,4},{4,0},{8,12},{12,8},{1,5},{5,1},{9,13},{13,9},{2,6},{6,2},{1... | collective-permute-start | bytes 8650760 | tf_op jit(solution)/shard_map/ppermute | solution.py:865
  500.8 135.7 %reduce-scatter.7.cloned.1.call-start = ((), (), s32[]{:S(2)}) async-start(), calls=%async_computation.8 | async-start | bytes 1802240 | tf_op jit(solution)/shard_map/reduce_scatter | solution.py:1029
  500.9 40.3 %collective-permute-start.41 = (bf16[256,2816]{1,0:T(8,128)(2,1)}, bf16[256,2816]{1,0:T(8,128)(2,1)S(1)}, u32[]{:S(2)}, u32[]{:S(2)}) collective-permute-start(bf16[256,2816]{1,0:T(8,128)(2,1)} %fusion.14), channel_id=1, source_target_pairs={{0,8},{4,12},{8,0},{12,4},{1,9},{5,13},{9,1},{13,5},{2,10},{6,14},... | collective-permute-start | bytes 4325384 | tf_op jit(solution)/shard_map/ppermute | solution.py:865
  523.8 49.7 %collective-permute-start.45 = (bf16[256,2816]{1,0:T(8,128)(2,1)}, bf16[256,2816]{1,0:T(8,128)(2,1)}, u32[]{:S(2)}, u32[]{:S(2)}) collective-permute-start(bf16[256,2816]{1,0:T(8,128)(2,1)} %fusion.13), channel_id=1, source_target_pairs={{0,8},{4,12},{8,0},{12,4},{1,9},{5,13},{9,1},{13,5},{2,10},{6,14},... | collective-permute-start | bytes 4325384 | tf_op jit(solution)/shard_map/ppermute | solution.py:865
  544.7 123.2 %reduce-scatter.9.cloned.1.call-start = ((), (), s32[]{:S(2)}) async-start(), calls=%async_computation.9 | async-start | bytes 1802240 | tf_op jit(solution)/shard_map/reduce_scatter | solution.py:1029
  590.1 93.2 %reduce-scatter.11.cloned.1.call-start = ((), (), s32[]{:S(2)}) async-start(), calls=%async_computation.10 | async-start | bytes 1802240 | tf_op jit(solution)/shard_map/reduce_scatter | solution.py:1029
  590.2 34.8 %collective-permute-start.49 = (bf16[704,1024]{1,0:T(8,128)(2,1)}, bf16[704,1024]{1,0:T(8,128)(2,1)}, u32[]{:S(2)}, u32[]{:S(2)}) collective-permute-start(bf16[704,1024]{1,0:T(8,128)(2,1)} %fusion.11), channel_id=1, source_target_pairs={{0,8},{4,12},{8,0},{12,4},{1,9},{5,13},{9,1},{13,5},{2,10},{6,14},... | collective-permute-start | bytes 4325384 | tf_op jit(solution)/shard_map/ppermute | solution.py:865
  598.5 34.4 %collective-permute-start.47 = (bf16[64,3200]{1,0:T(8,128)(2,1)}, bf16[64,3200]{1,0:T(8,128)(2,1)}, u32[]{:S(2)}, u32[]{:S(2)}) collective-permute-start(bf16[64,3200]{1,0:T(8,128)(2,1)} %fusion.23), channel_id=1, source_target_pairs={{0,8},{4,12},{8,0},{12,4},{1,9},{5,13},{9,1},{13,5},{2,10},{6,14},... | collective-permute-start | bytes 1228808 | tf_op jit(solution)/shard_map/ppermute | solution.py:865
  636.5 22.7 %collective-permute-start.48 = (bf16[64,3200]{1,0:T(8,128)(2,1)}, bf16[64,3200]{1,0:T(8,128)(2,1)}, u32[]{:S(2)}, u32[]{:S(2)}) collective-permute-start(bf16[64,3200]{1,0:T(8,128)(2,1)} %get-tuple-element.266), channel_id=1, source_target_pairs={{0,1},{1,2},{2,3},{3,0},{4,5},{5,6},{6,7},{7,4},{8,9},{9,10},{10,1... | collective-permute-start | bytes 1228808 | tf_op jit(solution)/shard_map/ppermute | solution.py:865
  (79 other events, 671.2 us)
Sparse Core Ops, SparseCore 0:
  9.6 44.0 all-gather.3
  55.2 50.2 all-gather.5
  107.1 33.1 all-gather.7
  501.0 26.2 reduce-scatter.4
  544.8 32.5 reduce-scatter.6
  590.3 32.5 reduce-scatter.8
  629.5 41.1 reduce-scatter.10

commit v6 on v5

--- a/solution.py
+++ b/solution.py
@@ -23,6 +23,7 @@
 HALO = 128
 BLOCK = 128
 WIDE = 256
+BROAD = 512
 NEVER = -1e30
 
 
@@ -146,7 +147,7 @@
 def project(store, slots, moment, scalars, own, arrived, params):
     rows, width = arrived.shape
     gain_one, packed = params[:2]
-    tile = WIDE
+    tile = BROAD
     at_start = lambda j: (0, 0)
     halo_spec = pl.BlockSpec((2, HALO, tile), lambda j, s: (0, 0, j))
     return slot_call(
@@ -800,26 +801,26 @@
     gain_one, packed = params[:2]
     at_tile = lambda j: (0, j)
     at_start = lambda j: (0, 0)
-    halo_spec = pl.BlockSpec((2, HALO, WIDE), lambda j, s: (0, 0, j))
+    halo_spec = pl.BlockSpec((2, HALO, BROAD), lambda j, s: (0, 0, j))
     return slot_call(
         project_back_kernel,
-        (width // WIDE,),
+        (width // BROAD,),
         scalars,
         [store["grad_queries"], center, below, above, store["source"], gain_one, grad_res]
         + [packed] * 3,
         [
-            pl.BlockSpec((None, rows, WIDE), lambda j, s: (moment, 0, j)),
-            pl.BlockSpec((2, rows, WIDE), lambda j, s: (0, 0, j)),
+            pl.BlockSpec((None, rows, BROAD), lambda j, s: (moment, 0, j)),
+            pl.BlockSpec((2, rows, BROAD), lambda j, s: (0, 0, j)),
             halo_spec,
             halo_spec,
             pl.BlockSpec((None, rows, width), lambda j, s: (s[1], 0, 0)),
             whole_spec((1, width)),
             whole_spec((rows, width)),
         ]
-        + [packed_spec(packed, number, WIDE) for number in range(3)],
-        [
-            ("grad_keys", (rows, width), (rows, WIDE), at_tile, jnp.bfloat16),
-            ("grad_values", (rows, width), (rows, WIDE), at_tile, jnp.bfloat16),
+        + [packed_spec(packed, number, BROAD) for number in range(3)],
+        [
+            ("grad_keys", (rows, width), (rows, BROAD), at_tile, jnp.bfloat16),
+            ("grad_values", (rows, width), (rows, BROAD), at_tile, jnp.bfloat16),
             ("gain_one", (8, width), (8, width), at_start, jnp.float32),
         ],
         [((rows, width), jnp.bfloat16, whole_spec((rows, width)))],

time: 710 us -> 707 us (level)
  transfers between devices with their start and end apart: 63 -> 63, of which waited for: 29 -> 29; matrix products, arithmetic and copies ran while one was open for 16% -> 16% of each run, Pallas kernels for 10% -> 9%
where the time goes in v6:
time: 707 us; the launch traced here: 702 us
  waiting for transfers between devices  233 us (33%)
  Pallas kernels  205 us (29%)
  starting transfers between devices  106 us (15%)
  other arithmetic  58.1 us (8%)
  local copies, waits for them, and re-layouts  58 us (8%)
  matrix products  27.3 us (4%)
  between operations  15.1 us (2%)
    pallas_call x14, Pallas kernels, call(): pl.pallas_call(kernel, out_shape=outs, grid_spec=pltpu.PrefetchScalarGrid...  189 us
    ppermute x40, waiting for transfers between devices, __call__(): self.sent.append(lax.ppermute(cells, self.axis, self.pairs))  188 us
    ppermute x40, starting transfers between devices, __call__(): self.sent.append(lax.ppermute(cells, self.axis, self.pairs))  59.9 us
    ppermute x16, starting transfers between devices, shifted(): return lax.ppermute(shard, axis, pairs)  45.6 us
    ppermute x16, waiting for transfers between devices, shifted(): return lax.ppermute(shard, axis, pairs)  39 us
    convert_element_type x11, other arithmetic, plus(): return (left.astype(jnp.float32) + right.astype(jnp.float32)).astype(kind)  33 us
    unnamed x101, local copies, waits for them, and re-layouts  25.6 us
    dot_general x4, matrix products, product(): jnp.dot(left.T, both(right, is_first), preferred_element_type=jnp.float32)  21.4 us
  transfers between devices with their start and end apart: 63, of which 29 were waited for; matrix products, arithmetic and copies ran while one was open for 16% of the time, Pallas kernels for 9%

profile of v6, /device:TPU:0, one launch (start us, length us, event | category | flops | bytes accessed | tf_op | source)
XLA Modules:
  0.0 701.6 jit_solution(10638682785487346936)
XLA Ops:
  15.5 21.0 %collective-permute-done.3.refs_4_ = bf16[272,1024]{1,0:T(8,128)(2,1)S(1)} collective-permute-done((bf16[272,1024]{1,0:T(8,128)(2,1)S(1)}, bf16[272,1024]{1,0:T(8,128)(2,1)S(1)}, u32[]{:S(2)}, u32[]{:S(2)}) %collective-permute-start.3) | collective-permute-done | bytes 557088 | tf_op jit(solution)/shard_map/ppermute | solution.py:866
  38.3 10.3 %collective-permute-done.5.refs_6_ = bf16[272,1024]{1,0:T(8,128)(2,1)S(1)} collective-permute-done((bf16[272,1024]{1,0:T(8,128)(2,1)S(1)}, bf16[272,1024]{1,0:T(8,128)(2,1)S(1)}, u32[]{:S(2)}, u32[]{:S(2)}) %collective-permute-start.5) | collective-permute-done | bytes 557088 | tf_op jit(solution)/shard_map/ppermute | solution.py:866
  55.7 21.3 %collective-permute-done.7.refs_8_ = bf16[272,1024]{1,0:T(8,128)(2,1)S(1)} collective-permute-done((bf16[272,1024]{1,0:T(8,128)(2,1)S(1)}, bf16[272,1024]{1,0:T(8,128)(2,1)S(1)}, u32[]{:S(2)}, u32[]{:S(2)}) %collective-permute-start.7) | collective-permute-done | bytes 557088 | tf_op jit(solution)/shard_map/ppermute | solution.py:866
  80.8 18.5 %collective-permute-done.1.refs_2_ = bf16[272,1024]{1,0:T(8,128)(2,1)S(1)} collective-permute-done((bf16[272,1024]{1,0:T(8,128)(2,1)S(1)}, bf16[272,1024]{1,0:T(8,128)(2,1)S(1)}, u32[]{:S(2)}, u32[]{:S(2)}) %collective-permute-start.1) | collective-permute-done | bytes 557088 | tf_op jit(solution)/shard_map/ppermute | solution.py:866
  99.3 7.1 %collective-permute-done.11.refs_12_ = bf16[272,1024]{1,0:T(8,128)(2,1)S(1)} collective-permute-done((bf16[272,1024]{1,0:T(8,128)(2,1)S(1)}, bf16[272,1024]{1,0:T(8,128)(2,1)S(1)}, u32[]{:S(2)}, u32[]{:S(2)}) %collective-permute-start.11) | collective-permute-done | bytes 557088 | tf_op jit(solution)/shard_map/ppermute | solution.py:866
  110.6 9.8 %collective-permute-done.9.refs_10_ = bf16[272,1024]{1,0:T(8,128)(2,1)} collective-permute-done((bf16[272,1024]{1,0:T(8,128)(2,1)S(1)}, bf16[272,1024]{1,0:T(8,128)(2,1)}, u32[]{:S(2)}, u32[]{:S(2)}) %collective-permute-start.9) | collective-permute-done | bytes 557088 | tf_op jit(solution)/shard_map/ppermute | solution.py:866
  140.8 6.9 shard_map.204
  153.6 7.2 %collective-permute-done.16.refs_2_ = bf16[4,64,2816]{2,1,0:T(8,128)(2,1)} collective-permute-done((bf16[4,64,2816]{2,1,0:T(8,128)(2,1)}, bf16[4,64,2816]{2,1,0:T(8,128)(2,1)}, u32[]{:S(2)}, u32[]{:S(2)}) %collective-permute-start.16) | collective-permute-done | bytes 1441824 | tf_op jit(solution)/shard_map/ppermute | solution.py:866
  173.1 10.3 %shard_map.205 = (bf16[3,576,1024]{2,1,0:T(8,128)(2,1)}, bf16[3,576,1024]{2,1,0:T(8,128)(2,1)}, bf16[3,320,1024]{2,1,0:T(8,128)(2,1)}, f32[3,320,512]{2,1,0:T(8,...) custom-call(s32[3]{0:T(128)} %stack.53.idx, bf16[3,320,1024]{2,1,0:T(8,128)(2,1)} %get-tuple-element.136.q.rest_2_, ...), custom_call_target="tpu_custom_call" | custom-call | flops 1677721600 | bytes 8650752 | tf_op jit(solution)/shard_map/pallas_call | solution.py:31
  208.9 12.7 %shard_map.209 = (bf16[3,320,2816]{2,1,0:T(8,128)(2,1)}, bf16[3,320,2816]{2,1,0:T(8,128)(2,1)}, bf16[3,320,2816]{2,1,0:T(8,128)(2,1)}, bf16[320,1024]{1,0:T(8,128)(2,1)}) custom-call(s32[3]{0:T(128)} %stack.53.idx, bf16[3,320,1024]{2,1,0:T(8,128)(2,1)} %get-tuple-element.143.two.rest_8_, f32[3,320,1024]{2,1,0:T(8,128)} %get-tuple-element.144.residual.rest_7_, ...), custom_call_target="tpu_custom_call" | custom-call | flops 5536481280 | bytes 20578304 | tf_op jit(solution)/shard_map/pallas_call | solution.py:31
  225.6 14.0 %collective-permute-done.26.arrived = bf16[320,1024]{1,0:T(8,128)(2,1)S(1)} collective-permute-done((bf16[320,1024]{1,0:T(8,128)(2,1)}, bf16[320,1024]{1,0:T(8,128)(2,1)S(1)}, u32[]{:S(2)}, u32[]{:S(2)}) %collective-permute-start.26) | collective-permute-done | bytes 655392 | tf_op jit(solution)/shard_map/ppermute | solution.py:20
  240.4 6.9 shard_map.210
  255.5 34.3 %shard_map.211 = (bf16[3,576,1024]{2,1,0:T(8,128)(2,1)}, bf16[3,576,1024]{2,1,0:T(8,128)(2,1)}, bf16[3,320,1024]{2,1,0:T(8,128)(2,1)}, f32[3,320,512]{2,1,0:T(8,...) custom-call(s32[3]{0:T(128)} %pad_add_fusion.2.idx, ...), custom_call_target="tpu_custom_call", output_to_operand_aliasing={{0}: (15, {}), {1}: (16, {}), {2}: (17, {}), {3}: (18, {}),... | custom-call | flops 7214202880 | bytes 25952256 | tf_op jit(solution)/shard_map/pallas_call | solution.py:31
  289.7 11.2 %shard_map.212 = (bf16[3,320,1024]{2,1,0:T(8,128)(2,1)}, f32[2,320,1024]{2,1,0:T(8,128)}, bf16[2,128,1024]{2,1,0:T(8,128)(2,1)}, bf16[2,128,1024]{2,1,0:T(8,128)(2,1)}) custom-call(s32[3]{0:T(128)} %pad_add_fusion.5.idx, bf16[3,320,1024]{2,1,0:T(8,128)(2,1)} %get-tuple-element.152.q.rest_2_, bf16[3,576,1024]{2,1,0:T(8,128)(2,1)} %get-tuple-element.165.keys.rest_3_, ...), custom_call_target="tpu_custom_call" | custom-call | flops 5033164800 | bytes 7864320 | tf_op jit(solution)/shard_map/pallas_call | solution.py:31
  300.9 9.1 %collective-permute-start.30 = (bf16[2,128,1024]{2,1,0:T(8,128)(2,1)}, bf16[2,128,1024]{2,1,0:T(8,128)(2,1)S(1)}, u32[]{:S(2)}, u32[]{:S(2)}) collective-permute-start(bf16[2,128,1024]{2,1,0:T(8,128)(2,1)} %get-tuple-element.172), channel_id=1, source_target_pairs={{0,4},{4,8},{8,12},{1,5},{5,9},{9,13},{2,6},{6,10},{10,14},{3,7},{... | collective-permute-start | bytes 1572872 | tf_op jit(solution)/shard_map/ppermute | solution.py:20
  316.2 8.5 %shard_map.213 = (bf16[3,320,1024]{2,1,0:T(8,128)(2,1)}, bf16[3,320,1024]{2,1,0:T(8,128)(2,1)}, f32[3,8,1024]{2,1,0:T(8,128)}, bf16[320,1024]{1,0:T(8,128)(2,1)}) custom-call(s32[3]{0:T(128)} %pad_add_fusion.5.idx, bf16[3,320,1024]{2,1,0:T(8,128)(2,1)} %get-tuple-element.170.grad_q.rest_0_, f32[2,320,1024]{2,1,0:T(8,128)} %get-tuple-element.171.center, ...), custom_call_target="tpu_custom_call" | custom-call | flops 2013265920 | bytes 12845056 | tf_op jit(solution)/shard_map/pallas_call | solution.py:31
  345.9 34.5 %shard_map.215 = (bf16[3,576,1024]{2,1,0:T(8,128)(2,1)}, bf16[3,576,1024]{2,1,0:T(8,128)(2,1)}, bf16[3,320,1024]{2,1,0:T(8,128)(2,1)}, f32[3,320,512]{2,1,0:T(8,...) custom-call(s32[3]{0:T(128)} %pad_add_fusion.1.idx, ...), custom_call_target="tpu_custom_call", output_to_operand_aliasing={{0}: (15, {}), {1}: (16, {}), {2}: (17, {}), {3}: (18, {}),... | custom-call | flops 7214202880 | bytes 25952256 | tf_op jit(solution)/shard_map/pallas_call | solution.py:31
  380.4 11.1 %shard_map.216 = (bf16[3,320,1024]{2,1,0:T(8,128)(2,1)}, f32[2,320,1024]{2,1,0:T(8,128)}, bf16[2,128,1024]{2,1,0:T(8,128)(2,1)}, bf16[2,128,1024]{2,1,0:T(8,128)(2,1)}) custom-call(s32[3]{0:T(128)} %pad_add_fusion.6.idx, bf16[3,320,1024]{2,1,0:T(8,128)(2,1)} %get-tuple-element.178.q, ...), custom_call_target="tpu_custom_call", output_to_operand_aliasing={{0}: (8, {})} | custom-call | flops 5033164800 | bytes 7864320 | tf_op jit(solution)/shard_map/pallas_call | solution.py:31
  391.5 8.6 %collective-permute-start.35 = (bf16[2,128,1024]{2,1,0:T(8,128)(2,1)}, bf16[2,128,1024]{2,1,0:T(8,128)(2,1)S(1)}, u32[]{:S(2)}, u32[]{:S(2)}) collective-permute-start(bf16[2,128,1024]{2,1,0:T(8,128)(2,1)} %get-tuple-element.201), channel_id=1, source_target_pairs={{0,4},{4,8},{8,12},{1,5},{5,9},{9,13},{2,6},{6,10},{10,14},{3,7},{... | collective-permute-start | bytes 1572872 | tf_op jit(solution)/shard_map/ppermute | solution.py:20
  404.9 8.6 %shard_map.217 = (bf16[3,320,1024]{2,1,0:T(8,128)(2,1)}, bf16[3,320,1024]{2,1,0:T(8,128)(2,1)}, f32[3,8,1024]{2,1,0:T(8,128)}, bf16[320,1024]{1,0:T(8,128)(2,1)}) custom-call(s32[3]{0:T(128)} %pad_add_fusion.6.idx, bf16[3,320,1024]{2,1,0:T(8,128)(2,1)} %get-tuple-element.199.grad_q.rest_0_, ...), custom_call_target="tpu_custom_call", output_to_operand_aliasing={{0}: (11, {}), {1}: (12, {}), {2}: (13, {})} | custom-call | flops 2013265920 | bytes 12845056 | tf_op jit(solution)/shard_map/pallas_call | solution.py:31
  417.1 10.4 %collective-permute-done.37.arrived = bf16[320,1024]{1,0:T(8,128)(2,1)S(1)} collective-permute-done((bf16[320,1024]{1,0:T(8,128)(2,1)}, bf16[320,1024]{1,0:T(8,128)(2,1)S(1)}, u32[]{:S(2)}, u32[]{:S(2)}) %collective-permute-start.37) | collective-permute-done | bytes 655392 | tf_op jit(solution)/shard_map/ppermute | solution.py:20
  428.3 17.3 %shard_map.218 = (bf16[3,320,1024]{2,1,0:T(8,128)(2,1)}, bf16[3,320,2816]{2,1,0:T(8,128)(2,1)}, bf16[3,320,2816]{2,1,0:T(8,128)(2,1)}, bf16[3,320,1024]{2,1,0:T(...) custom-call(s32[3]{0:T(128)} %pad_add_fusion.idx, ...), custom_call_target="tpu_custom_call", output_to_operand_aliasing={{0}: (11, {}), {1}: (12, {}), {2}: (13, {}), {3}: (14, {}),... | custom-call | flops 6207569920 | bytes 17301504 | tf_op jit(solution)/shard_map/pallas_call | solution.py:31
  445.6 7.0 bitcast_convert_fusion
  487.4 7.1 %convolution_convert_fusion.1 = bf16[2816,1024]{1,0:T(8,128)(2,1)S(1)} fusion(bf16[640,2816]{1,0:T(8,128)(2,1)} %bitcast.278, bf16[640,1024]{1,0:T(8,128)(2,1)} %bitcast.282), kind=kOutput, calls=%fused_computation.6 | convolution fusion | flops 3693871104 | bytes 10682368 | tf_op jit(solution)/shard_map/dot_general | solution.py:1152
  502.0 11.2 %shard_map.219 = (bf16[3,320,1024]{2,1,0:T(8,128)(2,1)}, f32[2,320,1024]{2,1,0:T(8,128)}, bf16[2,128,1024]{2,1,0:T(8,128)(2,1)}, bf16[2,128,1024]{2,1,0:T(8,128)(2,1)}) custom-call(s32[3]{0:T(128)} %pad_add_fusion.idx, bf16[3,320,1024]{2,1,0:T(8,128)(2,1)} %get-tuple-element.178.q, ...), custom_call_target="tpu_custom_call", output_to_operand_aliasing={{0}: (8, {})} | custom-call | flops 5033164800 | bytes 7864320 | tf_op jit(solution)/shard_map/pallas_call | solution.py:31
  520.8 17.4 %collective-permute-start.45 = (bf16[256,2816]{1,0:T(8,128)(2,1)}, bf16[256,2816]{1,0:T(8,128)(2,1)}, u32[]{:S(2)}, u32[]{:S(2)}) collective-permute-start(bf16[256,2816]{1,0:T(8,128)(2,1)} %fusion.13), channel_id=1, source_target_pairs={{0,8},{4,12},{8,0},{12,4},{1,9},{5,13},{9,1},{13,5},{2,10},{6,14},... | collective-permute-start | bytes 4325384 | tf_op jit(solution)/shard_map/ppermute | solution.py:866
  545.3 8.9 %shard_map.220 = (bf16[3,320,1024]{2,1,0:T(8,128)(2,1)}, bf16[3,320,1024]{2,1,0:T(8,128)(2,1)}, f32[3,8,1024]{2,1,0:T(8,128)}, bf16[320,1024]{1,0:T(8,128)(2,1)}) custom-call(s32[3]{0:T(128)} %pad_add_fusion.idx, bf16[3,320,1024]{2,1,0:T(8,128)(2,1)} %get-tuple-element.228.grad_q, ...), custom_call_target="tpu_custom_call", output_to_operand_aliasing={{0}: (11, {}), {1}: (12, {}), {2}: (13, {})} | custom-call | flops 2013265920 | bytes 12845056 | tf_op jit(solution)/shard_map/pallas_call | solution.py:31
  558.1 12.4 %collective-permute-done.45 = bf16[256,2816]{1,0:T(8,128)(2,1)} collective-permute-done((bf16[256,2816]{1,0:T(8,128)(2,1)}, bf16[256,2816]{1,0:T(8,128)(2,1)}, u32[]{:S(2)}, u32[]{:S(2)}) %collective-permute-start.45) | collective-permute-done | bytes 1441824 | tf_op jit(solution)/shard_map/ppermute | solution.py:866
  598.2 24.0 %collective-permute-done.49 = bf16[704,1024]{1,0:T(8,128)(2,1)} collective-permute-done((bf16[704,1024]{1,0:T(8,128)(2,1)}, bf16[704,1024]{1,0:T(8,128)(2,1)}, u32[]{:S(2)}, u32[]{:S(2)}) %collective-permute-start.49) | collective-permute-done | bytes 1441824 | tf_op jit(solution)/shard_map/ppermute | solution.py:866
  635.5 7.8 %collective-permute-done.50 = bf16[64,3200]{1,0:T(8,128)(2,1)} collective-permute-done((bf16[64,3200]{1,0:T(8,128)(2,1)}, bf16[64,3200]{1,0:T(8,128)(2,1)}, u32[]{:S(2)}, u32[]{:S(2)}) %collective-permute-start.50) | collective-permute-done | bytes 409632 | tf_op jit(solution)/shard_map/ppermute | solution.py:866
  643.2 13.0 %collective-permute-done.48 = bf16[64,3200]{1,0:T(8,128)(2,1)} collective-permute-done((bf16[64,3200]{1,0:T(8,128)(2,1)}, bf16[64,3200]{1,0:T(8,128)(2,1)}, u32[]{:S(2)}, u32[]{:S(2)}) %collective-permute-start.48) | collective-permute-done | bytes 409632 | tf_op jit(solution)/shard_map/ppermute | solution.py:866
  669.4 7.0 collective-permute-done.51
  (295 shorter events, 271.1 us)
Async XLA Ops:
  7.2 46.5 %all-gather.4.cloned.1.call-start = ((), (), s32[]{:S(2)}) async-start(), calls=%async_computation.4 | async-start | bytes 1802240 | tf_op jit(solution)/shard_map/all_gather | solution.py:889
  7.9 118.5 %all-gather.6.cloned.1.call-start = ((), (), s32[]{:S(2)}) async-start(), calls=%async_computation.5 | async-start | bytes 1802240 | tf_op jit(solution)/shard_map/all_gather | solution.py:889
  12.4 24.1 %collective-permute-start.3 = (bf16[272,1024]{1,0:T(8,128)(2,1)S(1)}, bf16[272,1024]{1,0:T(8,128)(2,1)S(1)}, u32[]{:S(2)}, u32[]{:S(2)}) collective-permute-start(bf16[272,1024]{1,0:T(8,128)(2,1)S(1)} %fusion.42.refs_0_), channel_id=1, source_target_pairs={{0,1},{1,2},{2,3},{3,0},{4,5},{5,6},{6,7},{7,4},{8,9},{9,10},{10,1... | collective-permute-start | bytes 1671176 | tf_op jit(solution)/shard_map/ppermute | solution.py:866
  15.4 150.1 %all-gather.8.cloned.1.call-start = ((), (), s32[]{:S(2)}) async-start(), calls=%async_computation.6 | async-start | bytes 1802240 | tf_op jit(solution)/shard_map/all_gather | solution.py:889
  53.6 53.3 %collective-permute-start.13 = (bf16[4,64,2816]{2,1,0:T(8,128)(2,1)}, bf16[4,64,2816]{2,1,0:T(8,128)(2,1)}, u32[]{:S(2)}, u32[]{:S(2)}) collective-permute-start(bf16[4,64,2816]{2,1,0:T(8,128)(2,1)} %all-gather.4.cloned.1.call-done.refs_0_), channel_id=1, source_target_pairs={{0,8},{4,12},{8,0},{12,4},{1,9},{5,13},{9,1},{13,5},{2,10},{6,14},... | collective-permute-start | bytes 4325384 | tf_op jit(solution)/shard_map/ppermute | solution.py:866
  55.2 21.9 %collective-permute-start.7 = (bf16[272,1024]{1,0:T(8,128)(2,1)S(1)}, bf16[272,1024]{1,0:T(8,128)(2,1)S(1)}, u32[]{:S(2)}, u32[]{:S(2)}) collective-permute-start(bf16[272,1024]{1,0:T(8,128)(2,1)S(1)} %collective-permute-done.3.refs_4_), channel_id=1, source_target_pairs={{0,1},{1,2},{2,3},{3,0},{4,5},{5,6},{6,7},{7,4},{8,9},{9,10},{10,1... | collective-permute-start | bytes 1671176 | tf_op jit(solution)/shard_map/ppermute | solution.py:866
  55.2 44.2 %collective-permute-start.1 = (bf16[272,1024]{1,0:T(8,128)(2,1)S(1)}, bf16[272,1024]{1,0:T(8,128)(2,1)S(1)}, u32[]{:S(2)}, u32[]{:S(2)}) collective-permute-start(bf16[272,1024]{1,0:T(8,128)(2,1)S(1)} %fusion.42.refs_0_), channel_id=1, source_target_pairs={{0,8},{4,12},{8,0},{12,4},{1,9},{5,13},{9,1},{13,5},{2,10},{6,14},... | collective-permute-start | bytes 1671176 | tf_op jit(solution)/shard_map/ppermute | solution.py:866
  77.0 29.4 %collective-permute-start.11 = (bf16[272,1024]{1,0:T(8,128)(2,1)S(1)}, bf16[272,1024]{1,0:T(8,128)(2,1)S(1)}, u32[]{:S(2)}, u32[]{:S(2)}) collective-permute-start(bf16[272,1024]{1,0:T(8,128)(2,1)S(1)} %collective-permute-done.7.refs_8_), channel_id=1, source_target_pairs={{0,1},{1,2},{2,3},{3,0},{4,5},{5,6},{6,7},{7,4},{8,9},{9,10},{10,1... | collective-permute-start | bytes 1671176 | tf_op jit(solution)/shard_map/ppermute | solution.py:866
  80.2 28.3 %collective-permute-start = (bf16[272,1024]{1,0:T(8,128)(2,1)S(1)}, bf16[272,1024]{1,0:T(8,128)(2,1)}, u32[]{:S(2)}, u32[]{:S(2)}) collective-permute-start(bf16[272,1024]{1,0:T(8,128)(2,1)S(1)} %fusion.42.refs_0_), channel_id=1, source_target_pairs={{0,4},{4,0},{8,12},{12,8},{1,5},{5,1},{9,13},{13,9},{2,6},{6,2},{1... | collective-permute-start | bytes 1671176 | tf_op jit(solution)/shard_map/ppermute | solution.py:866
  80.2 510.5 %reduce-scatter.5.cloned.1.call-start = ((), (), s32[]{:S(2)}) async-start(), calls=%async_computation.7 | async-start | bytes 1310720 | tf_op jit(solution)/shard_map/reduce_scatter | solution.py:999
  80.3 28.3 %collective-permute-start.4 = (bf16[272,1024]{1,0:T(8,128)(2,1)S(1)}, bf16[272,1024]{1,0:T(8,128)(2,1)S(1)}, u32[]{:S(2)}, u32[]{:S(2)}) collective-permute-start(bf16[272,1024]{1,0:T(8,128)(2,1)S(1)} %collective-permute-done.3.refs_4_), channel_id=1, source_target_pairs={{0,4},{4,0},{8,12},{12,8},{1,5},{5,1},{9,13},{13,9},{2,6},{6,2},{1... | collective-permute-start | bytes 1671176 | tf_op jit(solution)/shard_map/ppermute | solution.py:866
  107.0 19.5 %collective-permute-start.14 = (bf16[272,1024]{1,0:T(8,128)(2,1)S(1)}, bf16[272,1024]{1,0:T(8,128)(2,1)}, u32[]{:S(2)}, u32[]{:S(2)}) collective-permute-start(bf16[272,1024]{1,0:T(8,128)(2,1)S(1)} %collective-permute-done.11.refs_12_), channel_id=1, source_target_pairs={{0,8},{4,12},{8,0},{12,4},{1,9},{5,13},{9,1},{13,5},{2,10},{6,14},... | collective-permute-start | bytes 1671176 | tf_op jit(solution)/shard_map/ppermute | solution.py:866
  109.3 21.8 %collective-permute-start.6 = (bf16[272,1024]{1,0:T(8,128)(2,1)S(1)}, bf16[272,1024]{1,0:T(8,128)(2,1)}, u32[]{:S(2)}, u32[]{:S(2)}) collective-permute-start(bf16[272,1024]{1,0:T(8,128)(2,1)S(1)} %collective-permute-done.5.refs_6_), channel_id=1, source_target_pairs={{0,4},{4,0},{8,12},{12,8},{1,5},{5,1},{9,13},{13,9},{2,6},{6,2},{1... | collective-permute-start | bytes 1671176 | tf_op jit(solution)/shard_map/ppermute | solution.py:866
  110.6 20.5 %collective-permute-start.12 = (bf16[272,1024]{1,0:T(8,128)(2,1)S(1)}, bf16[272,1024]{1,0:T(8,128)(2,1)}, u32[]{:S(2)}, u32[]{:S(2)}) collective-permute-start(bf16[272,1024]{1,0:T(8,128)(2,1)S(1)} %collective-permute-done.11.refs_12_), channel_id=1, source_target_pairs={{0,4},{4,0},{8,12},{12,8},{1,5},{5,1},{9,13},{13,9},{2,6},{6,2},{1... | collective-permute-start | bytes 1671176 | tf_op jit(solution)/shard_map/ppermute | solution.py:866
  126.4 34.3 %collective-permute-start.16 = (bf16[4,64,2816]{2,1,0:T(8,128)(2,1)}, bf16[4,64,2816]{2,1,0:T(8,128)(2,1)}, u32[]{:S(2)}, u32[]{:S(2)}) collective-permute-start(bf16[4,64,2816]{2,1,0:T(8,128)(2,1)} %all-gather.6.cloned.1.call-done.refs_0_), channel_id=1, source_target_pairs={{0,8},{4,12},{8,0},{12,4},{1,9},{5,13},{9,1},{13,5},{2,10},{6,14},... | collective-permute-start | bytes 4325384 | tf_op jit(solution)/shard_map/ppermute | solution.py:866
  152.3 31.2 %collective-permute-start.21 = (bf16[4,64,2816]{2,1,0:T(8,128)(2,1)S(1)}, bf16[4,64,2816]{2,1,0:T(8,128)(2,1)}, u32[]{:S(2)}, u32[]{:S(2)}) collective-permute-start(bf16[4,64,2816]{2,1,0:T(8,128)(2,1)S(1)} %copy-done.4), channel_id=1, source_target_pairs={{0,4},{4,0},{8,12},{12,8},{1,5},{5,1},{9,13},{13,9},{2,6},{6,2},{1... | collective-permute-start | bytes 4325384 | tf_op jit(solution)/shard_map/ppermute | solution.py:866
  153.5 35.8 %collective-permute-start.19 = (bf16[4,64,2816]{2,1,0:T(8,128)(2,1)S(1)}, bf16[4,64,2816]{2,1,0:T(8,128)(2,1)}, u32[]{:S(2)}, u32[]{:S(2)}) collective-permute-start(bf16[4,64,2816]{2,1,0:T(8,128)(2,1)S(1)} %copy-done.3), channel_id=1, source_target_pairs={{0,4},{4,0},{8,12},{12,8},{1,5},{5,1},{9,13},{13,9},{2,6},{6,2},{1... | collective-permute-start | bytes 4325384 | tf_op jit(solution)/shard_map/ppermute | solution.py:866
  160.8 23.0 %collective-permute-start.22 = (bf16[4,64,2816]{2,1,0:T(8,128)(2,1)}, bf16[4,64,2816]{2,1,0:T(8,128)(2,1)}, u32[]{:S(2)}, u32[]{:S(2)}) collective-permute-start(bf16[4,64,2816]{2,1,0:T(8,128)(2,1)} %collective-permute-done.16.refs_2_), channel_id=1, source_target_pairs={{0,4},{4,0},{8,12},{12,8},{1,5},{5,1},{9,13},{13,9},{2,6},{6,2},{1... | collective-permute-start | bytes 4325384 | tf_op jit(solution)/shard_map/ppermute | solution.py:866
  160.8 28.5 %collective-permute-start.20 = (bf16[4,64,2816]{2,1,0:T(8,128)(2,1)}, bf16[4,64,2816]{2,1,0:T(8,128)(2,1)}, u32[]{:S(2)}, u32[]{:S(2)}) collective-permute-start(bf16[4,64,2816]{2,1,0:T(8,128)(2,1)} %collective-permute-done.13.refs_2_), channel_id=1, source_target_pairs={{0,4},{4,0},{8,12},{12,8},{1,5},{5,1},{9,13},{13,9},{2,6},{6,2},{1... | collective-permute-start | bytes 4325384 | tf_op jit(solution)/shard_map/ppermute | solution.py:866
  165.5 34.9 %collective-permute-start.24 = (bf16[4,176,1024]{2,1,0:T(8,128)(2,1)}, bf16[4,176,1024]{2,1,0:T(8,128)(2,1)}, u32[]{:S(2)}, u32[]{:S(2)}) collective-permute-start(bf16[4,176,1024]{2,1,0:T(8,128)(2,1)} %all-gather.8.cloned.1.call-done.refs_0_), channel_id=1, source_target_pairs={{0,8},{4,12},{8,0},{12,4},{1,9},{5,13},{9,1},{13,5},{2,10},{6,14},... | collective-permute-start | bytes 4325384 | tf_op jit(solution)/shard_map/ppermute | solution.py:866
  324.8 20.2 %collective-permute-start.34 = (bf16[320,1024]{1,0:T(8,128)(2,1)}, bf16[320,1024]{1,0:T(8,128)(2,1)S(1)}, u32[]{:S(2)}, u32[]{:S(2)}) collective-permute-start(bf16[320,1024]{1,0:T(8,128)(2,1)} %get-tuple-element.175), channel_id=1, source_target_pairs={{16,0},{17,1},{18,2},{19,3},{20,4},{21,5},{22,6},{23,7},{24,8},{25... | collective-permute-start | bytes 1966088 | tf_op jit(solution)/shard_map/ppermute | solution.py:20
  456.8 27.4 %collective-permute-start.38 = (bf16[2,256,2816]{2,1,0:T(8,128)(2,1)}, bf16[2,256,2816]{2,1,0:T(8,128)(2,1)}, u32[]{:S(2)}, u32[]{:S(2)}) collective-permute-start(bf16[2,256,2816]{2,1,0:T(8,128)(2,1)} %dynamic-slice_bitcast_fusion.3), channel_id=1, source_target_pairs={{0,4},{4,0},{8,12},{12,8},{1,5},{5,1},{9,13},{13,9},{2,6},{6,2},{1... | collective-permute-start | bytes 8650760 | tf_op jit(solution)/shard_map/ppermute | solution.py:866
  476.6 21.6 %collective-permute-start.40 = (bf16[2,256,2816]{2,1,0:T(8,128)(2,1)}, bf16[2,256,2816]{2,1,0:T(8,128)(2,1)S(1)}, u32[]{:S(2)}, u32[]{:S(2)}) collective-permute-start(bf16[2,256,2816]{2,1,0:T(8,128)(2,1)} %dynamic-slice_bitcast_fusion.2), channel_id=1, source_target_pairs={{0,4},{4,0},{8,12},{12,8},{1,5},{5,1},{9,13},{13,9},{2,6},{6,2},{1... | collective-permute-start | bytes 8650760 | tf_op jit(solution)/shard_map/ppermute | solution.py:866
  497.9 44.0 %collective-permute-start.42 = (bf16[2,704,1024]{2,1,0:T(8,128)(2,1)}, bf16[2,704,1024]{2,1,0:T(8,128)(2,1)}, u32[]{:S(2)}, u32[]{:S(2)}) collective-permute-start(bf16[2,704,1024]{2,1,0:T(8,128)(2,1)} %dynamic-slice_bitcast_fusion.1), channel_id=1, source_target_pairs={{0,4},{4,0},{8,12},{12,8},{1,5},{5,1},{9,13},{13,9},{2,6},{6,2},{1... | collective-permute-start | bytes 8650760 | tf_op jit(solution)/shard_map/ppermute | solution.py:866
  497.9 135.7 %reduce-scatter.7.cloned.1.call-start = ((), (), s32[]{:S(2)}) async-start(), calls=%async_computation.8 | async-start | bytes 1802240 | tf_op jit(solution)/shard_map/reduce_scatter | solution.py:1030
  498.0 40.3 %collective-permute-start.41 = (bf16[256,2816]{1,0:T(8,128)(2,1)}, bf16[256,2816]{1,0:T(8,128)(2,1)S(1)}, u32[]{:S(2)}, u32[]{:S(2)}) collective-permute-start(bf16[256,2816]{1,0:T(8,128)(2,1)} %fusion.14), channel_id=1, source_target_pairs={{0,8},{4,12},{8,0},{12,4},{1,9},{5,13},{9,1},{13,5},{2,10},{6,14},... | collective-permute-start | bytes 4325384 | tf_op jit(solution)/shard_map/ppermute | solution.py:866
  520.8 49.7 %collective-permute-start.45 = (bf16[256,2816]{1,0:T(8,128)(2,1)}, bf16[256,2816]{1,0:T(8,128)(2,1)}, u32[]{:S(2)}, u32[]{:S(2)}) collective-permute-start(bf16[256,2816]{1,0:T(8,128)(2,1)} %fusion.13), channel_id=1, source_target_pairs={{0,8},{4,12},{8,0},{12,4},{1,9},{5,13},{9,1},{13,5},{2,10},{6,14},... | collective-permute-start | bytes 4325384 | tf_op jit(solution)/shard_map/ppermute | solution.py:866
  541.8 123.2 %reduce-scatter.9.cloned.1.call-start = ((), (), s32[]{:S(2)}) async-start(), calls=%async_computation.9 | async-start | bytes 1802240 | tf_op jit(solution)/shard_map/reduce_scatter | solution.py:1030
  587.2 93.2 %reduce-scatter.11.cloned.1.call-start = ((), (), s32[]{:S(2)}) async-start(), calls=%async_computation.10 | async-start | bytes 1802240 | tf_op jit(solution)/shard_map/reduce_scatter | solution.py:1030
  587.3 34.8 %collective-permute-start.49 = (bf16[704,1024]{1,0:T(8,128)(2,1)}, bf16[704,1024]{1,0:T(8,128)(2,1)}, u32[]{:S(2)}, u32[]{:S(2)}) collective-permute-start(bf16[704,1024]{1,0:T(8,128)(2,1)} %fusion.11), channel_id=1, source_target_pairs={{0,8},{4,12},{8,0},{12,4},{1,9},{5,13},{9,1},{13,5},{2,10},{6,14},... | collective-permute-start | bytes 4325384 | tf_op jit(solution)/shard_map/ppermute | solution.py:866
  595.6 34.4 %collective-permute-start.47 = (bf16[64,3200]{1,0:T(8,128)(2,1)}, bf16[64,3200]{1,0:T(8,128)(2,1)}, u32[]{:S(2)}, u32[]{:S(2)}) collective-permute-start(bf16[64,3200]{1,0:T(8,128)(2,1)} %fusion.23), channel_id=1, source_target_pairs={{0,8},{4,12},{8,0},{12,4},{1,9},{5,13},{9,1},{13,5},{2,10},{6,14},... | collective-permute-start | bytes 1228808 | tf_op jit(solution)/shard_map/ppermute | solution.py:866
  633.6 22.7 %collective-permute-start.48 = (bf16[64,3200]{1,0:T(8,128)(2,1)}, bf16[64,3200]{1,0:T(8,128)(2,1)}, u32[]{:S(2)}, u32[]{:S(2)}) collective-permute-start(bf16[64,3200]{1,0:T(8,128)(2,1)} %get-tuple-element.266), channel_id=1, source_target_pairs={{0,1},{1,2},{2,3},{3,0},{4,5},{5,6},{6,7},{7,4},{8,9},{9,10},{10,1... | collective-permute-start | bytes 1228808 | tf_op jit(solution)/shard_map/ppermute | solution.py:866
  (79 other events, 671.4 us)
Sparse Core Ops, SparseCore 0:
  9.6 44.0 all-gather.3
  55.2 50.2 all-gather.5
  107.1 33.1 all-gather.7
  498.0 26.2 reduce-scatter.4
  541.9 32.5 reduce-scatter.6
  587.3 32.5 reduce-scatter.8
  626.6 41.1 reduce-scatter.10

commit v7 on v6

--- a/solution.py
+++ b/solution.py
@@ -1210,7 +1210,6 @@
     lines, gate_sum, up_sum, down_sum, out_sum = (
         sums[name] for name in ("lines", "gate", "up", "down", "out")
     )
-    up_sum.add(grad_sources[-1])
     gain_rows = jnp.concatenate(
         [
             jnp.sum(lax.dynamic_slice_in_dim(store[name], is_first, micro_count, 0), 0)
@@ -1227,10 +1226,11 @@
             jnp.pad(picked.astype(jnp.bfloat16), ((0, 0), (right.shape[1], 0))),
         ]
     )
-    left = after(jnp.concatenate([both("normed", 1 - is_first), gain_rows]), up_sum.level)
+    left = jnp.concatenate([both("normed", 1 - is_first), gain_rows])
     qkv_part = jnp.dot(left.T, right, preferred_element_type=jnp.float32).astype(jnp.bfloat16)
+    up_sum.add(qkv_part)
     grad_up_w = up_sum.finish()
-    down_sum.add(qkv_part, grad_up_w)
+    down_sum.add(up_sum.level)
     qkv_all = ring_scatter(qkv_part, lines)
     grad_out_w = out_sum.cross().add().finish()
     grad_gate_w, grad_down_w = gate_sum.finish(), down_sum.finish()

time: 707 us -> 695 us (0.983)
  waiting for transfers between devices: 233 us -> 223 us
    ppermute x40, waiting for transfers between devices: 188 us -> 178 us  [__call__(): self.sent.append(lax.ppermute(cells, self.axis, self.pairs))]
    unnamed x101 -> x97, local copies, waits for them, and re-layouts: 25.6 us -> 27 us
  transfers between devices with their start and end apart: 63 -> 63, of which waited for: 29 -> 29; matrix products, arithmetic and copies ran while one was open for 16% -> 15% of each run, Pallas kernels for 9% -> 10%
where the time goes in v7:
time: 695 us; the launch traced here: 690 us
  waiting for transfers between devices  223 us (32%)
  Pallas kernels  205 us (29%)
  starting transfers between devices  107 us (15%)
  local copies, waits for them, and re-layouts  57.3 us (8%)
  other arithmetic  55.5 us (8%)
  matrix products  27.3 us (4%)
  between operations  15.1 us (2%)
    pallas_call x14, Pallas kernels, call(): pl.pallas_call(kernel, out_shape=outs, grid_spec=pltpu.PrefetchScalarGrid...  189 us
    ppermute x40, waiting for transfers between devices, __call__(): self.sent.append(lax.ppermute(cells, self.axis, self.pairs))  178 us
    ppermute x40, starting transfers between devices, __call__(): self.sent.append(lax.ppermute(cells, self.axis, self.pairs))  61 us
    ppermute x16, starting transfers between devices, shifted(): return lax.ppermute(shard, axis, pairs)  45.6 us
    ppermute x16, waiting for transfers between devices, shifted(): return lax.ppermute(shard, axis, pairs)  39 us
    convert_element_type x11, other arithmetic, plus(): return (left.astype(jnp.float32) + right.astype(jnp.float32)).astype(kind)  33 us
    unnamed x97, local copies, waits for them, and re-layouts  27 us
    dot_general x4, matrix products, product(): jnp.dot(left.T, both(right, is_first), preferred_element_type=jnp.float32)  21.4 us
  transfers between devices with their start and end apart: 63, of which 29 were waited for; matrix products, arithmetic and copies ran while one was open for 15% of the time, Pallas kernels for 10%

profile of v7, /device:TPU:0, one launch (start us, length us, event | category | flops | bytes accessed | tf_op | source)
XLA Modules:
  0.0 689.8 jit_solution(11852248026203531354)
XLA Ops:
  15.5 21.0 %collective-permute-done.3.refs_4_ = bf16[272,1024]{1,0:T(8,128)(2,1)S(1)} collective-permute-done((bf16[272,1024]{1,0:T(8,128)(2,1)S(1)}, bf16[272,1024]{1,0:T(8,128)(2,1)S(1)}, u32[]{:S(2)}, u32[]{:S(2)}) %collective-permute-start.3) | collective-permute-done | bytes 557088 | tf_op jit(solution)/shard_map/ppermute | solution.py:866
  38.3 10.3 %collective-permute-done.5.refs_6_ = bf16[272,1024]{1,0:T(8,128)(2,1)S(1)} collective-permute-done((bf16[272,1024]{1,0:T(8,128)(2,1)S(1)}, bf16[272,1024]{1,0:T(8,128)(2,1)S(1)}, u32[]{:S(2)}, u32[]{:S(2)}) %collective-permute-start.5) | collective-permute-done | bytes 557088 | tf_op jit(solution)/shard_map/ppermute | solution.py:866
  55.7 21.3 %collective-permute-done.7.refs_8_ = bf16[272,1024]{1,0:T(8,128)(2,1)S(1)} collective-permute-done((bf16[272,1024]{1,0:T(8,128)(2,1)S(1)}, bf16[272,1024]{1,0:T(8,128)(2,1)S(1)}, u32[]{:S(2)}, u32[]{:S(2)}) %collective-permute-start.7) | collective-permute-done | bytes 557088 | tf_op jit(solution)/shard_map/ppermute | solution.py:866
  80.8 18.5 %collective-permute-done.1.refs_2_ = bf16[272,1024]{1,0:T(8,128)(2,1)S(1)} collective-permute-done((bf16[272,1024]{1,0:T(8,128)(2,1)S(1)}, bf16[272,1024]{1,0:T(8,128)(2,1)S(1)}, u32[]{:S(2)}, u32[]{:S(2)}) %collective-permute-start.1) | collective-permute-done | bytes 557088 | tf_op jit(solution)/shard_map/ppermute | solution.py:866
  99.3 7.1 %collective-permute-done.11.refs_12_ = bf16[272,1024]{1,0:T(8,128)(2,1)S(1)} collective-permute-done((bf16[272,1024]{1,0:T(8,128)(2,1)S(1)}, bf16[272,1024]{1,0:T(8,128)(2,1)S(1)}, u32[]{:S(2)}, u32[]{:S(2)}) %collective-permute-start.11) | collective-permute-done | bytes 557088 | tf_op jit(solution)/shard_map/ppermute | solution.py:866
  110.6 9.8 %collective-permute-done.9.refs_10_ = bf16[272,1024]{1,0:T(8,128)(2,1)} collective-permute-done((bf16[272,1024]{1,0:T(8,128)(2,1)S(1)}, bf16[272,1024]{1,0:T(8,128)(2,1)}, u32[]{:S(2)}, u32[]{:S(2)}) %collective-permute-start.9) | collective-permute-done | bytes 557088 | tf_op jit(solution)/shard_map/ppermute | solution.py:866
  131.2 6.8 shard_map.203
  140.7 6.9 %shard_map.204 = (bf16[3,320,1024]{2,1,0:T(8,128)(2,1)}, bf16[3,320,1024]{2,1,0:T(8,128)(2,1)}, bf16[3,320,1024]{2,1,0:T(8,128)(2,1)}, bf16[2,320,1024]{2,1,0:T(...) custom-call(s32[3]{0:T(128)} %stack.53.idx, bf16[320,1024]{1,0:T(8,128)(2,1)} %get-tuple-element.267.own, ...), custom_call_target="tpu_custom_call" | custom-call | flops 2013265920 | bytes 10878976 | tf_op jit(solution)/shard_map/pallas_call | solution.py:31
  153.6 7.2 %collective-permute-done.16.refs_2_ = bf16[4,64,2816]{2,1,0:T(8,128)(2,1)} collective-permute-done((bf16[4,64,2816]{2,1,0:T(8,128)(2,1)}, bf16[4,64,2816]{2,1,0:T(8,128)(2,1)}, u32[]{:S(2)}, u32[]{:S(2)}) %collective-permute-start.16) | collective-permute-done | bytes 1441824 | tf_op jit(solution)/shard_map/ppermute | solution.py:866
  173.2 10.3 %shard_map.205 = (bf16[3,576,1024]{2,1,0:T(8,128)(2,1)}, bf16[3,576,1024]{2,1,0:T(8,128)(2,1)}, bf16[3,320,1024]{2,1,0:T(8,128)(2,1)}, f32[3,320,512]{2,1,0:T(8,...) custom-call(s32[3]{0:T(128)} %stack.53.idx, bf16[3,320,1024]{2,1,0:T(8,128)(2,1)} %get-tuple-element.135.q.rest_2_, ...), custom_call_target="tpu_custom_call" | custom-call | flops 1677721600 | bytes 8650752 | tf_op jit(solution)/shard_map/pallas_call | solution.py:31
  208.9 12.7 %shard_map.209 = (bf16[3,320,2816]{2,1,0:T(8,128)(2,1)}, bf16[3,320,2816]{2,1,0:T(8,128)(2,1)}, bf16[3,320,2816]{2,1,0:T(8,128)(2,1)}, bf16[320,1024]{1,0:T(8,128)(2,1)}) custom-call(s32[3]{0:T(128)} %stack.53.idx, bf16[3,320,1024]{2,1,0:T(8,128)(2,1)} %get-tuple-element.142.two.rest_8_, f32[3,320,1024]{2,1,0:T(8,128)} %get-tuple-element.143.residual.rest_7_, ...), custom_call_target="tpu_custom_call" | custom-call | flops 5536481280 | bytes 20578304 | tf_op jit(solution)/shard_map/pallas_call | solution.py:31
  225.6 14.0 %collective-permute-done.26.arrived = bf16[320,1024]{1,0:T(8,128)(2,1)S(1)} collective-permute-done((bf16[320,1024]{1,0:T(8,128)(2,1)}, bf16[320,1024]{1,0:T(8,128)(2,1)S(1)}, u32[]{:S(2)}, u32[]{:S(2)}) %collective-permute-start.26) | collective-permute-done | bytes 655392 | tf_op jit(solution)/shard_map/ppermute | solution.py:20
  240.4 6.9 %shard_map.210 = (bf16[3,320,1024]{2,1,0:T(8,128)(2,1)}, bf16[3,320,1024]{2,1,0:T(8,128)(2,1)}, bf16[3,320,1024]{2,1,0:T(8,128)(2,1)}, bf16[2,320,1024]{2,1,0:T(...) custom-call(s32[3]{0:T(128)} %pad_add_fusion.2.idx, ...), custom_call_target="tpu_custom_call", output_to_operand_aliasing={{0}: (7, {}), {1}: (8, {}), {2}: (9, {})} | custom-call | flops 2013265920 | bytes 10878976 | tf_op jit(solution)/shard_map/pallas_call | solution.py:31
  255.5 34.3 %shard_map.211 = (bf16[3,576,1024]{2,1,0:T(8,128)(2,1)}, bf16[3,576,1024]{2,1,0:T(8,128)(2,1)}, bf16[3,320,1024]{2,1,0:T(8,128)(2,1)}, f32[3,320,512]{2,1,0:T(8,...) custom-call(s32[3]{0:T(128)} %pad_add_fusion.2.idx, ...), custom_call_target="tpu_custom_call", output_to_operand_aliasing={{0}: (15, {}), {1}: (16, {}), {2}: (17, {}), {3}: (18, {}),... | custom-call | flops 7214202880 | bytes 25952256 | tf_op jit(solution)/shard_map/pallas_call | solution.py:31
  289.8 11.2 %shard_map.212 = (bf16[3,320,1024]{2,1,0:T(8,128)(2,1)}, f32[2,320,1024]{2,1,0:T(8,128)}, bf16[2,128,1024]{2,1,0:T(8,128)(2,1)}, bf16[2,128,1024]{2,1,0:T(8,128)(2,1)}) custom-call(s32[3]{0:T(128)} %pad_add_fusion.5.idx, bf16[3,320,1024]{2,1,0:T(8,128)(2,1)} %get-tuple-element.151.q.rest_2_, bf16[3,576,1024]{2,1,0:T(8,128)(2,1)} %get-tuple-element.164.keys.rest_3_, ...), custom_call_target="tpu_custom_call" | custom-call | flops 5033164800 | bytes 7864320 | tf_op jit(solution)/shard_map/pallas_call | solution.py:31
  301.0 9.1 %collective-permute-start.30 = (bf16[2,128,1024]{2,1,0:T(8,128)(2,1)}, bf16[2,128,1024]{2,1,0:T(8,128)(2,1)S(1)}, u32[]{:S(2)}, u32[]{:S(2)}) collective-permute-start(bf16[2,128,1024]{2,1,0:T(8,128)(2,1)} %get-tuple-element.171), channel_id=1, source_target_pairs={{0,4},{4,8},{8,12},{1,5},{5,9},{9,13},{2,6},{6,10},{10,14},{3,7},{... | collective-permute-start | bytes 1572872 | tf_op jit(solution)/shard_map/ppermute | solution.py:20
  316.3 8.5 %shard_map.213 = (bf16[3,320,1024]{2,1,0:T(8,128)(2,1)}, bf16[3,320,1024]{2,1,0:T(8,128)(2,1)}, f32[3,8,1024]{2,1,0:T(8,128)}, bf16[320,1024]{1,0:T(8,128)(2,1)}) custom-call(s32[3]{0:T(128)} %pad_add_fusion.5.idx, bf16[3,320,1024]{2,1,0:T(8,128)(2,1)} %get-tuple-element.169.grad_q.rest_0_, f32[2,320,1024]{2,1,0:T(8,128)} %get-tuple-element.170.center, ...), custom_call_target="tpu_custom_call" | custom-call | flops 2013265920 | bytes 12845056 | tf_op jit(solution)/shard_map/pallas_call | solution.py:31
  330.4 6.7 shard_map.214
  346.0 34.5 %shard_map.215 = (bf16[3,576,1024]{2,1,0:T(8,128)(2,1)}, bf16[3,576,1024]{2,1,0:T(8,128)(2,1)}, bf16[3,320,1024]{2,1,0:T(8,128)(2,1)}, f32[3,320,512]{2,1,0:T(8,...) custom-call(s32[3]{0:T(128)} %pad_add_fusion.1.idx, ...), custom_call_target="tpu_custom_call", output_to_operand_aliasing={{0}: (15, {}), {1}: (16, {}), {2}: (17, {}), {3}: (18, {}),... | custom-call | flops 7214202880 | bytes 25952256 | tf_op jit(solution)/shard_map/pallas_call | solution.py:31
  380.5 11.1 %shard_map.216 = (bf16[3,320,1024]{2,1,0:T(8,128)(2,1)}, f32[2,320,1024]{2,1,0:T(8,128)}, bf16[2,128,1024]{2,1,0:T(8,128)(2,1)}, bf16[2,128,1024]{2,1,0:T(8,128)(2,1)}) custom-call(s32[3]{0:T(128)} %pad_add_fusion.6.idx, bf16[3,320,1024]{2,1,0:T(8,128)(2,1)} %get-tuple-element.177.q, ...), custom_call_target="tpu_custom_call", output_to_operand_aliasing={{0}: (8, {})} | custom-call | flops 5033164800 | bytes 7864320 | tf_op jit(solution)/shard_map/pallas_call | solution.py:31
  391.6 8.6 %collective-permute-start.35 = (bf16[2,128,1024]{2,1,0:T(8,128)(2,1)}, bf16[2,128,1024]{2,1,0:T(8,128)(2,1)S(1)}, u32[]{:S(2)}, u32[]{:S(2)}) collective-permute-start(bf16[2,128,1024]{2,1,0:T(8,128)(2,1)} %get-tuple-element.200), channel_id=1, source_target_pairs={{0,4},{4,8},{8,12},{1,5},{5,9},{9,13},{2,6},{6,10},{10,14},{3,7},{... | collective-permute-start | bytes 1572872 | tf_op jit(solution)/shard_map/ppermute | solution.py:20
  405.0 8.7 %shard_map.217 = (bf16[3,320,1024]{2,1,0:T(8,128)(2,1)}, bf16[3,320,1024]{2,1,0:T(8,128)(2,1)}, f32[3,8,1024]{2,1,0:T(8,128)}, bf16[320,1024]{1,0:T(8,128)(2,1)}) custom-call(s32[3]{0:T(128)} %pad_add_fusion.6.idx, bf16[3,320,1024]{2,1,0:T(8,128)(2,1)} %get-tuple-element.198.grad_q.rest_0_, ...), custom_call_target="tpu_custom_call", output_to_operand_aliasing={{0}: (11, {}), {1}: (12, {}), {2}: (13, {})} | custom-call | flops 2013265920 | bytes 12845056 | tf_op jit(solution)/shard_map/pallas_call | solution.py:31
  417.2 10.4 %collective-permute-done.37.arrived = bf16[320,1024]{1,0:T(8,128)(2,1)S(1)} collective-permute-done((bf16[320,1024]{1,0:T(8,128)(2,1)}, bf16[320,1024]{1,0:T(8,128)(2,1)S(1)}, u32[]{:S(2)}, u32[]{:S(2)}) %collective-permute-start.37) | collective-permute-done | bytes 655392 | tf_op jit(solution)/shard_map/ppermute | solution.py:20
  428.5 17.4 %shard_map.218 = (bf16[3,320,1024]{2,1,0:T(8,128)(2,1)}, bf16[3,320,2816]{2,1,0:T(8,128)(2,1)}, bf16[3,320,2816]{2,1,0:T(8,128)(2,1)}, bf16[3,320,1024]{2,1,0:T(...) custom-call(s32[3]{0:T(128)} %pad_add_fusion.idx, ...), custom_call_target="tpu_custom_call", output_to_operand_aliasing={{0}: (11, {}), {1}: (12, {}), {2}: (13, {}), {3}: (14, {}),... | custom-call | flops 6207569920 | bytes 17301504 | tf_op jit(solution)/shard_map/pallas_call | solution.py:31
  445.8 7.0 %bitcast_convert_fusion = bf16[1024,2816]{1,0:T(8,128)(2,1)S(1)} fusion(bf16[2,320,1024]{2,1,0:T(8,128)(2,1)S(1)} %get-tuple-element.283, bf16[3,320,2816]{2,1,0:T(8,128)(2,1)} %get-tuple-element.218, s32[]{:T(128)S(6)} %select_n.249), kind=kOutput, calls=%fused_computation | convolution fusion | flops 3693871104 | bytes 10682372 | tf_op jit(solution)/shard_map/dot_general | solution.py:1152
  487.7 7.1 %convolution_convert_fusion.1 = bf16[2816,1024]{1,0:T(8,128)(2,1)S(1)} fusion(bf16[640,2816]{1,0:T(8,128)(2,1)} %bitcast.277, bf16[640,1024]{1,0:T(8,128)(2,1)} %bitcast.282), kind=kOutput, calls=%fused_computation.6 | convolution fusion | flops 3693871104 | bytes 10682368 | tf_op jit(solution)/shard_map/dot_general | solution.py:1152
  502.3 11.2 %shard_map.219 = (bf16[3,320,1024]{2,1,0:T(8,128)(2,1)}, f32[2,320,1024]{2,1,0:T(8,128)}, bf16[2,128,1024]{2,1,0:T(8,128)(2,1)}, bf16[2,128,1024]{2,1,0:T(8,128)(2,1)}) custom-call(s32[3]{0:T(128)} %pad_add_fusion.idx, bf16[3,320,1024]{2,1,0:T(8,128)(2,1)} %get-tuple-element.177.q, ...), custom_call_target="tpu_custom_call", output_to_operand_aliasing={{0}: (8, {})} | custom-call | flops 5033164800 | bytes 7864320 | tf_op jit(solution)/shard_map/pallas_call | solution.py:31
  521.1 17.4 %collective-permute-start.46 = (bf16[256,2816]{1,0:T(8,128)(2,1)}, bf16[256,2816]{1,0:T(8,128)(2,1)}, u32[]{:S(2)}, u32[]{:S(2)}) collective-permute-start(bf16[256,2816]{1,0:T(8,128)(2,1)} %fusion.13), channel_id=1, source_target_pairs={{0,8},{4,12},{8,0},{12,4},{1,9},{5,13},{9,1},{13,5},{2,10},{6,14},... | collective-permute-start | bytes 4325384 | tf_op jit(solution)/shard_map/ppermute | solution.py:866
  545.6 8.9 %shard_map.220 = (bf16[3,320,1024]{2,1,0:T(8,128)(2,1)}, bf16[3,320,1024]{2,1,0:T(8,128)(2,1)}, f32[3,8,1024]{2,1,0:T(8,128)}, bf16[320,1024]{1,0:T(8,128)(2,1)}) custom-call(s32[3]{0:T(128)} %pad_add_fusion.idx, bf16[3,320,1024]{2,1,0:T(8,128)(2,1)} %get-tuple-element.227.grad_q, ...), custom_call_target="tpu_custom_call", output_to_operand_aliasing={{0}: (11, {}), {1}: (12, {}), {2}: (13, {})} | custom-call | flops 2013265920 | bytes 12845056 | tf_op jit(solution)/shard_map/pallas_call | solution.py:31
  585.2 24.1 %collective-permute-done.49 = bf16[704,1024]{1,0:T(8,128)(2,1)} collective-permute-done((bf16[704,1024]{1,0:T(8,128)(2,1)}, bf16[704,1024]{1,0:T(8,128)(2,1)}, u32[]{:S(2)}, u32[]{:S(2)}) %collective-permute-start.49) | collective-permute-done | bytes 1441824 | tf_op jit(solution)/shard_map/ppermute | solution.py:866
  622.3 9.3 %collective-permute-done.50 = bf16[64,3200]{1,0:T(8,128)(2,1)} collective-permute-done((bf16[64,3200]{1,0:T(8,128)(2,1)}, bf16[64,3200]{1,0:T(8,128)(2,1)}, u32[]{:S(2)}, u32[]{:S(2)}) %collective-permute-start.50) | collective-permute-done | bytes 409632 | tf_op jit(solution)/shard_map/ppermute | solution.py:866
  631.6 11.4 %collective-permute-done.48 = bf16[64,3200]{1,0:T(8,128)(2,1)} collective-permute-done((bf16[64,3200]{1,0:T(8,128)(2,1)}, bf16[64,3200]{1,0:T(8,128)(2,1)}, u32[]{:S(2)}, u32[]{:S(2)}) %collective-permute-start.48) | collective-permute-done | bytes 409632 | tf_op jit(solution)/shard_map/ppermute | solution.py:866
  (290 shorter events, 264.8 us)
Async XLA Ops:
  7.2 46.5 %all-gather.4.cloned.1.call-start = ((), (), s32[]{:S(2)}) async-start(), calls=%async_computation.4 | async-start | bytes 1802240 | tf_op jit(solution)/shard_map/all_gather | solution.py:889
  7.9 118.5 %all-gather.6.cloned.1.call-start = ((), (), s32[]{:S(2)}) async-start(), calls=%async_computation.5 | async-start | bytes 1802240 | tf_op jit(solution)/shard_map/all_gather | solution.py:889
  12.4 24.1 %collective-permute-start.3 = (bf16[272,1024]{1,0:T(8,128)(2,1)S(1)}, bf16[272,1024]{1,0:T(8,128)(2,1)S(1)}, u32[]{:S(2)}, u32[]{:S(2)}) collective-permute-start(bf16[272,1024]{1,0:T(8,128)(2,1)S(1)} %fusion.47.refs_0_), channel_id=1, source_target_pairs={{0,1},{1,2},{2,3},{3,0},{4,5},{5,6},{6,7},{7,4},{8,9},{9,10},{10,1... | collective-permute-start | bytes 1671176 | tf_op jit(solution)/shard_map/ppermute | solution.py:866
  15.4 150.1 %all-gather.8.cloned.1.call-start = ((), (), s32[]{:S(2)}) async-start(), calls=%async_computation.6 | async-start | bytes 1802240 | tf_op jit(solution)/shard_map/all_gather | solution.py:889
  53.6 53.3 %collective-permute-start.13 = (bf16[4,64,2816]{2,1,0:T(8,128)(2,1)}, bf16[4,64,2816]{2,1,0:T(8,128)(2,1)}, u32[]{:S(2)}, u32[]{:S(2)}) collective-permute-start(bf16[4,64,2816]{2,1,0:T(8,128)(2,1)} %all-gather.4.cloned.1.call-done.refs_0_), channel_id=1, source_target_pairs={{0,8},{4,12},{8,0},{12,4},{1,9},{5,13},{9,1},{13,5},{2,10},{6,14},... | collective-permute-start | bytes 4325384 | tf_op jit(solution)/shard_map/ppermute | solution.py:866
  55.2 21.9 %collective-permute-start.7 = (bf16[272,1024]{1,0:T(8,128)(2,1)S(1)}, bf16[272,1024]{1,0:T(8,128)(2,1)S(1)}, u32[]{:S(2)}, u32[]{:S(2)}) collective-permute-start(bf16[272,1024]{1,0:T(8,128)(2,1)S(1)} %collective-permute-done.3.refs_4_), channel_id=1, source_target_pairs={{0,1},{1,2},{2,3},{3,0},{4,5},{5,6},{6,7},{7,4},{8,9},{9,10},{10,1... | collective-permute-start | bytes 1671176 | tf_op jit(solution)/shard_map/ppermute | solution.py:866
  55.2 44.2 %collective-permute-start.1 = (bf16[272,1024]{1,0:T(8,128)(2,1)S(1)}, bf16[272,1024]{1,0:T(8,128)(2,1)S(1)}, u32[]{:S(2)}, u32[]{:S(2)}) collective-permute-start(bf16[272,1024]{1,0:T(8,128)(2,1)S(1)} %fusion.47.refs_0_), channel_id=1, source_target_pairs={{0,8},{4,12},{8,0},{12,4},{1,9},{5,13},{9,1},{13,5},{2,10},{6,14},... | collective-permute-start | bytes 1671176 | tf_op jit(solution)/shard_map/ppermute | solution.py:866
  77.0 29.4 %collective-permute-start.11 = (bf16[272,1024]{1,0:T(8,128)(2,1)S(1)}, bf16[272,1024]{1,0:T(8,128)(2,1)S(1)}, u32[]{:S(2)}, u32[]{:S(2)}) collective-permute-start(bf16[272,1024]{1,0:T(8,128)(2,1)S(1)} %collective-permute-done.7.refs_8_), channel_id=1, source_target_pairs={{0,1},{1,2},{2,3},{3,0},{4,5},{5,6},{6,7},{7,4},{8,9},{9,10},{10,1... | collective-permute-start | bytes 1671176 | tf_op jit(solution)/shard_map/ppermute | solution.py:866
  80.2 28.3 %collective-permute-start = (bf16[272,1024]{1,0:T(8,128)(2,1)S(1)}, bf16[272,1024]{1,0:T(8,128)(2,1)}, u32[]{:S(2)}, u32[]{:S(2)}) collective-permute-start(bf16[272,1024]{1,0:T(8,128)(2,1)S(1)} %fusion.47.refs_0_), channel_id=1, source_target_pairs={{0,4},{4,0},{8,12},{12,8},{1,5},{5,1},{9,13},{13,9},{2,6},{6,2},{1... | collective-permute-start | bytes 1671176 | tf_op jit(solution)/shard_map/ppermute | solution.py:866
  80.2 498.2 %reduce-scatter.5.cloned.1.call-start = ((), (), s32[]{:S(2)}) async-start(), calls=%async_computation.7 | async-start | bytes 1310720 | tf_op jit(solution)/shard_map/reduce_scatter | solution.py:999
  80.3 28.3 %collective-permute-start.4 = (bf16[272,1024]{1,0:T(8,128)(2,1)S(1)}, bf16[272,1024]{1,0:T(8,128)(2,1)S(1)}, u32[]{:S(2)}, u32[]{:S(2)}) collective-permute-start(bf16[272,1024]{1,0:T(8,128)(2,1)S(1)} %collective-permute-done.3.refs_4_), channel_id=1, source_target_pairs={{0,4},{4,0},{8,12},{12,8},{1,5},{5,1},{9,13},{13,9},{2,6},{6,2},{1... | collective-permute-start | bytes 1671176 | tf_op jit(solution)/shard_map/ppermute | solution.py:866
  107.0 19.5 %collective-permute-start.14 = (bf16[272,1024]{1,0:T(8,128)(2,1)S(1)}, bf16[272,1024]{1,0:T(8,128)(2,1)}, u32[]{:S(2)}, u32[]{:S(2)}) collective-permute-start(bf16[272,1024]{1,0:T(8,128)(2,1)S(1)} %collective-permute-done.11.refs_12_), channel_id=1, source_target_pairs={{0,8},{4,12},{8,0},{12,4},{1,9},{5,13},{9,1},{13,5},{2,10},{6,14},... | collective-permute-start | bytes 1671176 | tf_op jit(solution)/shard_map/ppermute | solution.py:866
  109.3 21.8 %collective-permute-start.6 = (bf16[272,1024]{1,0:T(8,128)(2,1)S(1)}, bf16[272,1024]{1,0:T(8,128)(2,1)}, u32[]{:S(2)}, u32[]{:S(2)}) collective-permute-start(bf16[272,1024]{1,0:T(8,128)(2,1)S(1)} %collective-permute-done.5.refs_6_), channel_id=1, source_target_pairs={{0,4},{4,0},{8,12},{12,8},{1,5},{5,1},{9,13},{13,9},{2,6},{6,2},{1... | collective-permute-start | bytes 1671176 | tf_op jit(solution)/shard_map/ppermute | solution.py:866
  110.6 20.5 %collective-permute-start.12 = (bf16[272,1024]{1,0:T(8,128)(2,1)S(1)}, bf16[272,1024]{1,0:T(8,128)(2,1)}, u32[]{:S(2)}, u32[]{:S(2)}) collective-permute-start(bf16[272,1024]{1,0:T(8,128)(2,1)S(1)} %collective-permute-done.11.refs_12_), channel_id=1, source_target_pairs={{0,4},{4,0},{8,12},{12,8},{1,5},{5,1},{9,13},{13,9},{2,6},{6,2},{1... | collective-permute-start | bytes 1671176 | tf_op jit(solution)/shard_map/ppermute | solution.py:866
  126.4 34.3 %collective-permute-start.16 = (bf16[4,64,2816]{2,1,0:T(8,128)(2,1)}, bf16[4,64,2816]{2,1,0:T(8,128)(2,1)}, u32[]{:S(2)}, u32[]{:S(2)}) collective-permute-start(bf16[4,64,2816]{2,1,0:T(8,128)(2,1)} %all-gather.6.cloned.1.call-done.refs_0_), channel_id=1, source_target_pairs={{0,8},{4,12},{8,0},{12,4},{1,9},{5,13},{9,1},{13,5},{2,10},{6,14},... | collective-permute-start | bytes 4325384 | tf_op jit(solution)/shard_map/ppermute | solution.py:866
  152.3 31.2 %collective-permute-start.21 = (bf16[4,64,2816]{2,1,0:T(8,128)(2,1)S(1)}, bf16[4,64,2816]{2,1,0:T(8,128)(2,1)}, u32[]{:S(2)}, u32[]{:S(2)}) collective-permute-start(bf16[4,64,2816]{2,1,0:T(8,128)(2,1)S(1)} %copy-done.4), channel_id=1, source_target_pairs={{0,4},{4,0},{8,12},{12,8},{1,5},{5,1},{9,13},{13,9},{2,6},{6,2},{1... | collective-permute-start | bytes 4325384 | tf_op jit(solution)/shard_map/ppermute | solution.py:866
  153.5 35.8 %collective-permute-start.19 = (bf16[4,64,2816]{2,1,0:T(8,128)(2,1)S(1)}, bf16[4,64,2816]{2,1,0:T(8,128)(2,1)}, u32[]{:S(2)}, u32[]{:S(2)}) collective-permute-start(bf16[4,64,2816]{2,1,0:T(8,128)(2,1)S(1)} %copy-done.3), channel_id=1, source_target_pairs={{0,4},{4,0},{8,12},{12,8},{1,5},{5,1},{9,13},{13,9},{2,6},{6,2},{1... | collective-permute-start | bytes 4325384 | tf_op jit(solution)/shard_map/ppermute | solution.py:866
  160.8 23.0 %collective-permute-start.22 = (bf16[4,64,2816]{2,1,0:T(8,128)(2,1)}, bf16[4,64,2816]{2,1,0:T(8,128)(2,1)}, u32[]{:S(2)}, u32[]{:S(2)}) collective-permute-start(bf16[4,64,2816]{2,1,0:T(8,128)(2,1)} %collective-permute-done.16.refs_2_), channel_id=1, source_target_pairs={{0,4},{4,0},{8,12},{12,8},{1,5},{5,1},{9,13},{13,9},{2,6},{6,2},{1... | collective-permute-start | bytes 4325384 | tf_op jit(solution)/shard_map/ppermute | solution.py:866
  160.8 28.5 %collective-permute-start.20 = (bf16[4,64,2816]{2,1,0:T(8,128)(2,1)}, bf16[4,64,2816]{2,1,0:T(8,128)(2,1)}, u32[]{:S(2)}, u32[]{:S(2)}) collective-permute-start(bf16[4,64,2816]{2,1,0:T(8,128)(2,1)} %collective-permute-done.13.refs_2_), channel_id=1, source_target_pairs={{0,4},{4,0},{8,12},{12,8},{1,5},{5,1},{9,13},{13,9},{2,6},{6,2},{1... | collective-permute-start | bytes 4325384 | tf_op jit(solution)/shard_map/ppermute | solution.py:866
  165.5 34.9 %collective-permute-start.24 = (bf16[4,176,1024]{2,1,0:T(8,128)(2,1)}, bf16[4,176,1024]{2,1,0:T(8,128)(2,1)}, u32[]{:S(2)}, u32[]{:S(2)}) collective-permute-start(bf16[4,176,1024]{2,1,0:T(8,128)(2,1)} %all-gather.8.cloned.1.call-done.refs_0_), channel_id=1, source_target_pairs={{0,8},{4,12},{8,0},{12,4},{1,9},{5,13},{9,1},{13,5},{2,10},{6,14},... | collective-permute-start | bytes 4325384 | tf_op jit(solution)/shard_map/ppermute | solution.py:866
  324.9 20.1 %collective-permute-start.34 = (bf16[320,1024]{1,0:T(8,128)(2,1)}, bf16[320,1024]{1,0:T(8,128)(2,1)S(1)}, u32[]{:S(2)}, u32[]{:S(2)}) collective-permute-start(bf16[320,1024]{1,0:T(8,128)(2,1)} %get-tuple-element.174), channel_id=1, source_target_pairs={{16,0},{17,1},{18,2},{19,3},{20,4},{21,5},{22,6},{23,7},{24,8},{25... | collective-permute-start | bytes 1966088 | tf_op jit(solution)/shard_map/ppermute | solution.py:20
  457.1 27.4 %collective-permute-start.38 = (bf16[2,256,2816]{2,1,0:T(8,128)(2,1)}, bf16[2,256,2816]{2,1,0:T(8,128)(2,1)}, u32[]{:S(2)}, u32[]{:S(2)}) collective-permute-start(bf16[2,256,2816]{2,1,0:T(8,128)(2,1)} %dynamic-slice_bitcast_fusion.3), channel_id=1, source_target_pairs={{0,4},{4,0},{8,12},{12,8},{1,5},{5,1},{9,13},{13,9},{2,6},{6,2},{1... | collective-permute-start | bytes 8650760 | tf_op jit(solution)/shard_map/ppermute | solution.py:866
  476.9 21.6 %collective-permute-start.40 = (bf16[2,256,2816]{2,1,0:T(8,128)(2,1)}, bf16[2,256,2816]{2,1,0:T(8,128)(2,1)S(1)}, u32[]{:S(2)}, u32[]{:S(2)}) collective-permute-start(bf16[2,256,2816]{2,1,0:T(8,128)(2,1)} %dynamic-slice_bitcast_fusion.2), channel_id=1, source_target_pairs={{0,4},{4,0},{8,12},{12,8},{1,5},{5,1},{9,13},{13,9},{2,6},{6,2},{1... | collective-permute-start | bytes 8650760 | tf_op jit(solution)/shard_map/ppermute | solution.py:866
  498.2 43.8 %collective-permute-start.42 = (bf16[2,704,1024]{2,1,0:T(8,128)(2,1)}, bf16[2,704,1024]{2,1,0:T(8,128)(2,1)}, u32[]{:S(2)}, u32[]{:S(2)}) collective-permute-start(bf16[2,704,1024]{2,1,0:T(8,128)(2,1)} %dynamic-slice_bitcast_fusion.1), channel_id=1, source_target_pairs={{0,4},{4,0},{8,12},{12,8},{1,5},{5,1},{9,13},{13,9},{2,6},{6,2},{1... | collective-permute-start | bytes 8650760 | tf_op jit(solution)/shard_map/ppermute | solution.py:866
  498.2 122.2 %reduce-scatter.7.cloned.1.call-start = ((), (), s32[]{:S(2)}) async-start(), calls=%async_computation.8 | async-start | bytes 1802240 | tf_op jit(solution)/shard_map/reduce_scatter | solution.py:1030
  498.3 40.2 %collective-permute-start.41 = (bf16[256,2816]{1,0:T(8,128)(2,1)}, bf16[256,2816]{1,0:T(8,128)(2,1)S(1)}, u32[]{:S(2)}, u32[]{:S(2)}) collective-permute-start(bf16[256,2816]{1,0:T(8,128)(2,1)} %fusion.14), channel_id=1, source_target_pairs={{0,8},{4,12},{8,0},{12,4},{1,9},{5,13},{9,1},{13,5},{2,10},{6,14},... | collective-permute-start | bytes 4325384 | tf_op jit(solution)/shard_map/ppermute | solution.py:866
  521.1 49.7 %collective-permute-start.46 = (bf16[256,2816]{1,0:T(8,128)(2,1)}, bf16[256,2816]{1,0:T(8,128)(2,1)}, u32[]{:S(2)}, u32[]{:S(2)}) collective-permute-start(bf16[256,2816]{1,0:T(8,128)(2,1)} %fusion.13), channel_id=1, source_target_pairs={{0,8},{4,12},{8,0},{12,4},{1,9},{5,13},{9,1},{13,5},{2,10},{6,14},... | collective-permute-start | bytes 4325384 | tf_op jit(solution)/shard_map/ppermute | solution.py:866
  541.9 110.9 %reduce-scatter.9.cloned.1.call-start = ((), (), s32[]{:S(2)}) async-start(), calls=%async_computation.9 | async-start | bytes 1802240 | tf_op jit(solution)/shard_map/reduce_scatter | solution.py:1030
  574.4 93.9 %reduce-scatter.11.cloned.1.call-start = ((), (), s32[]{:S(2)}) async-start(), calls=%async_computation.10 | async-start | bytes 1802240 | tf_op jit(solution)/shard_map/reduce_scatter | solution.py:1030
  574.5 34.8 %collective-permute-start.49 = (bf16[704,1024]{1,0:T(8,128)(2,1)}, bf16[704,1024]{1,0:T(8,128)(2,1)}, u32[]{:S(2)}, u32[]{:S(2)}) collective-permute-start(bf16[704,1024]{1,0:T(8,128)(2,1)} %fusion.11), channel_id=1, source_target_pairs={{0,8},{4,12},{8,0},{12,4},{1,9},{5,13},{9,1},{13,5},{2,10},{6,14},... | collective-permute-start | bytes 4325384 | tf_op jit(solution)/shard_map/ppermute | solution.py:866
  583.3 34.5 %collective-permute-start.47 = (bf16[64,3200]{1,0:T(8,128)(2,1)}, bf16[64,3200]{1,0:T(8,128)(2,1)}, u32[]{:S(2)}, u32[]{:S(2)}) collective-permute-start(bf16[64,3200]{1,0:T(8,128)(2,1)} %fusion.28), channel_id=1, source_target_pairs={{0,8},{4,12},{8,0},{12,4},{1,9},{5,13},{9,1},{13,5},{2,10},{6,14},... | collective-permute-start | bytes 1228808 | tf_op jit(solution)/shard_map/ppermute | solution.py:866
  620.4 22.6 %collective-permute-start.48 = (bf16[64,3200]{1,0:T(8,128)(2,1)}, bf16[64,3200]{1,0:T(8,128)(2,1)}, u32[]{:S(2)}, u32[]{:S(2)}) collective-permute-start(bf16[64,3200]{1,0:T(8,128)(2,1)} %get-tuple-element.264), channel_id=1, source_target_pairs={{0,1},{1,2},{2,3},{3,0},{4,5},{5,6},{6,7},{7,4},{8,9},{9,10},{10,1... | collective-permute-start | bytes 1228808 | tf_op jit(solution)/shard_map/ppermute | solution.py:866
  (77 other events, 629.2 us)
Sparse Core Ops, SparseCore 0:
  9.6 44.0 all-gather.3
  55.2 50.2 all-gather.5
  107.1 33.1 all-gather.7
  498.3 26.2 reduce-scatter.4
  542.1 32.5 reduce-scatter.6
  576.9 32.0 reduce-scatter.8
  613.7 42.1 reduce-scatter.10
